TPU v7x, 128 devices: a whole 4x4x4 slice. The times are simulated.
128 devices in a mesh: mp: 2 (over core), batch: 8 (over z, x_lo), vocab: 8 (over y, x_hi).
Axes of the slice: x: 4 (x_hi: 2, x_lo: 2; x = x_hi * 2 + x_lo), y: 4, z: 4, core: 2. Of those that a mesh axis runs over, the one named last changes fastest.
Arguments:
- hidden_teacher: bfloat16 [512, 4608], P(('batch', 'vocab'), 'mp'), may hold values from -6 to 6
- hidden_student: bfloat16 [512, 3584], P(('batch', 'vocab'), 'mp'), may hold values from -6 to 6
- teacher_weight: bfloat16 [4608, 131072], P('mp', ('batch', 'vocab')), may hold values from -0.4375 to 0.4375
- student_weight: bfloat16 [3584, 131072], P('mp', ('batch', 'vocab')), may hold values from -0.5 to 0.5
- token_weight: float32 [512], replicated, may hold values from 4 to 40
Outputs:
- divergence: float32 [512], replicated
- grad_hidden: bfloat16 [512, 3584], P(('batch', 'vocab'), 'mp')
- grad_weight: bfloat16 [3584, 131072], P('mp', ('batch', 'vocab'))
All inputs are finite; a program needn't handle non-finite values.
Results may differ from a plain program's by a relative error of at most 0.005.
Values may be sent and summed in bfloat16 or wider, within the bound.
No kernel may reach another device: no remote copies, remote signals or barrier semaphores. Data moves between devices by JAX's collectives and lax.ppermute only.
A program may use at most 128 MiB of HBM per device.

v0:
```python
import jax
import jax.numpy as jnp
from jax import lax
from jax.sharding import PartitionSpec as P

softcap_limit = 30.0


def capped(values):
    return softcap_limit * jnp.tanh(values / softcap_limit)


def statistics(teacher_raw, student_raw):
    teacher_capped = capped(teacher_raw)
    student_capped = capped(student_raw)
    teacher_exp = jnp.exp(teacher_capped - softcap_limit)
    student_exp = jnp.exp(student_capped - softcap_limit)
    sums = (
        jnp.sum(teacher_exp, axis=1),
        jnp.sum(student_exp, axis=1),
        jnp.sum(teacher_exp * (teacher_capped - student_capped), axis=1),
    )
    return (teacher_exp, student_exp, student_capped, sums)


def finish(teacher_exp, student_exp, student_capped, totals, token_weight):
    teacher_total, student_total, cross = totals
    divergence = cross / teacher_total - jnp.log(teacher_total) + jnp.log(student_total)
    slope = 1.0 - (student_capped / softcap_limit) ** 2
    probs_gap = student_exp / student_total[:, None] - teacher_exp / teacher_total[:, None]
    gap = (token_weight[:, None] * probs_gap * slope).astype(jnp.bfloat16)
    return (divergence, gap)


def local(hidden_teacher, hidden_student, teacher_weight, student_weight, token_weight):
    teacher_rows, student_rows = (
        lax.all_gather(hidden_teacher, ("batch", "vocab"), axis=0, tiled=True),
        lax.all_gather(hidden_student, ("batch", "vocab"), axis=0, tiled=True),
    )
    teacher_raw = jnp.dot(teacher_rows, teacher_weight, preferred_element_type=jnp.float32)
    student_raw = jnp.dot(student_rows, student_weight, preferred_element_type=jnp.float32)
    teacher_raw, student_raw = lax.psum((teacher_raw, student_raw), "mp")
    teacher_exp, student_exp, student_capped, sums = statistics(teacher_raw, student_raw)
    totals = lax.psum((sums[0], sums[1], sums[2]), ("batch", "vocab"))
    divergence, gap = finish(teacher_exp, student_exp, student_capped, totals, token_weight)
    grad_hidden = lax.psum_scatter(
        lax.dot_general(
            gap, student_weight, (((1,), (1,)), ((), ())), preferred_element_type=jnp.float32
        ),
        ("batch", "vocab"),
        scatter_dimension=0,
        tiled=True,
    ).astype(jnp.bfloat16)
    grad_weight = lax.dot_general(
        student_rows, gap, (((0,), (0,)), ((), ())), preferred_element_type=jnp.float32
    ).astype(jnp.bfloat16)
    return (divergence, grad_hidden, grad_weight)


def solution(mesh):
    placed = (
        P(("batch", "vocab"), "mp"),
        P(("batch", "vocab"), "mp"),
        P("mp", ("batch", "vocab")),
        P("mp", ("batch", "vocab")),
        P(),
    )
    return jax.shard_map(
        local,
        mesh=mesh,
        in_specs=placed,
        out_specs=(P(), P(("batch", "vocab"), "mp"), P("mp", ("batch", "vocab"))),
        check_vma=False,
    )
```

profile of v0, /device:TPU:0, one launch (start us, length us, event | category | flops | bytes accessed | tf_op | source)
XLA Modules:
  0.0 1291.6 jit_solution(10526508814470170677)
XLA Ops:
  7.2 0.0 all-gather.5.cloned.1.call-start
  7.2 0.7 all-gather.5.cloned.1.call-update
  7.9 0.0 all-gather.3.cloned.1.call-start
  7.9 0.7 all-gather.3.cloned.1.call-update
  8.6 0.0 all-reduce.4.cloned.1.call-start
  8.7 335.2 %all-gather.5.cloned.1.call-done = bf16[512,1792]{1,0:T(8,128)(2,1)} async-done(((bf16[8,1792]{1,0:T(8,128)(2,1)}), bf16[512,1792]{1,0:T(8,128)(2,1)}) %all-gather.5.cloned.1.call-update) | async-done | bytes 1835024 | tf_op jit(solution)/shard_map/all_gather | solution.py:38
  343.9 9.6 fusion.4
  353.5 323.8 %all-gather.3.cloned.1.call-done = bf16[512,2304]{1,0:T(8,128)(2,1)} async-done(((bf16[8,2304]{1,0:T(8,128)(2,1)}), bf16[512,2304]{1,0:T(8,128)(2,1)}) %all-gather.3.cloned.1.call-update) | async-done | bytes 2359312 | tf_op jit(solution)/shard_map/all_gather | solution.py:37
  677.4 9.7 fusion.3
  687.0 0.0 all-reduce.4.cloned.1.call-update
  687.1 0.0 reduce-scatter.2.cloned.1.call-start
  687.1 43.0 %all-reduce.4.cloned.1.call-done = (f32[512,2048]{1,0:T(8,128)}, f32[512,2048]{1,0:T(8,128)}) async-done(((f32[512,2048]{1,0:T(8,128)}, f32[512,2048]{1,0:T(8,128)}), (f32[512,2048]{1,0:T(8,128)}, f32[512,2048]{1,0:T(8,128)})) %all-reduce.4.cloned.1.call-update) | async-done | bytes 8388624 | tf_op jit(solution)/shard_map/psum | solution.py:42
  730.1 0.0 copy-start
  730.1 6.0 multiply_reduce_fusion
  736.1 181.4 %all-reduce = (f32[512]{0:T(512)S(1)}, f32[512]{0:T(512)S(1)}, f32[512]{0:T(512)S(1)}) all-reduce(f32[512]{0:T(512)S(1)} %get-tuple-element.8, f32[512]{0:T(512)S(1)} %get-tuple-element.7, f32[512]{0:T(512)S(1)} %get-tuple-element.6), channel_id=1, replica_groups=mesh['mp'=2,'batch'=8,'vocab'=8] {'batch','vocab'}, use_global_device_ids=true, to_apply=%region_7.0 | all-reduce | flops 1536 | bytes 12288 | tf_op jit(solution)/shard_map/psum | solution.py:44
  917.5 0.0 copy-done
  917.5 5.4 multiply_convert_fusion
  922.9 9.0 fusion.5
  931.9 0.0 reduce-scatter.2.cloned.1.call-update
  931.9 7.6 fusion
  939.5 10.4 copy.8
  949.9 0.6 log_add_fusion
  950.5 333.1 %reduce-scatter.2.cloned.1.call-done = f32[8,1792]{1,0:T(8,128)} async-done(((f32[512,1792]{1,0:T(8,128)}), f32[8,1792]{1,0:T(8,128)}) %reduce-scatter.2.cloned.1.call-update) | async-done | bytes 57360 | tf_op jit(solution)/shard_map/reduce_scatter | solution.py:46
  1283.6 1.4 convert_element_type.13
Async XLA Ops:
  7.2 336.7 %all-gather.5.cloned.1.call-start = ((), (), s32[]{:S(2)}) async-start(), calls=%async_computation.2 | async-start | bytes 1863680 | tf_op jit(solution)/shard_map/all_gather | solution.py:38
  7.9 669.5 %all-gather.3.cloned.1.call-start = ((), (), s32[]{:S(2)}) async-start(), calls=%async_computation.1 | async-start | bytes 2396160 | tf_op jit(solution)/shard_map/all_gather | solution.py:37
  8.6 721.4 %all-reduce.4.cloned.1.call-start = ((), (), s32[]{:S(2)}) async-start(), calls=%async_computation.4 | async-start | bytes 16777216 | tf_op jit(solution)/shard_map/psum | solution.py:42
  687.1 596.6 %reduce-scatter.2.cloned.1.call-start = ((), (), s32[]{:S(2)}) async-start(), calls=%async_computation.3 | async-start | bytes 3727360 | tf_op jit(solution)/shard_map/reduce_scatter | solution.py:46
  730.1 187.4 %copy-start = (f32[512]{0:T(512)S(1)}, f32[512]{0:T(512)}, u32[]{:S(2)}) copy-start(f32[512]{0:T(512)} %param.9) | copy-start | bytes 6148
Sparse Core Ops, SparseCore 0:
  9.6 334.2 all-gather.4
  345.5 331.7 all-gather.2
  687.2 42.8 all-reduce.3
  932.0 351.5 reduce-scatter.1
where the time goes:
time: 1290 us
  waiting for transfers between devices  1040 us (81%)
  blocking collectives  181 us (14%)
  matrix products  35.9 us (3%)
  between operations  13.8 us (1%)
  other arithmetic  13.4 us (1%)
    all_gather x1, waiting for transfers between devices, local(): lax.all_gather(hidden_student, ('batch', 'vocab'), axis=0, tiled=True)  335 us
    reduce_scatter x1, waiting for transfers between devices, local(): lax.psum_scatter(lax.dot_general(gap, student_weight, (((1,), (1,)), ((),...  333 us
    all_gather x1, waiting for transfers between devices, local(): lax.all_gather(hidden_teacher, ('batch', 'vocab'), axis=0, tiled=True)  324 us
    psum x1, blocking collectives, local(): totals = lax.psum((sums[0], sums[1], sums[2]), ('batch', 'vocab'))  181 us
    psum x1, waiting for transfers between devices, local(): teacher_raw, student_raw = lax.psum((teacher_raw, student_raw), 'mp')  43 us
  transfers between devices with their start and end apart: 4, of which 4 were waited for; matrix products, arithmetic and copies ran while one was open for 2% of the time, Pallas kernels for 0%

commit v1 on v0

v1 whole, which is shorter than its diff:
```python
import functools

import jax
import jax.numpy as jnp
import numpy as np
from jax import lax
from jax.experimental import pallas as pl
from jax.experimental.pallas import tpu as pltpu
from jax.sharding import PartitionSpec as P

softcap_limit = 30.0
tokens, teacher_width, student_width, vocab_local = 512, 2304, 1792, 2048
width = teacher_width + student_width
half = tokens // 2
everyone = ("mp", "batch", "vocab")
chips = ("batch", "vocab")
mega = 1024 * 1024

offsets = (0, 1, 3, 2)
stage_axes = (("y", "x"), ("x", "z"), ("z", "y"))


def place(index):
    core, z, x_lo, y, x_hi = np.unravel_index(index, (2, 4, 2, 4, 2))
    return {"core": int(core), "x": int(2 * x_hi + x_lo), "y": int(y), "z": int(z)}


def index_of(at):
    return int(
        np.ravel_multi_index(
            (at["core"], at["z"], at["x"] % 2, at["y"], at["x"] // 2), (2, 4, 2, 4, 2)
        )
    )


def moved(at, axis, by):
    return {**at, axis: (at[axis] + by) % 4}


def ring(axes, by):
    pairs = []
    for source in range(128):
        at = place(source)
        pairs.append((source, index_of(moved(at, axes[at["core"]], by))))
    return pairs


def send(block, axes, by):
    return lax.ppermute(block, everyone, ring(axes, by))


def swap(block):
    return lax.ppermute(block, "mp", [(0, 1), (1, 0)])


def row_table():
    table = np.zeros((128, 64), np.int32)
    for device in range(128):
        at = place(device)
        core = at["core"]
        for slot in range(64):
            owner = at
            for stage, digit in enumerate((slot % 4, slot // 4 % 4, slot // 16)):
                owner = moved(owner, stage_axes[stage][core], -offsets[digit])
            table[device, slot] = (index_of(owner) % 64 - 32 * core) % 64
    return table


def forward_first(order, x0, x1, x2, x3, teacher, student, rows, own, other):
    @pl.when(pl.program_id(0) == 0)
    def _():
        step = 512
        for at in range(0, width, step):
            cols = slice(at, at + step)
            block = jnp.concatenate([x[:, cols] for x in (x0, x1, x2, x3)], axis=0)
            rows[:, cols] = jnp.dot(
                order[...], block, preferred_element_type=jnp.float32
            ).astype(jnp.bfloat16)

    logits(rows, teacher, student, own, other)


def logits(rows, teacher, student, own, other):
    raw = jnp.dot(rows[:, :teacher_width], teacher[...], preferred_element_type=jnp.float32)
    own[0], other[0] = raw[:half], raw[half:]
    raw = jnp.dot(rows[:, teacher_width:], student[...], preferred_element_type=jnp.float32)
    own[1], other[1] = raw[:half], raw[half:]


def whole():
    return pl.BlockSpec(memory_space=pltpu.VMEM)


def forward(rows, teacher_weight, student_weight, chunk, n_chunks, tile=256):
    steps = vocab_local // n_chunks // tile
    at = lambda j: (0, chunk * steps + j)
    weights = [
        pl.BlockSpec((teacher_width, tile), at),
        pl.BlockSpec((student_width, tile), at),
    ]
    out = pl.BlockSpec((2, half, tile), lambda j: (0, 0, j))
    shape = jax.ShapeDtypeStruct((2, half, steps * tile), jnp.float32)
    params = pltpu.CompilerParams(vmem_limit_bytes=40 * mega)
    if chunk == 0:
        return pl.pallas_call(
            forward_first,
            grid=(steps,),
            in_specs=[whole()] * 5 + weights,
            out_specs=[whole(), out, out],
            out_shape=[jax.ShapeDtypeStruct((tokens, width), jnp.bfloat16), shape, shape],
            compiler_params=params,
        )(*rows, teacher_weight, student_weight)
    return pl.pallas_call(
        logits,
        grid=(steps,),
        in_specs=[whole()] + weights,
        out_specs=[out, out],
        out_shape=[shape, shape],
        compiler_params=params,
    )(rows, teacher_weight, student_weight)


def statistics_kernel(own, other, student_part, teacher_part, sums):
    @pl.when(pl.program_id(0) == 0)
    def _():
        sums[...] = jnp.zeros_like(sums)

    def lanes(values):
        total = values[:, :128]
        for at in range(128, values.shape[1], 128):
            total += values[:, at : at + 128]
        return total

    teacher_tanh = jnp.tanh((own[0] + other[0]) * (1.0 / softcap_limit))
    student_tanh = jnp.tanh((own[1] + other[1]) * (1.0 / softcap_limit))
    teacher_exp = jnp.exp(softcap_limit * teacher_tanh - softcap_limit)
    student_exp = jnp.exp(softcap_limit * student_tanh - softcap_limit)
    slope = 1.0 - student_tanh * student_tanh
    student_part[...] = student_exp * slope
    teacher_part[...] = teacher_exp * slope
    sums[0] += lanes(teacher_exp)
    sums[1] += lanes(student_exp)
    sums[2] += lanes(teacher_exp * (softcap_limit * (teacher_tanh - student_tanh)))


def statistics(own, other, tile=256):
    cols = own.shape[2]
    raw = pl.BlockSpec((2, half, tile), lambda j: (0, 0, j))
    part = pl.BlockSpec((half, tile), lambda j: (0, j))
    shape = jax.ShapeDtypeStruct((half, cols), jnp.float32)
    return pl.pallas_call(
        statistics_kernel,
        grid=(cols // tile,),
        in_specs=[raw, raw],
        out_specs=[part, part, whole()],
        out_shape=[shape, shape, jax.ShapeDtypeStruct((3, half, 128), jnp.float32)],
        compiler_params=pltpu.CompilerParams(vmem_limit_bytes=24 * mega),
    )(own, other)


def grad_hidden_kernel(order, own, other, weight, keep, send1, send2, send3, gap):
    @pl.when(pl.program_id(0) == 0)
    def _():
        step = 512
        for at in range(0, vocab_local, step):
            cols = slice(at, at + step)
            block = jnp.concatenate([own[:, cols], other[:, cols]], axis=0)
            gap[:, cols] = lax.dot_general(
                order[...], block, (((0,), (0,)), ((), ())), preferred_element_type=jnp.float32
            ).astype(jnp.bfloat16)

    term = lax.dot_general(
        gap[...], weight[...], (((1,), (1,)), ((), ())), preferred_element_type=jnp.float32
    )
    keep[...] = term[:128]
    send1[...] = term[128:256].astype(jnp.bfloat16)
    send2[...] = term[256:384].astype(jnp.bfloat16)
    send3[...] = term[384:].astype(jnp.bfloat16)


def grad_hidden_term(order, own, other, weight, tile=256):
    out = pl.BlockSpec((128, tile), lambda j: (0, j))
    return pl.pallas_call(
        grad_hidden_kernel,
        grid=(student_width // tile,),
        in_specs=[whole()] * 3 + [pl.BlockSpec((tile, vocab_local), lambda j: (j, 0))],
        out_specs=[out] * 4,
        out_shape=[jax.ShapeDtypeStruct((128, student_width), jnp.float32)]
        + [jax.ShapeDtypeStruct((128, student_width), jnp.bfloat16)] * 3,
        scratch_shapes=[pltpu.VMEM((tokens, vocab_local), jnp.bfloat16)],
        compiler_params=pltpu.CompilerParams(vmem_limit_bytes=24 * mega),
    )(order, own, other, weight)


def grad_weight_kernel(rows, own, other, out):
    over_rows = (((0,), (0,)), ((), ()))
    out[...] = (
        lax.dot_general(rows[:half], own[...], over_rows, preferred_element_type=jnp.float32)
        + lax.dot_general(rows[half:], other[...], over_rows, preferred_element_type=jnp.float32)
    ).astype(jnp.bfloat16)


def grad_weight_of(rows, own, other, tile=256):
    first = teacher_width // tile
    return pl.pallas_call(
        grad_weight_kernel,
        grid=(student_width // tile,),
        in_specs=[pl.BlockSpec((tokens, tile), lambda j: (0, first + j)), whole(), whole()],
        out_specs=pl.BlockSpec((tile, vocab_local), lambda j: (j, 0)),
        out_shape=jax.ShapeDtypeStruct((student_width, vocab_local), jnp.bfloat16),
        compiler_params=pltpu.CompilerParams(vmem_limit_bytes=24 * mega),
    )(rows, own, other)


def local(hidden_teacher, hidden_student, teacher_weight, student_weight, token_weight):
    core = lax.axis_index("mp")
    places = jnp.asarray(row_table())[lax.axis_index(everyone)]
    places = jnp.repeat(places * 8, 8) + jnp.tile(jnp.arange(8), 64)
    order = (jnp.arange(tokens)[:, None] == places[None, :]).astype(jnp.bfloat16)

    block = jnp.concatenate([hidden_teacher, hidden_student], axis=1)
    for axes in stage_axes[:2]:
        block = jnp.concatenate([block] + [send(block, axes, by) for by in offsets[1:]], axis=0)
    blocks = [block] + [send(block, stage_axes[2], by) for by in offsets[1:]]

    rows, own0, other0 = forward((order, *blocks), teacher_weight, student_weight, 0, 2)
    other0 = swap(other0)
    own1, other1 = forward(rows, teacher_weight, student_weight, 1, 2)
    other1 = swap(other1)
    student_part0, teacher_part0, sums0 = statistics(own0, other0)
    student_part1, teacher_part1, sums1 = statistics(own1, other1)
    sums = jnp.sum(sums0 + sums1, axis=2).reshape(6, 128)
    shared = lax.all_to_all(jnp.broadcast_to(sums[None], (64, 6, 128)), chips, 0, 0)
    teacher_total, student_total, cross = jnp.sum(shared, axis=0).reshape(3, half)

    weight_here = lax.dynamic_slice_in_dim(token_weight, core * half, half)
    student_scale = (weight_here / student_total)[:, None]
    teacher_scale = (weight_here / teacher_total)[:, None]
    gap = jnp.concatenate(
        [
            (student_part0 * student_scale - teacher_part0 * teacher_scale).astype(jnp.bfloat16),
            (student_part1 * student_scale - teacher_part1 * teacher_scale).astype(jnp.bfloat16),
        ],
        axis=1,
    )
    gap_other = swap(gap)

    keep, *sends = grad_hidden_term(order, gap, gap_other, student_weight)
    received = [send(b, stage_axes[2], -by) for b, by in zip(sends, offsets[1:])]
    grad_weight = grad_weight_of(rows, gap, gap_other)
    total = keep + sum(r.astype(jnp.float32) for r in received)
    for axes in stage_axes[1::-1]:
        size = total.shape[0] // 4
        parts = [total[i * size : (i + 1) * size] for i in range(4)]
        received = [send(p, axes, -by) for p, by in zip(parts[1:], offsets[1:])]
        total = parts[0] + sum(received)
    grad_hidden = total.astype(jnp.bfloat16)

    divergence = cross / teacher_total - jnp.log(teacher_total) + jnp.log(student_total)
    divergence_other = swap(divergence)
    divergence = jnp.where(
        core == 0,
        jnp.concatenate([divergence, divergence_other]),
        jnp.concatenate([divergence_other, divergence]),
    )
    return (divergence, grad_hidden, grad_weight)


def solution(mesh):
    placed = (
        P(("batch", "vocab"), "mp"),
        P(("batch", "vocab"), "mp"),
        P("mp", ("batch", "vocab")),
        P("mp", ("batch", "vocab")),
        P(),
    )
    return jax.shard_map(
        local,
        mesh=mesh,
        in_specs=placed,
        out_specs=(P(), P(("batch", "vocab"), "mp"), P("mp", ("batch", "vocab"))),
        check_vma=False,
    )
```

time: 1290 us -> 155 us (0.12)
  waiting for transfers between devices: 1040 us -> 65.9 us
  blocking collectives: 181 us -> 0 us
  matrix products: 35.9 us -> 0 us
  starting transfers between devices: 0.16 us -> 36 us
  Pallas kernels: 0 us -> 35.5 us
  between operations: 13.8 us -> 0.84 us
    all_gather x2 -> x0, waiting for transfers between devices: 659 us -> none  [the longest x1 335 us: local(): lax.all_gather(hidden_student, ('batch', 'vocab'), axis=0, tiled=True)]
    reduce_scatter x1 -> x0, waiting for transfers between devices: 333 us -> none  [local(): lax.psum_scatter(lax.dot_general(gap, student_weight, (((1,), (1,)), ((),...]
    psum x1 -> x0, blocking collectives: 181 us -> none  [local(): totals = lax.psum((sums[0], sums[1], sums[2]), ('batch', 'vocab'))]
    ppermute x0 -> x22, waiting for transfers between devices: none -> 55.2 us  [the longest x18 50 us: send(): return lax.ppermute(block, everyone, ring(axes, by))]
    psum x1 -> x0, waiting for transfers between devices: 43 us -> none  [local(): teacher_raw, student_raw = lax.psum((teacher_raw, student_raw), 'mp')]
    dot_general x4 -> x0, matrix products: 35.9 us -> none  [the longest x1 9.67 us: local(): jnp.dot(teacher_rows, teacher_weight, preferred_element_type=jnp.float32)]
    pallas_call x0 -> x6, Pallas kernels: none -> 35.5 us  [the longest x1 10.2 us: forward(): pl.pallas_call(forward_first, grid=(steps,), in_specs=[whole()] * 5 + wei...]
    ppermute x0 -> x22, starting transfers between devices: none -> 28.7 us  [the longest x18 28.2 us: send(): return lax.ppermute(block, everyone, ring(axes, by))]
  transfers between devices with their start and end apart: 4 -> 23, of which waited for: 4 -> 17; matrix products, arithmetic and copies ran while one was open for 2% -> 2% of each run, Pallas kernels for 0% -> 11%
where the time goes in v1:
time: 155 us; the launch traced here: 154 us
  waiting for transfers between devices  65.9 us (43%)
  starting transfers between devices  36 us (23%)
  Pallas kernels  35.5 us (23%)
  local copies, waits for them, and re-layouts  10.5 us (7%)
  other arithmetic  5.68 us (4%)
    ppermute x18, waiting for transfers between devices, send(): return lax.ppermute(block, everyone, ring(axes, by))  50 us
    ppermute x18, starting transfers between devices, send(): return lax.ppermute(block, everyone, ring(axes, by))  28.2 us
    all_to_all x1, waiting for transfers between devices, local(): lax.all_to_all(jnp.broadcast_to(sums[None], (64, 6, 128)), chips, 0, 0)  10.6 us
    pallas_call x1, Pallas kernels, forward(): pl.pallas_call(forward_first, grid=(steps,), in_specs=[whole()] * 5 + wei...  10.2 us
    pallas_call x1, Pallas kernels, forward(): pl.pallas_call(logits, grid=(steps,), in_specs=[whole()] + weights, out_s...  8.59 us
    unnamed x18, local copies, waits for them, and re-layouts  8.05 us
    all_to_all x1, starting transfers between devices, local(): lax.all_to_all(jnp.broadcast_to(sums[None], (64, 6, 128)), chips, 0, 0)  7.3 us
    pallas_call x1, Pallas kernels, grad_weight_of(): pl.pallas_call(grad_weight_kernel, grid=(student_width // tile,), in_spec...  6.97 us
  transfers between devices with their start and end apart: 23, of which 17 were waited for; matrix products, arithmetic and copies ran while one was open for 2% of the time, Pallas kernels for 11%

profile of v1, /device:TPU:0, one launch (start us, length us, event | category | flops | bytes accessed | tf_op | source)
XLA Modules:
  0.0 154.3 jit_solution(8472260589450266959)
XLA Ops:
  0.6 0.8 constant_dynamic-update-slice_fusion.1
  1.4 0.8 constant_dynamic-update-slice_fusion
  2.2 1.7 %collective-permute-start = (bf16[8,4096]{1,0:T(8,128)(2,1)S(1)}, bf16[8,4096]{1,0:T(8,128)(2,1)S(1)}, u32[]{:S(2)}, u32[]{:S(2)}) collective-permute-start(bf16[8,4096]{1,0:T(8,128)(2,1)S(1)} %get-tuple-element.41), channel_id=1, source_target_pairs={{0,2},{1,3},{2,4},{3,5},{4,6},{5,7},{6,0},{7,1},{8,10},{9,11},{10,... | collective-permute-start | bytes 196616 | tf_op jit(solution)/shard_map/ppermute | solution.py:49
  3.8 1.6 %collective-permute-start.1 = (bf16[8,4096]{1,0:T(8,128)(2,1)S(1)}, bf16[8,4096]{1,0:T(8,128)(2,1)S(1)}, u32[]{:S(2)}, u32[]{:S(2)}) collective-permute-start(bf16[8,4096]{1,0:T(8,128)(2,1)S(1)} %get-tuple-element.41), channel_id=1, source_target_pairs={{0,6},{1,7},{2,0},{3,1},{4,2},{5,3},{6,4},{7,5},{8,14},{9,15},{10,... | collective-permute-start | bytes 196616 | tf_op jit(solution)/shard_map/ppermute | solution.py:49
  5.4 2.1 %collective-permute-start.2 = (bf16[8,4096]{1,0:T(8,128)(2,1)S(1)}, bf16[8,4096]{1,0:T(8,128)(2,1)S(1)}, u32[]{:S(2)}, u32[]{:S(2)}) collective-permute-start(bf16[8,4096]{1,0:T(8,128)(2,1)S(1)} %get-tuple-element.41), channel_id=1, source_target_pairs={{0,4},{1,5},{2,6},{3,7},{4,0},{5,1},{6,2},{7,3},{8,12},{9,13},{10,... | collective-permute-start | bytes 196616 | tf_op jit(solution)/shard_map/ppermute | solution.py:49
  8.1 3.1 %collective-permute-done.2 = bf16[8,4096]{1,0:T(8,128)(2,1)S(1)} collective-permute-done((bf16[8,4096]{1,0:T(8,128)(2,1)S(1)}, bf16[8,4096]{1,0:T(8,128)(2,1)S(1)}, u32[]{:S(2)}, u32[]{:S(2)}) %collective-permute-start.2) | collective-permute-done | bytes 65568 | tf_op jit(solution)/shard_map/ppermute | solution.py:49
  11.2 1.6 %collective-permute-start.3 = (bf16[32,4096]{1,0:T(8,128)(2,1)S(1)}, bf16[32,4096]{1,0:T(8,128)(2,1)S(1)}, u32[]{:S(2)}, u32[]{:S(2)}) collective-permute-start(bf16[32,4096]{1,0:T(8,128)(2,1)S(1)} %pad_maximum_fusion.1), channel_id=1, source_target_pairs={{0,8},{1,9},{2,10},{3,11},{4,12},{5,13},{6,14},{7,15},{8,1},{9,0},... | collective-permute-start | bytes 786440 | tf_op jit(solution)/shard_map/ppermute | solution.py:49
  12.8 1.7 %collective-permute-start.4 = (bf16[32,4096]{1,0:T(8,128)(2,1)S(1)}, bf16[32,4096]{1,0:T(8,128)(2,1)S(1)}, u32[]{:S(2)}, u32[]{:S(2)}) collective-permute-start(bf16[32,4096]{1,0:T(8,128)(2,1)S(1)} %pad_maximum_fusion.1), channel_id=1, source_target_pairs={{0,9},{1,8},{2,11},{3,10},{4,13},{5,12},{6,15},{7,14},{8,0},{9,1},... | collective-permute-start | bytes 786440 | tf_op jit(solution)/shard_map/ppermute | solution.py:49
  14.5 1.9 %collective-permute-start.5 = (bf16[32,4096]{1,0:T(8,128)(2,1)S(1)}, bf16[32,4096]{1,0:T(8,128)(2,1)S(1)}, u32[]{:S(2)}, u32[]{:S(2)}) collective-permute-start(bf16[32,4096]{1,0:T(8,128)(2,1)S(1)} %pad_maximum_fusion.1), channel_id=1, source_target_pairs={{0,1},{1,0},{2,3},{3,2},{4,5},{5,4},{6,7},{7,6},{8,9},{9,8},{10,11... | collective-permute-start | bytes 786440 | tf_op jit(solution)/shard_map/ppermute | solution.py:49
  16.4 2.4 %collective-permute-done.3 = bf16[32,4096]{1,0:T(8,128)(2,1)S(1)} collective-permute-done((bf16[32,4096]{1,0:T(8,128)(2,1)S(1)}, bf16[32,4096]{1,0:T(8,128)(2,1)S(1)}, u32[]{:S(2)}, u32[]{:S(2)}) %collective-permute-start.3) | collective-permute-done | bytes 262176 | tf_op jit(solution)/shard_map/ppermute | solution.py:49
  19.2 3.5 %collective-permute-done.5 = bf16[32,4096]{1,0:T(8,128)(2,1)S(1)} collective-permute-done((bf16[32,4096]{1,0:T(8,128)(2,1)S(1)}, bf16[32,4096]{1,0:T(8,128)(2,1)S(1)}, u32[]{:S(2)}, u32[]{:S(2)}) %collective-permute-start.5) | collective-permute-done | bytes 262176 | tf_op jit(solution)/shard_map/ppermute | solution.py:49
  22.7 2.0 %collective-permute-start.6 = (bf16[128,4096]{1,0:T(8,128)(2,1)S(1)}, bf16[128,4096]{1,0:T(8,128)(2,1)S(1)}, u32[]{:S(2)}, u32[]{:S(2)}) collective-permute-start(bf16[128,4096]{1,0:T(8,128)(2,1)S(1)} %constant_dynamic-update-slice_fusion.2.x0), channel_id=1, source_target_pairs={{0,16},{1,17},{2,18},{3,19},{4,20},{5,21},{6,22},{7,23},{8,24},{9,... | collective-permute-start | bytes 3145736 | tf_op jit(solution)/shard_map/ppermute | solution.py:49
  24.7 2.2 %collective-permute-start.7 = (bf16[128,4096]{1,0:T(8,128)(2,1)S(1)}, bf16[128,4096]{1,0:T(8,128)(2,1)}, u32[]{:S(2)}, u32[]{:S(2)}) collective-permute-start(bf16[128,4096]{1,0:T(8,128)(2,1)S(1)} %constant_dynamic-update-slice_fusion.2.x0), channel_id=1, source_target_pairs={{0,48},{1,49},{2,50},{3,51},{4,52},{5,53},{6,54},{7,55},{8,56},{9,... | collective-permute-start | bytes 3145736 | tf_op jit(solution)/shard_map/ppermute | solution.py:49
  26.9 1.8 %collective-permute-start.8 = (bf16[128,4096]{1,0:T(8,128)(2,1)S(1)}, bf16[128,4096]{1,0:T(8,128)(2,1)}, u32[]{:S(2)}, u32[]{:S(2)}) collective-permute-start(bf16[128,4096]{1,0:T(8,128)(2,1)S(1)} %constant_dynamic-update-slice_fusion.2.x0), channel_id=1, source_target_pairs={{0,32},{1,33},{2,34},{3,35},{4,36},{5,37},{6,38},{7,39},{8,40},{9,... | collective-permute-start | bytes 3145736 | tf_op jit(solution)/shard_map/ppermute | solution.py:49
  28.7 0.7 multiply_bitcast_fusion
  29.7 9.9 %collective-permute-done.6.x1 = bf16[128,4096]{1,0:T(8,128)(2,1)S(1)} collective-permute-done((bf16[128,4096]{1,0:T(8,128)(2,1)S(1)}, bf16[128,4096]{1,0:T(8,128)(2,1)S(1)}, u32[]{:S(2)}, u32[]{:S(2)}) %collective-permute-start.6) | collective-permute-done | bytes 1048608 | tf_op jit(solution)/shard_map/ppermute | solution.py:49
  39.6 10.9 %collective-permute-done.7.x2 = bf16[128,4096]{1,0:T(8,128)(2,1)} collective-permute-done((bf16[128,4096]{1,0:T(8,128)(2,1)S(1)}, bf16[128,4096]{1,0:T(8,128)(2,1)}, u32[]{:S(2)}, u32[]{:S(2)}) %collective-permute-start.7) | collective-permute-done | bytes 1048608 | tf_op jit(solution)/shard_map/ppermute | solution.py:49
  50.5 1.9 %collective-permute-done.8.x3 = bf16[128,4096]{1,0:T(8,128)(2,1)} collective-permute-done((bf16[128,4096]{1,0:T(8,128)(2,1)S(1)}, bf16[128,4096]{1,0:T(8,128)(2,1)}, u32[]{:S(2)}, u32[]{:S(2)}) %collective-permute-start.8) | collective-permute-done | bytes 1048608 | tf_op jit(solution)/shard_map/ppermute | solution.py:49
  52.4 10.2 %shard_map.85 = (bf16[512,4096]{1,0:T(8,128)(2,1)S(1)}, f32[2,256,1024]{2,1,0:T(8,128)S(1)}, f32[2,256,1024]{2,1,0:T(8,128)S(1)}) custom-call(bf16[512,512]{1,0:T(8,128)(2,1)S(1)} %fusion.order, bf16[128,4096]{1,0:T(8,128)(2,1)S(1)} %constant_dynamic-update-slice_fusion.2.x0, bf16[128,4096]{1,0:T(8,128)(2,1)S(1)} %collective-permute-done.6.x1, ...), custom_call_target="tpu_custom_call" | custom-call | tf_op jit(solution)/shard_map/pallas_call | solution.py:105
  62.7 8.6 %shard_map.87 = (f32[2,256,1024]{2,1,0:T(8,128)S(1)}, f32[2,256,1024]{2,1,0:T(8,128)S(1)}) custom-call(bf16[512,4096]{1,0:T(8,128)(2,1)S(1)} %get-tuple-element.21.rows, bf16[2304,2048]{1,0:T(8,128)(2,1)} %teacher.3, bf16[1792,2048]{1,0:T(8,128)(2,1)} %weight.1), custom_call_target="tpu_custom_call" | custom-call | tf_op jit(solution)/shard_map/pallas_call | solution.py:113
  71.4 1.5 shard_map.86
  73.0 2.6 %collective-permute-done.10.other = f32[2,256,1024]{2,1,0:T(8,128)S(1)} collective-permute-done((f32[2,256,1024]{2,1,0:T(8,128)S(1)}, f32[2,256,1024]{2,1,0:T(8,128)S(1)}, u32[]{:S(2)}, u32[]{:S(2)}) %collective-permute-start.10) | collective-permute-done | bytes 2097184 | tf_op jit(solution)/shard_map/ppermute | solution.py:53
  75.6 1.5 shard_map.88
  77.1 1.0 copy-done.3
  78.1 1.0 copy-done.4
  79.2 0.7 broadcast_in_dim.16
  80.0 7.3 %all-to-all-start = ((f32[64,6,128]{2,1,0:T(8,128)}), f32[64,6,128]{2,1,0:T(8,128)S(1)}, u32[]{:S(2)}, u32[]{:S(2)}) async-start(f32[64,6,128]{2,1,0:T(8,128)} %broadcast_in_dim.16), calls=%async_computation | async-start | bytes 524288 | tf_op jit(solution)/shard_map/all_to_all | solution.py:233
  87.3 10.6 %all-to-all-done = f32[64,6,128]{2,1,0:T(8,128)S(1)} async-done(((f32[64,6,128]{2,1,0:T(8,128)}), f32[64,6,128]{2,1,0:T(8,128)S(1)}, u32[]{:S(2)}, u32[]{:S(2)}) %all-to-all-start) | async-done | bytes 196640 | tf_op jit(solution)/shard_map/all_to_all | solution.py:233
  98.0 1.9 %subtract_convert_fusion.1 = (bf16[256,1024]{1,0:T(8,128)(2,1)S(1)}, bf16[256,1024]{1,0:T(8,128)(2,1)S(1)}) fusion(f32[256,1024]{1,0:T(8,128)S(1)} %get-tuple-element.26, f32[256,1024]{1,0:T(8,128)S(1)} %get-tuple-element.25, f32[256]{0:T(256)S(1)} %get-tuple-element.44, f32[256]{0:T(256)S(1)} %get-tuple-element.43, f32[256,1024]{1,0:T(8,128)} %copy-done.4, ...), kind=kLoop, calls=%fused_computation.2 | loop fusion | flops 2097152 | bytes 5244928 | tf_op jit(solution)/shard_map/convert_element_type | solution.py:241
  100.2 2.6 %collective-permute-done.12.other = bf16[256,2048]{1,0:T(8,128)(2,1)S(1)} collective-permute-done((bf16[256,2048]{1,0:T(8,128)(2,1)S(1)}, bf16[256,2048]{1,0:T(8,128)(2,1)S(1)}, u32[]{:S(2)}, u32[]{:S(2)}) %collective-permute-start.12) | collective-permute-done | bytes 1048608 | tf_op jit(solution)/shard_map/ppermute | solution.py:53
  102.9 3.1 %copy-done = bf16[1792,2048]{1,0:T(8,128)(2,1)S(1)} copy-done((bf16[1792,2048]{1,0:T(8,128)(2,1)S(1)}, bf16[1792,2048]{1,0:T(8,128)(2,1)}, u32[]{:S(2)}) %copy-start) | copy-done | bytes 7340056
  106.0 6.7 %shard_map.89 = (f32[128,1792]{1,0:T(8,128)S(1)}, bf16[128,1792]{1,0:T(8,128)(2,1)S(1)}, bf16[128,1792]{1,0:T(8,128)(2,1)S(1)}, bf16[128,1792]{1,0:T(8,128)(2,1)S(1)}) custom-call(bf16[512,512]{1,0:T(8,128)(2,1)S(1)} %fusion.order, bf16[256,2048]{1,0:T(8,128)(2,1)S(1)} %pad_maximum_fusion.own, bf16[256,2048]{1,0:T(8,128)(2,1)S(1)} %collective-permute-done.12.other, ...), custom_call_target="tpu_custom_call" | custom-call | tf_op jit(solution)/shard_map/pallas_call | solution.py:183
  112.7 1.7 %collective-permute-start.15 = (bf16[128,1792]{1,0:T(8,128)(2,1)S(1)}, bf16[128,1792]{1,0:T(8,128)(2,1)S(1)}, u32[]{:S(2)}, u32[]{:S(2)}) collective-permute-start(bf16[128,1792]{1,0:T(8,128)(2,1)S(1)} %get-tuple-element.32), channel_id=1, source_target_pairs={{0,32},{1,33},{2,34},{3,35},{4,36},{5,37},{6,38},{7,39},{8,40},{9,... | collective-permute-start | bytes 1376264 | tf_op jit(solution)/shard_map/ppermute | solution.py:49
  114.7 2.9 %collective-permute-start.13 = (bf16[128,1792]{1,0:T(8,128)(2,1)S(1)}, bf16[128,1792]{1,0:T(8,128)(2,1)S(1)}, u32[]{:S(2)}, u32[]{:S(2)}) collective-permute-start(bf16[128,1792]{1,0:T(8,128)(2,1)S(1)} %get-tuple-element.30), channel_id=1, source_target_pairs={{0,48},{1,49},{2,50},{3,51},{4,52},{5,53},{6,54},{7,55},{8,56},{9,... | collective-permute-start | bytes 1376264 | tf_op jit(solution)/shard_map/ppermute | solution.py:49
  117.6 5.2 %collective-permute-done.15 = bf16[128,1792]{1,0:T(8,128)(2,1)S(1)} collective-permute-done((bf16[128,1792]{1,0:T(8,128)(2,1)S(1)}, bf16[128,1792]{1,0:T(8,128)(2,1)S(1)}, u32[]{:S(2)}, u32[]{:S(2)}) %collective-permute-start.15) | collective-permute-done | bytes 458784 | tf_op jit(solution)/shard_map/ppermute | solution.py:49
  122.9 4.8 %collective-permute-done.14 = bf16[128,1792]{1,0:T(8,128)(2,1)S(1)} collective-permute-done((bf16[128,1792]{1,0:T(8,128)(2,1)S(1)}, bf16[128,1792]{1,0:T(8,128)(2,1)S(1)}, u32[]{:S(2)}, u32[]{:S(2)}) %collective-permute-start.14) | collective-permute-done | bytes 458784 | tf_op jit(solution)/shard_map/ppermute | solution.py:49
  127.9 0.8 fusion.4
  128.7 1.3 collective-permute-start.18
  130.0 2.0 %collective-permute-start.16 = (f32[32,1792]{1,0:T(8,128)}, f32[32,1792]{1,0:T(8,128)}, u32[]{:S(2)}, u32[]{:S(2)}) collective-permute-start(f32[32,1792]{1,0:T(8,128)} %get-tuple-element.35), channel_id=1, source_target_pairs={{0,9},{1,8},{2,11},{3,10},{4,13},{5,12},{6,15},{7,14},{8,0},{9,1},... | collective-permute-start | bytes 688136 | tf_op jit(solution)/shard_map/ppermute | solution.py:49
  132.0 4.4 %collective-permute-done.18 = f32[32,1792]{1,0:T(8,128)S(1)} collective-permute-done((f32[32,1792]{1,0:T(8,128)}, f32[32,1792]{1,0:T(8,128)S(1)}, u32[]{:S(2)}, u32[]{:S(2)}) %collective-permute-start.18) | collective-permute-done | bytes 229408 | tf_op jit(solution)/shard_map/ppermute | solution.py:49
  136.4 1.3 collective-permute-done.16
  137.7 1.6 %collective-permute-done.17 = f32[32,1792]{1,0:T(8,128)} collective-permute-done((f32[32,1792]{1,0:T(8,128)S(1)}, f32[32,1792]{1,0:T(8,128)}, u32[]{:S(2)}, u32[]{:S(2)}) %collective-permute-start.17) | collective-permute-done | bytes 229408 | tf_op jit(solution)/shard_map/ppermute | solution.py:49
  139.3 1.1 slice_add_fusion
  140.4 1.5 collective-permute-start.21
  141.9 1.8 %collective-permute-start.19 = (f32[8,1792]{1,0:T(8,128)S(1)}, f32[8,1792]{1,0:T(8,128)S(1)}, u32[]{:S(2)}, u32[]{:S(2)}) collective-permute-start(f32[8,1792]{1,0:T(8,128)S(1)} %get-tuple-element.38), channel_id=1, source_target_pairs={{0,6},{1,7},{2,0},{3,1},{4,2},{5,3},{6,4},{7,5},{8,14},{9,15},{10,... | collective-permute-start | bytes 172040 | tf_op jit(solution)/shard_map/ppermute | solution.py:49
  144.5 2.2 %copy-done.2 = bf16[512,4096]{1,0:T(8,128)(2,1)S(1)} copy-done((bf16[512,4096]{1,0:T(8,128)(2,1)S(1)}, bf16[512,4096]{1,0:T(8,128)(2,1)}, u32[]{:S(2)}) %copy-start.2) | copy-done | bytes 4194328
  146.7 7.0 %shard_map.90 = bf16[1792,2048]{1,0:T(8,128)(2,1)} custom-call(bf16[512,4096]{1,0:T(8,128)(2,1)S(1)} %copy-done.2, bf16[256,2048]{1,0:T(8,128)(2,1)S(1)} %pad_maximum_fusion.own, bf16[256,2048]{1,0:T(8,128)(2,1)S(1)} %collective-permute-done.12.other), custom_call_target="tpu_custom_call" | custom-call | tf_op jit(solution)/shard_map/pallas_call | solution.py:205
  153.7 0.6 fusion.1
  (42 shorter events, 3.6 us)
Async XLA Ops:
  2.2 5.5 %collective-permute-start = (bf16[8,4096]{1,0:T(8,128)(2,1)S(1)}, bf16[8,4096]{1,0:T(8,128)(2,1)S(1)}, u32[]{:S(2)}, u32[]{:S(2)}) collective-permute-start(bf16[8,4096]{1,0:T(8,128)(2,1)S(1)} %get-tuple-element.41), channel_id=1, source_target_pairs={{0,2},{1,3},{2,4},{3,5},{4,6},{5,7},{6,0},{7,1},{8,10},{9,11},{10,... | collective-permute-start | bytes 196616 | tf_op jit(solution)/shard_map/ppermute | solution.py:49
  3.8 4.3 %collective-permute-start.1 = (bf16[8,4096]{1,0:T(8,128)(2,1)S(1)}, bf16[8,4096]{1,0:T(8,128)(2,1)S(1)}, u32[]{:S(2)}, u32[]{:S(2)}) collective-permute-start(bf16[8,4096]{1,0:T(8,128)(2,1)S(1)} %get-tuple-element.41), channel_id=1, source_target_pairs={{0,6},{1,7},{2,0},{3,1},{4,2},{5,3},{6,4},{7,5},{8,14},{9,15},{10,... | collective-permute-start | bytes 196616 | tf_op jit(solution)/shard_map/ppermute | solution.py:49
  5.4 5.8 %collective-permute-start.2 = (bf16[8,4096]{1,0:T(8,128)(2,1)S(1)}, bf16[8,4096]{1,0:T(8,128)(2,1)S(1)}, u32[]{:S(2)}, u32[]{:S(2)}) collective-permute-start(bf16[8,4096]{1,0:T(8,128)(2,1)S(1)} %get-tuple-element.41), channel_id=1, source_target_pairs={{0,4},{1,5},{2,6},{3,7},{4,0},{5,1},{6,2},{7,3},{8,12},{9,13},{10,... | collective-permute-start | bytes 196616 | tf_op jit(solution)/shard_map/ppermute | solution.py:49
  11.2 7.7 %collective-permute-start.3 = (bf16[32,4096]{1,0:T(8,128)(2,1)S(1)}, bf16[32,4096]{1,0:T(8,128)(2,1)S(1)}, u32[]{:S(2)}, u32[]{:S(2)}) collective-permute-start(bf16[32,4096]{1,0:T(8,128)(2,1)S(1)} %pad_maximum_fusion.1), channel_id=1, source_target_pairs={{0,8},{1,9},{2,10},{3,11},{4,12},{5,13},{6,14},{7,15},{8,1},{9,0},... | collective-permute-start | bytes 786440 | tf_op jit(solution)/shard_map/ppermute | solution.py:49
  12.8 6.4 %collective-permute-start.4 = (bf16[32,4096]{1,0:T(8,128)(2,1)S(1)}, bf16[32,4096]{1,0:T(8,128)(2,1)S(1)}, u32[]{:S(2)}, u32[]{:S(2)}) collective-permute-start(bf16[32,4096]{1,0:T(8,128)(2,1)S(1)} %pad_maximum_fusion.1), channel_id=1, source_target_pairs={{0,9},{1,8},{2,11},{3,10},{4,13},{5,12},{6,15},{7,14},{8,0},{9,1},... | collective-permute-start | bytes 786440 | tf_op jit(solution)/shard_map/ppermute | solution.py:49
  14.5 8.2 %collective-permute-start.5 = (bf16[32,4096]{1,0:T(8,128)(2,1)S(1)}, bf16[32,4096]{1,0:T(8,128)(2,1)S(1)}, u32[]{:S(2)}, u32[]{:S(2)}) collective-permute-start(bf16[32,4096]{1,0:T(8,128)(2,1)S(1)} %pad_maximum_fusion.1), channel_id=1, source_target_pairs={{0,1},{1,0},{2,3},{3,2},{4,5},{5,4},{6,7},{7,6},{8,9},{9,8},{10,11... | collective-permute-start | bytes 786440 | tf_op jit(solution)/shard_map/ppermute | solution.py:49
  22.7 16.9 %collective-permute-start.6 = (bf16[128,4096]{1,0:T(8,128)(2,1)S(1)}, bf16[128,4096]{1,0:T(8,128)(2,1)S(1)}, u32[]{:S(2)}, u32[]{:S(2)}) collective-permute-start(bf16[128,4096]{1,0:T(8,128)(2,1)S(1)} %constant_dynamic-update-slice_fusion.2.x0), channel_id=1, source_target_pairs={{0,16},{1,17},{2,18},{3,19},{4,20},{5,21},{6,22},{7,23},{8,24},{9,... | collective-permute-start | bytes 3145736 | tf_op jit(solution)/shard_map/ppermute | solution.py:49
  24.7 25.8 %collective-permute-start.7 = (bf16[128,4096]{1,0:T(8,128)(2,1)S(1)}, bf16[128,4096]{1,0:T(8,128)(2,1)}, u32[]{:S(2)}, u32[]{:S(2)}) collective-permute-start(bf16[128,4096]{1,0:T(8,128)(2,1)S(1)} %constant_dynamic-update-slice_fusion.2.x0), channel_id=1, source_target_pairs={{0,48},{1,49},{2,50},{3,51},{4,52},{5,53},{6,54},{7,55},{8,56},{9,... | collective-permute-start | bytes 3145736 | tf_op jit(solution)/shard_map/ppermute | solution.py:49
  26.9 25.5 %collective-permute-start.8 = (bf16[128,4096]{1,0:T(8,128)(2,1)S(1)}, bf16[128,4096]{1,0:T(8,128)(2,1)}, u32[]{:S(2)}, u32[]{:S(2)}) collective-permute-start(bf16[128,4096]{1,0:T(8,128)(2,1)S(1)} %constant_dynamic-update-slice_fusion.2.x0), channel_id=1, source_target_pairs={{0,32},{1,33},{2,34},{3,35},{4,36},{5,37},{6,38},{7,39},{8,40},{9,... | collective-permute-start | bytes 3145736 | tf_op jit(solution)/shard_map/ppermute | solution.py:49
  62.6 8.7 %copy-start.1 = (bf16[512,4096]{1,0:T(8,128)(2,1)}, bf16[512,4096]{1,0:T(8,128)(2,1)S(1)}, u32[]{:S(2)}) copy-start(bf16[512,4096]{1,0:T(8,128)(2,1)S(1)} %get-tuple-element.21.rows) | copy-start | bytes 12582916
  62.6 8.8 %collective-permute-start.9 = (f32[2,256,1024]{2,1,0:T(8,128)S(1)}, f32[2,256,1024]{2,1,0:T(8,128)S(1)}, u32[]{:S(2)}, u32[]{:S(2)}) collective-permute-start(f32[2,256,1024]{2,1,0:T(8,128)S(1)} %get-tuple-element.19), channel_id=1, source_target_pairs={{0,64},{64,0},{1,65},{65,1},{2,66},{66,2},{3,67},{67,3},{4,68},{68... | collective-permute-start | bytes 6291464 | tf_op jit(solution)/shard_map/ppermute | solution.py:53
  71.3 4.2 %collective-permute-start.10 = (f32[2,256,1024]{2,1,0:T(8,128)S(1)}, f32[2,256,1024]{2,1,0:T(8,128)S(1)}, u32[]{:S(2)}, u32[]{:S(2)}) collective-permute-start(f32[2,256,1024]{2,1,0:T(8,128)S(1)} %get-tuple-element.23), channel_id=1, source_target_pairs={{0,64},{64,0},{1,65},{65,1},{2,66},{66,2},{3,67},{67,3},{4,68},{68... | collective-permute-start | bytes 6291464 | tf_op jit(solution)/shard_map/ppermute | solution.py:53
  75.6 22.4 %copy-start.5 = (f32[512]{0:T(512)S(1)}, f32[512]{0:T(512)}, u32[]{:S(2)}) copy-start(f32[512]{0:T(512)} %param.10) | copy-start | bytes 6148
  77.1 1.0 copy-start.3
  78.1 1.0 copy-start.4
  80.0 17.9 %all-to-all-start = ((f32[64,6,128]{2,1,0:T(8,128)}), f32[64,6,128]{2,1,0:T(8,128)S(1)}, u32[]{:S(2)}, u32[]{:S(2)}) async-start(f32[64,6,128]{2,1,0:T(8,128)} %broadcast_in_dim.16), calls=%async_computation | async-start | bytes 524288 | tf_op jit(solution)/shard_map/all_to_all | solution.py:233
  100.0 2.9 %collective-permute-start.12 = (bf16[256,2048]{1,0:T(8,128)(2,1)S(1)}, bf16[256,2048]{1,0:T(8,128)(2,1)S(1)}, u32[]{:S(2)}, u32[]{:S(2)}) collective-permute-start(bf16[256,2048]{1,0:T(8,128)(2,1)S(1)} %pad_maximum_fusion.own), channel_id=1, source_target_pairs={{0,64},{64,0},{1,65},{65,1},{2,66},{66,2},{3,67},{67,3},{4,68},{68... | collective-permute-start | bytes 3145736 | tf_op jit(solution)/shard_map/ppermute | solution.py:53
  102.9 3.1 %copy-start = (bf16[1792,2048]{1,0:T(8,128)(2,1)S(1)}, bf16[1792,2048]{1,0:T(8,128)(2,1)}, u32[]{:S(2)}) copy-start(bf16[1792,2048]{1,0:T(8,128)(2,1)} %weight.1) | copy-start | bytes 22020100
  112.7 10.2 %collective-permute-start.15 = (bf16[128,1792]{1,0:T(8,128)(2,1)S(1)}, bf16[128,1792]{1,0:T(8,128)(2,1)S(1)}, u32[]{:S(2)}, u32[]{:S(2)}) collective-permute-start(bf16[128,1792]{1,0:T(8,128)(2,1)S(1)} %get-tuple-element.32), channel_id=1, source_target_pairs={{0,32},{1,33},{2,34},{3,35},{4,36},{5,37},{6,38},{7,39},{8,40},{9,... | collective-permute-start | bytes 1376264 | tf_op jit(solution)/shard_map/ppermute | solution.py:49
  114.4 13.3 %collective-permute-start.14 = (bf16[128,1792]{1,0:T(8,128)(2,1)S(1)}, bf16[128,1792]{1,0:T(8,128)(2,1)S(1)}, u32[]{:S(2)}, u32[]{:S(2)}) collective-permute-start(bf16[128,1792]{1,0:T(8,128)(2,1)S(1)} %get-tuple-element.31), channel_id=1, source_target_pairs={{0,16},{1,17},{2,18},{3,19},{4,20},{5,21},{6,22},{7,23},{8,24},{9,... | collective-permute-start | bytes 1376264 | tf_op jit(solution)/shard_map/ppermute | solution.py:49
  114.7 13.0 %collective-permute-start.13 = (bf16[128,1792]{1,0:T(8,128)(2,1)S(1)}, bf16[128,1792]{1,0:T(8,128)(2,1)S(1)}, u32[]{:S(2)}, u32[]{:S(2)}) collective-permute-start(bf16[128,1792]{1,0:T(8,128)(2,1)S(1)} %get-tuple-element.30), channel_id=1, source_target_pairs={{0,48},{1,49},{2,50},{3,51},{4,52},{5,53},{6,54},{7,55},{8,56},{9,... | collective-permute-start | bytes 1376264 | tf_op jit(solution)/shard_map/ppermute | solution.py:49
  128.7 7.7 %collective-permute-start.18 = (f32[32,1792]{1,0:T(8,128)}, f32[32,1792]{1,0:T(8,128)S(1)}, u32[]{:S(2)}, u32[]{:S(2)}) collective-permute-start(f32[32,1792]{1,0:T(8,128)} %get-tuple-element.34), channel_id=1, source_target_pairs={{0,1},{1,0},{2,3},{3,2},{4,5},{5,4},{6,7},{7,6},{8,9},{9,8},{10,11... | collective-permute-start | bytes 688136 | tf_op jit(solution)/shard_map/ppermute | solution.py:49
  130.0 7.7 %collective-permute-start.16 = (f32[32,1792]{1,0:T(8,128)}, f32[32,1792]{1,0:T(8,128)}, u32[]{:S(2)}, u32[]{:S(2)}) collective-permute-start(f32[32,1792]{1,0:T(8,128)} %get-tuple-element.35), channel_id=1, source_target_pairs={{0,9},{1,8},{2,11},{3,10},{4,13},{5,12},{6,15},{7,14},{8,0},{9,1},... | collective-permute-start | bytes 688136 | tf_op jit(solution)/shard_map/ppermute | solution.py:49
  132.0 7.3 %collective-permute-start.17 = (f32[32,1792]{1,0:T(8,128)S(1)}, f32[32,1792]{1,0:T(8,128)}, u32[]{:S(2)}, u32[]{:S(2)}) collective-permute-start(f32[32,1792]{1,0:T(8,128)S(1)} %get-tuple-element.33), channel_id=1, source_target_pairs={{0,8},{1,9},{2,10},{3,11},{4,12},{5,13},{6,14},{7,15},{8,1},{9,0},... | collective-permute-start | bytes 688136 | tf_op jit(solution)/shard_map/ppermute | solution.py:49
  132.0 11.9 %collective-permute-start.11 = (f32[256]{0:T(256)S(1)}, f32[256]{0:T(256)S(1)}, u32[]{:S(2)}, u32[]{:S(2)}) collective-permute-start(f32[256]{0:T(256)S(1)} %get-tuple-element.45), channel_id=1, source_target_pairs={{0,64},{64,0},{1,65},{65,1},{2,66},{66,2},{3,67},{67,3},{4,68},{68... | collective-permute-start | bytes 3080 | tf_op jit(solution)/shard_map/ppermute | solution.py:53
  140.4 13.2 %collective-permute-start.21 = (f32[8,1792]{1,0:T(8,128)S(1)}, f32[8,1792]{1,0:T(8,128)S(1)}, u32[]{:S(2)}, u32[]{:S(2)}) collective-permute-start(f32[8,1792]{1,0:T(8,128)S(1)} %get-tuple-element.37), channel_id=1, source_target_pairs={{0,4},{1,5},{2,6},{3,7},{4,0},{5,1},{6,2},{7,3},{8,12},{9,13},{10,... | collective-permute-start | bytes 172040 | tf_op jit(solution)/shard_map/ppermute | solution.py:49
  141.9 11.8 %collective-permute-start.19 = (f32[8,1792]{1,0:T(8,128)S(1)}, f32[8,1792]{1,0:T(8,128)S(1)}, u32[]{:S(2)}, u32[]{:S(2)}) collective-permute-start(f32[8,1792]{1,0:T(8,128)S(1)} %get-tuple-element.38), channel_id=1, source_target_pairs={{0,6},{1,7},{2,0},{3,1},{4,2},{5,3},{6,4},{7,5},{8,14},{9,15},{10,... | collective-permute-start | bytes 172040 | tf_op jit(solution)/shard_map/ppermute | solution.py:49
  143.7 10.0 %collective-permute-start.20 = (f32[8,1792]{1,0:T(8,128)S(1)}, f32[8,1792]{1,0:T(8,128)S(1)}, u32[]{:S(2)}, u32[]{:S(2)}) collective-permute-start(f32[8,1792]{1,0:T(8,128)S(1)} %get-tuple-element.36), channel_id=1, source_target_pairs={{0,2},{1,3},{2,4},{3,5},{4,6},{5,7},{6,0},{7,1},{8,10},{9,11},{10,... | collective-permute-start | bytes 172040 | tf_op jit(solution)/shard_map/ppermute | solution.py:49
  144.5 2.2 %copy-start.2 = (bf16[512,4096]{1,0:T(8,128)(2,1)S(1)}, bf16[512,4096]{1,0:T(8,128)(2,1)}, u32[]{:S(2)}) copy-start(bf16[512,4096]{1,0:T(8,128)(2,1)} %copy-done.1) | copy-start | bytes 12582916

commit v2 on v1

v2 whole, which is shorter than its diff:
```python
import functools

import jax
import jax.numpy as jnp
import numpy as np
from jax import lax
from jax.experimental import pallas as pl
from jax.experimental.pallas import tpu as pltpu
from jax.sharding import PartitionSpec as P

softcap_limit = 30.0
tokens, teacher_width, student_width, vocab_local = 512, 2304, 1792, 2048
width = teacher_width + student_width
half = tokens // 2
everyone = ("mp", "batch", "vocab")
mega = 1024 * 1024

offsets = (0, 1, 3, 2)
teacher_axes = (("y", "z"), ("x", "x"), ("z", "y"))
student_axes = (("y", "z"), ("z", "y"), ("x", "x"))
reduce_axes = (("z", "y"), ("x", "z"), ("y", "x"))


def place(index):
    core, z, x_lo, y, x_hi = np.unravel_index(index, (2, 4, 2, 4, 2))
    return {"core": int(core), "x": int(2 * x_hi + x_lo), "y": int(y), "z": int(z)}


def index_of(at):
    return int(
        np.ravel_multi_index(
            (at["core"], at["z"], at["x"] % 2, at["y"], at["x"] // 2), (2, 4, 2, 4, 2)
        )
    )


def moved(at, axis, by):
    return {**at, axis: (at[axis] + by) % 4}


def ring(axes, by):
    pairs = []
    for source in range(128):
        at = place(source)
        pairs.append((source, index_of(moved(at, axes[at["core"]], by))))
    return pairs


def send(block, axes, by):
    return lax.ppermute(block, everyone, ring(axes, by))


def swap(block):
    return lax.ppermute(block, "mp", [(0, 1), (1, 0)])


def row_table(axes_of):
    table = np.zeros((128, 64), np.int32)
    for device in range(128):
        at = place(device)
        core = at["core"]
        for slot in range(64):
            owner = at
            for stage, digit in enumerate((slot % 4, slot // 4 % 4, slot // 16)):
                owner = moved(owner, axes_of[stage][core], -offsets[digit])
            table[device, slot] = (index_of(owner) % 64 - 32 * core) % 64
    return table


def gathered(order, blocks, rows):
    step = 256
    for at in range(0, rows.shape[1], step):
        cols = slice(at, at + step)
        block = jnp.concatenate([x[:, cols] for x in blocks], axis=0)
        rows[:, cols] = jnp.dot(
            order[...], block, preferred_element_type=jnp.float32
        ).astype(jnp.bfloat16)


def first_kernel(order, x0, x1, x2, x3, weight, own, other, rows):
    @pl.when(pl.program_id(0) == 0)
    def _():
        gathered(order, (x0, x1, x2, x3), rows)

    next_kernel(rows, weight, own, other)


def next_kernel(rows, weight, own, other):
    raw = jnp.dot(rows[...], weight[...], preferred_element_type=jnp.float32)
    own[...], other[...] = raw[:half], raw[half:]


def setup_kernel(tables, token_weight, teacher_order, student_order, reduce_order, weight_here, first_core):
    me = lax.axis_index(everyone)
    core = lax.axis_index("mp")
    for i, order in enumerate((teacher_order, student_order, reduce_order)):
        places = tables[i, pl.ds(me, 1), :]
        rows = lax.broadcasted_iota(jnp.int32, (tokens, tokens), 0)
        order[...] = jnp.where(rows == places, 1.0, 0.0).astype(jnp.bfloat16)
    weight_here[...] = token_weight[pl.ds(core * 2, 2), :]
    first_core[...] = jnp.full(first_core.shape, 1.0, jnp.float32) * (core == 0).astype(jnp.float32)


def setup(token_weight):
    tables = np.stack([row_table(a) for a in (teacher_axes, student_axes, reduce_axes[::-1])])
    tables = np.repeat(tables * 8, 8, axis=2) + np.tile(np.arange(8, dtype=np.int32), 64)
    order = jax.ShapeDtypeStruct((tokens, tokens), jnp.bfloat16)
    small = jax.ShapeDtypeStruct((2, 128), jnp.float32)
    return pl.pallas_call(
        setup_kernel,
        in_specs=[whole()] * 2,
        out_specs=[whole()] * 5,
        out_shape=[order] * 3 + [small] * 2,
        compiler_params=pltpu.CompilerParams(vmem_limit_bytes=4 * mega),
        cost_estimate=cost(0, 24 * mega),
    )(jnp.asarray(tables.astype(np.int32)), token_weight.reshape(4, 128))


def cost(macs, moved, transcendentals=0):
    return pl.CostEstimate(flops=2 * macs, bytes_accessed=moved, transcendentals=transcendentals)


def whole():
    return pl.BlockSpec(memory_space=pltpu.VMEM)


def forward(rows, weight, chunk, n_chunks, keep_rows=False, tile=256, limit=8):
    steps = vocab_local // n_chunks // tile
    depth = weight.shape[0]
    weight_spec = pl.BlockSpec((depth, tile), lambda j: (0, chunk * steps + j))
    out = pl.BlockSpec((half, tile), lambda j: (0, j))
    shape = jax.ShapeDtypeStruct((half, steps * tile), jnp.float32)
    held = jax.ShapeDtypeStruct((tokens, depth), jnp.bfloat16)
    params = pltpu.CompilerParams(vmem_limit_bytes=limit * mega)
    work = cost(tokens * depth * steps * tile, (2 * depth + 4 * tokens) * steps * tile)
    if chunk == 0:
        return pl.pallas_call(
            first_kernel,
            grid=(steps,),
            in_specs=[whole()] * 5 + [weight_spec],
            out_specs=[out, out] + [whole()] * keep_rows,
            out_shape=[shape, shape] + [held] * keep_rows,
            scratch_shapes=[] if keep_rows else [pltpu.VMEM(held.shape, held.dtype)],
            compiler_params=params,
            cost_estimate=work,
        )(*rows, weight)
    return pl.pallas_call(
        next_kernel,
        grid=(steps,),
        in_specs=[whole(), weight_spec],
        out_specs=[out, out],
        out_shape=[shape, shape],
        compiler_params=params,
        cost_estimate=work,
    )(rows, weight)


def lanes(values):
    total = values[:, :128]
    for at in range(128, values.shape[1], 128):
        total += values[:, at : at + 128]
    return total


def statistics_kernel(last, before, t_own, t_other, s_own, s_other, student_part, teacher_part, out, sums):
    @pl.when(pl.program_id(0) == 0)
    def _():
        sums[...] = before[...] if last else jnp.zeros_like(sums)

    teacher_tanh = jnp.tanh((t_own[...] + t_other[...]) * (1.0 / softcap_limit))
    student_tanh = jnp.tanh((s_own[...] + s_other[...]) * (1.0 / softcap_limit))
    teacher_exp = jnp.exp(softcap_limit * teacher_tanh - softcap_limit)
    student_exp = jnp.exp(softcap_limit * student_tanh - softcap_limit)
    slope = 1.0 - student_tanh * student_tanh
    student_part[...] = student_exp * slope
    teacher_part[...] = teacher_exp * slope
    sums[0] += lanes(teacher_exp)
    sums[1] += lanes(student_exp)
    sums[2] += lanes(teacher_exp * (softcap_limit * (teacher_tanh - student_tanh)))

    @pl.when(pl.program_id(0) == pl.num_programs(0) - 1)
    def _():
        if last:
            rows = [
                jnp.sum(sums[i, at : at + 128].T, axis=0, keepdims=True)
                for i in range(3)
                for at in (0, 128)
            ]
            out[...] = jnp.concatenate(rows + [jnp.zeros((2, 128), jnp.float32)], axis=0)
        else:
            out[...] = sums[...]


def statistics(teacher, student, chunk, before=None, tile=256):
    cols = student[0].shape[1]
    steps = cols // tile
    last = before is not None
    from_teacher = pl.BlockSpec((half, tile), lambda j: (0, chunk * steps + j))
    part = pl.BlockSpec((half, tile), lambda j: (0, j))
    shape = jax.ShapeDtypeStruct((half, cols), jnp.float32)
    sums = (3, half, 128)
    kernel = functools.partial(statistics_kernel, last)
    if not last:
        kernel = functools.partial(statistics_kernel, last, None)
    return pl.pallas_call(
        kernel,
        grid=(steps,),
        in_specs=[whole()] * last + [from_teacher] * 2 + [part] * 2,
        out_specs=[part, part, whole()],
        out_shape=[
            shape,
            shape,
            jax.ShapeDtypeStruct((8, 128) if last else sums, jnp.float32),
        ],
        scratch_shapes=[pltpu.VMEM(sums, jnp.float32)],
        compiler_params=pltpu.CompilerParams(vmem_limit_bytes=7 * mega),
        cost_estimate=cost(10 * half * cols, 24 * half * cols, 4 * half * cols),
    )(*([before] if last else []), *teacher, *student)


def gap_kernel(total, token_weight, student0, teacher0, student1, teacher1, gap, divergence):
    teacher_total, student_total, cross = total[0:2], total[2:4], total[4:6]
    divergence[...] = cross / teacher_total - jnp.log(teacher_total) + jnp.log(student_total)
    rows = [token_weight[...] / student_total, token_weight[...] / teacher_total, total[0:4]]
    scales = jnp.concatenate(rows, axis=0).T
    cols = student0.shape[1]
    for i in range(2):
        at = slice(128 * i, 128 * (i + 1))
        student_scale, teacher_scale = scales[:, i : i + 1], scales[:, 2 + i : 3 + i]
        for first, student, teacher in ((0, student0, teacher0), (cols, student1, teacher1)):
            gap[at, first : first + cols] = (
                student[at] * student_scale - teacher[at] * teacher_scale
            ).astype(jnp.bfloat16)


def gap_of(total, token_weight, parts):
    return pl.pallas_call(
        gap_kernel,
        in_specs=[whole()] * 6,
        out_specs=[whole(), whole()],
        out_shape=[
            jax.ShapeDtypeStruct((half, vocab_local), jnp.bfloat16),
            jax.ShapeDtypeStruct((2, 128), jnp.float32),
        ],
        compiler_params=pltpu.CompilerParams(vmem_limit_bytes=4 * mega),
        cost_estimate=cost(2 * half * vocab_local, 10 * half * vocab_local),
    )(total, token_weight, *parts)


def grad_hidden_kernel(order, own, other, weight, keep, send1, send2, send3, gap):
    @pl.when(pl.program_id(0) == 0)
    def _():
        step = 512
        for at in range(0, vocab_local, step):
            cols = slice(at, at + step)
            block = jnp.concatenate([own[:, cols], other[:, cols]], axis=0)
            gap[:, cols] = lax.dot_general(
                order[...], block, (((0,), (0,)), ((), ())), preferred_element_type=jnp.float32
            ).astype(jnp.bfloat16)

    term = lax.dot_general(
        gap[...], weight[...], (((1,), (1,)), ((), ())), preferred_element_type=jnp.float32
    )
    keep[...] = term[:128]
    send1[...] = term[128:256].astype(jnp.bfloat16)
    send2[...] = term[256:384].astype(jnp.bfloat16)
    send3[...] = term[384:].astype(jnp.bfloat16)


def grad_hidden_term(order, own, other, weight, tile=256):
    out = pl.BlockSpec((128, tile), lambda j: (0, j))
    return pl.pallas_call(
        grad_hidden_kernel,
        grid=(student_width // tile,),
        in_specs=[whole()] * 3 + [pl.BlockSpec((tile, vocab_local), lambda j: (j, 0))],
        out_specs=[out] * 4,
        out_shape=[jax.ShapeDtypeStruct((128, student_width), jnp.float32)]
        + [jax.ShapeDtypeStruct((128, student_width), jnp.bfloat16)] * 3,
        scratch_shapes=[pltpu.VMEM((tokens, vocab_local), jnp.bfloat16)],
        compiler_params=pltpu.CompilerParams(vmem_limit_bytes=8 * mega),
        cost_estimate=cost(tokens * student_width * vocab_local, 2 * student_width * vocab_local),
    )(order, own, other, weight)


def grad_weight_kernel(rows, own, other, out):
    over_rows = (((0,), (0,)), ((), ()))
    out[...] = (
        lax.dot_general(rows[:half], own[...], over_rows, preferred_element_type=jnp.float32)
        + lax.dot_general(rows[half:], other[...], over_rows, preferred_element_type=jnp.float32)
    ).astype(jnp.bfloat16)


def grad_weight_of(rows, own, other, tile=256):
    return pl.pallas_call(
        grad_weight_kernel,
        grid=(student_width // tile,),
        in_specs=[pl.BlockSpec((tokens, tile), lambda j: (0, j)), whole(), whole()],
        out_specs=pl.BlockSpec((tile, vocab_local), lambda j: (j, 0)),
        out_shape=jax.ShapeDtypeStruct((student_width, vocab_local), jnp.bfloat16),
        compiler_params=pltpu.CompilerParams(vmem_limit_bytes=8 * mega),
        cost_estimate=cost(tokens * student_width * vocab_local, 2 * student_width * vocab_local),
    )(rows, own, other)


def local(hidden_teacher, hidden_student, teacher_weight, student_weight, token_weight):
    teacher_order, student_order, reduce_order, weight_here, first_core = setup(token_weight)

    def shared_along(block, axes):
        return [block] + [send(block, axes, by) for by in offsets[1:]]

    def joined(blocks):
        return jnp.concatenate(blocks, axis=0)

    block = joined(
        shared_along(jnp.concatenate([hidden_teacher, hidden_student], axis=1), teacher_axes[0])
    )
    teacher, student = block[:, :teacher_width], block[:, teacher_width:]
    student = joined(shared_along(student, student_axes[1]))
    teacher = joined(shared_along(teacher, teacher_axes[1]))
    teacher, student = lax.optimization_barrier((teacher, student))
    teacher = shared_along(teacher, teacher_axes[2])
    student = shared_along(student, student_axes[2])

    teacher_own, teacher_other = forward((teacher_order, *teacher), teacher_weight, 0, 1)
    teacher_other, student[1], student[2], student[3] = lax.optimization_barrier(
        (teacher_other, student[1], student[2], student[3])
    )
    teacher_raw = (teacher_own, swap(teacher_other))
    own, other, rows = forward((student_order, *student), student_weight, 0, 2, keep_rows=True)
    student_raw0 = (own, swap(other))
    own, other = forward(rows, student_weight, 1, 2)
    student_raw1 = (own, swap(other))
    student_part0, teacher_part0, sums = statistics(teacher_raw, student_raw0, 0)
    student_part1, teacher_part1, sums = statistics(teacher_raw, student_raw1, 1, sums)
    for axes in reduce_axes:
        sums = sum(shared_along(sums, axes))
    gap, divergence = gap_of(
        sums, weight_here, (student_part0, teacher_part0, student_part1, teacher_part1)
    )
    gap_other = swap(gap)

    keep, *sends = grad_hidden_term(reduce_order, gap, gap_other, student_weight)
    received = [send(b, reduce_axes[0], -by) for b, by in zip(sends, offsets[1:])]
    divergence_other = swap(divergence)
    grad_weight = grad_weight_of(rows, gap, gap_other)
    keep, grad_weight, divergence_other = lax.optimization_barrier(
        (keep, grad_weight, divergence_other)
    )
    total = keep + sum(r.astype(jnp.float32) for r in received)
    for axes, kind in zip(reduce_axes[1:], (jnp.bfloat16, jnp.float32)):
        size = total.shape[0] // 4
        parts = [total[i * size : (i + 1) * size] for i in range(4)]
        received = [send(p.astype(kind), axes, -by) for p, by in zip(parts[1:], offsets[1:])]
        total = parts[0] + sum(r.astype(jnp.float32) for r in received)
    grad_hidden = total.astype(jnp.bfloat16)

    first_core = first_core > 0.5
    divergence = jnp.concatenate(
        [
            jnp.where(first_core, divergence, divergence_other),
            jnp.where(first_core, divergence_other, divergence),
        ]
    ).reshape(tokens)
    return (divergence, grad_hidden, grad_weight)


def solution(mesh):
    placed = (
        P(("batch", "vocab"), "mp"),
        P(("batch", "vocab"), "mp"),
        P("mp", ("batch", "vocab")),
        P("mp", ("batch", "vocab")),
        P(),
    )
    return jax.shard_map(
        local,
        mesh=mesh,
        in_specs=placed,
        out_specs=(P(), P(("batch", "vocab"), "mp"), P("mp", ("batch", "vocab"))),
        check_vma=False,
    )
```

time: 155 us -> 139 us (0.90)
  waiting for transfers between devices: 65.9 us -> 51.7 us
  starting transfers between devices: 36 us -> 44.9 us
  local copies, waits for them, and re-layouts: 10.5 us -> 5.49 us
  other arithmetic: 5.68 us -> 1.6 us
    ppermute x18 -> x33, starting transfers between devices: 28.2 us -> 44 us  [send(): return lax.ppermute(block, everyone, ring(axes, by))]
    all_to_all x1 -> x0, waiting for transfers between devices: 10.6 us -> none  [local(): lax.all_to_all(jnp.broadcast_to(sums[None], (64, 6, 128)), chips, 0, 0)]
    all_to_all x1 -> x0, starting transfers between devices: 7.3 us -> none  [local(): lax.all_to_all(jnp.broadcast_to(sums[None], (64, 6, 128)), chips, 0, 0)]
    unnamed x18 -> x11, local copies, waits for them, and re-layouts: 8.05 us -> 4.69 us
    convert_element_type x2 -> x0, other arithmetic: 1.99 us -> none  [the longest x1 1.85 us: local(): (student_part0 * student_scale - teacher_part0 * teacher_scale).astype(jn...]
    ppermute x18 -> x33, waiting for transfers between devices: 50 us -> 48 us  [send(): return lax.ppermute(block, everyone, ring(axes, by))]
    ppermute x4 -> x5, waiting for transfers between devices: 5.26 us -> 3.7 us  [swap(): return lax.ppermute(block, 'mp', [(0, 1), (1, 0)])]
    pallas_call x4 -> x7, Pallas kernels: 21.8 us -> 20.9 us  [the longest x2 13.6 us: forward(): pl.pallas_call(first_kernel, grid=(steps,), in_specs=[whole()] * 5 + [wei...]
  transfers between devices with their start and end apart: 23 -> 38, of which waited for: 17 -> 23; matrix products, arithmetic and copies ran while one was open for 2% -> 0% of each run, Pallas kernels for 11% -> 18%
where the time goes in v2:
time: 139 us
  waiting for transfers between devices  51.7 us (37%)
  starting transfers between devices  44.9 us (32%)
  Pallas kernels  34.5 us (25%)
  local copies, waits for them, and re-layouts  5.49 us (4%)
  other arithmetic  1.6 us (1%)
    ppermute x33, waiting for transfers between devices, send(): return lax.ppermute(block, everyone, ring(axes, by))  48 us
    ppermute x33, starting transfers between devices, send(): return lax.ppermute(block, everyone, ring(axes, by))  44 us
    pallas_call x2, Pallas kernels, forward(): pl.pallas_call(first_kernel, grid=(steps,), in_specs=[whole()] * 5 + [wei...  13.6 us
    pallas_call x1, Pallas kernels, grad_weight_of(): pl.pallas_call(grad_weight_kernel, grid=(student_width // tile,), in_spec...  6.89 us
    pallas_call x1, Pallas kernels, grad_hidden_term(): pl.pallas_call(grad_hidden_kernel, grid=(student_width // tile,), in_spec...  6.74 us
    unnamed x11, local copies, waits for them, and re-layouts  4.69 us
    ppermute x5, waiting for transfers between devices, swap(): return lax.ppermute(block, 'mp', [(0, 1), (1, 0)])  3.7 us
    pallas_call x2, Pallas kernels, statistics(): pl.pallas_call(kernel, grid=(steps,), in_specs=[whole()] * last + [from_t...  3.27 us
  transfers between devices with their start and end apart: 38, of which 23 were waited for; matrix products, arithmetic and copies ran while one was open for 0% of the time, Pallas kernels for 18%

profile of v2, /device:TPU:0, one launch (start us, length us, event | category | flops | bytes accessed | tf_op | source)
XLA Modules:
  0.0 139.1 jit_solution(2675538403595766887)
XLA Ops:
  0.7 0.8 constant_dynamic-update-slice_fusion.1
  2.2 1.7 %collective-permute-start = (bf16[8,4096]{1,0:T(8,128)(2,1)S(1)}, bf16[8,4096]{1,0:T(8,128)(2,1)S(1)}, u32[]{:S(2)}, u32[]{:S(2)}) collective-permute-start(bf16[8,4096]{1,0:T(8,128)(2,1)S(1)} %constant_dynamic-update-slice_fusion), channel_id=1, source_target_pairs={{0,2},{1,3},{2,4},{3,5},{4,6},{5,7},{6,0},{7,1},{8,10},{9,11},{10,... | collective-permute-start | bytes 196616 | tf_op jit(solution)/shard_map/ppermute | solution.py:50
  3.9 1.6 %collective-permute-start.1 = (bf16[8,4096]{1,0:T(8,128)(2,1)S(1)}, bf16[8,4096]{1,0:T(8,128)(2,1)S(1)}, u32[]{:S(2)}, u32[]{:S(2)}) collective-permute-start(bf16[8,4096]{1,0:T(8,128)(2,1)S(1)} %constant_dynamic-update-slice_fusion), channel_id=1, source_target_pairs={{0,6},{1,7},{2,0},{3,1},{4,2},{5,3},{6,4},{7,5},{8,14},{9,15},{10,... | collective-permute-start | bytes 196616 | tf_op jit(solution)/shard_map/ppermute | solution.py:50
  5.5 2.1 %collective-permute-start.2 = (bf16[8,4096]{1,0:T(8,128)(2,1)S(1)}, bf16[8,4096]{1,0:T(8,128)(2,1)S(1)}, u32[]{:S(2)}, u32[]{:S(2)}) collective-permute-start(bf16[8,4096]{1,0:T(8,128)(2,1)S(1)} %constant_dynamic-update-slice_fusion), channel_id=1, source_target_pairs={{0,4},{1,5},{2,6},{3,7},{4,0},{5,1},{6,2},{7,3},{8,12},{9,13},{10,... | collective-permute-start | bytes 196616 | tf_op jit(solution)/shard_map/ppermute | solution.py:50
  8.2 3.1 %collective-permute-done.2 = bf16[8,4096]{1,0:T(8,128)(2,1)S(1)} collective-permute-done((bf16[8,4096]{1,0:T(8,128)(2,1)S(1)}, bf16[8,4096]{1,0:T(8,128)(2,1)S(1)}, u32[]{:S(2)}, u32[]{:S(2)}) %collective-permute-start.2) | collective-permute-done | bytes 65568 | tf_op jit(solution)/shard_map/ppermute | solution.py:50
  11.3 2.1 %collective-permute-start.6 = (bf16[32,1792]{1,0:T(8,128)(2,1)S(1)}, bf16[32,1792]{1,0:T(8,128)(2,1)S(1)}, u32[]{:S(2)}, u32[]{:S(2)}) collective-permute-start(bf16[32,1792]{1,0:T(8,128)(2,1)S(1)} %pad_maximum_fusion.3), channel_id=1, source_target_pairs={{0,16},{1,17},{2,18},{3,19},{4,20},{5,21},{6,22},{7,23},{8,24},{9,... | collective-permute-start | bytes 344072 | tf_op jit(solution)/shard_map/ppermute | solution.py:50
  13.3 2.2 %collective-permute-start.7 = (bf16[32,1792]{1,0:T(8,128)(2,1)S(1)}, bf16[32,1792]{1,0:T(8,128)(2,1)S(1)}, u32[]{:S(2)}, u32[]{:S(2)}) collective-permute-start(bf16[32,1792]{1,0:T(8,128)(2,1)S(1)} %pad_maximum_fusion.3), channel_id=1, source_target_pairs={{0,48},{1,49},{2,50},{3,51},{4,52},{5,53},{6,54},{7,55},{8,56},{9,... | collective-permute-start | bytes 344072 | tf_op jit(solution)/shard_map/ppermute | solution.py:50
  15.5 1.8 %collective-permute-start.8 = (bf16[32,1792]{1,0:T(8,128)(2,1)S(1)}, bf16[32,1792]{1,0:T(8,128)(2,1)S(1)}, u32[]{:S(2)}, u32[]{:S(2)}) collective-permute-start(bf16[32,1792]{1,0:T(8,128)(2,1)S(1)} %pad_maximum_fusion.3), channel_id=1, source_target_pairs={{0,32},{1,33},{2,34},{3,35},{4,36},{5,37},{6,38},{7,39},{8,40},{9,... | collective-permute-start | bytes 344072 | tf_op jit(solution)/shard_map/ppermute | solution.py:50
  17.4 1.6 %collective-permute-start.3 = (bf16[32,2304]{1,0:T(8,128)(2,1)S(1)}, bf16[32,2304]{1,0:T(8,128)(2,1)S(1)}, u32[]{:S(2)}, u32[]{:S(2)}) collective-permute-start(bf16[32,2304]{1,0:T(8,128)(2,1)S(1)} %slice.43), channel_id=1, source_target_pairs={{0,8},{1,9},{2,10},{3,11},{4,12},{5,13},{6,14},{7,15},{8,1},{9,0},... | collective-permute-start | bytes 442376 | tf_op jit(solution)/shard_map/ppermute | solution.py:50
  18.9 1.7 %collective-permute-start.4 = (bf16[32,2304]{1,0:T(8,128)(2,1)S(1)}, bf16[32,2304]{1,0:T(8,128)(2,1)S(1)}, u32[]{:S(2)}, u32[]{:S(2)}) collective-permute-start(bf16[32,2304]{1,0:T(8,128)(2,1)S(1)} %slice.43), channel_id=1, source_target_pairs={{0,9},{1,8},{2,11},{3,10},{4,13},{5,12},{6,15},{7,14},{8,0},{9,1},... | collective-permute-start | bytes 442376 | tf_op jit(solution)/shard_map/ppermute | solution.py:50
  20.7 1.8 %collective-permute-start.5 = (bf16[32,2304]{1,0:T(8,128)(2,1)S(1)}, bf16[32,2304]{1,0:T(8,128)(2,1)S(1)}, u32[]{:S(2)}, u32[]{:S(2)}) collective-permute-start(bf16[32,2304]{1,0:T(8,128)(2,1)S(1)} %slice.43), channel_id=1, source_target_pairs={{0,1},{1,0},{2,3},{3,2},{4,5},{5,4},{6,7},{7,6},{8,9},{9,8},{10,11... | collective-permute-start | bytes 442376 | tf_op jit(solution)/shard_map/ppermute | solution.py:50
  22.5 2.5 %collective-permute-done.3 = bf16[32,2304]{1,0:T(8,128)(2,1)S(1)} collective-permute-done((bf16[32,2304]{1,0:T(8,128)(2,1)S(1)}, bf16[32,2304]{1,0:T(8,128)(2,1)S(1)}, u32[]{:S(2)}, u32[]{:S(2)}) %collective-permute-start.3) | collective-permute-done | bytes 147488 | tf_op jit(solution)/shard_map/ppermute | solution.py:50
  25.1 2.3 %collective-permute-done.5 = bf16[32,2304]{1,0:T(8,128)(2,1)S(1)} collective-permute-done((bf16[32,2304]{1,0:T(8,128)(2,1)S(1)}, bf16[32,2304]{1,0:T(8,128)(2,1)S(1)}, u32[]{:S(2)}, u32[]{:S(2)}) %collective-permute-start.5) | collective-permute-done | bytes 147488 | tf_op jit(solution)/shard_map/ppermute | solution.py:50
  27.4 1.1 collective-permute-start.10
  28.5 2.0 %collective-permute-start.11 = (bf16[128,2304]{1,0:T(8,128)(2,1)S(1)}, bf16[128,2304]{1,0:T(8,128)(2,1)S(1)}, u32[]{:S(2)}, u32[]{:S(2)}) collective-permute-start(bf16[128,2304]{1,0:T(8,128)(2,1)S(1)} %pad_maximum_fusion.x0), channel_id=1, source_target_pairs={{0,32},{1,33},{2,34},{3,35},{4,36},{5,37},{6,38},{7,39},{8,40},{9,... | collective-permute-start | bytes 1769480 | tf_op jit(solution)/shard_map/ppermute | solution.py:50
  31.1 2.8 %collective-permute-start.13 = (bf16[128,1792]{1,0:T(8,128)(2,1)S(1)}, bf16[128,1792]{1,0:T(8,128)(2,1)S(1)}, u32[]{:S(2)}, u32[]{:S(2)}) collective-permute-start(bf16[128,1792]{1,0:T(8,128)(2,1)S(1)} %pad_maximum_fusion.1.x0), channel_id=1, source_target_pairs={{0,9},{1,8},{2,11},{3,10},{4,13},{5,12},{6,15},{7,14},{8,0},{9,1},... | collective-permute-start | bytes 1376264 | tf_op jit(solution)/shard_map/ppermute | solution.py:50
  33.8 3.5 %collective-permute-done.10.x2 = bf16[128,2304]{1,0:T(8,128)(2,1)S(1)} collective-permute-done((bf16[128,2304]{1,0:T(8,128)(2,1)S(1)}, bf16[128,2304]{1,0:T(8,128)(2,1)S(1)}, u32[]{:S(2)}, u32[]{:S(2)}) %collective-permute-start.10) | collective-permute-done | bytes 589856 | tf_op jit(solution)/shard_map/ppermute | solution.py:50
  37.3 1.8 %collective-permute-start.14 = (bf16[128,1792]{1,0:T(8,128)(2,1)S(1)}, bf16[128,1792]{1,0:T(8,128)(2,1)S(1)}, u32[]{:S(2)}, u32[]{:S(2)}) collective-permute-start(bf16[128,1792]{1,0:T(8,128)(2,1)S(1)} %pad_maximum_fusion.1.x0), channel_id=1, source_target_pairs={{0,1},{1,0},{2,3},{3,2},{4,5},{5,4},{6,7},{7,6},{8,9},{9,8},{10,11... | collective-permute-start | bytes 1376264 | tf_op jit(solution)/shard_map/ppermute | solution.py:50
  40.0 6.2 %collective-permute-done.9.x1 = bf16[128,2304]{1,0:T(8,128)(2,1)S(1)} collective-permute-done((bf16[128,2304]{1,0:T(8,128)(2,1)S(1)}, bf16[128,2304]{1,0:T(8,128)(2,1)S(1)}, u32[]{:S(2)}, u32[]{:S(2)}) %collective-permute-start.9) | collective-permute-done | bytes 589856 | tf_op jit(solution)/shard_map/ppermute | solution.py:50
  46.2 3.8 %copy-done.2 = bf16[2304,2048]{1,0:T(8,128)(2,1)S(1)} copy-done((bf16[2304,2048]{1,0:T(8,128)(2,1)S(1)}, bf16[2304,2048]{1,0:T(8,128)(2,1)}, u32[]{:S(2)}) %copy-start.2) | copy-done | bytes 9437208
  50.0 9.3 %shard_map.86 = (f32[256,2048]{1,0:T(8,128)S(1)}, f32[256,2048]{1,0:T(8,128)S(1)}) custom-call(bf16[512,512]{1,0:T(8,128)(2,1)S(1)} %get-tuple-element.37.order, bf16[128,2304]{1,0:T(8,128)(2,1)S(1)} %pad_maximum_fusion.x0, bf16[128,2304]{1,0:T(8,128)(2,1)S(1)} %collective-permute-done.9.x1, bf16[128,2304]{1,0:T(8,128)(2,1)S(1)} %collective-permute-done.10.x2, ...), custom_call_target="tpu_custom_call" | custom-call | flops 4831838208 | bytes 13631488 | tf_op jit(solution)/shard_map/pallas_call | solution.py:137
  59.4 4.4 %shard_map.87 = (f32[256,1024]{1,0:T(8,128)S(1)}, f32[256,1024]{1,0:T(8,128)S(1)}, bf16[512,1792]{1,0:T(8,128)(2,1)S(1)}) custom-call(bf16[512,512]{1,0:T(8,128)(2,1)S(1)} %get-tuple-element.43.order, bf16[128,1792]{1,0:T(8,128)(2,1)S(1)} %pad_maximum_fusion.1.x0, bf16[128,1792]{1,0:T(8,128)(2,1)S(1)} %collective-permute-done.12.x1, ...), custom_call_target="tpu_custom_call" | custom-call | flops 1879048192 | bytes 5767168 | tf_op jit(solution)/shard_map/pallas_call | solution.py:137
  64.4 3.3 %shard_map.89 = (f32[256,1024]{1,0:T(8,128)S(1)}, f32[256,1024]{1,0:T(8,128)S(1)}) custom-call(bf16[512,1792]{1,0:T(8,128)(2,1)S(1)} %get-tuple-element.50.rows, bf16[1792,2048]{1,0:T(8,128)(2,1)S(1)} %bitcast.4), custom_call_target="tpu_custom_call" | custom-call | flops 1879048192 | bytes 5767168 | tf_op jit(solution)/shard_map/pallas_call | solution.py:147
  67.8 1.6 %shard_map.88 = (f32[256,1024]{1,0:T(8,128)S(1)}, f32[256,1024]{1,0:T(8,128)S(1)}, f32[3,256,128]{2,1,0:T(8,128)S(1)}) custom-call(f32[256,2048]{1,0:T(8,128)S(1)} %get-tuple-element.39.t_own, f32[256,2048]{1,0:T(8,128)S(1)} %collective-permute-done.15.t_other, f32[256,1024]{1,0:T(8,128)S(1)} %get-tuple-element.47.s_own, ...), custom_call_target="tpu_custom_call" | custom-call | flops 5242880 | bytes 6291456 | tf_op jit(solution)/shard_map/pallas_call | solution.py:205
  69.3 1.0 collective-permute-done.17.s_other
  70.4 1.7 %shard_map.90 = (f32[256,1024]{1,0:T(8,128)S(1)}, f32[256,1024]{1,0:T(8,128)S(1)}, f32[8,128]{1,0:T(8,128)S(1)}) custom-call(f32[3,256,128]{2,1,0:T(8,128)S(1)} %get-tuple-element.49.before, f32[256,2048]{1,0:T(8,128)S(1)} %get-tuple-element.39.t_own, f32[256,2048]{1,0:T(8,128)S(1)} %collective-permute-done.15.t_other, ...), custom_call_target="tpu_custom_call" | custom-call | flops 5242880 | bytes 6291456 | tf_op jit(solution)/shard_map/pallas_call | solution.py:205
  72.7 2.7 %collective-permute-start.19 = (f32[8,128]{1,0:T(8,128)S(1)}, f32[8,128]{1,0:T(8,128)S(1)}, u32[]{:S(2)}, u32[]{:S(2)}) collective-permute-start(f32[8,128]{1,0:T(8,128)S(1)} %get-tuple-element.53), channel_id=1, source_target_pairs={{0,48},{1,49},{2,50},{3,51},{4,52},{5,53},{6,54},{7,55},{8,56},{9,... | collective-permute-start | bytes 12296 | tf_op jit(solution)/shard_map/ppermute | solution.py:50
  75.4 0.8 collective-permute-start.20
  77.0 3.5 %collective-permute-done.20 = f32[8,128]{1,0:T(8,128)S(1)} collective-permute-done((f32[8,128]{1,0:T(8,128)S(1)}, f32[8,128]{1,0:T(8,128)S(1)}, u32[]{:S(2)}, u32[]{:S(2)}) %collective-permute-start.20) | collective-permute-done | bytes 4128 | tf_op jit(solution)/shard_map/ppermute | solution.py:50
  81.3 2.5 %collective-permute-start.22 = (f32[8,128]{1,0:T(8,128)S(1)}, f32[8,128]{1,0:T(8,128)S(1)}, u32[]{:S(2)}, u32[]{:S(2)}) collective-permute-start(f32[8,128]{1,0:T(8,128)S(1)} %add_add_fusion.3), channel_id=1, source_target_pairs={{0,9},{1,8},{2,11},{3,10},{4,13},{5,12},{6,15},{7,14},{8,0},{9,1},... | collective-permute-start | bytes 12296 | tf_op jit(solution)/shard_map/ppermute | solution.py:50
  84.1 1.2 collective-permute-done.21
  85.4 3.5 %collective-permute-done.23 = f32[8,128]{1,0:T(8,128)S(1)} collective-permute-done((f32[8,128]{1,0:T(8,128)S(1)}, f32[8,128]{1,0:T(8,128)S(1)}, u32[]{:S(2)}, u32[]{:S(2)}) %collective-permute-start.23) | collective-permute-done | bytes 4128 | tf_op jit(solution)/shard_map/ppermute | solution.py:50
  89.5 2.6 %collective-permute-start.25 = (f32[8,128]{1,0:T(8,128)S(1)}, f32[8,128]{1,0:T(8,128)S(1)}, u32[]{:S(2)}, u32[]{:S(2)}) collective-permute-start(f32[8,128]{1,0:T(8,128)S(1)} %add_add_fusion.2), channel_id=1, source_target_pairs={{0,6},{1,7},{2,0},{3,1},{4,2},{5,3},{6,4},{7,5},{8,14},{9,15},{10,... | collective-permute-start | bytes 12296 | tf_op jit(solution)/shard_map/ppermute | solution.py:50
  92.6 1.1 collective-permute-done.24
  93.7 3.5 %collective-permute-done.26 = f32[8,128]{1,0:T(8,128)S(1)} collective-permute-done((f32[8,128]{1,0:T(8,128)S(1)}, f32[8,128]{1,0:T(8,128)S(1)}, u32[]{:S(2)}, u32[]{:S(2)}) %collective-permute-start.26) | collective-permute-done | bytes 4128 | tf_op jit(solution)/shard_map/ppermute | solution.py:50
  97.8 2.6 %collective-permute-done.27.other = bf16[256,2048]{1,0:T(8,128)(2,1)S(1)} collective-permute-done((bf16[256,2048]{1,0:T(8,128)(2,1)S(1)}, bf16[256,2048]{1,0:T(8,128)(2,1)S(1)}, u32[]{:S(2)}, u32[]{:S(2)}) %collective-permute-start.27) | collective-permute-done | bytes 1048608 | tf_op jit(solution)/shard_map/ppermute | solution.py:54
  100.4 6.7 %shard_map.92 = (f32[128,1792]{1,0:T(8,128)S(1)}, bf16[128,1792]{1,0:T(8,128)(2,1)S(1)}, bf16[128,1792]{1,0:T(8,128)(2,1)S(1)}, bf16[128,1792]{1,0:T(8,128)(2,1)S(1)}) custom-call(bf16[512,512]{1,0:T(8,128)(2,1)S(1)} %get-tuple-element.60.order, bf16[256,2048]{1,0:T(8,128)(2,1)S(1)} %get-tuple-element.61.own, ...), custom_call_target="tpu_custom_call" | custom-call | flops 3758096384 | bytes 7340032 | tf_op jit(solution)/shard_map/pallas_call | solution.py:272
  107.3 2.0 %collective-permute-start.30 = (bf16[128,1792]{1,0:T(8,128)(2,1)S(1)}, bf16[128,1792]{1,0:T(8,128)(2,1)S(1)}, u32[]{:S(2)}, u32[]{:S(2)}) collective-permute-start(bf16[128,1792]{1,0:T(8,128)(2,1)S(1)} %get-tuple-element.66), channel_id=1, source_target_pairs={{0,16},{1,17},{2,18},{3,19},{4,20},{5,21},{6,22},{7,23},{8,24},{9,... | collective-permute-start | bytes 1376264 | tf_op jit(solution)/shard_map/ppermute | solution.py:50
  110.1 6.9 %shard_map.93 = bf16[1792,2048]{1,0:T(8,128)(2,1)} custom-call(bf16[512,1792]{1,0:T(8,128)(2,1)S(1)} %get-tuple-element.50.rows, bf16[256,2048]{1,0:T(8,128)(2,1)S(1)} %get-tuple-element.61.own, bf16[256,2048]{1,0:T(8,128)(2,1)S(1)} %collective-permute-done.27.other), custom_call_target="tpu_custom_call" | custom-call | flops 3758096384 | bytes 7340032 | tf_op jit(solution)/shard_map/pallas_call | solution.py:294
  117.0 4.9 %collective-permute-done.30 = bf16[128,1792]{1,0:T(8,128)(2,1)S(1)} collective-permute-done((bf16[128,1792]{1,0:T(8,128)(2,1)S(1)}, bf16[128,1792]{1,0:T(8,128)(2,1)S(1)}, u32[]{:S(2)}, u32[]{:S(2)}) %collective-permute-start.30) | collective-permute-done | bytes 458784 | tf_op jit(solution)/shard_map/ppermute | solution.py:50
  122.8 1.5 %collective-permute-start.33 = (bf16[32,1792]{1,0:T(8,128)(2,1)S(1)}, bf16[32,1792]{1,0:T(8,128)(2,1)S(1)}, u32[]{:S(2)}, u32[]{:S(2)}) collective-permute-start(bf16[32,1792]{1,0:T(8,128)(2,1)S(1)} %get-tuple-element.73), channel_id=1, source_target_pairs={{0,8},{1,9},{2,10},{3,11},{4,12},{5,13},{6,14},{7,15},{8,1},{9,0},... | collective-permute-start | bytes 344072 | tf_op jit(solution)/shard_map/ppermute | solution.py:50
  124.6 2.4 %collective-permute-done.32 = bf16[32,1792]{1,0:T(8,128)(2,1)S(1)} collective-permute-done((bf16[32,1792]{1,0:T(8,128)(2,1)S(1)}, bf16[32,1792]{1,0:T(8,128)(2,1)S(1)}, u32[]{:S(2)}, u32[]{:S(2)}) %collective-permute-start.32) | collective-permute-done | bytes 114720 | tf_op jit(solution)/shard_map/ppermute | solution.py:50
  127.1 1.7 %collective-permute-done.33 = bf16[32,1792]{1,0:T(8,128)(2,1)S(1)} collective-permute-done((bf16[32,1792]{1,0:T(8,128)(2,1)S(1)}, bf16[32,1792]{1,0:T(8,128)(2,1)S(1)}, u32[]{:S(2)}, u32[]{:S(2)}) %collective-permute-start.33) | collective-permute-done | bytes 114720 | tf_op jit(solution)/shard_map/ppermute | solution.py:50
  128.8 1.8 %collective-permute-done.34 = bf16[32,1792]{1,0:T(8,128)(2,1)S(1)} collective-permute-done((bf16[32,1792]{1,0:T(8,128)(2,1)S(1)}, bf16[32,1792]{1,0:T(8,128)(2,1)S(1)}, u32[]{:S(2)}, u32[]{:S(2)}) %collective-permute-start.34) | collective-permute-done | bytes 114720 | tf_op jit(solution)/shard_map/ppermute | solution.py:50
  131.0 1.8 %collective-permute-start.36 = (f32[8,1792]{1,0:T(8,128)S(1)}, f32[8,1792]{1,0:T(8,128)S(1)}, u32[]{:S(2)}, u32[]{:S(2)}) collective-permute-start(f32[8,1792]{1,0:T(8,128)S(1)} %get-tuple-element.74), channel_id=1, source_target_pairs={{0,2},{1,3},{2,4},{3,5},{4,6},{5,7},{6,0},{7,1},{8,10},{9,11},{10,... | collective-permute-start | bytes 172040 | tf_op jit(solution)/shard_map/ppermute | solution.py:50
  133.8 1.1 collective-permute-done.35
  134.9 1.5 %collective-permute-done.36 = f32[8,1792]{1,0:T(8,128)S(1)} collective-permute-done((f32[8,1792]{1,0:T(8,128)S(1)}, f32[8,1792]{1,0:T(8,128)S(1)}, u32[]{:S(2)}, u32[]{:S(2)}) %collective-permute-start.36) | collective-permute-done | bytes 57376 | tf_op jit(solution)/shard_map/ppermute | solution.py:50
  136.4 2.1 %collective-permute-done.37 = f32[8,1792]{1,0:T(8,128)S(1)} collective-permute-done((f32[8,1792]{1,0:T(8,128)S(1)}, f32[8,1792]{1,0:T(8,128)S(1)}, u32[]{:S(2)}, u32[]{:S(2)}) %collective-permute-start.37) | collective-permute-done | bytes 57376 | tf_op jit(solution)/shard_map/ppermute | solution.py:50
  (65 shorter events, 11.9 us)
Async XLA Ops:
  0.6 38.5 %copy-start = (s32[3,128,512]{2,1,0:T(8,128)S(1)}, s32[3,128,512]{2,1,0:T(8,128)}, u32[]{:S(2)}) copy-start(s32[3,128,512]{2,1,0:T(8,128)} %constant.4.clone.tables) | copy-start | bytes 2359300
  0.6 38.5 %copy-start.1 = (f32[512]{0:T(512)S(1)}, f32[512]{0:T(512)}, u32[]{:S(2)}) copy-start(f32[512]{0:T(512)} %param.10) | copy-start | bytes 6148
  2.2 5.5 %collective-permute-start = (bf16[8,4096]{1,0:T(8,128)(2,1)S(1)}, bf16[8,4096]{1,0:T(8,128)(2,1)S(1)}, u32[]{:S(2)}, u32[]{:S(2)}) collective-permute-start(bf16[8,4096]{1,0:T(8,128)(2,1)S(1)} %constant_dynamic-update-slice_fusion), channel_id=1, source_target_pairs={{0,2},{1,3},{2,4},{3,5},{4,6},{5,7},{6,0},{7,1},{8,10},{9,11},{10,... | collective-permute-start | bytes 196616 | tf_op jit(solution)/shard_map/ppermute | solution.py:50
  3.9 4.3 %collective-permute-start.1 = (bf16[8,4096]{1,0:T(8,128)(2,1)S(1)}, bf16[8,4096]{1,0:T(8,128)(2,1)S(1)}, u32[]{:S(2)}, u32[]{:S(2)}) collective-permute-start(bf16[8,4096]{1,0:T(8,128)(2,1)S(1)} %constant_dynamic-update-slice_fusion), channel_id=1, source_target_pairs={{0,6},{1,7},{2,0},{3,1},{4,2},{5,3},{6,4},{7,5},{8,14},{9,15},{10,... | collective-permute-start | bytes 196616 | tf_op jit(solution)/shard_map/ppermute | solution.py:50
  5.5 5.8 %collective-permute-start.2 = (bf16[8,4096]{1,0:T(8,128)(2,1)S(1)}, bf16[8,4096]{1,0:T(8,128)(2,1)S(1)}, u32[]{:S(2)}, u32[]{:S(2)}) collective-permute-start(bf16[8,4096]{1,0:T(8,128)(2,1)S(1)} %constant_dynamic-update-slice_fusion), channel_id=1, source_target_pairs={{0,4},{1,5},{2,6},{3,7},{4,0},{5,1},{6,2},{7,3},{8,12},{9,13},{10,... | collective-permute-start | bytes 196616 | tf_op jit(solution)/shard_map/ppermute | solution.py:50
  11.3 9.4 %collective-permute-start.6 = (bf16[32,1792]{1,0:T(8,128)(2,1)S(1)}, bf16[32,1792]{1,0:T(8,128)(2,1)S(1)}, u32[]{:S(2)}, u32[]{:S(2)}) collective-permute-start(bf16[32,1792]{1,0:T(8,128)(2,1)S(1)} %pad_maximum_fusion.3), channel_id=1, source_target_pairs={{0,16},{1,17},{2,18},{3,19},{4,20},{5,21},{6,22},{7,23},{8,24},{9,... | collective-permute-start | bytes 344072 | tf_op jit(solution)/shard_map/ppermute | solution.py:50
  13.3 9.2 %collective-permute-start.7 = (bf16[32,1792]{1,0:T(8,128)(2,1)S(1)}, bf16[32,1792]{1,0:T(8,128)(2,1)S(1)}, u32[]{:S(2)}, u32[]{:S(2)}) collective-permute-start(bf16[32,1792]{1,0:T(8,128)(2,1)S(1)} %pad_maximum_fusion.3), channel_id=1, source_target_pairs={{0,48},{1,49},{2,50},{3,51},{4,52},{5,53},{6,54},{7,55},{8,56},{9,... | collective-permute-start | bytes 344072 | tf_op jit(solution)/shard_map/ppermute | solution.py:50
  15.5 7.0 %collective-permute-start.8 = (bf16[32,1792]{1,0:T(8,128)(2,1)S(1)}, bf16[32,1792]{1,0:T(8,128)(2,1)S(1)}, u32[]{:S(2)}, u32[]{:S(2)}) collective-permute-start(bf16[32,1792]{1,0:T(8,128)(2,1)S(1)} %pad_maximum_fusion.3), channel_id=1, source_target_pairs={{0,32},{1,33},{2,34},{3,35},{4,36},{5,37},{6,38},{7,39},{8,40},{9,... | collective-permute-start | bytes 344072 | tf_op jit(solution)/shard_map/ppermute | solution.py:50
  17.4 7.7 %collective-permute-start.3 = (bf16[32,2304]{1,0:T(8,128)(2,1)S(1)}, bf16[32,2304]{1,0:T(8,128)(2,1)S(1)}, u32[]{:S(2)}, u32[]{:S(2)}) collective-permute-start(bf16[32,2304]{1,0:T(8,128)(2,1)S(1)} %slice.43), channel_id=1, source_target_pairs={{0,8},{1,9},{2,10},{3,11},{4,12},{5,13},{6,14},{7,15},{8,1},{9,0},... | collective-permute-start | bytes 442376 | tf_op jit(solution)/shard_map/ppermute | solution.py:50
  18.9 6.1 %collective-permute-start.4 = (bf16[32,2304]{1,0:T(8,128)(2,1)S(1)}, bf16[32,2304]{1,0:T(8,128)(2,1)S(1)}, u32[]{:S(2)}, u32[]{:S(2)}) collective-permute-start(bf16[32,2304]{1,0:T(8,128)(2,1)S(1)} %slice.43), channel_id=1, source_target_pairs={{0,9},{1,8},{2,11},{3,10},{4,13},{5,12},{6,15},{7,14},{8,0},{9,1},... | collective-permute-start | bytes 442376 | tf_op jit(solution)/shard_map/ppermute | solution.py:50
  20.7 6.6 %collective-permute-start.5 = (bf16[32,2304]{1,0:T(8,128)(2,1)S(1)}, bf16[32,2304]{1,0:T(8,128)(2,1)S(1)}, u32[]{:S(2)}, u32[]{:S(2)}) collective-permute-start(bf16[32,2304]{1,0:T(8,128)(2,1)S(1)} %slice.43), channel_id=1, source_target_pairs={{0,1},{1,0},{2,3},{3,2},{4,5},{5,4},{6,7},{7,6},{8,9},{9,8},{10,11... | collective-permute-start | bytes 442376 | tf_op jit(solution)/shard_map/ppermute | solution.py:50
  27.4 10.0 %collective-permute-start.10 = (bf16[128,2304]{1,0:T(8,128)(2,1)S(1)}, bf16[128,2304]{1,0:T(8,128)(2,1)S(1)}, u32[]{:S(2)}, u32[]{:S(2)}) collective-permute-start(bf16[128,2304]{1,0:T(8,128)(2,1)S(1)} %pad_maximum_fusion.x0), channel_id=1, source_target_pairs={{0,48},{1,49},{2,50},{3,51},{4,52},{5,53},{6,54},{7,55},{8,56},{9,... | collective-permute-start | bytes 1769480 | tf_op jit(solution)/shard_map/ppermute | solution.py:50
  28.5 11.5 %collective-permute-start.11 = (bf16[128,2304]{1,0:T(8,128)(2,1)S(1)}, bf16[128,2304]{1,0:T(8,128)(2,1)S(1)}, u32[]{:S(2)}, u32[]{:S(2)}) collective-permute-start(bf16[128,2304]{1,0:T(8,128)(2,1)S(1)} %pad_maximum_fusion.x0), channel_id=1, source_target_pairs={{0,32},{1,33},{2,34},{3,35},{4,36},{5,37},{6,38},{7,39},{8,40},{9,... | collective-permute-start | bytes 1769480 | tf_op jit(solution)/shard_map/ppermute | solution.py:50
  30.5 15.7 %collective-permute-start.9 = (bf16[128,2304]{1,0:T(8,128)(2,1)S(1)}, bf16[128,2304]{1,0:T(8,128)(2,1)S(1)}, u32[]{:S(2)}, u32[]{:S(2)}) collective-permute-start(bf16[128,2304]{1,0:T(8,128)(2,1)S(1)} %pad_maximum_fusion.x0), channel_id=1, source_target_pairs={{0,16},{1,17},{2,18},{3,19},{4,20},{5,21},{6,22},{7,23},{8,24},{9,... | collective-permute-start | bytes 1769480 | tf_op jit(solution)/shard_map/ppermute | solution.py:50
  30.6 28.7 %collective-permute-start.12 = (bf16[128,1792]{1,0:T(8,128)(2,1)S(1)}, bf16[128,1792]{1,0:T(8,128)(2,1)S(1)}, u32[]{:S(2)}, u32[]{:S(2)}) collective-permute-start(bf16[128,1792]{1,0:T(8,128)(2,1)S(1)} %pad_maximum_fusion.1.x0), channel_id=1, source_target_pairs={{0,8},{1,9},{2,10},{3,11},{4,12},{5,13},{6,14},{7,15},{8,1},{9,0},... | collective-permute-start | bytes 1376264 | tf_op jit(solution)/shard_map/ppermute | solution.py:50
  31.1 28.3 %collective-permute-start.13 = (bf16[128,1792]{1,0:T(8,128)(2,1)S(1)}, bf16[128,1792]{1,0:T(8,128)(2,1)S(1)}, u32[]{:S(2)}, u32[]{:S(2)}) collective-permute-start(bf16[128,1792]{1,0:T(8,128)(2,1)S(1)} %pad_maximum_fusion.1.x0), channel_id=1, source_target_pairs={{0,9},{1,8},{2,11},{3,10},{4,13},{5,12},{6,15},{7,14},{8,0},{9,1},... | collective-permute-start | bytes 1376264 | tf_op jit(solution)/shard_map/ppermute | solution.py:50
  37.3 22.0 %collective-permute-start.14 = (bf16[128,1792]{1,0:T(8,128)(2,1)S(1)}, bf16[128,1792]{1,0:T(8,128)(2,1)S(1)}, u32[]{:S(2)}, u32[]{:S(2)}) collective-permute-start(bf16[128,1792]{1,0:T(8,128)(2,1)S(1)} %pad_maximum_fusion.1.x0), channel_id=1, source_target_pairs={{0,1},{1,0},{2,3},{3,2},{4,5},{5,4},{6,7},{7,6},{8,9},{9,8},{10,11... | collective-permute-start | bytes 1376264 | tf_op jit(solution)/shard_map/ppermute | solution.py:50
  46.2 13.2 %slice-start = ((s8[7340032]{0:T(1024)(128)(4,1)}), s8[4194304]{0:T(1024)(128)(4,1)S(1)}, s32[]{:S(2)}) async-start(s8[7340032]{0:T(1024)(128)(4,1)} %bitcast.3), calls=%async_computation | async-start | bytes 8388608
  46.2 3.8 %copy-start.2 = (bf16[2304,2048]{1,0:T(8,128)(2,1)S(1)}, bf16[2304,2048]{1,0:T(8,128)(2,1)}, u32[]{:S(2)}) copy-start(bf16[2304,2048]{1,0:T(8,128)(2,1)} %weight.4) | copy-start | bytes 28311556
  50.0 9.4 %slice-start.1 = ((s8[7340032]{0:T(1024)(128)(4,1)}), s8[3145728]{0:T(1024)(128)(4,1)S(1)}, s32[]{:S(2)}) async-start(s8[7340032]{0:T(1024)(128)(4,1)} %bitcast.3), calls=%async_computation.1 | async-start | bytes 6291456
  59.3 8.4 %collective-permute-start.15 = (f32[256,2048]{1,0:T(8,128)S(1)}, f32[256,2048]{1,0:T(8,128)S(1)}, u32[]{:S(2)}, u32[]{:S(2)}) collective-permute-start(f32[256,2048]{1,0:T(8,128)S(1)} %get-tuple-element.42), channel_id=1, source_target_pairs={{0,64},{64,0},{1,65},{65,1},{2,66},{66,2},{3,67},{67,3},{4,68},{68... | collective-permute-start | bytes 6291464 | tf_op jit(solution)/shard_map/ppermute | solution.py:54
  63.8 3.9 %collective-permute-start.16 = (f32[256,1024]{1,0:T(8,128)S(1)}, f32[256,1024]{1,0:T(8,128)S(1)}, u32[]{:S(2)}, u32[]{:S(2)}) collective-permute-start(f32[256,1024]{1,0:T(8,128)S(1)} %get-tuple-element.48), channel_id=1, source_target_pairs={{0,64},{64,0},{1,65},{65,1},{2,66},{66,2},{3,67},{67,3},{4,68},{68... | collective-permute-start | bytes 3145736 | tf_op jit(solution)/shard_map/ppermute | solution.py:54
  67.6 2.7 %collective-permute-start.17 = (f32[256,1024]{1,0:T(8,128)S(1)}, f32[256,1024]{1,0:T(8,128)S(1)}, u32[]{:S(2)}, u32[]{:S(2)}) collective-permute-start(f32[256,1024]{1,0:T(8,128)S(1)} %get-tuple-element.52), channel_id=1, source_target_pairs={{0,64},{64,0},{1,65},{65,1},{2,66},{66,2},{3,67},{67,3},{4,68},{68... | collective-permute-start | bytes 3145736 | tf_op jit(solution)/shard_map/ppermute | solution.py:54
  72.1 4.9 %collective-permute-start.18 = (f32[8,128]{1,0:T(8,128)S(1)}, f32[8,128]{1,0:T(8,128)S(1)}, u32[]{:S(2)}, u32[]{:S(2)}) collective-permute-start(f32[8,128]{1,0:T(8,128)S(1)} %get-tuple-element.53), channel_id=1, source_target_pairs={{0,16},{1,17},{2,18},{3,19},{4,20},{5,21},{6,22},{7,23},{8,24},{9,... | collective-permute-start | bytes 12296 | tf_op jit(solution)/shard_map/ppermute | solution.py:50
  72.7 4.3 %collective-permute-start.19 = (f32[8,128]{1,0:T(8,128)S(1)}, f32[8,128]{1,0:T(8,128)S(1)}, u32[]{:S(2)}, u32[]{:S(2)}) collective-permute-start(f32[8,128]{1,0:T(8,128)S(1)} %get-tuple-element.53), channel_id=1, source_target_pairs={{0,48},{1,49},{2,50},{3,51},{4,52},{5,53},{6,54},{7,55},{8,56},{9,... | collective-permute-start | bytes 12296 | tf_op jit(solution)/shard_map/ppermute | solution.py:50
  75.4 5.1 %collective-permute-start.20 = (f32[8,128]{1,0:T(8,128)S(1)}, f32[8,128]{1,0:T(8,128)S(1)}, u32[]{:S(2)}, u32[]{:S(2)}) collective-permute-start(f32[8,128]{1,0:T(8,128)S(1)} %get-tuple-element.53), channel_id=1, source_target_pairs={{0,32},{1,33},{2,34},{3,35},{4,36},{5,37},{6,38},{7,39},{8,40},{9,... | collective-permute-start | bytes 12296 | tf_op jit(solution)/shard_map/ppermute | solution.py:50
  80.5 4.8 %collective-permute-start.21 = (f32[8,128]{1,0:T(8,128)S(1)}, f32[8,128]{1,0:T(8,128)S(1)}, u32[]{:S(2)}, u32[]{:S(2)}) collective-permute-start(f32[8,128]{1,0:T(8,128)S(1)} %add_add_fusion.3), channel_id=1, source_target_pairs={{0,8},{1,9},{2,10},{3,11},{4,12},{5,13},{6,14},{7,15},{8,1},{9,0},... | collective-permute-start | bytes 12296 | tf_op jit(solution)/shard_map/ppermute | solution.py:50
  81.3 4.1 %collective-permute-start.22 = (f32[8,128]{1,0:T(8,128)S(1)}, f32[8,128]{1,0:T(8,128)S(1)}, u32[]{:S(2)}, u32[]{:S(2)}) collective-permute-start(f32[8,128]{1,0:T(8,128)S(1)} %add_add_fusion.3), channel_id=1, source_target_pairs={{0,9},{1,8},{2,11},{3,10},{4,13},{5,12},{6,15},{7,14},{8,0},{9,1},... | collective-permute-start | bytes 12296 | tf_op jit(solution)/shard_map/ppermute | solution.py:50
  83.8 5.1 %collective-permute-start.23 = (f32[8,128]{1,0:T(8,128)S(1)}, f32[8,128]{1,0:T(8,128)S(1)}, u32[]{:S(2)}, u32[]{:S(2)}) collective-permute-start(f32[8,128]{1,0:T(8,128)S(1)} %add_add_fusion.3), channel_id=1, source_target_pairs={{0,1},{1,0},{2,3},{3,2},{4,5},{5,4},{6,7},{7,6},{8,9},{9,8},{10,11... | collective-permute-start | bytes 12296 | tf_op jit(solution)/shard_map/ppermute | solution.py:50
  88.9 4.8 %collective-permute-start.24 = (f32[8,128]{1,0:T(8,128)S(1)}, f32[8,128]{1,0:T(8,128)S(1)}, u32[]{:S(2)}, u32[]{:S(2)}) collective-permute-start(f32[8,128]{1,0:T(8,128)S(1)} %add_add_fusion.2), channel_id=1, source_target_pairs={{0,2},{1,3},{2,4},{3,5},{4,6},{5,7},{6,0},{7,1},{8,10},{9,11},{10,... | collective-permute-start | bytes 12296 | tf_op jit(solution)/shard_map/ppermute | solution.py:50
  89.5 4.2 %collective-permute-start.25 = (f32[8,128]{1,0:T(8,128)S(1)}, f32[8,128]{1,0:T(8,128)S(1)}, u32[]{:S(2)}, u32[]{:S(2)}) collective-permute-start(f32[8,128]{1,0:T(8,128)S(1)} %add_add_fusion.2), channel_id=1, source_target_pairs={{0,6},{1,7},{2,0},{3,1},{4,2},{5,3},{6,4},{7,5},{8,14},{9,15},{10,... | collective-permute-start | bytes 12296 | tf_op jit(solution)/shard_map/ppermute | solution.py:50
  92.1 5.1 %collective-permute-start.26 = (f32[8,128]{1,0:T(8,128)S(1)}, f32[8,128]{1,0:T(8,128)S(1)}, u32[]{:S(2)}, u32[]{:S(2)}) collective-permute-start(f32[8,128]{1,0:T(8,128)S(1)} %add_add_fusion.2), channel_id=1, source_target_pairs={{0,4},{1,5},{2,6},{3,7},{4,0},{5,1},{6,2},{7,3},{8,12},{9,13},{10,... | collective-permute-start | bytes 12296 | tf_op jit(solution)/shard_map/ppermute | solution.py:50
  97.7 2.7 %collective-permute-start.27 = (bf16[256,2048]{1,0:T(8,128)(2,1)S(1)}, bf16[256,2048]{1,0:T(8,128)(2,1)S(1)}, u32[]{:S(2)}, u32[]{:S(2)}) collective-permute-start(bf16[256,2048]{1,0:T(8,128)(2,1)S(1)} %get-tuple-element.61.own), channel_id=1, source_target_pairs={{0,64},{64,0},{1,65},{65,1},{2,66},{66,2},{3,67},{67,3},{4,68},{68... | collective-permute-start | bytes 3145736 | tf_op jit(solution)/shard_map/ppermute | solution.py:54
  107.2 9.8 %collective-permute-start.29 = (bf16[128,1792]{1,0:T(8,128)(2,1)S(1)}, bf16[128,1792]{1,0:T(8,128)(2,1)S(1)}, u32[]{:S(2)}, u32[]{:S(2)}) collective-permute-start(bf16[128,1792]{1,0:T(8,128)(2,1)S(1)} %get-tuple-element.65), channel_id=1, source_target_pairs={{0,48},{1,49},{2,50},{3,51},{4,52},{5,53},{6,54},{7,55},{8,56},{9,... | collective-permute-start | bytes 1376264 | tf_op jit(solution)/shard_map/ppermute | solution.py:50
  107.3 14.7 %collective-permute-start.30 = (bf16[128,1792]{1,0:T(8,128)(2,1)S(1)}, bf16[128,1792]{1,0:T(8,128)(2,1)S(1)}, u32[]{:S(2)}, u32[]{:S(2)}) collective-permute-start(bf16[128,1792]{1,0:T(8,128)(2,1)S(1)} %get-tuple-element.66), channel_id=1, source_target_pairs={{0,16},{1,17},{2,18},{3,19},{4,20},{5,21},{6,22},{7,23},{8,24},{9,... | collective-permute-start | bytes 1376264 | tf_op jit(solution)/shard_map/ppermute | solution.py:50
  109.3 12.7 %collective-permute-start.31 = (bf16[128,1792]{1,0:T(8,128)(2,1)S(1)}, bf16[128,1792]{1,0:T(8,128)(2,1)S(1)}, u32[]{:S(2)}, u32[]{:S(2)}) collective-permute-start(bf16[128,1792]{1,0:T(8,128)(2,1)S(1)} %get-tuple-element.67), channel_id=1, source_target_pairs={{0,32},{1,33},{2,34},{3,35},{4,36},{5,37},{6,38},{7,39},{8,40},{9,... | collective-permute-start | bytes 1376264 | tf_op jit(solution)/shard_map/ppermute | solution.py:50
  110.1 6.9 %collective-permute-start.28 = (f32[2,128]{1,0:T(2,128)S(1)}, f32[2,128]{1,0:T(2,128)S(1)}, u32[]{:S(2)}, u32[]{:S(2)}) collective-permute-start(f32[2,128]{1,0:T(2,128)S(1)} %get-tuple-element.59), channel_id=1, source_target_pairs={{0,64},{64,0},{1,65},{65,1},{2,66},{66,2},{3,67},{67,3},{4,68},{68... | collective-permute-start | bytes 3080 | tf_op jit(solution)/shard_map/ppermute | solution.py:54
  122.2 4.9 %collective-permute-start.32 = (bf16[32,1792]{1,0:T(8,128)(2,1)S(1)}, bf16[32,1792]{1,0:T(8,128)(2,1)S(1)}, u32[]{:S(2)}, u32[]{:S(2)}) collective-permute-start(bf16[32,1792]{1,0:T(8,128)(2,1)S(1)} %get-tuple-element.71), channel_id=1, source_target_pairs={{0,9},{1,8},{2,11},{3,10},{4,13},{5,12},{6,15},{7,14},{8,0},{9,1},... | collective-permute-start | bytes 344072 | tf_op jit(solution)/shard_map/ppermute | solution.py:50
  122.8 6.0 %collective-permute-start.33 = (bf16[32,1792]{1,0:T(8,128)(2,1)S(1)}, bf16[32,1792]{1,0:T(8,128)(2,1)S(1)}, u32[]{:S(2)}, u32[]{:S(2)}) collective-permute-start(bf16[32,1792]{1,0:T(8,128)(2,1)S(1)} %get-tuple-element.73), channel_id=1, source_target_pairs={{0,8},{1,9},{2,10},{3,11},{4,12},{5,13},{6,14},{7,15},{8,1},{9,0},... | collective-permute-start | bytes 344072 | tf_op jit(solution)/shard_map/ppermute | solution.py:50
  124.3 6.3 %collective-permute-start.34 = (bf16[32,1792]{1,0:T(8,128)(2,1)S(1)}, bf16[32,1792]{1,0:T(8,128)(2,1)S(1)}, u32[]{:S(2)}, u32[]{:S(2)}) collective-permute-start(bf16[32,1792]{1,0:T(8,128)(2,1)S(1)} %get-tuple-element.72), channel_id=1, source_target_pairs={{0,1},{1,0},{2,3},{3,2},{4,5},{5,4},{6,7},{7,6},{8,9},{9,8},{10,11... | collective-permute-start | bytes 344072 | tf_op jit(solution)/shard_map/ppermute | solution.py:50
  130.7 4.2 %collective-permute-start.35 = (f32[8,1792]{1,0:T(8,128)S(1)}, f32[8,1792]{1,0:T(8,128)S(1)}, u32[]{:S(2)}, u32[]{:S(2)}) collective-permute-start(f32[8,1792]{1,0:T(8,128)S(1)} %get-tuple-element.76), channel_id=1, source_target_pairs={{0,6},{1,7},{2,0},{3,1},{4,2},{5,3},{6,4},{7,5},{8,14},{9,15},{10,... | collective-permute-start | bytes 172040 | tf_op jit(solution)/shard_map/ppermute | solution.py:50
  131.0 5.4 %collective-permute-start.36 = (f32[8,1792]{1,0:T(8,128)S(1)}, f32[8,1792]{1,0:T(8,128)S(1)}, u32[]{:S(2)}, u32[]{:S(2)}) collective-permute-start(f32[8,1792]{1,0:T(8,128)S(1)} %get-tuple-element.74), channel_id=1, source_target_pairs={{0,2},{1,3},{2,4},{3,5},{4,6},{5,7},{6,0},{7,1},{8,10},{9,11},{10,... | collective-permute-start | bytes 172040 | tf_op jit(solution)/shard_map/ppermute | solution.py:50
  132.8 5.7 %collective-permute-start.37 = (f32[8,1792]{1,0:T(8,128)S(1)}, f32[8,1792]{1,0:T(8,128)S(1)}, u32[]{:S(2)}, u32[]{:S(2)}) collective-permute-start(f32[8,1792]{1,0:T(8,128)S(1)} %get-tuple-element.75), channel_id=1, source_target_pairs={{0,4},{1,5},{2,6},{3,7},{4,0},{5,1},{6,2},{7,3},{8,12},{9,13},{10,... | collective-permute-start | bytes 172040 | tf_op jit(solution)/shard_map/ppermute | solution.py:50

commit v3 on v2

v3 whole, which is shorter than its diff:
```python
import functools

import jax
import jax.numpy as jnp
import numpy as np
from jax import lax
from jax.experimental import pallas as pl
from jax.experimental.pallas import tpu as pltpu
from jax.sharding import PartitionSpec as P

softcap_limit = 30.0
tokens, teacher_width, student_width, vocab_local = 512, 2304, 1792, 2048
width = teacher_width + student_width
half = tokens // 2
apart = 1536
everyone = ("mp", "batch", "vocab")
mega = 1024 * 1024

offsets = (0, 1, 3, 2)
main_axes = (("y", "z"), ("x", "x"), ("z", "y"))
apart_axes = (("y", "z"), ("z", "y"), ("x", "x"))
reduce_axes = (("z", "y"), ("x", "z"), ("y", "x"))


def place(index):
    core, z, x_lo, y, x_hi = np.unravel_index(index, (2, 4, 2, 4, 2))
    return {"core": int(core), "x": int(2 * x_hi + x_lo), "y": int(y), "z": int(z)}


def index_of(at):
    return int(
        np.ravel_multi_index(
            (at["core"], at["z"], at["x"] % 2, at["y"], at["x"] // 2), (2, 4, 2, 4, 2)
        )
    )


def moved(at, axis, by):
    return {**at, axis: (at[axis] + by) % 4}


def ring(axes, by):
    pairs = []
    for source in range(128):
        at = place(source)
        pairs.append((source, index_of(moved(at, axes[at["core"]], by))))
    return pairs


def send(block, axes, by):
    return lax.ppermute(block, everyone, ring(axes, by))


def swap(block):
    return lax.ppermute(block, "mp", [(0, 1), (1, 0)])


def side_by_side_kernel(teacher, student, out, held_teacher, held_student, arrived):
    copies = [
        pltpu.make_async_copy(teacher, held_teacher, arrived.at[0]),
        pltpu.make_async_copy(student, held_student, arrived.at[1]),
    ]
    for copy in copies:
        copy.start()
    for copy in copies:
        copy.wait()
    out[:, :apart] = held_student[:, :apart]
    out[:, apart : apart + teacher_width] = held_teacher[...]
    out[:, apart + teacher_width :] = held_student[:, apart:]


def side_by_side(teacher, student):
    return pl.pallas_call(
        side_by_side_kernel,
        in_specs=[pl.BlockSpec(memory_space=pl.ANY)] * 2,
        out_specs=whole(),
        out_shape=jax.ShapeDtypeStruct((teacher.shape[0], width), teacher.dtype),
        scratch_shapes=[
            pltpu.VMEM(teacher.shape, teacher.dtype),
            pltpu.VMEM(student.shape, student.dtype),
            pltpu.SemaphoreType.DMA((2,)),
        ],
        compiler_params=pltpu.CompilerParams(vmem_limit_bytes=mega),
        cost_estimate=cost(0, 4 * teacher.shape[0] * width),
    )(teacher, student)


def gathered(order, blocks, first, rows):
    step = 256
    for at in range(0, rows.shape[1], step):
        cols = slice(first + at, first + at + step)
        block = jnp.concatenate([x[:, cols] for x in blocks], axis=0)
        rows[:, at : at + step] = jnp.dot(
            order[...], block, preferred_element_type=jnp.float32
        ).astype(jnp.bfloat16)


def logits(rows, weight, first, own, other):
    step = 512
    for at in range(0, own.shape[1], step):
        raw = jnp.dot(
            rows[...], weight[:, first + at : first + at + step], preferred_element_type=jnp.float32
        )
        own[:, at : at + step], other[:, at : at + step] = raw[:half], raw[half:]


def teacher_kernel(order, x0, x1, x2, x3, weight, own, other, rows):
    gathered(order, (x0, x1, x2, x3), 0, rows)
    logits(rows, weight, 0, own, other)


def student_kernel(main_order, apart_order, *refs):
    main, separate, (weight, own, other, rows) = refs[:4], refs[4:8], refs[8:]
    gathered(apart_order, separate, 0, rows.at[:, :apart])
    gathered(main_order, main, teacher_width, rows.at[:, apart:])
    logits(rows, weight, 0, own, other)


def student_rest_kernel(rows, weight, own, other):
    logits(rows, weight, vocab_local - own.shape[1], own, other)


def own_place(token, at, axes_of, core):
    block, row = token // 8, token % 8
    for stage, axes in enumerate(axes_of):
        digit = (block >> (2 * stage)) & 3
        offset = digit ^ (digit >> 1)
        for axis in at:
            taken = (axes[0] == axis) * (1 - core) + (axes[1] == axis) * core
            at[axis] = at[axis] - taken * offset
    x, y, z = (at[axis] & 3 for axis in "xyz")
    owner = z * 16 + (x & 1) * 8 + y * 2 + (x >> 1)
    return ((owner - 32 * core) & 63) * 8 + row


def setup_kernel(token_weight, _, main_order, apart_order, reduce_order, weight_here, first_core):
    core = lax.axis_index("mp")
    batch, vocab = lax.axis_index("batch"), lax.axis_index("vocab")
    at = {"x": (vocab % 2) * 2 + batch % 2, "y": vocab // 2, "z": batch // 2}
    token = lax.broadcasted_iota(jnp.int32, (1, tokens), 1)
    rows = lax.broadcasted_iota(jnp.int32, (tokens, tokens), 0)
    for order, axes_of in (
        (main_order, main_axes),
        (apart_order, apart_axes),
        (reduce_order, reduce_axes[::-1]),
    ):
        places = own_place(token, dict(at), axes_of, core)
        order[...] = jnp.where(rows == places, 1.0, 0.0).astype(jnp.bfloat16)
    weight_here[...] = token_weight[pl.ds(core * 2, 2), :]
    first_core[...] = jnp.full(first_core.shape, 1.0, jnp.float32) * (core == 0).astype(jnp.float32)


def setup(token_weight, weight):
    order = jax.ShapeDtypeStruct((tokens, tokens), jnp.bfloat16)
    small = jax.ShapeDtypeStruct((2, 128), jnp.float32)
    return pl.pallas_call(
        setup_kernel,
        in_specs=[whole(), pl.BlockSpec(memory_space=pl.ANY)],
        out_specs=[whole()] * 5,
        out_shape=[order] * 3 + [small] * 2,
        compiler_params=pltpu.CompilerParams(vmem_limit_bytes=4 * mega),
        cost_estimate=cost(0, 2 * mega),
    )(token_weight.reshape(4, 128), weight)


def cost(macs, moved, transcendentals=0):
    return pl.CostEstimate(flops=2 * macs, bytes_accessed=moved, transcendentals=transcendentals)


def whole():
    return pl.BlockSpec(memory_space=pltpu.VMEM)


def raw_shapes(cols):
    return [jax.ShapeDtypeStruct((half, cols), jnp.float32)] * 2


def teacher_logits(order, blocks, weight):
    return pl.pallas_call(
        teacher_kernel,
        in_specs=[whole()] * 6,
        out_specs=[whole()] * 2,
        out_shape=raw_shapes(vocab_local),
        scratch_shapes=[pltpu.VMEM((tokens, teacher_width), jnp.bfloat16)],
        compiler_params=pltpu.CompilerParams(vmem_limit_bytes=24 * mega),
        cost_estimate=cost(tokens * weight.size, 2 * weight.size),
    )(order, *blocks, weight)


def student_logits(main_order, apart_order, main, separate, weight, cols):
    return pl.pallas_call(
        student_kernel,
        in_specs=[whole()] * 11,
        out_specs=[whole()] * 3,
        out_shape=raw_shapes(cols) + [jax.ShapeDtypeStruct((tokens, student_width), jnp.bfloat16)],
        compiler_params=pltpu.CompilerParams(vmem_limit_bytes=20 * mega),
        cost_estimate=cost(tokens * student_width * cols, 2 * weight.size),
    )(main_order, apart_order, *main, *separate, weight)


def student_rest(rows, weight, cols):
    return pl.pallas_call(
        student_rest_kernel,
        in_specs=[whole()] * 2,
        out_specs=[whole()] * 2,
        out_shape=raw_shapes(cols),
        compiler_params=pltpu.CompilerParams(vmem_limit_bytes=16 * mega),
        cost_estimate=cost(tokens * student_width * cols, 2 * weight.size),
    )(rows, weight)


def lanes(values):
    total = values[:, :128]
    for at in range(128, values.shape[1], 128):
        total += values[:, at : at + 128]
    return total


def statistics_kernel(last, before, t_own, t_other, s_own, s_other, student_part, teacher_part, out, sums):
    @pl.when(pl.program_id(0) == 0)
    def _():
        sums[...] = before[...] if last else jnp.zeros_like(sums)

    teacher_tanh = jnp.tanh((t_own[...] + t_other[...]) * (1.0 / softcap_limit))
    student_tanh = jnp.tanh((s_own[...] + s_other[...]) * (1.0 / softcap_limit))
    teacher_exp = jnp.exp(softcap_limit * teacher_tanh - softcap_limit)
    student_exp = jnp.exp(softcap_limit * student_tanh - softcap_limit)
    slope = 1.0 - student_tanh * student_tanh
    student_part[...] = student_exp * slope
    teacher_part[...] = teacher_exp * slope
    sums[0] += lanes(teacher_exp)
    sums[1] += lanes(student_exp)
    sums[2] += lanes(teacher_exp * (softcap_limit * (teacher_tanh - student_tanh)))

    @pl.when(pl.program_id(0) == pl.num_programs(0) - 1)
    def _():
        if last:
            rows = [
                jnp.sum(sums[i, at : at + 128].T, axis=0, keepdims=True)
                for i in range(3)
                for at in (0, 128)
            ]
            out[...] = jnp.concatenate(rows + [jnp.zeros((2, 128), jnp.float32)], axis=0)
        else:
            out[...] = sums[...]


def statistics(teacher, student, chunk, before=None, tile=256):
    cols = student[0].shape[1]
    steps = cols // tile
    last = before is not None
    from_teacher = pl.BlockSpec((half, tile), lambda j: (0, chunk * steps + j))
    part = pl.BlockSpec((half, tile), lambda j: (0, j))
    shape = jax.ShapeDtypeStruct((half, cols), jnp.float32)
    sums = (3, half, 128)
    kernel = functools.partial(statistics_kernel, last)
    if not last:
        kernel = functools.partial(statistics_kernel, last, None)
    return pl.pallas_call(
        kernel,
        grid=(steps,),
        in_specs=[whole()] * last + [from_teacher] * 2 + [part] * 2,
        out_specs=[part, part, whole()],
        out_shape=[
            shape,
            shape,
            jax.ShapeDtypeStruct((8, 128) if last else sums, jnp.float32),
        ],
        scratch_shapes=[pltpu.VMEM(sums, jnp.float32)],
        compiler_params=pltpu.CompilerParams(vmem_limit_bytes=7 * mega),
        cost_estimate=cost(10 * half * cols, 24 * half * cols, 4 * half * cols),
    )(*([before] if last else []), *teacher, *student)


def gap_kernel(total, token_weight, student0, teacher0, student1, teacher1, gap, divergence):
    teacher_total, student_total, cross = total[0:2], total[2:4], total[4:6]
    divergence[...] = cross / teacher_total - jnp.log(teacher_total) + jnp.log(student_total)
    rows = [token_weight[...] / student_total, token_weight[...] / teacher_total, total[0:4]]
    scales = jnp.concatenate(rows, axis=0).T
    cols = student0.shape[1]
    for i in range(2):
        at = slice(128 * i, 128 * (i + 1))
        student_scale, teacher_scale = scales[:, i : i + 1], scales[:, 2 + i : 3 + i]
        for first, student, teacher in ((0, student0, teacher0), (cols, student1, teacher1)):
            gap[at, first : first + cols] = (
                student[at] * student_scale - teacher[at] * teacher_scale
            ).astype(jnp.bfloat16)


def gap_of(total, token_weight, parts):
    return pl.pallas_call(
        gap_kernel,
        in_specs=[whole()] * 6,
        out_specs=[whole(), whole()],
        out_shape=[
            jax.ShapeDtypeStruct((half, vocab_local), jnp.bfloat16),
            jax.ShapeDtypeStruct((2, 128), jnp.float32),
        ],
        compiler_params=pltpu.CompilerParams(vmem_limit_bytes=4 * mega),
        cost_estimate=cost(2 * half * vocab_local, 10 * half * vocab_local),
    )(total, token_weight, *parts)


part = student_width // 2


def hidden_term(gap, weight, keep, sends):
    term = lax.dot_general(gap, weight, (((1,), (1,)), ((), ())), preferred_element_type=jnp.float32)
    keep[...] = term[:128]
    for i, send in enumerate(sends):
        send[...] = term[128 * (i + 1) : 128 * (i + 2)].astype(jnp.bfloat16)


def hidden_first_kernel(order, own, other, weight, gap, keep, *sends):
    step = 512
    for at in range(0, vocab_local, step):
        cols = slice(at, at + step)
        block = jnp.concatenate([own[:, cols], other[:, cols]], axis=0)
        gap[:, cols] = lax.dot_general(
            order[...], block, (((0,), (0,)), ((), ())), preferred_element_type=jnp.float32
        ).astype(jnp.bfloat16)
    hidden_term(gap[...], weight[:part], keep, sends)


def hidden_second_kernel(gap, weight, keep, *sends):
    hidden_term(gap[...], weight[part:], keep, sends)


def hidden_shapes():
    return [jax.ShapeDtypeStruct((128, part), jnp.float32)] + [
        jax.ShapeDtypeStruct((128, part), jnp.bfloat16)
    ] * 3


def hidden_first(order, own, other, weight):
    return pl.pallas_call(
        hidden_first_kernel,
        in_specs=[whole()] * 4,
        out_specs=[whole()] * 5,
        out_shape=[jax.ShapeDtypeStruct((tokens, vocab_local), jnp.bfloat16)] + hidden_shapes(),
        compiler_params=pltpu.CompilerParams(vmem_limit_bytes=20 * mega),
        cost_estimate=cost(tokens * weight.size // 2, weight.size),
    )(order, own, other, weight)


def hidden_second(gap, weight):
    return pl.pallas_call(
        hidden_second_kernel,
        in_specs=[whole()] * 2,
        out_specs=[whole()] * 4,
        out_shape=hidden_shapes(),
        compiler_params=pltpu.CompilerParams(vmem_limit_bytes=18 * mega),
        cost_estimate=cost(tokens * weight.size // 2, weight.size),
    )(gap, weight)


def total_of(keep, received, at, size):
    rows = pl.ds(at, size)
    return keep[rows] + sum(r[rows].astype(jnp.float32) for r in received)


def first_sum_kernel(*refs):
    halves, (keep, *sends) = (refs[:4], refs[4:8]), refs[8:]
    for i, (mine, *received) in enumerate(halves):
        cols = slice(i * part, (i + 1) * part)
        keep[:, cols] = total_of(mine, received, 0, 32)
        for j, send in enumerate(sends):
            send[:, cols] = total_of(mine, received, 32 * (j + 1), 32).astype(send.dtype)


def first_sum(halves):
    shape = (32, student_width)
    return pl.pallas_call(
        first_sum_kernel,
        in_specs=[whole()] * 8,
        out_specs=[whole()] * 4,
        out_shape=[jax.ShapeDtypeStruct(shape, jnp.float32)]
        + [jax.ShapeDtypeStruct(shape, jnp.bfloat16)] * 3,
        compiler_params=pltpu.CompilerParams(vmem_limit_bytes=6 * mega),
        cost_estimate=cost(128 * student_width * 4, 2 * mega),
    )(*halves[0], *halves[1])


def second_sum_kernel(mine, *refs):
    received, (keep, *sends) = refs[:3], refs[3:]
    total = mine[...] + sum(r[...].astype(jnp.float32) for r in received)
    keep[...] = total[:8]
    for j, send in enumerate(sends):
        send[...] = total[8 * (j + 1) : 8 * (j + 2)]


def second_sum(mine, received):
    return pl.pallas_call(
        second_sum_kernel,
        in_specs=[whole()] * 4,
        out_specs=[whole()] * 4,
        out_shape=[jax.ShapeDtypeStruct((8, student_width), jnp.float32)] * 4,
        compiler_params=pltpu.CompilerParams(vmem_limit_bytes=3 * mega),
        cost_estimate=cost(32 * student_width * 4, mega),
    )(mine, *received)


def weight_kernel(rows, own, other, *refs):
    over_rows = (((0,), (0,)), ((), ()))
    refs[-1][...] = (
        lax.dot_general(rows[:half], own[...], over_rows, preferred_element_type=jnp.float32)
        + lax.dot_general(rows[half:], other[...], over_rows, preferred_element_type=jnp.float32)
    ).astype(jnp.bfloat16)


def grad_weight_part(rows, own, other, first, steps, before=None, tile=256):
    more = [] if before is None else [before]
    return pl.pallas_call(
        weight_kernel,
        grid=(steps,),
        in_specs=[pl.BlockSpec((tokens, tile), lambda j: (0, first + j)), whole(), whole()]
        + [pl.BlockSpec(memory_space=pl.ANY)] * len(more),
        out_specs=pl.BlockSpec((tile, vocab_local), lambda j: (first + j, 0)),
        out_shape=jax.ShapeDtypeStruct((student_width, vocab_local), jnp.bfloat16),
        input_output_aliases={3: 0} if more else {},
        compiler_params=pltpu.CompilerParams(vmem_limit_bytes=9 * mega),
        cost_estimate=cost(tokens * steps * tile * vocab_local, 2 * steps * tile * vocab_local),
    )(rows, own, other, *more)


def local(hidden_teacher, hidden_student, teacher_weight, student_weight, token_weight):
    main_order, apart_order, reduce_order, weight_here, first_core = setup(
        token_weight, teacher_weight
    )

    def shared_along(block, axes):
        return [block] + [send(block, axes, by) for by in offsets[1:]]

    def joined(blocks):
        return jnp.concatenate(blocks, axis=0)

    block = joined(shared_along(side_by_side(hidden_teacher, hidden_student), main_axes[0]))
    separate, main = block[:, :apart], block[:, apart:]
    main, separate = shared_along(main, main_axes[1]), shared_along(separate, apart_axes[1])
    main, *separate = lax.optimization_barrier((joined(main), *separate))
    separate = joined(separate)
    main = shared_along(main, main_axes[2])
    separate = shared_along(separate, apart_axes[2])
    teacher_own, teacher_other = teacher_logits(main_order, main, teacher_weight)
    teacher_other, *separate = lax.optimization_barrier((teacher_other, *separate))
    teacher_raw = (teacher_own, swap(teacher_other))
    cols = vocab_local // 2
    own, other, rows = student_logits(main_order, apart_order, main, separate, student_weight, cols)
    student_raw0 = (own, swap(other))
    own, other = student_rest(rows, student_weight, cols)
    student_raw1 = (own, swap(other))
    student_part0, teacher_part0, sums = statistics(teacher_raw, student_raw0, 0)
    student_part1, teacher_part1, sums = statistics(teacher_raw, student_raw1, 1, sums)
    for axes in reduce_axes:
        sums = sum(shared_along(sums, axes))
    gap, divergence = gap_of(
        sums, weight_here, (student_part0, teacher_part0, student_part1, teacher_part1)
    )
    gap_other = swap(gap)

    def sent_back(sends, axes):
        return [send(b, axes, -by) for b, by in zip(sends, offsets[1:])]

    gap_order, keep0, *sends = hidden_first(reduce_order, gap, gap_other, student_weight)
    received0 = sent_back(sends, reduce_axes[0])
    keep1, *sends = hidden_second(gap_order, student_weight)
    received1 = sent_back(sends, reduce_axes[0])
    divergence_other = swap(divergence)
    grad_weight = grad_weight_part(rows, gap, gap_other, 0, 4)
    keep0, grad_weight, divergence_other = lax.optimization_barrier(
        (keep0, grad_weight, divergence_other)
    )
    keep, *sends = first_sum(((keep0, *received0), (keep1, *received1)))
    received = sent_back(sends, reduce_axes[1])
    grad_weight = grad_weight_part(rows, gap, gap_other, 4, 3, grad_weight)
    keep, grad_weight = lax.optimization_barrier((keep, grad_weight))
    keep, *sends = second_sum(keep, received)
    received = sent_back(sends, reduce_axes[2])
    grad_hidden = (keep + sum(received)).astype(jnp.bfloat16)

    first_core = first_core > 0.5
    divergence = jnp.concatenate(
        [
            jnp.where(first_core, divergence, divergence_other),
            jnp.where(first_core, divergence_other, divergence),
        ]
    ).reshape(tokens)
    return (divergence, grad_hidden, grad_weight)


def solution(mesh):
    placed = (
        P(("batch", "vocab"), "mp"),
        P(("batch", "vocab"), "mp"),
        P("mp", ("batch", "vocab")),
        P("mp", ("batch", "vocab")),
        P(),
    )
    return jax.shard_map(
        local,
        mesh=mesh,
        in_specs=placed,
        out_specs=(P(), P(("batch", "vocab"), "mp"), P("mp", ("batch", "vocab"))),
        check_vma=False,
    )
```

time: 139 us -> 130 us (0.935)
  waiting for transfers between devices: 51.7 us -> 43.2 us
  Pallas kernels: 34.5 us -> 29.2 us
  starting transfers between devices: 44.9 us -> 48.8 us
    ppermute x33 -> x36, waiting for transfers between devices: 48 us -> 39.5 us  [send(): return lax.ppermute(block, everyone, ring(axes, by))]
    pallas_call x6 -> x11, Pallas kernels: 30.8 us -> 25.5 us  [the longest x2 7.67 us: grad_weight_part(): pl.pallas_call(weight_kernel, grid=(steps,), in_specs=[pl.BlockSpec((toke...]
    ppermute x33 -> x36, starting transfers between devices: 44 us -> 47.6 us  [send(): return lax.ppermute(block, everyone, ring(axes, by))]
    unnamed x11 -> x17, local copies, waits for them, and re-layouts: 4.69 us -> 5.9 us
  transfers between devices with their start and end apart: 38 -> 41, of which waited for: 23 -> 24; matrix products, arithmetic and copies ran while one was open for 0% -> 1% of each run, Pallas kernels for 18% -> 18%
where the time goes in v3:
time: 130 us; the launch traced here: 129 us
  starting transfers between devices  48.8 us (38%)
  waiting for transfers between devices  43.2 us (33%)
  Pallas kernels  29.2 us (22%)
  local copies, waits for them, and re-layouts  5.93 us (5%)
  other arithmetic  1.31 us (1%)
    ppermute x36, starting transfers between devices, send(): return lax.ppermute(block, everyone, ring(axes, by))  47.6 us
    ppermute x36, waiting for transfers between devices, send(): return lax.ppermute(block, everyone, ring(axes, by))  39.5 us
    pallas_call x2, Pallas kernels, grad_weight_part(): pl.pallas_call(weight_kernel, grid=(steps,), in_specs=[pl.BlockSpec((toke...  7.67 us
    pallas_call x1, Pallas kernels, teacher_logits(): pl.pallas_call(teacher_kernel, in_specs=[whole()] * 6, out_specs=[whole()...  6.25 us
    unnamed x17, local copies, waits for them, and re-layouts  5.9 us
    ppermute x5, waiting for transfers between devices, swap(): return lax.ppermute(block, 'mp', [(0, 1), (1, 0)])  3.71 us
    pallas_call x1, Pallas kernels, hidden_first(): pl.pallas_call(hidden_first_kernel, in_specs=[whole()] * 4, out_specs=[wh...  3.44 us
    pallas_call x2, Pallas kernels, statistics(): pl.pallas_call(kernel, grid=(steps,), in_specs=[whole()] * last + [from_t...  3.27 us
  transfers between devices with their start and end apart: 41, of which 24 were waited for; matrix products, arithmetic and copies ran while one was open for 1% of the time, Pallas kernels for 18%

profile of v3, /device:TPU:0, one launch (start us, length us, event | category | flops | bytes accessed | tf_op | source)
XLA Modules:
  0.0 129.3 jit_solution(15592595837799877053)
XLA Ops:
  2.2 3.4 %collective-permute-start.2 = (bf16[8,4096]{1,0:T(8,128)(2,1)S(1)}, bf16[8,4096]{1,0:T(8,128)(2,1)S(1)}, u32[]{:S(2)}, u32[]{:S(2)}) collective-permute-start(bf16[8,4096]{1,0:T(8,128)(2,1)S(1)} %shard_map.77), channel_id=1, source_target_pairs={{0,4},{1,5},{2,6},{3,7},{4,0},{5,1},{6,2},{7,3},{8,12},{9,13},{10,... | collective-permute-start | bytes 196616 | tf_op jit(solution)/shard_map/ppermute | solution.py:51
  5.6 1.1 collective-permute-start.1
  6.6 1.0 collective-permute-start
  7.6 3.7 %copy-done = bf16[2304,2048]{1,0:T(8,128)(2,1)S(1)} copy-done((bf16[2304,2048]{1,0:T(8,128)(2,1)S(1)}, bf16[2304,2048]{1,0:T(8,128)(2,1)}, u32[]{:S(2)}) %copy-start) | copy-done | bytes 9437208
  12.5 3.1 %collective-permute-start.5 = (bf16[32,2560]{1,0:T(8,128)(2,1)S(1)}, bf16[32,2560]{1,0:T(8,128)(2,1)S(1)}, u32[]{:S(2)}, u32[]{:S(2)}) collective-permute-start(bf16[32,2560]{1,0:T(8,128)(2,1)S(1)} %slice.8), channel_id=1, source_target_pairs={{0,1},{1,0},{2,3},{3,2},{4,5},{5,4},{6,7},{7,6},{8,9},{9,8},{10,11... | collective-permute-start | bytes 491528 | tf_op jit(solution)/shard_map/ppermute | solution.py:51
  15.6 1.1 collective-permute-start.4
  17.6 4.0 %collective-permute-start.8 = (bf16[32,1536]{1,0:T(8,128)(2,1)S(1)}, bf16[32,1536]{1,0:T(8,128)(2,1)S(1)}, u32[]{:S(2)}, u32[]{:S(2)}) collective-permute-start(bf16[32,1536]{1,0:T(8,128)(2,1)S(1)} %pad_maximum_fusion.2), channel_id=1, source_target_pairs={{0,32},{1,33},{2,34},{3,35},{4,36},{5,37},{6,38},{7,39},{8,40},{9,... | collective-permute-start | bytes 294920 | tf_op jit(solution)/shard_map/ppermute | solution.py:51
  22.3 1.3 %collective-permute-start.6 = (bf16[32,1536]{1,0:T(8,128)(2,1)S(1)}, bf16[32,1536]{1,0:T(8,128)(2,1)S(1)}, u32[]{:S(2)}, u32[]{:S(2)}) collective-permute-start(bf16[32,1536]{1,0:T(8,128)(2,1)S(1)} %pad_maximum_fusion.2), channel_id=1, source_target_pairs={{0,16},{1,17},{2,18},{3,19},{4,20},{5,21},{6,22},{7,23},{8,24},{9,... | collective-permute-start | bytes 294920 | tf_op jit(solution)/shard_map/ppermute | solution.py:51
  24.2 2.1 %collective-permute-done.7 = bf16[32,1536]{1,0:T(8,128)(2,1)S(1)} collective-permute-done((bf16[32,1536]{1,0:T(8,128)(2,1)S(1)}, bf16[32,1536]{1,0:T(8,128)(2,1)S(1)}, u32[]{:S(2)}, u32[]{:S(2)}) %collective-permute-start.7) | collective-permute-done | bytes 98336 | tf_op jit(solution)/shard_map/ppermute | solution.py:51
  26.2 1.9 %collective-permute-done.6 = bf16[32,1536]{1,0:T(8,128)(2,1)S(1)} collective-permute-done((bf16[32,1536]{1,0:T(8,128)(2,1)S(1)}, bf16[32,1536]{1,0:T(8,128)(2,1)S(1)}, u32[]{:S(2)}, u32[]{:S(2)}) %collective-permute-start.6) | collective-permute-done | bytes 98336 | tf_op jit(solution)/shard_map/ppermute | solution.py:51
  28.1 1.2 collective-permute-start.11
  29.3 1.6 %collective-permute-start.10 = (bf16[128,2560]{1,0:T(8,128)(2,1)S(1)}, bf16[128,2560]{1,0:T(8,128)(2,1)S(1)}, u32[]{:S(2)}, u32[]{:S(2)}) collective-permute-start(bf16[128,2560]{1,0:T(8,128)(2,1)S(1)} %pad_maximum_fusion.x0.refs_0_), channel_id=1, source_target_pairs={{0,48},{1,49},{2,50},{3,51},{4,52},{5,53},{6,54},{7,55},{8,56},{9,... | collective-permute-start | bytes 1966088 | tf_op jit(solution)/shard_map/ppermute | solution.py:51
  31.3 1.8 %collective-permute-start.14 = (bf16[128,1536]{1,0:T(8,128)(2,1)S(1)}, bf16[128,1536]{1,0:T(8,128)(2,1)S(1)}, u32[]{:S(2)}, u32[]{:S(2)}) collective-permute-start(bf16[128,1536]{1,0:T(8,128)(2,1)S(1)} %constant_dynamic-update-slice_fusion.refs_4_), channel_id=1, source_target_pairs={{0,1},{1,0},{2,3},{3,2},{4,5},{5,4},{6,7},{7,6},{8,9},{9,8},{10,11... | collective-permute-start | bytes 1179656 | tf_op jit(solution)/shard_map/ppermute | solution.py:51
  33.1 1.6 %collective-permute-start.13 = (bf16[128,1536]{1,0:T(8,128)(2,1)S(1)}, bf16[128,1536]{1,0:T(8,128)(2,1)S(1)}, u32[]{:S(2)}, u32[]{:S(2)}) collective-permute-start(bf16[128,1536]{1,0:T(8,128)(2,1)S(1)} %constant_dynamic-update-slice_fusion.refs_4_), channel_id=1, source_target_pairs={{0,9},{1,8},{2,11},{3,10},{4,13},{5,12},{6,15},{7,14},{8,0},{9,1},... | collective-permute-start | bytes 1179656 | tf_op jit(solution)/shard_map/ppermute | solution.py:51
  34.7 5.6 %collective-permute-done.11.x3.refs_3_ = bf16[128,2560]{1,0:T(8,128)(2,1)S(1)} collective-permute-done((bf16[128,2560]{1,0:T(8,128)(2,1)S(1)}, bf16[128,2560]{1,0:T(8,128)(2,1)S(1)}, u32[]{:S(2)}, u32[]{:S(2)}) %collective-permute-start.11) | collective-permute-done | bytes 655392 | tf_op jit(solution)/shard_map/ppermute | solution.py:51
  40.9 4.5 %collective-permute-done.10.x2.refs_2_ = bf16[128,2560]{1,0:T(8,128)(2,1)S(1)} collective-permute-done((bf16[128,2560]{1,0:T(8,128)(2,1)S(1)}, bf16[128,2560]{1,0:T(8,128)(2,1)S(1)}, u32[]{:S(2)}, u32[]{:S(2)}) %collective-permute-start.10) | collective-permute-done | bytes 655392 | tf_op jit(solution)/shard_map/ppermute | solution.py:51
  45.4 1.8 %collective-permute-done.9.x1.refs_1_ = bf16[128,2560]{1,0:T(8,128)(2,1)S(1)} collective-permute-done((bf16[128,2560]{1,0:T(8,128)(2,1)S(1)}, bf16[128,2560]{1,0:T(8,128)(2,1)S(1)}, u32[]{:S(2)}, u32[]{:S(2)}) %collective-permute-start.9) | collective-permute-done | bytes 655392 | tf_op jit(solution)/shard_map/ppermute | solution.py:51
  47.2 6.3 %shard_map.78 = (f32[256,2048]{1,0:T(8,128)S(1)}, f32[256,2048]{1,0:T(8,128)S(1)}) custom-call(bf16[512,512]{1,0:T(8,128)(2,1)S(1)} %get-tuple-element.56.order.main_order, bf16[128,2560]{1,0:T(8,128)(2,1)S(1)} %pad_maximum_fusion.x0.refs_0_, bf16[128,2560]{1,0:T(8,128)(2,1)S(1)} %collective-permute-done.9.x1.refs_1_, ...), custom_call_target="tpu_custom_call" | custom-call | flops 4831838208 | bytes 9437184 | tf_op jit(solution)/shard_map/pallas_call | solution.py:179
  53.6 3.0 %shard_map.79 = (f32[256,1024]{1,0:T(8,128)S(1)}, f32[256,1024]{1,0:T(8,128)S(1)}, bf16[512,1792]{1,0:T(8,128)(2,1)S(1)}) custom-call(bf16[512,512]{1,0:T(8,128)(2,1)S(1)} %get-tuple-element.56.order.main_order, bf16[512,512]{1,0:T(8,128)(2,1)S(1)} %get-tuple-element.65.apart_order, bf16[128,2560]{1,0:T(8,128)(2,1)S(1)} %pad_maximum_fusion.x0.refs_0_, ...), custom_call_target="tpu_custom_call" | custom-call | flops 1879048192 | bytes 7340032 | tf_op jit(solution)/shard_map/pallas_call | solution.py:191
  57.4 2.1 %shard_map.81 = (f32[256,1024]{1,0:T(8,128)S(1)}, f32[256,1024]{1,0:T(8,128)S(1)}) custom-call(bf16[512,1792]{1,0:T(8,128)(2,1)S(1)} %get-tuple-element.73.rows, bf16[1792,2048]{1,0:T(8,128)(2,1)S(1)} %bitcast.4), custom_call_target="tpu_custom_call" | custom-call | flops 1879048192 | bytes 7340032 | tf_op jit(solution)/shard_map/pallas_call | solution.py:202
  59.7 1.6 %shard_map.80 = (f32[256,1024]{1,0:T(8,128)S(1)}, f32[256,1024]{1,0:T(8,128)S(1)}, f32[3,256,128]{2,1,0:T(8,128)S(1)}) custom-call(f32[256,2048]{1,0:T(8,128)S(1)} %get-tuple-element.58.t_own, f32[256,2048]{1,0:T(8,128)S(1)} %collective-permute-done.15.t_other, f32[256,1024]{1,0:T(8,128)S(1)} %get-tuple-element.70.s_own, ...), custom_call_target="tpu_custom_call" | custom-call | flops 5242880 | bytes 6291456 | tf_op jit(solution)/shard_map/pallas_call | solution.py:259
  62.2 1.7 %shard_map.82 = (f32[256,1024]{1,0:T(8,128)S(1)}, f32[256,1024]{1,0:T(8,128)S(1)}, f32[8,128]{1,0:T(8,128)S(1)}) custom-call(f32[3,256,128]{2,1,0:T(8,128)S(1)} %get-tuple-element.72.before, f32[256,2048]{1,0:T(8,128)S(1)} %get-tuple-element.58.t_own, f32[256,2048]{1,0:T(8,128)S(1)} %collective-permute-done.15.t_other, ...), custom_call_target="tpu_custom_call" | custom-call | flops 5242880 | bytes 6291456 | tf_op jit(solution)/shard_map/pallas_call | solution.py:259
  63.9 1.2 collective-permute-start.20
  65.1 1.6 %collective-permute-start.19 = (f32[8,128]{1,0:T(8,128)S(1)}, f32[8,128]{1,0:T(8,128)S(1)}, u32[]{:S(2)}, u32[]{:S(2)}) collective-permute-start(f32[8,128]{1,0:T(8,128)S(1)} %get-tuple-element.76), channel_id=1, source_target_pairs={{0,48},{1,49},{2,50},{3,51},{4,52},{5,53},{6,54},{7,55},{8,56},{9,... | collective-permute-start | bytes 12296 | tf_op jit(solution)/shard_map/ppermute | solution.py:51
  67.2 1.9 %collective-permute-done.20 = f32[8,128]{1,0:T(8,128)S(1)} collective-permute-done((f32[8,128]{1,0:T(8,128)S(1)}, f32[8,128]{1,0:T(8,128)S(1)}, u32[]{:S(2)}, u32[]{:S(2)}) %collective-permute-start.20) | collective-permute-done | bytes 4128 | tf_op jit(solution)/shard_map/ppermute | solution.py:51
  69.1 2.5 %collective-permute-done.18 = f32[8,128]{1,0:T(8,128)S(1)} collective-permute-done((f32[8,128]{1,0:T(8,128)S(1)}, f32[8,128]{1,0:T(8,128)S(1)}, u32[]{:S(2)}, u32[]{:S(2)}) %collective-permute-start.18) | collective-permute-done | bytes 4128 | tf_op jit(solution)/shard_map/ppermute | solution.py:51
  71.6 2.1 %collective-permute-start.23 = (f32[8,128]{1,0:T(8,128)S(1)}, f32[8,128]{1,0:T(8,128)S(1)}, u32[]{:S(2)}, u32[]{:S(2)}) collective-permute-start(f32[8,128]{1,0:T(8,128)S(1)} %add_add_fusion.2), channel_id=1, source_target_pairs={{0,1},{1,0},{2,3},{3,2},{4,5},{5,4},{6,7},{7,6},{8,9},{9,8},{10,11... | collective-permute-start | bytes 12296 | tf_op jit(solution)/shard_map/ppermute | solution.py:51
  73.7 1.2 collective-permute-start.22
  75.7 1.0 collective-permute-done.23
  77.3 2.4 %collective-permute-done.21 = f32[8,128]{1,0:T(8,128)S(1)} collective-permute-done((f32[8,128]{1,0:T(8,128)S(1)}, f32[8,128]{1,0:T(8,128)S(1)}, u32[]{:S(2)}, u32[]{:S(2)}) %collective-permute-start.21) | collective-permute-done | bytes 4128 | tf_op jit(solution)/shard_map/ppermute | solution.py:51
  79.7 1.6 %collective-permute-start.26 = (f32[8,128]{1,0:T(8,128)S(1)}, f32[8,128]{1,0:T(8,128)S(1)}, u32[]{:S(2)}, u32[]{:S(2)}) collective-permute-start(f32[8,128]{1,0:T(8,128)S(1)} %add_add_fusion.1), channel_id=1, source_target_pairs={{0,4},{1,5},{2,6},{3,7},{4,0},{5,1},{6,2},{7,3},{8,12},{9,13},{10,... | collective-permute-start | bytes 12296 | tf_op jit(solution)/shard_map/ppermute | solution.py:51
  81.3 2.1 %collective-permute-start.25 = (f32[8,128]{1,0:T(8,128)S(1)}, f32[8,128]{1,0:T(8,128)S(1)}, u32[]{:S(2)}, u32[]{:S(2)}) collective-permute-start(f32[8,128]{1,0:T(8,128)S(1)} %add_add_fusion.1), channel_id=1, source_target_pairs={{0,6},{1,7},{2,0},{3,1},{4,2},{5,3},{6,4},{7,5},{8,14},{9,15},{10,... | collective-permute-start | bytes 12296 | tf_op jit(solution)/shard_map/ppermute | solution.py:51
  83.5 1.3 %collective-permute-done.26 = f32[8,128]{1,0:T(8,128)S(1)} collective-permute-done((f32[8,128]{1,0:T(8,128)S(1)}, f32[8,128]{1,0:T(8,128)S(1)}, u32[]{:S(2)}, u32[]{:S(2)}) %collective-permute-start.26) | collective-permute-done | bytes 4128 | tf_op jit(solution)/shard_map/ppermute | solution.py:51
  84.9 3.4 %collective-permute-done.24 = f32[8,128]{1,0:T(8,128)S(1)} collective-permute-done((f32[8,128]{1,0:T(8,128)S(1)}, f32[8,128]{1,0:T(8,128)S(1)}, u32[]{:S(2)}, u32[]{:S(2)}) %collective-permute-start.24) | collective-permute-done | bytes 4128 | tf_op jit(solution)/shard_map/ppermute | solution.py:51
  88.8 2.6 %collective-permute-done.27.other = bf16[256,2048]{1,0:T(8,128)(2,1)S(1)} collective-permute-done((bf16[256,2048]{1,0:T(8,128)(2,1)S(1)}, bf16[256,2048]{1,0:T(8,128)(2,1)S(1)}, u32[]{:S(2)}, u32[]{:S(2)}) %collective-permute-start.27) | collective-permute-done | bytes 1048608 | tf_op jit(solution)/shard_map/ppermute | solution.py:55
  91.4 3.4 %shard_map.84 = (bf16[512,2048]{1,0:T(8,128)(2,1)S(1)}, f32[128,896]{1,0:T(8,128)S(1)}, bf16[128,896]{1,0:T(8,128)(2,1)S(1)}, bf16[128,896]{1,0:T(8,128)(2,1)S(1)}, bf16[128,896]{1,0:T(8,128)(2,1)S(1)}) custom-call(bf16[512,512]{1,0:T(8,128)(2,1)S(1)} %get-tuple-element.83.order, bf16[256,2048]{1,0:T(8,128)(2,1)S(1)} %get-tuple-element.84.own, ...), custom_call_target="tpu_custom_call" | custom-call | flops 1879048192 | bytes 3670016 | tf_op jit(solution)/shard_map/pallas_call | solution.py:336
  95.2 1.8 %collective-permute-start.30 = (bf16[128,896]{1,0:T(8,128)(2,1)S(1)}, bf16[128,896]{1,0:T(8,128)(2,1)S(1)}, u32[]{:S(2)}, u32[]{:S(2)}) collective-permute-start(bf16[128,896]{1,0:T(8,128)(2,1)S(1)} %get-tuple-element.89), channel_id=1, source_target_pairs={{0,16},{1,17},{2,18},{3,19},{4,20},{5,21},{6,22},{7,23},{8,24},{9,... | collective-permute-start | bytes 688136 | tf_op jit(solution)/shard_map/ppermute | solution.py:51
  97.4 2.4 %shard_map.86 = (f32[128,896]{1,0:T(8,128)S(1)}, bf16[128,896]{1,0:T(8,128)(2,1)S(1)}, bf16[128,896]{1,0:T(8,128)(2,1)S(1)}, bf16[128,896]{1,0:T(8,128)(2,1)S(1)}) custom-call(bf16[512,2048]{1,0:T(8,128)(2,1)S(1)} %get-tuple-element.91.gap, bf16[1792,2048]{1,0:T(8,128)(2,1)S(1)} %bitcast.4), custom_call_target="tpu_custom_call" | custom-call | flops 1879048192 | bytes 3670016 | tf_op jit(solution)/shard_map/pallas_call | solution.py:347
  99.8 2.3 %collective-permute-start.32 = (bf16[128,896]{1,0:T(8,128)(2,1)S(1)}, bf16[128,896]{1,0:T(8,128)(2,1)S(1)}, u32[]{:S(2)}, u32[]{:S(2)}) collective-permute-start(bf16[128,896]{1,0:T(8,128)(2,1)S(1)} %get-tuple-element.93), channel_id=1, source_target_pairs={{0,48},{1,49},{2,50},{3,51},{4,52},{5,53},{6,54},{7,55},{8,56},{9,... | collective-permute-start | bytes 688136 | tf_op jit(solution)/shard_map/ppermute | solution.py:51
  102.1 2.9 %collective-permute-start.34 = (bf16[128,896]{1,0:T(8,128)(2,1)S(1)}, bf16[128,896]{1,0:T(8,128)(2,1)S(1)}, u32[]{:S(2)}, u32[]{:S(2)}) collective-permute-start(bf16[128,896]{1,0:T(8,128)(2,1)S(1)} %get-tuple-element.95), channel_id=1, source_target_pairs={{0,32},{1,33},{2,34},{3,35},{4,36},{5,37},{6,38},{7,39},{8,40},{9,... | collective-permute-start | bytes 688136 | tf_op jit(solution)/shard_map/ppermute | solution.py:51
  105.0 4.2 %shard_map.85.refs_0_ = bf16[1792,2048]{1,0:T(8,128)(2,1)} custom-call(bf16[512,1792]{1,0:T(8,128)(2,1)S(1)} %get-tuple-element.73.rows, bf16[256,2048]{1,0:T(8,128)(2,1)S(1)} %get-tuple-element.84.own, bf16[256,2048]{1,0:T(8,128)(2,1)S(1)} %collective-permute-done.27.other), custom_call_target="tpu_custom_call" | custom-call | flops 2147483648 | bytes 4194304 | tf_op jit(solution)/shard_map/pallas_call | solution.py:413
  109.2 2.6 %collective-permute-done.33.refs_6_ = bf16[128,896]{1,0:T(8,128)(2,1)S(1)} collective-permute-done((bf16[128,896]{1,0:T(8,128)(2,1)S(1)}, bf16[128,896]{1,0:T(8,128)(2,1)S(1)}, u32[]{:S(2)}, u32[]{:S(2)}) %collective-permute-start.33) | collective-permute-done | bytes 229408 | tf_op jit(solution)/shard_map/ppermute | solution.py:51
  112.2 1.9 %collective-permute-start.36 = (bf16[32,1792]{1,0:T(8,128)(2,1)S(1)}, bf16[32,1792]{1,0:T(8,128)(2,1)S(1)}, u32[]{:S(2)}, u32[]{:S(2)}) collective-permute-start(bf16[32,1792]{1,0:T(8,128)(2,1)S(1)} %get-tuple-element.100), channel_id=1, source_target_pairs={{0,8},{1,9},{2,10},{3,11},{4,12},{5,13},{6,14},{7,15},{8,1},{9,0},... | collective-permute-start | bytes 344072 | tf_op jit(solution)/shard_map/ppermute | solution.py:51
  114.5 3.5 %shard_map.88 = bf16[1792,2048]{1,0:T(8,128)(2,1)} custom-call(bf16[512,1792]{1,0:T(8,128)(2,1)S(1)} %get-tuple-element.73.rows, bf16[256,2048]{1,0:T(8,128)(2,1)S(1)} %get-tuple-element.84.own, bf16[256,2048]{1,0:T(8,128)(2,1)S(1)} %collective-permute-done.27.other, bf16[1792,2048]{1,0:T(8,128)(2,1)} %shard_map.85.refs_0_), custom_call_target="tpu_custom_call", output_to_operand_aliasing={{}: (3, {})} | custom-call | flops 1610612736 | bytes 3145728 | tf_op jit(solution)/shard_map/pallas_call | solution.py:413
  118.2 2.7 %collective-permute-done.37.refs_2_ = bf16[32,1792]{1,0:T(8,128)(2,1)S(1)} collective-permute-done((bf16[32,1792]{1,0:T(8,128)(2,1)S(1)}, bf16[32,1792]{1,0:T(8,128)(2,1)S(1)}, u32[]{:S(2)}, u32[]{:S(2)}) %collective-permute-start.37) | collective-permute-done | bytes 114720 | tf_op jit(solution)/shard_map/ppermute | solution.py:51
  121.0 2.0 %collective-permute-start.39 = (f32[8,1792]{1,0:T(8,128)S(1)}, f32[8,1792]{1,0:T(8,128)S(1)}, u32[]{:S(2)}, u32[]{:S(2)}) collective-permute-start(f32[8,1792]{1,0:T(8,128)S(1)} %get-tuple-element.104), channel_id=1, source_target_pairs={{0,2},{1,3},{2,4},{3,5},{4,6},{5,7},{6,0},{7,1},{8,10},{9,11},{10,... | collective-permute-start | bytes 172040 | tf_op jit(solution)/shard_map/ppermute | solution.py:51
  125.2 1.3 collective-permute-done.39
  126.5 2.2 %collective-permute-done.40 = f32[8,1792]{1,0:T(8,128)S(1)} collective-permute-done((f32[8,1792]{1,0:T(8,128)S(1)}, f32[8,1792]{1,0:T(8,128)S(1)}, u32[]{:S(2)}, u32[]{:S(2)}) %collective-permute-start.40) | collective-permute-done | bytes 57376 | tf_op jit(solution)/shard_map/ppermute | solution.py:51
  (77 shorter events, 15.1 us)
Async XLA Ops:
  0.6 0.8 copy-start.2
  1.4 0.7 copy-start.3
  2.2 10.2 %collective-permute-start.2 = (bf16[8,4096]{1,0:T(8,128)(2,1)S(1)}, bf16[8,4096]{1,0:T(8,128)(2,1)S(1)}, u32[]{:S(2)}, u32[]{:S(2)}) collective-permute-start(bf16[8,4096]{1,0:T(8,128)(2,1)S(1)} %shard_map.77), channel_id=1, source_target_pairs={{0,4},{1,5},{2,6},{3,7},{4,0},{5,1},{6,2},{7,3},{8,12},{9,13},{10,... | collective-permute-start | bytes 196616 | tf_op jit(solution)/shard_map/ppermute | solution.py:51
  5.6 6.8 %collective-permute-start.1 = (bf16[8,4096]{1,0:T(8,128)(2,1)S(1)}, bf16[8,4096]{1,0:T(8,128)(2,1)S(1)}, u32[]{:S(2)}, u32[]{:S(2)}) collective-permute-start(bf16[8,4096]{1,0:T(8,128)(2,1)S(1)} %shard_map.77), channel_id=1, source_target_pairs={{0,6},{1,7},{2,0},{3,1},{4,2},{5,3},{6,4},{7,5},{8,14},{9,15},{10,... | collective-permute-start | bytes 196616 | tf_op jit(solution)/shard_map/ppermute | solution.py:51
  6.6 5.8 %collective-permute-start = (bf16[8,4096]{1,0:T(8,128)(2,1)S(1)}, bf16[8,4096]{1,0:T(8,128)(2,1)S(1)}, u32[]{:S(2)}, u32[]{:S(2)}) collective-permute-start(bf16[8,4096]{1,0:T(8,128)(2,1)S(1)} %shard_map.77), channel_id=1, source_target_pairs={{0,2},{1,3},{2,4},{3,5},{4,6},{5,7},{6,0},{7,1},{8,10},{9,11},{10,... | collective-permute-start | bytes 196616 | tf_op jit(solution)/shard_map/ppermute | solution.py:51
  7.6 3.7 %copy-start = (bf16[2304,2048]{1,0:T(8,128)(2,1)S(1)}, bf16[2304,2048]{1,0:T(8,128)(2,1)}, u32[]{:S(2)}) copy-start(bf16[2304,2048]{1,0:T(8,128)(2,1)} %weight.4) | copy-start | bytes 28311556
  11.3 0.7 copy-start.4
  12.0 35.2 %copy-start.1 = (bf16[2304,2048]{1,0:T(8,128)(2,1)S(1)}, bf16[2304,2048]{1,0:T(8,128)(2,1)}, u32[]{:S(2)}) copy-start(bf16[2304,2048]{1,0:T(8,128)(2,1)} %weight.4) | copy-start | bytes 28311556
  12.5 9.8 %collective-permute-start.5 = (bf16[32,2560]{1,0:T(8,128)(2,1)S(1)}, bf16[32,2560]{1,0:T(8,128)(2,1)S(1)}, u32[]{:S(2)}, u32[]{:S(2)}) collective-permute-start(bf16[32,2560]{1,0:T(8,128)(2,1)S(1)} %slice.8), channel_id=1, source_target_pairs={{0,1},{1,0},{2,3},{3,2},{4,5},{5,4},{6,7},{7,6},{8,9},{9,8},{10,11... | collective-permute-start | bytes 491528 | tf_op jit(solution)/shard_map/ppermute | solution.py:51
  15.6 8.0 %collective-permute-start.4 = (bf16[32,2560]{1,0:T(8,128)(2,1)S(1)}, bf16[32,2560]{1,0:T(8,128)(2,1)S(1)}, u32[]{:S(2)}, u32[]{:S(2)}) collective-permute-start(bf16[32,2560]{1,0:T(8,128)(2,1)S(1)} %slice.8), channel_id=1, source_target_pairs={{0,9},{1,8},{2,11},{3,10},{4,13},{5,12},{6,15},{7,14},{8,0},{9,1},... | collective-permute-start | bytes 491528 | tf_op jit(solution)/shard_map/ppermute | solution.py:51
  16.7 7.2 %collective-permute-start.3 = (bf16[32,2560]{1,0:T(8,128)(2,1)S(1)}, bf16[32,2560]{1,0:T(8,128)(2,1)S(1)}, u32[]{:S(2)}, u32[]{:S(2)}) collective-permute-start(bf16[32,2560]{1,0:T(8,128)(2,1)S(1)} %slice.8), channel_id=1, source_target_pairs={{0,8},{1,9},{2,10},{3,11},{4,12},{5,13},{6,14},{7,15},{8,1},{9,0},... | collective-permute-start | bytes 491528 | tf_op jit(solution)/shard_map/ppermute | solution.py:51
  17.6 6.5 %collective-permute-start.8 = (bf16[32,1536]{1,0:T(8,128)(2,1)S(1)}, bf16[32,1536]{1,0:T(8,128)(2,1)S(1)}, u32[]{:S(2)}, u32[]{:S(2)}) collective-permute-start(bf16[32,1536]{1,0:T(8,128)(2,1)S(1)} %pad_maximum_fusion.2), channel_id=1, source_target_pairs={{0,32},{1,33},{2,34},{3,35},{4,36},{5,37},{6,38},{7,39},{8,40},{9,... | collective-permute-start | bytes 294920 | tf_op jit(solution)/shard_map/ppermute | solution.py:51
  21.6 4.7 %collective-permute-start.7 = (bf16[32,1536]{1,0:T(8,128)(2,1)S(1)}, bf16[32,1536]{1,0:T(8,128)(2,1)S(1)}, u32[]{:S(2)}, u32[]{:S(2)}) collective-permute-start(bf16[32,1536]{1,0:T(8,128)(2,1)S(1)} %pad_maximum_fusion.2), channel_id=1, source_target_pairs={{0,48},{1,49},{2,50},{3,51},{4,52},{5,53},{6,54},{7,55},{8,56},{9,... | collective-permute-start | bytes 294920 | tf_op jit(solution)/shard_map/ppermute | solution.py:51
  22.3 5.8 %collective-permute-start.6 = (bf16[32,1536]{1,0:T(8,128)(2,1)S(1)}, bf16[32,1536]{1,0:T(8,128)(2,1)S(1)}, u32[]{:S(2)}, u32[]{:S(2)}) collective-permute-start(bf16[32,1536]{1,0:T(8,128)(2,1)S(1)} %pad_maximum_fusion.2), channel_id=1, source_target_pairs={{0,16},{1,17},{2,18},{3,19},{4,20},{5,21},{6,22},{7,23},{8,24},{9,... | collective-permute-start | bytes 294920 | tf_op jit(solution)/shard_map/ppermute | solution.py:51
  28.1 12.2 %collective-permute-start.11 = (bf16[128,2560]{1,0:T(8,128)(2,1)S(1)}, bf16[128,2560]{1,0:T(8,128)(2,1)S(1)}, u32[]{:S(2)}, u32[]{:S(2)}) collective-permute-start(bf16[128,2560]{1,0:T(8,128)(2,1)S(1)} %pad_maximum_fusion.x0.refs_0_), channel_id=1, source_target_pairs={{0,32},{1,33},{2,34},{3,35},{4,36},{5,37},{6,38},{7,39},{8,40},{9,... | collective-permute-start | bytes 1966088 | tf_op jit(solution)/shard_map/ppermute | solution.py:51
  29.3 16.1 %collective-permute-start.10 = (bf16[128,2560]{1,0:T(8,128)(2,1)S(1)}, bf16[128,2560]{1,0:T(8,128)(2,1)S(1)}, u32[]{:S(2)}, u32[]{:S(2)}) collective-permute-start(bf16[128,2560]{1,0:T(8,128)(2,1)S(1)} %pad_maximum_fusion.x0.refs_0_), channel_id=1, source_target_pairs={{0,48},{1,49},{2,50},{3,51},{4,52},{5,53},{6,54},{7,55},{8,56},{9,... | collective-permute-start | bytes 1966088 | tf_op jit(solution)/shard_map/ppermute | solution.py:51
  30.9 16.3 %collective-permute-start.9 = (bf16[128,2560]{1,0:T(8,128)(2,1)S(1)}, bf16[128,2560]{1,0:T(8,128)(2,1)S(1)}, u32[]{:S(2)}, u32[]{:S(2)}) collective-permute-start(bf16[128,2560]{1,0:T(8,128)(2,1)S(1)} %pad_maximum_fusion.x0.refs_0_), channel_id=1, source_target_pairs={{0,16},{1,17},{2,18},{3,19},{4,20},{5,21},{6,22},{7,23},{8,24},{9,... | collective-permute-start | bytes 1966088 | tf_op jit(solution)/shard_map/ppermute | solution.py:51
  31.3 22.1 %collective-permute-start.14 = (bf16[128,1536]{1,0:T(8,128)(2,1)S(1)}, bf16[128,1536]{1,0:T(8,128)(2,1)S(1)}, u32[]{:S(2)}, u32[]{:S(2)}) collective-permute-start(bf16[128,1536]{1,0:T(8,128)(2,1)S(1)} %constant_dynamic-update-slice_fusion.refs_4_), channel_id=1, source_target_pairs={{0,1},{1,0},{2,3},{3,2},{4,5},{5,4},{6,7},{7,6},{8,9},{9,8},{10,11... | collective-permute-start | bytes 1179656 | tf_op jit(solution)/shard_map/ppermute | solution.py:51
  33.1 20.4 %collective-permute-start.13 = (bf16[128,1536]{1,0:T(8,128)(2,1)S(1)}, bf16[128,1536]{1,0:T(8,128)(2,1)S(1)}, u32[]{:S(2)}, u32[]{:S(2)}) collective-permute-start(bf16[128,1536]{1,0:T(8,128)(2,1)S(1)} %constant_dynamic-update-slice_fusion.refs_4_), channel_id=1, source_target_pairs={{0,9},{1,8},{2,11},{3,10},{4,13},{5,12},{6,15},{7,14},{8,0},{9,1},... | collective-permute-start | bytes 1179656 | tf_op jit(solution)/shard_map/ppermute | solution.py:51
  40.3 13.2 %collective-permute-start.12 = (bf16[128,1536]{1,0:T(8,128)(2,1)S(1)}, bf16[128,1536]{1,0:T(8,128)(2,1)S(1)}, u32[]{:S(2)}, u32[]{:S(2)}) collective-permute-start(bf16[128,1536]{1,0:T(8,128)(2,1)S(1)} %constant_dynamic-update-slice_fusion.refs_4_), channel_id=1, source_target_pairs={{0,8},{1,9},{2,10},{3,11},{4,12},{5,13},{6,14},{7,15},{8,1},{9,0},... | collective-permute-start | bytes 1179656 | tf_op jit(solution)/shard_map/ppermute | solution.py:51
  47.2 6.4 %slice-start = ((s8[7340032]{0:T(1024)(128)(4,1)}), s8[4194304]{0:T(1024)(128)(4,1)S(1)}, s32[]{:S(2)}) async-start(s8[7340032]{0:T(1024)(128)(4,1)} %bitcast.3), calls=%async_computation | async-start | bytes 8388608
  47.2 6.4 %slice-start.1 = ((s8[7340032]{0:T(1024)(128)(4,1)}), s8[3145728]{0:T(1024)(128)(4,1)S(1)}, s32[]{:S(2)}) async-start(s8[7340032]{0:T(1024)(128)(4,1)} %bitcast.3), calls=%async_computation.1 | async-start | bytes 6291456
  53.5 6.2 %collective-permute-start.15 = (f32[256,2048]{1,0:T(8,128)S(1)}, f32[256,2048]{1,0:T(8,128)S(1)}, u32[]{:S(2)}, u32[]{:S(2)}) collective-permute-start(f32[256,2048]{1,0:T(8,128)S(1)} %get-tuple-element.64), channel_id=1, source_target_pairs={{0,64},{64,0},{1,65},{65,1},{2,66},{66,2},{3,67},{67,3},{4,68},{68... | collective-permute-start | bytes 6291464 | tf_op jit(solution)/shard_map/ppermute | solution.py:55
  56.6 3.0 %collective-permute-start.16 = (f32[256,1024]{1,0:T(8,128)S(1)}, f32[256,1024]{1,0:T(8,128)S(1)}, u32[]{:S(2)}, u32[]{:S(2)}) collective-permute-start(f32[256,1024]{1,0:T(8,128)S(1)} %get-tuple-element.71), channel_id=1, source_target_pairs={{0,64},{64,0},{1,65},{65,1},{2,66},{66,2},{3,67},{67,3},{4,68},{68... | collective-permute-start | bytes 3145736 | tf_op jit(solution)/shard_map/ppermute | solution.py:55
  59.4 2.7 %collective-permute-start.17 = (f32[256,1024]{1,0:T(8,128)S(1)}, f32[256,1024]{1,0:T(8,128)S(1)}, u32[]{:S(2)}, u32[]{:S(2)}) collective-permute-start(f32[256,1024]{1,0:T(8,128)S(1)} %get-tuple-element.75), channel_id=1, source_target_pairs={{0,64},{64,0},{1,65},{65,1},{2,66},{66,2},{3,67},{67,3},{4,68},{68... | collective-permute-start | bytes 3145736 | tf_op jit(solution)/shard_map/ppermute | solution.py:55
  63.9 5.2 %collective-permute-start.20 = (f32[8,128]{1,0:T(8,128)S(1)}, f32[8,128]{1,0:T(8,128)S(1)}, u32[]{:S(2)}, u32[]{:S(2)}) collective-permute-start(f32[8,128]{1,0:T(8,128)S(1)} %get-tuple-element.76), channel_id=1, source_target_pairs={{0,32},{1,33},{2,34},{3,35},{4,36},{5,37},{6,38},{7,39},{8,40},{9,... | collective-permute-start | bytes 12296 | tf_op jit(solution)/shard_map/ppermute | solution.py:51
  65.1 4.0 %collective-permute-start.19 = (f32[8,128]{1,0:T(8,128)S(1)}, f32[8,128]{1,0:T(8,128)S(1)}, u32[]{:S(2)}, u32[]{:S(2)}) collective-permute-start(f32[8,128]{1,0:T(8,128)S(1)} %get-tuple-element.76), channel_id=1, source_target_pairs={{0,48},{1,49},{2,50},{3,51},{4,52},{5,53},{6,54},{7,55},{8,56},{9,... | collective-permute-start | bytes 12296 | tf_op jit(solution)/shard_map/ppermute | solution.py:51
  66.8 4.8 %collective-permute-start.18 = (f32[8,128]{1,0:T(8,128)S(1)}, f32[8,128]{1,0:T(8,128)S(1)}, u32[]{:S(2)}, u32[]{:S(2)}) collective-permute-start(f32[8,128]{1,0:T(8,128)S(1)} %get-tuple-element.76), channel_id=1, source_target_pairs={{0,16},{1,17},{2,18},{3,19},{4,20},{5,21},{6,22},{7,23},{8,24},{9,... | collective-permute-start | bytes 12296 | tf_op jit(solution)/shard_map/ppermute | solution.py:51
  71.6 5.1 %collective-permute-start.23 = (f32[8,128]{1,0:T(8,128)S(1)}, f32[8,128]{1,0:T(8,128)S(1)}, u32[]{:S(2)}, u32[]{:S(2)}) collective-permute-start(f32[8,128]{1,0:T(8,128)S(1)} %add_add_fusion.2), channel_id=1, source_target_pairs={{0,1},{1,0},{2,3},{3,2},{4,5},{5,4},{6,7},{7,6},{8,9},{9,8},{10,11... | collective-permute-start | bytes 12296 | tf_op jit(solution)/shard_map/ppermute | solution.py:51
  73.7 3.6 %collective-permute-start.22 = (f32[8,128]{1,0:T(8,128)S(1)}, f32[8,128]{1,0:T(8,128)S(1)}, u32[]{:S(2)}, u32[]{:S(2)}) collective-permute-start(f32[8,128]{1,0:T(8,128)S(1)} %add_add_fusion.2), channel_id=1, source_target_pairs={{0,9},{1,8},{2,11},{3,10},{4,13},{5,12},{6,15},{7,14},{8,0},{9,1},... | collective-permute-start | bytes 12296 | tf_op jit(solution)/shard_map/ppermute | solution.py:51
  74.9 4.8 %collective-permute-start.21 = (f32[8,128]{1,0:T(8,128)S(1)}, f32[8,128]{1,0:T(8,128)S(1)}, u32[]{:S(2)}, u32[]{:S(2)}) collective-permute-start(f32[8,128]{1,0:T(8,128)S(1)} %add_add_fusion.2), channel_id=1, source_target_pairs={{0,8},{1,9},{2,10},{3,11},{4,12},{5,13},{6,14},{7,15},{8,1},{9,0},... | collective-permute-start | bytes 12296 | tf_op jit(solution)/shard_map/ppermute | solution.py:51
  79.7 5.1 %collective-permute-start.26 = (f32[8,128]{1,0:T(8,128)S(1)}, f32[8,128]{1,0:T(8,128)S(1)}, u32[]{:S(2)}, u32[]{:S(2)}) collective-permute-start(f32[8,128]{1,0:T(8,128)S(1)} %add_add_fusion.1), channel_id=1, source_target_pairs={{0,4},{1,5},{2,6},{3,7},{4,0},{5,1},{6,2},{7,3},{8,12},{9,13},{10,... | collective-permute-start | bytes 12296 | tf_op jit(solution)/shard_map/ppermute | solution.py:51
  81.3 3.6 %collective-permute-start.25 = (f32[8,128]{1,0:T(8,128)S(1)}, f32[8,128]{1,0:T(8,128)S(1)}, u32[]{:S(2)}, u32[]{:S(2)}) collective-permute-start(f32[8,128]{1,0:T(8,128)S(1)} %add_add_fusion.1), channel_id=1, source_target_pairs={{0,6},{1,7},{2,0},{3,1},{4,2},{5,3},{6,4},{7,5},{8,14},{9,15},{10,... | collective-permute-start | bytes 12296 | tf_op jit(solution)/shard_map/ppermute | solution.py:51
  83.5 4.8 %collective-permute-start.24 = (f32[8,128]{1,0:T(8,128)S(1)}, f32[8,128]{1,0:T(8,128)S(1)}, u32[]{:S(2)}, u32[]{:S(2)}) collective-permute-start(f32[8,128]{1,0:T(8,128)S(1)} %add_add_fusion.1), channel_id=1, source_target_pairs={{0,2},{1,3},{2,4},{3,5},{4,6},{5,7},{6,0},{7,1},{8,10},{9,11},{10,... | collective-permute-start | bytes 12296 | tf_op jit(solution)/shard_map/ppermute | solution.py:51
  88.7 2.7 %collective-permute-start.27 = (bf16[256,2048]{1,0:T(8,128)(2,1)S(1)}, bf16[256,2048]{1,0:T(8,128)(2,1)S(1)}, u32[]{:S(2)}, u32[]{:S(2)}) collective-permute-start(bf16[256,2048]{1,0:T(8,128)(2,1)S(1)} %get-tuple-element.84.own), channel_id=1, source_target_pairs={{0,64},{64,0},{1,65},{65,1},{2,66},{66,2},{3,67},{67,3},{4,68},{68... | collective-permute-start | bytes 3145736 | tf_op jit(solution)/shard_map/ppermute | solution.py:55
  94.9 7.2 %collective-permute-start.29 = (bf16[128,896]{1,0:T(8,128)(2,1)S(1)}, bf16[128,896]{1,0:T(8,128)(2,1)S(1)}, u32[]{:S(2)}, u32[]{:S(2)}) collective-permute-start(bf16[128,896]{1,0:T(8,128)(2,1)S(1)} %get-tuple-element.88), channel_id=1, source_target_pairs={{0,48},{1,49},{2,50},{3,51},{4,52},{5,53},{6,54},{7,55},{8,56},{9,... | collective-permute-start | bytes 688136 | tf_op jit(solution)/shard_map/ppermute | solution.py:51
  95.1 7.1 %collective-permute-start.28 = (f32[2,128]{1,0:T(2,128)S(1)}, f32[2,128]{1,0:T(2,128)S(1)}, u32[]{:S(2)}, u32[]{:S(2)}) collective-permute-start(f32[2,128]{1,0:T(2,128)S(1)} %get-tuple-element.82), channel_id=1, source_target_pairs={{0,64},{64,0},{1,65},{65,1},{2,66},{66,2},{3,67},{67,3},{4,68},{68... | collective-permute-start | bytes 3080 | tf_op jit(solution)/shard_map/ppermute | solution.py:55
  95.2 14.0 %collective-permute-start.30 = (bf16[128,896]{1,0:T(8,128)(2,1)S(1)}, bf16[128,896]{1,0:T(8,128)(2,1)S(1)}, u32[]{:S(2)}, u32[]{:S(2)}) collective-permute-start(bf16[128,896]{1,0:T(8,128)(2,1)S(1)} %get-tuple-element.89), channel_id=1, source_target_pairs={{0,16},{1,17},{2,18},{3,19},{4,20},{5,21},{6,22},{7,23},{8,24},{9,... | collective-permute-start | bytes 688136 | tf_op jit(solution)/shard_map/ppermute | solution.py:51
  97.0 12.2 %collective-permute-start.31 = (bf16[128,896]{1,0:T(8,128)(2,1)S(1)}, bf16[128,896]{1,0:T(8,128)(2,1)S(1)}, u32[]{:S(2)}, u32[]{:S(2)}) collective-permute-start(bf16[128,896]{1,0:T(8,128)(2,1)S(1)} %get-tuple-element.90), channel_id=1, source_target_pairs={{0,32},{1,33},{2,34},{3,35},{4,36},{5,37},{6,38},{7,39},{8,40},{9,... | collective-permute-start | bytes 688136 | tf_op jit(solution)/shard_map/ppermute | solution.py:51
  99.8 9.4 %collective-permute-start.32 = (bf16[128,896]{1,0:T(8,128)(2,1)S(1)}, bf16[128,896]{1,0:T(8,128)(2,1)S(1)}, u32[]{:S(2)}, u32[]{:S(2)}) collective-permute-start(bf16[128,896]{1,0:T(8,128)(2,1)S(1)} %get-tuple-element.93), channel_id=1, source_target_pairs={{0,48},{1,49},{2,50},{3,51},{4,52},{5,53},{6,54},{7,55},{8,56},{9,... | collective-permute-start | bytes 688136 | tf_op jit(solution)/shard_map/ppermute | solution.py:51
  102.1 9.7 %collective-permute-start.33 = (bf16[128,896]{1,0:T(8,128)(2,1)S(1)}, bf16[128,896]{1,0:T(8,128)(2,1)S(1)}, u32[]{:S(2)}, u32[]{:S(2)}) collective-permute-start(bf16[128,896]{1,0:T(8,128)(2,1)S(1)} %get-tuple-element.94), channel_id=1, source_target_pairs={{0,16},{1,17},{2,18},{3,19},{4,20},{5,21},{6,22},{7,23},{8,24},{9,... | collective-permute-start | bytes 688136 | tf_op jit(solution)/shard_map/ppermute | solution.py:51
  102.1 9.7 %collective-permute-start.34 = (bf16[128,896]{1,0:T(8,128)(2,1)S(1)}, bf16[128,896]{1,0:T(8,128)(2,1)S(1)}, u32[]{:S(2)}, u32[]{:S(2)}) collective-permute-start(bf16[128,896]{1,0:T(8,128)(2,1)S(1)} %get-tuple-element.95), channel_id=1, source_target_pairs={{0,32},{1,33},{2,34},{3,35},{4,36},{5,37},{6,38},{7,39},{8,40},{9,... | collective-permute-start | bytes 688136 | tf_op jit(solution)/shard_map/ppermute | solution.py:51
  112.0 5.9 %collective-permute-start.35 = (bf16[32,1792]{1,0:T(8,128)(2,1)S(1)}, bf16[32,1792]{1,0:T(8,128)(2,1)S(1)}, u32[]{:S(2)}, u32[]{:S(2)}) collective-permute-start(bf16[32,1792]{1,0:T(8,128)(2,1)S(1)} %get-tuple-element.99), channel_id=1, source_target_pairs={{0,9},{1,8},{2,11},{3,10},{4,13},{5,12},{6,15},{7,14},{8,0},{9,1},... | collective-permute-start | bytes 344072 | tf_op jit(solution)/shard_map/ppermute | solution.py:51
  112.2 6.0 %collective-permute-start.36 = (bf16[32,1792]{1,0:T(8,128)(2,1)S(1)}, bf16[32,1792]{1,0:T(8,128)(2,1)S(1)}, u32[]{:S(2)}, u32[]{:S(2)}) collective-permute-start(bf16[32,1792]{1,0:T(8,128)(2,1)S(1)} %get-tuple-element.100), channel_id=1, source_target_pairs={{0,8},{1,9},{2,10},{3,11},{4,12},{5,13},{6,14},{7,15},{8,1},{9,0},... | collective-permute-start | bytes 344072 | tf_op jit(solution)/shard_map/ppermute | solution.py:51
  114.1 6.8 %collective-permute-start.37 = (bf16[32,1792]{1,0:T(8,128)(2,1)S(1)}, bf16[32,1792]{1,0:T(8,128)(2,1)S(1)}, u32[]{:S(2)}, u32[]{:S(2)}) collective-permute-start(bf16[32,1792]{1,0:T(8,128)(2,1)S(1)} %get-tuple-element.101), channel_id=1, source_target_pairs={{0,1},{1,0},{2,3},{3,2},{4,5},{5,4},{6,7},{7,6},{8,9},{9,8},{10,11... | collective-permute-start | bytes 344072 | tf_op jit(solution)/shard_map/ppermute | solution.py:51
  120.9 4.2 %collective-permute-start.38 = (f32[8,1792]{1,0:T(8,128)S(1)}, f32[8,1792]{1,0:T(8,128)S(1)}, u32[]{:S(2)}, u32[]{:S(2)}) collective-permute-start(f32[8,1792]{1,0:T(8,128)S(1)} %get-tuple-element.103), channel_id=1, source_target_pairs={{0,6},{1,7},{2,0},{3,1},{4,2},{5,3},{6,4},{7,5},{8,14},{9,15},{10,... | collective-permute-start | bytes 172040 | tf_op jit(solution)/shard_map/ppermute | solution.py:51
  121.0 5.5 %collective-permute-start.39 = (f32[8,1792]{1,0:T(8,128)S(1)}, f32[8,1792]{1,0:T(8,128)S(1)}, u32[]{:S(2)}, u32[]{:S(2)}) collective-permute-start(f32[8,1792]{1,0:T(8,128)S(1)} %get-tuple-element.104), channel_id=1, source_target_pairs={{0,2},{1,3},{2,4},{3,5},{4,6},{5,7},{6,0},{7,1},{8,10},{9,11},{10,... | collective-permute-start | bytes 172040 | tf_op jit(solution)/shard_map/ppermute | solution.py:51
  123.0 5.7 %collective-permute-start.40 = (f32[8,1792]{1,0:T(8,128)S(1)}, f32[8,1792]{1,0:T(8,128)S(1)}, u32[]{:S(2)}, u32[]{:S(2)}) collective-permute-start(f32[8,1792]{1,0:T(8,128)S(1)} %get-tuple-element.105), channel_id=1, source_target_pairs={{0,4},{1,5},{2,6},{3,7},{4,0},{5,1},{6,2},{7,3},{8,12},{9,13},{10,... | collective-permute-start | bytes 172040 | tf_op jit(solution)/shard_map/ppermute | solution.py:51

commit v4 on v3

v4 whole, which is shorter than its diff:
```python
import functools

import jax
import jax.numpy as jnp
import numpy as np
from jax import lax
from jax.experimental import pallas as pl
from jax.experimental.pallas import tpu as pltpu
from jax.sharding import PartitionSpec as P

softcap_limit = 30.0
tokens, teacher_width, student_width, vocab_local = 512, 2304, 1792, 2048
width = teacher_width + student_width
half = tokens // 2
apart = 1536
everyone = ("mp", "batch", "vocab")
mega = 1024 * 1024

offsets = (0, 1, 3, 2)
main_axes = (("y", "z"), ("x", "x"), ("z", "y"))
apart_axes = (("y", "z"), ("z", "y"), ("x", "x"))
reduce_axes = (("z", "y"), ("x", "z"), ("y", "x"))


def place(index):
    core, z, x_lo, y, x_hi = np.unravel_index(index, (2, 4, 2, 4, 2))
    return {"core": int(core), "x": int(2 * x_hi + x_lo), "y": int(y), "z": int(z)}


def index_of(at):
    return int(
        np.ravel_multi_index(
            (at["core"], at["z"], at["x"] % 2, at["y"], at["x"] // 2), (2, 4, 2, 4, 2)
        )
    )


def moved(at, axis, by):
    return {**at, axis: (at[axis] + by) % 4}


def ring(axes, by):
    pairs = []
    for source in range(128):
        at = place(source)
        pairs.append((source, index_of(moved(at, axes[at["core"]], by))))
    return pairs


def send(block, axes, by):
    return lax.ppermute(block, everyone, ring(axes, by))


def swap(block):
    return lax.ppermute(block, "mp", [(0, 1), (1, 0)])


def side_by_side_kernel(teacher, student, out, held_teacher, held_student, arrived):
    copies = [
        pltpu.make_async_copy(teacher, held_teacher, arrived.at[0]),
        pltpu.make_async_copy(student, held_student, arrived.at[1]),
    ]
    for copy in copies:
        copy.start()
    for copy in copies:
        copy.wait()
    out[:, :apart] = held_student[:, :apart]
    out[:, apart : apart + teacher_width] = held_teacher[...]
    out[:, apart + teacher_width :] = held_student[:, apart:]


def side_by_side(teacher, student):
    return pl.pallas_call(
        side_by_side_kernel,
        in_specs=[pl.BlockSpec(memory_space=pl.ANY)] * 2,
        out_specs=whole(),
        out_shape=jax.ShapeDtypeStruct((teacher.shape[0], width), teacher.dtype),
        scratch_shapes=[
            pltpu.VMEM(teacher.shape, teacher.dtype),
            pltpu.VMEM(student.shape, student.dtype),
            pltpu.SemaphoreType.DMA((2,)),
        ],
        compiler_params=pltpu.CompilerParams(vmem_limit_bytes=mega),
        cost_estimate=cost(0, 4 * teacher.shape[0] * width),
    )(teacher, student)


def gathered(order, blocks, first, rows):
    step = 256
    for at in range(0, rows.shape[1], step):
        cols = slice(first + at, first + at + step)
        block = jnp.concatenate([x[:, cols] for x in blocks], axis=0)
        rows[:, at : at + step] = jnp.dot(
            order[...], block, preferred_element_type=jnp.float32
        ).astype(jnp.bfloat16)


def logits(rows, weight, first, own, other):
    step = 512
    for at in range(0, own.shape[1], step):
        raw = jnp.dot(
            rows[...], weight[:, first + at : first + at + step], preferred_element_type=jnp.float32
        )
        own[:, at : at + step], other[:, at : at + step] = raw[:half], raw[half:]


def placed(places, which, block):
    return pl.ds(pl.multiple_of(places[which, block], 8), 8)


def teacher_kernel(places, x0, x1, x2, x3, weight, own, other, rows, raw):
    for i, x in enumerate((x0, x1, x2, x3)):
        rows[128 * i : 128 * (i + 1)] = x[:, :teacher_width]
    step = raw.shape[2]
    for i, at in enumerate(range(0, vocab_local, step)):
        cols, held = slice(at, at + step), raw.at[i % 2]
        term = jnp.dot(rows[...], weight[:, cols], preferred_element_type=jnp.float32)
        for block in range(64):
            held[placed(places, 0, block)] = term[8 * block : 8 * (block + 1)]
        own[:, cols], other[:, cols] = held[:half], held[half:]


def student_kernel(main_order, apart_order, *refs):
    main, separate, (weight, own, other, rows) = refs[:4], refs[4:8], refs[8:]
    gathered(apart_order, separate, 0, rows.at[:, :apart])
    gathered(main_order, main, teacher_width, rows.at[:, apart:])
    logits(rows, weight, 0, own, other)


def student_rest_kernel(rows, weight, own, other):
    logits(rows, weight, vocab_local - own.shape[1], own, other)


def own_place(token, at, axes_of, core):
    block, row = token // 8, token % 8
    for stage, axes in enumerate(axes_of):
        digit = (block >> (2 * stage)) & 3
        offset = digit ^ (digit >> 1)
        for axis in at:
            taken = (axes[0] == axis) * (1 - core) + (axes[1] == axis) * core
            at[axis] = at[axis] - taken * offset
    x, y, z = (at[axis] & 3 for axis in "xyz")
    owner = z * 16 + (x & 1) * 8 + y * 2 + (x >> 1)
    return ((owner - 32 * core) & 63) * 8 + row


def setup_kernel(_, main_order, apart_order, places, first_core):
    core = lax.axis_index("mp")
    batch, vocab = lax.axis_index("batch"), lax.axis_index("vocab")
    at = {"x": (vocab % 2) * 2 + batch % 2, "y": vocab // 2, "z": batch // 2}
    token = lax.broadcasted_iota(jnp.int32, (1, tokens), 1)
    rows = lax.broadcasted_iota(jnp.int32, (tokens, tokens), 0)
    for order, axes_of in ((main_order, main_axes), (apart_order, apart_axes)):
        goal = own_place(token, dict(at), axes_of, core)
        order[...] = jnp.where(rows == goal, 1.0, 0.0).astype(jnp.bfloat16)
    block = lax.broadcasted_iota(jnp.int32, (1, 128), 1) % 64 * 8
    for i, axes_of in enumerate((main_axes, reduce_axes[::-1])):
        places[i : i + 1] = own_place(block, dict(at), axes_of, core)
    first_core[...] = jnp.full(first_core.shape, 1.0, jnp.float32) * (core == 0).astype(jnp.float32)


def setup(weight):
    order = jax.ShapeDtypeStruct((tokens, tokens), jnp.bfloat16)
    small = jax.ShapeDtypeStruct((2, 128), jnp.float32)
    return pl.pallas_call(
        setup_kernel,
        in_specs=[pl.BlockSpec(memory_space=pl.ANY)],
        out_specs=[whole()] * 4,
        out_shape=[order] * 2 + [jax.ShapeDtypeStruct((2, 128), jnp.int32), small],
        compiler_params=pltpu.CompilerParams(vmem_limit_bytes=4 * mega),
        cost_estimate=cost(0, 2 * mega),
    )(weight)


def cost(macs, moved, transcendentals=0):
    return pl.CostEstimate(flops=2 * macs, bytes_accessed=moved, transcendentals=transcendentals)


def whole():
    return pl.BlockSpec(memory_space=pltpu.VMEM)


def raw_shapes(cols):
    return [jax.ShapeDtypeStruct((half, cols), jnp.float32)] * 2


def scalars():
    return pl.BlockSpec(memory_space=pltpu.SMEM)


def teacher_logits(places, blocks, weight):
    return pl.pallas_call(
        teacher_kernel,
        in_specs=[scalars()] + [whole()] * 5,
        out_specs=[whole()] * 2,
        out_shape=raw_shapes(vocab_local),
        scratch_shapes=[
            pltpu.VMEM((tokens, teacher_width), jnp.bfloat16),
            pltpu.VMEM((2, tokens, 512), jnp.float32),
        ],
        compiler_params=pltpu.CompilerParams(vmem_limit_bytes=26 * mega),
        cost_estimate=cost(tokens * weight.size, 2 * weight.size),
    )(places, *blocks, weight)


def student_logits(main_order, apart_order, main, separate, weight, cols):
    return pl.pallas_call(
        student_kernel,
        in_specs=[whole()] * 11,
        out_specs=[whole()] * 3,
        out_shape=raw_shapes(cols) + [jax.ShapeDtypeStruct((tokens, student_width), jnp.bfloat16)],
        compiler_params=pltpu.CompilerParams(vmem_limit_bytes=20 * mega),
        cost_estimate=cost(tokens * student_width * cols, 2 * weight.size),
    )(main_order, apart_order, *main, *separate, weight)


def student_rest(rows, weight, cols):
    return pl.pallas_call(
        student_rest_kernel,
        in_specs=[whole()] * 2,
        out_specs=[whole()] * 2,
        out_shape=raw_shapes(cols),
        compiler_params=pltpu.CompilerParams(vmem_limit_bytes=16 * mega),
        cost_estimate=cost(tokens * student_width * cols, 2 * weight.size),
    )(rows, weight)


def lanes(values):
    total = values[:, :128]
    for at in range(128, values.shape[1], 128):
        total += values[:, at : at + 128]
    return total


def capped_exp(own, other):
    ratio = jnp.tanh((own[...] + other[...]) * (1.0 / softcap_limit))
    return ratio, jnp.exp(softcap_limit * ratio - softcap_limit)


def teacher_statistics_kernel(own, other, tanh, exp, total):
    @pl.when(pl.program_id(0) == 0)
    def _():
        total[...] = jnp.zeros_like(total)

    tanh[...], exp[...] = capped_exp(own, other)
    total[...] += lanes(exp[...])


def teacher_statistics(own, other, tile=256):
    block = pl.BlockSpec((half, tile), lambda j: (0, j))
    return pl.pallas_call(
        teacher_statistics_kernel,
        grid=(vocab_local // tile,),
        in_specs=[block] * 2,
        out_specs=[block] * 2 + [whole()],
        out_shape=raw_shapes(vocab_local) + [jax.ShapeDtypeStruct((half, 128), jnp.float32)],
        compiler_params=pltpu.CompilerParams(vmem_limit_bytes=7 * mega),
        cost_estimate=cost(4 * half * vocab_local, 16 * half * vocab_local, 2 * half * vocab_local),
    )(own, other)


def student_statistics_kernel(last, *refs):
    before, teacher_total = refs[:2] if last else (None, None)
    tanh, exp, own, other, student_part, teacher_part, out, sums = refs[2 if last else 0 :]

    @pl.when(pl.program_id(0) == 0)
    def _():
        sums[...] = before[...] if last else jnp.zeros_like(sums)

    student_tanh, student_exp = capped_exp(own, other)
    slope = 1.0 - student_tanh * student_tanh
    student_part[...] = student_exp * slope
    teacher_part[...] = exp[...] * slope
    sums[0] += lanes(student_exp)
    sums[1] += lanes(exp[...] * (softcap_limit * (tanh[...] - student_tanh)))

    @pl.when(pl.program_id(0) == pl.num_programs(0) - 1)
    def _():
        if last:
            rows = [
                jnp.sum(total[at : at + 128].T, axis=0, keepdims=True)
                for total in (teacher_total, sums.at[0], sums.at[1])
                for at in (0, 128)
            ]
            out[...] = jnp.concatenate(rows + [jnp.zeros((2, 128), jnp.float32)], axis=0)
        else:
            out[...] = sums[...]


def student_statistics(teacher, student, first, before=None, tile=256):
    cols = student[0].shape[1]
    last = before is not None
    from_teacher = pl.BlockSpec((half, tile), lambda j: (0, first // tile + j))
    part = pl.BlockSpec((half, tile), lambda j: (0, j))
    sums = (2, half, 128)
    tanh, exp, teacher_total = teacher
    return pl.pallas_call(
        functools.partial(student_statistics_kernel, last),
        grid=(cols // tile,),
        in_specs=[whole()] * (2 * last) + [from_teacher] * 2 + [part] * 2,
        out_specs=[part, part, whole()],
        out_shape=raw_shapes(cols) + [jax.ShapeDtypeStruct((8, 128) if last else sums, jnp.float32)],
        scratch_shapes=[pltpu.VMEM(sums, jnp.float32)],
        compiler_params=pltpu.CompilerParams(vmem_limit_bytes=7 * mega),
        cost_estimate=cost(8 * half * cols, 24 * half * cols, 2 * half * cols),
    )(*([before, teacher_total] if last else []), tanh, exp, *student)


def gap_kernel(total, token_weight, student0, teacher0, student1, teacher1, gap, divergence):
    teacher_total, student_total, cross = total[0:2], total[2:4], total[4:6]
    divergence[...] = cross / teacher_total - jnp.log(teacher_total) + jnp.log(student_total)
    mine = token_weight[pl.ds(lax.axis_index("mp") * 2, 2), :]
    rows = [mine / student_total, mine / teacher_total, total[0:4]]
    scales = jnp.concatenate(rows, axis=0).T
    cols = student0.shape[1]
    for i in range(2):
        at = slice(128 * i, 128 * (i + 1))
        student_scale, teacher_scale = scales[:, i : i + 1], scales[:, 2 + i : 3 + i]
        for first, student, teacher in ((0, student0, teacher0), (cols, student1, teacher1)):
            gap[at, first : first + student.shape[1]] = (
                student[at] * student_scale - teacher[at] * teacher_scale
            ).astype(jnp.bfloat16)


def gap_of(total, token_weight, parts):
    return pl.pallas_call(
        gap_kernel,
        in_specs=[whole()] * 6,
        out_specs=[whole(), whole()],
        out_shape=[
            jax.ShapeDtypeStruct((half, vocab_local), jnp.bfloat16),
            jax.ShapeDtypeStruct((2, 128), jnp.float32),
        ],
        compiler_params=pltpu.CompilerParams(vmem_limit_bytes=4 * mega),
        cost_estimate=cost(2 * half * vocab_local, 10 * half * vocab_local),
    )(total, token_weight, *parts)


def hidden_term(gap, weight):
    return lax.dot_general(
        gap[...], weight, (((1,), (1,)), ((), ())), preferred_element_type=jnp.float32
    )


def column_tiles(tile=256):
    return [slice(at, at + tile) for at in range(0, student_width, tile)]


def hidden_own_kernel(gap, weight, out):
    for cols in column_tiles():
        out[:, cols] = hidden_term(gap, weight[cols])


def hidden_own(gap, weight):
    return pl.pallas_call(
        hidden_own_kernel,
        in_specs=[whole()] * 2,
        out_specs=whole(),
        out_shape=jax.ShapeDtypeStruct((half, student_width), jnp.float32),
        compiler_params=pltpu.CompilerParams(vmem_limit_bytes=14 * mega),
        cost_estimate=cost(half * weight.size, 2 * weight.size),
    )(gap, weight)


def hidden_all_kernel(places, own, gap, weight, keep, send1, send2, send3, term):
    for cols in column_tiles():
        term[:half, cols] = own[:, cols]
        term[half:, cols] = hidden_term(gap, weight[cols])
        for pair in range(32):
            both = [term[placed(places, 1, 2 * pair + i), cols] for i in range(2)]
            both = jnp.concatenate(both, axis=0)
            out = (keep, send1, send2, send3)[pair // 8]
            at = 16 * (pair % 8)
            out[at : at + 16, cols] = both.astype(out.dtype)


def hidden_all(places, own, gap, weight):
    return pl.pallas_call(
        hidden_all_kernel,
        in_specs=[scalars()] + [whole()] * 3,
        out_specs=[whole()] * 4,
        out_shape=[jax.ShapeDtypeStruct((128, student_width), jnp.float32)]
        + [jax.ShapeDtypeStruct((128, student_width), jnp.bfloat16)] * 3,
        scratch_shapes=[pltpu.VMEM((tokens, student_width), jnp.float32)],
        compiler_params=pltpu.CompilerParams(vmem_limit_bytes=22 * mega),
        cost_estimate=cost(half * weight.size, 2 * weight.size),
    )(places, own, gap, weight)


def total_of(keep, received, at, size):
    rows = pl.ds(at, size)
    return keep[rows] + sum(r[rows].astype(jnp.float32) for r in received)


def first_sum_kernel(mine, *refs):
    received, (keep, *sends) = refs[:3], refs[3:]
    keep[...] = total_of(mine, received, 0, 32)
    for j, send in enumerate(sends):
        send[...] = total_of(mine, received, 32 * (j + 1), 32).astype(send.dtype)


def first_sum(mine, received):
    shape = (32, student_width)
    return pl.pallas_call(
        first_sum_kernel,
        in_specs=[whole()] * 4,
        out_specs=[whole()] * 4,
        out_shape=[jax.ShapeDtypeStruct(shape, jnp.float32)]
        + [jax.ShapeDtypeStruct(shape, jnp.bfloat16)] * 3,
        compiler_params=pltpu.CompilerParams(vmem_limit_bytes=6 * mega),
        cost_estimate=cost(128 * student_width * 4, 2 * mega),
    )(mine, *received)


def second_sum_kernel(mine, *refs):
    received, (keep, *sends) = refs[:3], refs[3:]
    total = mine[...] + sum(r[...].astype(jnp.float32) for r in received)
    keep[...] = total[:8]
    for j, send in enumerate(sends):
        send[...] = total[8 * (j + 1) : 8 * (j + 2)]


def second_sum(mine, received):
    return pl.pallas_call(
        second_sum_kernel,
        in_specs=[whole()] * 4,
        out_specs=[whole()] * 4,
        out_shape=[jax.ShapeDtypeStruct((8, student_width), jnp.float32)] * 4,
        compiler_params=pltpu.CompilerParams(vmem_limit_bytes=3 * mega),
        cost_estimate=cost(32 * student_width * 4, mega),
    )(mine, *received)


def grad_weight_kernel(rows, own, other, out):
    over_rows = (((0,), (0,)), ((), ()))
    out[...] = (
        lax.dot_general(rows[:half], own[...], over_rows, preferred_element_type=jnp.float32)
        + lax.dot_general(rows[half:], other[...], over_rows, preferred_element_type=jnp.float32)
    ).astype(jnp.bfloat16)


def grad_weight_of(rows, own, other, tile=256):
    return pl.pallas_call(
        grad_weight_kernel,
        grid=(student_width // tile,),
        in_specs=[pl.BlockSpec((tokens, tile), lambda j: (0, j)), whole(), whole()],
        out_specs=pl.BlockSpec((tile, vocab_local), lambda j: (j, 0)),
        out_shape=jax.ShapeDtypeStruct((student_width, vocab_local), jnp.bfloat16),
        compiler_params=pltpu.CompilerParams(vmem_limit_bytes=9 * mega),
        cost_estimate=cost(tokens * student_width * vocab_local, 2 * student_width * vocab_local),
    )(rows, own, other)


def local(hidden_teacher, hidden_student, teacher_weight, student_weight, token_weight):
    main_order, apart_order, places, first_core = setup(teacher_weight)

    def shared_along(block, axes):
        return [block] + [send(block, axes, by) for by in offsets[1:]]

    def joined(blocks):
        return jnp.concatenate(blocks, axis=0)

    block = joined(shared_along(side_by_side(hidden_teacher, hidden_student), main_axes[0]))
    separate, main = block[:, :apart], block[:, apart:]
    main, separate = shared_along(main, main_axes[1]), shared_along(separate, apart_axes[1])
    main = joined(main)
    _, *separate = lax.optimization_barrier((main, *separate))
    separate = joined(separate)
    main = shared_along(main, main_axes[2])
    separate = shared_along(separate, apart_axes[2])
    teacher_own, teacher_other = teacher_logits(places, main, teacher_weight)
    teacher_other, *separate = lax.optimization_barrier((teacher_other, *separate))
    teacher_other = swap(teacher_other)
    cols = 1536
    own0, other0, rows = student_logits(
        main_order, apart_order, main, separate, student_weight, cols
    )
    other0 = swap(other0)
    own1, other1 = student_rest(rows, student_weight, vocab_local - cols)
    teacher_own, other1 = lax.optimization_barrier((teacher_own, other1))
    other1 = swap(other1)
    teacher = teacher_statistics(teacher_own, teacher_other)
    student_part0, teacher_part0, sums = student_statistics(teacher, (own0, other0), 0)
    student_part1, teacher_part1, sums = student_statistics(teacher, (own1, other1), cols, sums)
    for axes in reduce_axes:
        sums = sum(shared_along(sums, axes))
    gap, divergence = gap_of(
        sums, token_weight.reshape(4, 128), (student_part0, teacher_part0, student_part1, teacher_part1)
    )
    gap_other, divergence_other = lax.optimization_barrier((swap(gap), swap(divergence)))

    def sent_back(sends, axes):
        return [send(b, axes, -by) for b, by in zip(sends, offsets[1:])]

    hidden = hidden_own(gap, student_weight)
    gap_other, hidden = lax.optimization_barrier((gap_other, hidden))
    keep, *sends = hidden_all(places, hidden, gap_other, student_weight)
    received = sent_back(sends, reduce_axes[0])
    grad_weight = grad_weight_of(rows, gap, gap_other)
    keep, grad_weight = lax.optimization_barrier((keep, grad_weight))
    keep, *sends = first_sum(keep, received)
    received = sent_back(sends, reduce_axes[1])
    keep, *sends = second_sum(keep, received)
    received = sent_back(sends, reduce_axes[2])
    grad_hidden = (keep + sum(received)).astype(jnp.bfloat16)

    first_core = first_core > 0.5
    divergence = jnp.concatenate(
        [
            jnp.where(first_core, divergence, divergence_other),
            jnp.where(first_core, divergence_other, divergence),
        ]
    ).reshape(tokens)
    return (divergence, grad_hidden, grad_weight)


def solution(mesh):
    placed = (
        P(("batch", "vocab"), "mp"),
        P(("batch", "vocab"), "mp"),
        P("mp", ("batch", "vocab")),
        P("mp", ("batch", "vocab")),
        P(),
    )
    return jax.shard_map(
        local,
        mesh=mesh,
        in_specs=placed,
        out_specs=(P(), P(("batch", "vocab"), "mp"), P("mp", ("batch", "vocab"))),
        check_vma=False,
    )
```

time: 130 us -> 123 us (0.946)
  waiting for transfers between devices: 43.2 us -> 40.7 us
  starting transfers between devices: 48.8 us -> 46.8 us
    ppermute x5, waiting for transfers between devices: 3.71 us -> 0.47 us  [swap(): return lax.ppermute(block, 'mp', [(0, 1), (1, 0)])]
    ppermute x36 -> x33, starting transfers between devices: 47.6 us -> 45.3 us  [send(): return lax.ppermute(block, everyone, ring(axes, by))]
    ppermute x36 -> x33, waiting for transfers between devices: 39.5 us -> 40.2 us  [send(): return lax.ppermute(block, everyone, ring(axes, by))]
  transfers between devices with their start and end apart: 41 -> 38, of which waited for: 24 -> 21; matrix products, arithmetic and copies ran while one was open for 1% -> 1% of each run, Pallas kernels for 18% -> 19%
where the time goes in v4:
time: 123 us
  starting transfers between devices  46.8 us (38%)
  waiting for transfers between devices  40.7 us (33%)
  Pallas kernels  28.2 us (23%)
  local copies, waits for them, and re-layouts  5.25 us (4%)
  other arithmetic  1.3 us (1%)
    ppermute x33, starting transfers between devices, send(): return lax.ppermute(block, everyone, ring(axes, by))  45.3 us
    ppermute x33, waiting for transfers between devices, send(): return lax.ppermute(block, everyone, ring(axes, by))  40.2 us
    pallas_call x1, Pallas kernels, grad_weight_of(): pl.pallas_call(grad_weight_kernel, grid=(student_width // tile,), in_spec...  6.91 us
    pallas_call x1, Pallas kernels, teacher_logits(): pl.pallas_call(teacher_kernel, in_specs=[scalars()] + [whole()] * 5, out_...  5.89 us
    unnamed x17, local copies, waits for them, and re-layouts  5.23 us
    pallas_call x1, Pallas kernels, student_logits(): pl.pallas_call(student_kernel, in_specs=[whole()] * 11, out_specs=[whole(...  3.96 us
    pallas_call x1, Pallas kernels, hidden_all(): pl.pallas_call(hidden_all_kernel, in_specs=[scalars()] + [whole()] * 3, o...  3.18 us
    pallas_call x2, Pallas kernels, student_statistics(): pl.pallas_call(functools.partial(student_statistics_kernel, last), grid=(...  2.66 us
  transfers between devices with their start and end apart: 38, of which 21 were waited for; matrix products, arithmetic and copies ran while one was open for 1% of the time, Pallas kernels for 19%

profile of v4, /device:TPU:0, one launch (start us, length us, event | category | flops | bytes accessed | tf_op | source)
XLA Modules:
  0.0 123.2 jit_solution(10440463468555536037)
XLA Ops:
  2.2 3.4 %collective-permute-start.2 = (bf16[8,4096]{1,0:T(8,128)(2,1)S(1)}, bf16[8,4096]{1,0:T(8,128)(2,1)S(1)}, u32[]{:S(2)}, u32[]{:S(2)}) collective-permute-start(bf16[8,4096]{1,0:T(8,128)(2,1)S(1)} %shard_map.77), channel_id=1, source_target_pairs={{0,4},{1,5},{2,6},{3,7},{4,0},{5,1},{6,2},{7,3},{8,12},{9,13},{10,... | collective-permute-start | bytes 196616 | tf_op jit(solution)/shard_map/ppermute | solution.py:51
  5.6 1.1 collective-permute-start.1
  6.6 1.0 collective-permute-start
  7.6 3.7 %copy-done = bf16[2304,2048]{1,0:T(8,128)(2,1)S(1)} copy-done((bf16[2304,2048]{1,0:T(8,128)(2,1)S(1)}, bf16[2304,2048]{1,0:T(8,128)(2,1)}, u32[]{:S(2)}) %copy-start) | copy-done | bytes 9437208
  12.2 3.1 %collective-permute-start.5 = (bf16[32,2560]{1,0:T(8,128)(2,1)S(1)}, bf16[32,2560]{1,0:T(8,128)(2,1)S(1)}, u32[]{:S(2)}, u32[]{:S(2)}) collective-permute-start(bf16[32,2560]{1,0:T(8,128)(2,1)S(1)} %slice.8), channel_id=1, source_target_pairs={{0,1},{1,0},{2,3},{3,2},{4,5},{5,4},{6,7},{7,6},{8,9},{9,8},{10,11... | collective-permute-start | bytes 491528 | tf_op jit(solution)/shard_map/ppermute | solution.py:51
  15.3 1.1 collective-permute-start.4
  16.4 0.9 collective-permute-start.3
  17.3 4.0 %collective-permute-start.11 = (bf16[32,1536]{1,0:T(8,128)(2,1)S(1)}, bf16[32,1536]{1,0:T(8,128)(2,1)S(1)}, u32[]{:S(2)}, u32[]{:S(2)}) collective-permute-start(bf16[32,1536]{1,0:T(8,128)(2,1)S(1)} %pad_maximum_fusion.2), channel_id=1, source_target_pairs={{0,32},{1,33},{2,34},{3,35},{4,36},{5,37},{6,38},{7,39},{8,40},{9,... | collective-permute-start | bytes 294920 | tf_op jit(solution)/shard_map/ppermute | solution.py:51
  22.0 1.3 %collective-permute-start.9 = (bf16[32,1536]{1,0:T(8,128)(2,1)S(1)}, bf16[32,1536]{1,0:T(8,128)(2,1)S(1)}, u32[]{:S(2)}, u32[]{:S(2)}) collective-permute-start(bf16[32,1536]{1,0:T(8,128)(2,1)S(1)} %pad_maximum_fusion.2), channel_id=1, source_target_pairs={{0,16},{1,17},{2,18},{3,19},{4,20},{5,21},{6,22},{7,23},{8,24},{9,... | collective-permute-start | bytes 294920 | tf_op jit(solution)/shard_map/ppermute | solution.py:51
  23.3 3.6 %collective-permute-start.8 = (bf16[128,2560]{1,0:T(8,128)(2,1)S(1)}, bf16[128,2560]{1,0:T(8,128)(2,1)S(1)}, u32[]{:S(2)}, u32[]{:S(2)}) collective-permute-start(bf16[128,2560]{1,0:T(8,128)(2,1)S(1)} %pad_maximum_fusion.x0.refs_0_), channel_id=1, source_target_pairs={{0,32},{1,33},{2,34},{3,35},{4,36},{5,37},{6,38},{7,39},{8,40},{9,... | collective-permute-start | bytes 1966088 | tf_op jit(solution)/shard_map/ppermute | solution.py:51
  27.7 1.3 %collective-permute-start.6 = (bf16[128,2560]{1,0:T(8,128)(2,1)S(1)}, bf16[128,2560]{1,0:T(8,128)(2,1)S(1)}, u32[]{:S(2)}, u32[]{:S(2)}) collective-permute-start(bf16[128,2560]{1,0:T(8,128)(2,1)S(1)} %pad_maximum_fusion.x0.refs_0_), channel_id=1, source_target_pairs={{0,16},{1,17},{2,18},{3,19},{4,20},{5,21},{6,22},{7,23},{8,24},{9,... | collective-permute-start | bytes 1966088 | tf_op jit(solution)/shard_map/ppermute | solution.py:51
  29.0 1.0 collective-permute-start.14
  30.0 1.4 %collective-permute-start.13 = (bf16[128,1536]{1,0:T(8,128)(2,1)S(1)}, bf16[128,1536]{1,0:T(8,128)(2,1)S(1)}, u32[]{:S(2)}, u32[]{:S(2)}) collective-permute-start(bf16[128,1536]{1,0:T(8,128)(2,1)S(1)} %constant_dynamic-update-slice_fusion.refs_4_), channel_id=1, source_target_pairs={{0,9},{1,8},{2,11},{3,10},{4,13},{5,12},{6,15},{7,14},{8,0},{9,1},... | collective-permute-start | bytes 1179656 | tf_op jit(solution)/shard_map/ppermute | solution.py:51
  31.5 4.1 %collective-permute-done.8.x3.refs_3_ = bf16[128,2560]{1,0:T(8,128)(2,1)S(1)} collective-permute-done((bf16[128,2560]{1,0:T(8,128)(2,1)S(1)}, bf16[128,2560]{1,0:T(8,128)(2,1)S(1)}, u32[]{:S(2)}, u32[]{:S(2)}) %collective-permute-start.8) | collective-permute-done | bytes 655392 | tf_op jit(solution)/shard_map/ppermute | solution.py:51
  36.4 7.2 %collective-permute-done.7.x2.refs_2_ = bf16[128,2560]{1,0:T(8,128)(2,1)S(1)} collective-permute-done((bf16[128,2560]{1,0:T(8,128)(2,1)S(1)}, bf16[128,2560]{1,0:T(8,128)(2,1)S(1)}, u32[]{:S(2)}, u32[]{:S(2)}) %collective-permute-start.7) | collective-permute-done | bytes 655392 | tf_op jit(solution)/shard_map/ppermute | solution.py:51
  43.6 5.9 %shard_map.78 = (f32[256,2048]{1,0:T(8,128)S(1)}, f32[256,2048]{1,0:T(8,128)S(1)}) custom-call(s32[2,128]{1,0:T(2,128)S(1)} %get-tuple-element.55.places, bf16[128,2560]{1,0:T(8,128)(2,1)S(1)} %pad_maximum_fusion.x0.refs_0_, bf16[128,2560]{1,0:T(8,128)(2,1)S(1)} %collective-permute-done.6.x1.refs_1_, ...), custom_call_target="tpu_custom_call" | custom-call | flops 4831838208 | bytes 9437184 | tf_op jit(solution)/shard_map/pallas_call | solution.py:192
  49.7 4.0 %shard_map.79 = (f32[256,1536]{1,0:T(8,128)S(1)}, f32[256,1536]{1,0:T(8,128)S(1)}, bf16[512,1792]{1,0:T(8,128)(2,1)S(1)}) custom-call(bf16[512,512]{1,0:T(8,128)(2,1)S(1)} %get-tuple-element.57.main_order, bf16[512,512]{1,0:T(8,128)(2,1)S(1)} %get-tuple-element.58.apart_order, bf16[128,2560]{1,0:T(8,128)(2,1)S(1)} %pad_maximum_fusion.x0.refs_0_, ...), custom_call_target="tpu_custom_call" | custom-call | flops 2818572288 | bytes 7340032 | tf_op jit(solution)/shard_map/pallas_call | solution.py:207
  54.4 1.1 shard_map.80
  55.6 1.4 %shard_map.81 = (f32[256,2048]{1,0:T(8,128)S(1)}, f32[256,2048]{1,0:T(8,128)S(1)}, f32[256,128]{1,0:T(8,128)S(1)}) custom-call(f32[256,2048]{1,0:T(8,128)S(1)} %get-tuple-element.70.own, f32[256,2048]{1,0:T(8,128)S(1)} %collective-permute-done.15.other), custom_call_target="tpu_custom_call" | custom-call | flops 4194304 | bytes 8388608 | tf_op jit(solution)/shard_map/pallas_call | solution.py:251
  57.4 1.8 %shard_map.82 = (f32[256,1536]{1,0:T(8,128)S(1)}, f32[256,1536]{1,0:T(8,128)S(1)}, f32[2,256,128]{2,1,0:T(8,128)S(1)}) custom-call(f32[256,2048]{1,0:T(8,128)S(1)} %get-tuple-element.72.refs_0_.refs_2_, f32[256,2048]{1,0:T(8,128)S(1)} %get-tuple-element.73.refs_1_.refs_3_, f32[256,1536]{1,0:T(8,128)S(1)} %get-tuple-element.74.refs_2_, ...), custom_call_target="tpu_custom_call" | custom-call | flops 6291456 | bytes 9437184 | tf_op jit(solution)/shard_map/pallas_call | solution.py:297
  59.2 0.8 shard_map.83
  60.1 2.5 %collective-permute-start.20 = (f32[8,128]{1,0:T(8,128)S(1)}, f32[8,128]{1,0:T(8,128)S(1)}, u32[]{:S(2)}, u32[]{:S(2)}) collective-permute-start(f32[8,128]{1,0:T(8,128)S(1)} %get-tuple-element.80), channel_id=1, source_target_pairs={{0,32},{1,33},{2,34},{3,35},{4,36},{5,37},{6,38},{7,39},{8,40},{9,... | collective-permute-start | bytes 12296 | tf_op jit(solution)/shard_map/ppermute | solution.py:51
  62.6 1.2 collective-permute-start.19
  63.8 0.8 collective-permute-start.18
  65.3 0.9 collective-permute-done.19
  66.2 2.4 %collective-permute-done.18 = f32[8,128]{1,0:T(8,128)S(1)} collective-permute-done((f32[8,128]{1,0:T(8,128)S(1)}, f32[8,128]{1,0:T(8,128)S(1)}, u32[]{:S(2)}, u32[]{:S(2)}) %collective-permute-start.18) | collective-permute-done | bytes 4128 | tf_op jit(solution)/shard_map/ppermute | solution.py:51
  68.6 1.6 %collective-permute-start.23 = (f32[8,128]{1,0:T(8,128)S(1)}, f32[8,128]{1,0:T(8,128)S(1)}, u32[]{:S(2)}, u32[]{:S(2)}) collective-permute-start(f32[8,128]{1,0:T(8,128)S(1)} %add_add_fusion.2), channel_id=1, source_target_pairs={{0,1},{1,0},{2,3},{3,2},{4,5},{5,4},{6,7},{7,6},{8,9},{9,8},{10,11... | collective-permute-start | bytes 12296 | tf_op jit(solution)/shard_map/ppermute | solution.py:51
  70.3 1.2 %collective-permute-start.22 = (f32[8,128]{1,0:T(8,128)S(1)}, f32[8,128]{1,0:T(8,128)S(1)}, u32[]{:S(2)}, u32[]{:S(2)}) collective-permute-start(f32[8,128]{1,0:T(8,128)S(1)} %add_add_fusion.2), channel_id=1, source_target_pairs={{0,9},{1,8},{2,11},{3,10},{4,13},{5,12},{6,15},{7,14},{8,0},{9,1},... | collective-permute-start | bytes 12296 | tf_op jit(solution)/shard_map/ppermute | solution.py:51
  72.3 1.4 %collective-permute-done.23 = f32[8,128]{1,0:T(8,128)S(1)} collective-permute-done((f32[8,128]{1,0:T(8,128)S(1)}, f32[8,128]{1,0:T(8,128)S(1)}, u32[]{:S(2)}, u32[]{:S(2)}) %collective-permute-start.23) | collective-permute-done | bytes 4128 | tf_op jit(solution)/shard_map/ppermute | solution.py:51
  73.9 2.4 %collective-permute-done.21 = f32[8,128]{1,0:T(8,128)S(1)} collective-permute-done((f32[8,128]{1,0:T(8,128)S(1)}, f32[8,128]{1,0:T(8,128)S(1)}, u32[]{:S(2)}, u32[]{:S(2)}) %collective-permute-start.21) | collective-permute-done | bytes 4128 | tf_op jit(solution)/shard_map/ppermute | solution.py:51
  76.3 2.7 %collective-permute-start.26 = (f32[8,128]{1,0:T(8,128)S(1)}, f32[8,128]{1,0:T(8,128)S(1)}, u32[]{:S(2)}, u32[]{:S(2)}) collective-permute-start(f32[8,128]{1,0:T(8,128)S(1)} %add_add_fusion.1), channel_id=1, source_target_pairs={{0,4},{1,5},{2,6},{3,7},{4,0},{5,1},{6,2},{7,3},{8,12},{9,13},{10,... | collective-permute-start | bytes 12296 | tf_op jit(solution)/shard_map/ppermute | solution.py:51
  79.1 1.1 collective-permute-start.25
  80.2 0.9 collective-permute-start.24
  81.5 1.2 collective-permute-done.25
  82.7 2.3 %collective-permute-done.24 = f32[8,128]{1,0:T(8,128)S(1)} collective-permute-done((f32[8,128]{1,0:T(8,128)S(1)}, f32[8,128]{1,0:T(8,128)S(1)}, u32[]{:S(2)}, u32[]{:S(2)}) %collective-permute-start.24) | collective-permute-done | bytes 4128 | tf_op jit(solution)/shard_map/ppermute | solution.py:51
  86.0 2.1 %shard_map.85.own = f32[256,1792]{1,0:T(8,128)S(1)} custom-call(bf16[256,2048]{1,0:T(8,128)(2,1)S(1)} %get-tuple-element.86.gap.own, bf16[1792,2048]{1,0:T(8,128)(2,1)S(1)} %bitcast.4), custom_call_target="tpu_custom_call" | custom-call | flops 1879048192 | bytes 7340032 | tf_op jit(solution)/shard_map/pallas_call | solution.py:355
  88.2 3.2 %shard_map.86 = (f32[128,1792]{1,0:T(8,128)S(1)}, bf16[128,1792]{1,0:T(8,128)(2,1)S(1)}, bf16[128,1792]{1,0:T(8,128)(2,1)S(1)}, bf16[128,1792]{1,0:T(8,128)(2,1)S(1)}) custom-call(s32[2,128]{1,0:T(2,128)S(1)} %get-tuple-element.55.places, f32[256,1792]{1,0:T(8,128)S(1)} %shard_map.85.own, bf16[256,2048]{1,0:T(8,128)(2,1)S(1)} %collective-permute-done.27.gap.other, ...), custom_call_target="tpu_custom_call" | custom-call | flops 1879048192 | bytes 7340032 | tf_op jit(solution)/shard_map/pallas_call | solution.py:378
  91.5 1.9 %collective-permute-start.30 = (bf16[128,1792]{1,0:T(8,128)(2,1)S(1)}, bf16[128,1792]{1,0:T(8,128)(2,1)S(1)}, u32[]{:S(2)}, u32[]{:S(2)}) collective-permute-start(bf16[128,1792]{1,0:T(8,128)(2,1)S(1)} %get-tuple-element.94), channel_id=1, source_target_pairs={{0,16},{1,17},{2,18},{3,19},{4,20},{5,21},{6,22},{7,23},{8,24},{9,... | collective-permute-start | bytes 1376264 | tf_op jit(solution)/shard_map/ppermute | solution.py:51
  93.4 6.9 %shard_map.87 = bf16[1792,2048]{1,0:T(8,128)(2,1)} custom-call(bf16[512,1792]{1,0:T(8,128)(2,1)S(1)} %get-tuple-element.68.rows, bf16[256,2048]{1,0:T(8,128)(2,1)S(1)} %get-tuple-element.86.gap.own, bf16[256,2048]{1,0:T(8,128)(2,1)S(1)} %collective-permute-done.27.gap.other), custom_call_target="tpu_custom_call" | custom-call | flops 3758096384 | bytes 7340032 | tf_op jit(solution)/shard_map/pallas_call | solution.py:443
  100.4 5.7 %collective-permute-done.30.refs_1_ = bf16[128,1792]{1,0:T(8,128)(2,1)S(1)} collective-permute-done((bf16[128,1792]{1,0:T(8,128)(2,1)S(1)}, bf16[128,1792]{1,0:T(8,128)(2,1)S(1)}, u32[]{:S(2)}, u32[]{:S(2)}) %collective-permute-start.30) | collective-permute-done | bytes 458784 | tf_op jit(solution)/shard_map/ppermute | solution.py:51
  106.5 1.9 %collective-permute-start.33 = (bf16[32,1792]{1,0:T(8,128)(2,1)S(1)}, bf16[32,1792]{1,0:T(8,128)(2,1)S(1)}, u32[]{:S(2)}, u32[]{:S(2)}) collective-permute-start(bf16[32,1792]{1,0:T(8,128)(2,1)S(1)} %get-tuple-element.98), channel_id=1, source_target_pairs={{0,8},{1,9},{2,10},{3,11},{4,12},{5,13},{6,14},{7,15},{8,1},{9,0},... | collective-permute-start | bytes 344072 | tf_op jit(solution)/shard_map/ppermute | solution.py:51
  108.7 2.5 %collective-permute-done.32.refs_0_ = bf16[32,1792]{1,0:T(8,128)(2,1)S(1)} collective-permute-done((bf16[32,1792]{1,0:T(8,128)(2,1)S(1)}, bf16[32,1792]{1,0:T(8,128)(2,1)S(1)}, u32[]{:S(2)}, u32[]{:S(2)}) %collective-permute-start.32) | collective-permute-done | bytes 114720 | tf_op jit(solution)/shard_map/ppermute | solution.py:51
  111.2 1.3 %collective-permute-done.33.refs_1_ = bf16[32,1792]{1,0:T(8,128)(2,1)S(1)} collective-permute-done((bf16[32,1792]{1,0:T(8,128)(2,1)S(1)}, bf16[32,1792]{1,0:T(8,128)(2,1)S(1)}, u32[]{:S(2)}, u32[]{:S(2)}) %collective-permute-start.33) | collective-permute-done | bytes 114720 | tf_op jit(solution)/shard_map/ppermute | solution.py:51
  112.5 2.2 %collective-permute-done.34.refs_2_ = bf16[32,1792]{1,0:T(8,128)(2,1)S(1)} collective-permute-done((bf16[32,1792]{1,0:T(8,128)(2,1)S(1)}, bf16[32,1792]{1,0:T(8,128)(2,1)S(1)}, u32[]{:S(2)}, u32[]{:S(2)}) %collective-permute-start.34) | collective-permute-done | bytes 114720 | tf_op jit(solution)/shard_map/ppermute | solution.py:51
  114.9 2.0 %collective-permute-start.36 = (f32[8,1792]{1,0:T(8,128)S(1)}, f32[8,1792]{1,0:T(8,128)S(1)}, u32[]{:S(2)}, u32[]{:S(2)}) collective-permute-start(f32[8,1792]{1,0:T(8,128)S(1)} %get-tuple-element.102), channel_id=1, source_target_pairs={{0,2},{1,3},{2,4},{3,5},{4,6},{5,7},{6,0},{7,1},{8,10},{9,11},{10,... | collective-permute-start | bytes 172040 | tf_op jit(solution)/shard_map/ppermute | solution.py:51
  117.9 1.1 collective-permute-done.35
  119.0 1.3 %collective-permute-done.36 = f32[8,1792]{1,0:T(8,128)S(1)} collective-permute-done((f32[8,1792]{1,0:T(8,128)S(1)}, f32[8,1792]{1,0:T(8,128)S(1)}, u32[]{:S(2)}, u32[]{:S(2)}) %collective-permute-start.36) | collective-permute-done | bytes 57376 | tf_op jit(solution)/shard_map/ppermute | solution.py:51
  120.3 2.2 %collective-permute-done.37 = f32[8,1792]{1,0:T(8,128)S(1)} collective-permute-done((f32[8,1792]{1,0:T(8,128)S(1)}, f32[8,1792]{1,0:T(8,128)S(1)}, u32[]{:S(2)}, u32[]{:S(2)}) %collective-permute-start.37) | collective-permute-done | bytes 57376 | tf_op jit(solution)/shard_map/ppermute | solution.py:51
  (71 shorter events, 11.7 us)
Async XLA Ops:
  0.6 0.8 copy-start.2
  1.4 0.7 copy-start.3
  2.2 9.4 %collective-permute-start.2 = (bf16[8,4096]{1,0:T(8,128)(2,1)S(1)}, bf16[8,4096]{1,0:T(8,128)(2,1)S(1)}, u32[]{:S(2)}, u32[]{:S(2)}) collective-permute-start(bf16[8,4096]{1,0:T(8,128)(2,1)S(1)} %shard_map.77), channel_id=1, source_target_pairs={{0,4},{1,5},{2,6},{3,7},{4,0},{5,1},{6,2},{7,3},{8,12},{9,13},{10,... | collective-permute-start | bytes 196616 | tf_op jit(solution)/shard_map/ppermute | solution.py:51
  5.6 6.0 %collective-permute-start.1 = (bf16[8,4096]{1,0:T(8,128)(2,1)S(1)}, bf16[8,4096]{1,0:T(8,128)(2,1)S(1)}, u32[]{:S(2)}, u32[]{:S(2)}) collective-permute-start(bf16[8,4096]{1,0:T(8,128)(2,1)S(1)} %shard_map.77), channel_id=1, source_target_pairs={{0,6},{1,7},{2,0},{3,1},{4,2},{5,3},{6,4},{7,5},{8,14},{9,15},{10,... | collective-permute-start | bytes 196616 | tf_op jit(solution)/shard_map/ppermute | solution.py:51
  6.6 5.5 %collective-permute-start = (bf16[8,4096]{1,0:T(8,128)(2,1)S(1)}, bf16[8,4096]{1,0:T(8,128)(2,1)S(1)}, u32[]{:S(2)}, u32[]{:S(2)}) collective-permute-start(bf16[8,4096]{1,0:T(8,128)(2,1)S(1)} %shard_map.77), channel_id=1, source_target_pairs={{0,2},{1,3},{2,4},{3,5},{4,6},{5,7},{6,0},{7,1},{8,10},{9,11},{10,... | collective-permute-start | bytes 196616 | tf_op jit(solution)/shard_map/ppermute | solution.py:51
  7.6 3.7 %copy-start = (bf16[2304,2048]{1,0:T(8,128)(2,1)S(1)}, bf16[2304,2048]{1,0:T(8,128)(2,1)}, u32[]{:S(2)}) copy-start(bf16[2304,2048]{1,0:T(8,128)(2,1)} %weight.4) | copy-start | bytes 28311556
  11.3 32.3 %copy-start.1 = (bf16[2304,2048]{1,0:T(8,128)(2,1)S(1)}, bf16[2304,2048]{1,0:T(8,128)(2,1)}, u32[]{:S(2)}) copy-start(bf16[2304,2048]{1,0:T(8,128)(2,1)} %weight.4) | copy-start | bytes 28311556
  12.2 9.8 %collective-permute-start.5 = (bf16[32,2560]{1,0:T(8,128)(2,1)S(1)}, bf16[32,2560]{1,0:T(8,128)(2,1)S(1)}, u32[]{:S(2)}, u32[]{:S(2)}) collective-permute-start(bf16[32,2560]{1,0:T(8,128)(2,1)S(1)} %slice.8), channel_id=1, source_target_pairs={{0,1},{1,0},{2,3},{3,2},{4,5},{5,4},{6,7},{7,6},{8,9},{9,8},{10,11... | collective-permute-start | bytes 491528 | tf_op jit(solution)/shard_map/ppermute | solution.py:51
  15.3 8.0 %collective-permute-start.4 = (bf16[32,2560]{1,0:T(8,128)(2,1)S(1)}, bf16[32,2560]{1,0:T(8,128)(2,1)S(1)}, u32[]{:S(2)}, u32[]{:S(2)}) collective-permute-start(bf16[32,2560]{1,0:T(8,128)(2,1)S(1)} %slice.8), channel_id=1, source_target_pairs={{0,9},{1,8},{2,11},{3,10},{4,13},{5,12},{6,15},{7,14},{8,0},{9,1},... | collective-permute-start | bytes 491528 | tf_op jit(solution)/shard_map/ppermute | solution.py:51
  16.4 6.9 %collective-permute-start.3 = (bf16[32,2560]{1,0:T(8,128)(2,1)S(1)}, bf16[32,2560]{1,0:T(8,128)(2,1)S(1)}, u32[]{:S(2)}, u32[]{:S(2)}) collective-permute-start(bf16[32,2560]{1,0:T(8,128)(2,1)S(1)} %slice.8), channel_id=1, source_target_pairs={{0,8},{1,9},{2,10},{3,11},{4,12},{5,13},{6,14},{7,15},{8,1},{9,0},... | collective-permute-start | bytes 491528 | tf_op jit(solution)/shard_map/ppermute | solution.py:51
  17.3 10.4 %collective-permute-start.11 = (bf16[32,1536]{1,0:T(8,128)(2,1)S(1)}, bf16[32,1536]{1,0:T(8,128)(2,1)S(1)}, u32[]{:S(2)}, u32[]{:S(2)}) collective-permute-start(bf16[32,1536]{1,0:T(8,128)(2,1)S(1)} %pad_maximum_fusion.2), channel_id=1, source_target_pairs={{0,32},{1,33},{2,34},{3,35},{4,36},{5,37},{6,38},{7,39},{8,40},{9,... | collective-permute-start | bytes 294920 | tf_op jit(solution)/shard_map/ppermute | solution.py:51
  21.3 7.7 %collective-permute-start.10 = (bf16[32,1536]{1,0:T(8,128)(2,1)S(1)}, bf16[32,1536]{1,0:T(8,128)(2,1)S(1)}, u32[]{:S(2)}, u32[]{:S(2)}) collective-permute-start(bf16[32,1536]{1,0:T(8,128)(2,1)S(1)} %pad_maximum_fusion.2), channel_id=1, source_target_pairs={{0,48},{1,49},{2,50},{3,51},{4,52},{5,53},{6,54},{7,55},{8,56},{9,... | collective-permute-start | bytes 294920 | tf_op jit(solution)/shard_map/ppermute | solution.py:51
  22.0 7.0 %collective-permute-start.9 = (bf16[32,1536]{1,0:T(8,128)(2,1)S(1)}, bf16[32,1536]{1,0:T(8,128)(2,1)S(1)}, u32[]{:S(2)}, u32[]{:S(2)}) collective-permute-start(bf16[32,1536]{1,0:T(8,128)(2,1)S(1)} %pad_maximum_fusion.2), channel_id=1, source_target_pairs={{0,16},{1,17},{2,18},{3,19},{4,20},{5,21},{6,22},{7,23},{8,24},{9,... | collective-permute-start | bytes 294920 | tf_op jit(solution)/shard_map/ppermute | solution.py:51
  23.3 12.3 %collective-permute-start.8 = (bf16[128,2560]{1,0:T(8,128)(2,1)S(1)}, bf16[128,2560]{1,0:T(8,128)(2,1)S(1)}, u32[]{:S(2)}, u32[]{:S(2)}) collective-permute-start(bf16[128,2560]{1,0:T(8,128)(2,1)S(1)} %pad_maximum_fusion.x0.refs_0_), channel_id=1, source_target_pairs={{0,32},{1,33},{2,34},{3,35},{4,36},{5,37},{6,38},{7,39},{8,40},{9,... | collective-permute-start | bytes 1966088 | tf_op jit(solution)/shard_map/ppermute | solution.py:51
  26.9 16.6 %collective-permute-start.7 = (bf16[128,2560]{1,0:T(8,128)(2,1)S(1)}, bf16[128,2560]{1,0:T(8,128)(2,1)S(1)}, u32[]{:S(2)}, u32[]{:S(2)}) collective-permute-start(bf16[128,2560]{1,0:T(8,128)(2,1)S(1)} %pad_maximum_fusion.x0.refs_0_), channel_id=1, source_target_pairs={{0,48},{1,49},{2,50},{3,51},{4,52},{5,53},{6,54},{7,55},{8,56},{9,... | collective-permute-start | bytes 1966088 | tf_op jit(solution)/shard_map/ppermute | solution.py:51
  27.7 15.9 %collective-permute-start.6 = (bf16[128,2560]{1,0:T(8,128)(2,1)S(1)}, bf16[128,2560]{1,0:T(8,128)(2,1)S(1)}, u32[]{:S(2)}, u32[]{:S(2)}) collective-permute-start(bf16[128,2560]{1,0:T(8,128)(2,1)S(1)} %pad_maximum_fusion.x0.refs_0_), channel_id=1, source_target_pairs={{0,16},{1,17},{2,18},{3,19},{4,20},{5,21},{6,22},{7,23},{8,24},{9,... | collective-permute-start | bytes 1966088 | tf_op jit(solution)/shard_map/ppermute | solution.py:51
  29.0 20.5 %collective-permute-start.14 = (bf16[128,1536]{1,0:T(8,128)(2,1)S(1)}, bf16[128,1536]{1,0:T(8,128)(2,1)S(1)}, u32[]{:S(2)}, u32[]{:S(2)}) collective-permute-start(bf16[128,1536]{1,0:T(8,128)(2,1)S(1)} %constant_dynamic-update-slice_fusion.refs_4_), channel_id=1, source_target_pairs={{0,1},{1,0},{2,3},{3,2},{4,5},{5,4},{6,7},{7,6},{8,9},{9,8},{10,11... | collective-permute-start | bytes 1179656 | tf_op jit(solution)/shard_map/ppermute | solution.py:51
  30.0 19.5 %collective-permute-start.13 = (bf16[128,1536]{1,0:T(8,128)(2,1)S(1)}, bf16[128,1536]{1,0:T(8,128)(2,1)S(1)}, u32[]{:S(2)}, u32[]{:S(2)}) collective-permute-start(bf16[128,1536]{1,0:T(8,128)(2,1)S(1)} %constant_dynamic-update-slice_fusion.refs_4_), channel_id=1, source_target_pairs={{0,9},{1,8},{2,11},{3,10},{4,13},{5,12},{6,15},{7,14},{8,0},{9,1},... | collective-permute-start | bytes 1179656 | tf_op jit(solution)/shard_map/ppermute | solution.py:51
  35.6 13.9 %collective-permute-start.12 = (bf16[128,1536]{1,0:T(8,128)(2,1)S(1)}, bf16[128,1536]{1,0:T(8,128)(2,1)S(1)}, u32[]{:S(2)}, u32[]{:S(2)}) collective-permute-start(bf16[128,1536]{1,0:T(8,128)(2,1)S(1)} %constant_dynamic-update-slice_fusion.refs_4_), channel_id=1, source_target_pairs={{0,8},{1,9},{2,10},{3,11},{4,12},{5,13},{6,14},{7,15},{8,1},{9,0},... | collective-permute-start | bytes 1179656 | tf_op jit(solution)/shard_map/ppermute | solution.py:51
  43.6 6.0 %slice-start = ((s8[7340032]{0:T(1024)(128)(4,1)}), s8[4194304]{0:T(1024)(128)(4,1)S(1)}, s32[]{:S(2)}) async-start(s8[7340032]{0:T(1024)(128)(4,1)} %bitcast.3), calls=%async_computation | async-start | bytes 8388608
  43.6 6.0 %slice-start.1 = ((s8[7340032]{0:T(1024)(128)(4,1)}), s8[3145728]{0:T(1024)(128)(4,1)S(1)}, s32[]{:S(2)}) async-start(s8[7340032]{0:T(1024)(128)(4,1)} %bitcast.3), calls=%async_computation.1 | async-start | bytes 6291456
  49.5 6.1 %collective-permute-start.15 = (f32[256,2048]{1,0:T(8,128)S(1)}, f32[256,2048]{1,0:T(8,128)S(1)}, u32[]{:S(2)}, u32[]{:S(2)}) collective-permute-start(f32[256,2048]{1,0:T(8,128)S(1)} %get-tuple-element.71), channel_id=1, source_target_pairs={{0,64},{64,0},{1,65},{65,1},{2,66},{66,2},{3,67},{67,3},{4,68},{68... | collective-permute-start | bytes 6291464 | tf_op jit(solution)/shard_map/ppermute | solution.py:55
  53.6 3.8 %collective-permute-start.16 = (f32[256,1536]{1,0:T(8,128)S(1)}, f32[256,1536]{1,0:T(8,128)S(1)}, u32[]{:S(2)}, u32[]{:S(2)}) collective-permute-start(f32[256,1536]{1,0:T(8,128)S(1)} %get-tuple-element.75), channel_id=1, source_target_pairs={{0,64},{64,0},{1,65},{65,1},{2,66},{66,2},{3,67},{67,3},{4,68},{68... | collective-permute-start | bytes 4718600 | tf_op jit(solution)/shard_map/ppermute | solution.py:55
  55.5 3.8 %collective-permute-start.17 = (f32[256,512]{1,0:T(8,128)S(1)}, f32[256,512]{1,0:T(8,128)S(1)}, u32[]{:S(2)}, u32[]{:S(2)}) collective-permute-start(f32[256,512]{1,0:T(8,128)S(1)} %get-tuple-element.79), channel_id=1, source_target_pairs={{0,64},{64,0},{1,65},{65,1},{2,66},{66,2},{3,67},{67,3},{4,68},{68... | collective-permute-start | bytes 1572872 | tf_op jit(solution)/shard_map/ppermute | solution.py:55
  59.2 25.8 %copy-start.4 = (f32[512]{0:T(512)S(1)}, f32[512]{0:T(512)}, u32[]{:S(2)}) copy-start(f32[512]{0:T(512)} %param.9) | copy-start | bytes 6148
  60.1 5.2 %collective-permute-start.20 = (f32[8,128]{1,0:T(8,128)S(1)}, f32[8,128]{1,0:T(8,128)S(1)}, u32[]{:S(2)}, u32[]{:S(2)}) collective-permute-start(f32[8,128]{1,0:T(8,128)S(1)} %get-tuple-element.80), channel_id=1, source_target_pairs={{0,32},{1,33},{2,34},{3,35},{4,36},{5,37},{6,38},{7,39},{8,40},{9,... | collective-permute-start | bytes 12296 | tf_op jit(solution)/shard_map/ppermute | solution.py:51
  62.6 3.6 %collective-permute-start.19 = (f32[8,128]{1,0:T(8,128)S(1)}, f32[8,128]{1,0:T(8,128)S(1)}, u32[]{:S(2)}, u32[]{:S(2)}) collective-permute-start(f32[8,128]{1,0:T(8,128)S(1)} %get-tuple-element.80), channel_id=1, source_target_pairs={{0,48},{1,49},{2,50},{3,51},{4,52},{5,53},{6,54},{7,55},{8,56},{9,... | collective-permute-start | bytes 12296 | tf_op jit(solution)/shard_map/ppermute | solution.py:51
  63.8 4.8 %collective-permute-start.18 = (f32[8,128]{1,0:T(8,128)S(1)}, f32[8,128]{1,0:T(8,128)S(1)}, u32[]{:S(2)}, u32[]{:S(2)}) collective-permute-start(f32[8,128]{1,0:T(8,128)S(1)} %get-tuple-element.80), channel_id=1, source_target_pairs={{0,16},{1,17},{2,18},{3,19},{4,20},{5,21},{6,22},{7,23},{8,24},{9,... | collective-permute-start | bytes 12296 | tf_op jit(solution)/shard_map/ppermute | solution.py:51
  68.6 5.1 %collective-permute-start.23 = (f32[8,128]{1,0:T(8,128)S(1)}, f32[8,128]{1,0:T(8,128)S(1)}, u32[]{:S(2)}, u32[]{:S(2)}) collective-permute-start(f32[8,128]{1,0:T(8,128)S(1)} %add_add_fusion.2), channel_id=1, source_target_pairs={{0,1},{1,0},{2,3},{3,2},{4,5},{5,4},{6,7},{7,6},{8,9},{9,8},{10,11... | collective-permute-start | bytes 12296 | tf_op jit(solution)/shard_map/ppermute | solution.py:51
  70.3 3.6 %collective-permute-start.22 = (f32[8,128]{1,0:T(8,128)S(1)}, f32[8,128]{1,0:T(8,128)S(1)}, u32[]{:S(2)}, u32[]{:S(2)}) collective-permute-start(f32[8,128]{1,0:T(8,128)S(1)} %add_add_fusion.2), channel_id=1, source_target_pairs={{0,9},{1,8},{2,11},{3,10},{4,13},{5,12},{6,15},{7,14},{8,0},{9,1},... | collective-permute-start | bytes 12296 | tf_op jit(solution)/shard_map/ppermute | solution.py:51
  71.5 4.8 %collective-permute-start.21 = (f32[8,128]{1,0:T(8,128)S(1)}, f32[8,128]{1,0:T(8,128)S(1)}, u32[]{:S(2)}, u32[]{:S(2)}) collective-permute-start(f32[8,128]{1,0:T(8,128)S(1)} %add_add_fusion.2), channel_id=1, source_target_pairs={{0,8},{1,9},{2,10},{3,11},{4,12},{5,13},{6,14},{7,15},{8,1},{9,0},... | collective-permute-start | bytes 12296 | tf_op jit(solution)/shard_map/ppermute | solution.py:51
  76.3 5.1 %collective-permute-start.26 = (f32[8,128]{1,0:T(8,128)S(1)}, f32[8,128]{1,0:T(8,128)S(1)}, u32[]{:S(2)}, u32[]{:S(2)}) collective-permute-start(f32[8,128]{1,0:T(8,128)S(1)} %add_add_fusion.1), channel_id=1, source_target_pairs={{0,4},{1,5},{2,6},{3,7},{4,0},{5,1},{6,2},{7,3},{8,12},{9,13},{10,... | collective-permute-start | bytes 12296 | tf_op jit(solution)/shard_map/ppermute | solution.py:51
  79.1 3.6 %collective-permute-start.25 = (f32[8,128]{1,0:T(8,128)S(1)}, f32[8,128]{1,0:T(8,128)S(1)}, u32[]{:S(2)}, u32[]{:S(2)}) collective-permute-start(f32[8,128]{1,0:T(8,128)S(1)} %add_add_fusion.1), channel_id=1, source_target_pairs={{0,6},{1,7},{2,0},{3,1},{4,2},{5,3},{6,4},{7,5},{8,14},{9,15},{10,... | collective-permute-start | bytes 12296 | tf_op jit(solution)/shard_map/ppermute | solution.py:51
  80.2 4.8 %collective-permute-start.24 = (f32[8,128]{1,0:T(8,128)S(1)}, f32[8,128]{1,0:T(8,128)S(1)}, u32[]{:S(2)}, u32[]{:S(2)}) collective-permute-start(f32[8,128]{1,0:T(8,128)S(1)} %add_add_fusion.1), channel_id=1, source_target_pairs={{0,2},{1,3},{2,4},{3,5},{4,6},{5,7},{6,0},{7,1},{8,10},{9,11},{10,... | collective-permute-start | bytes 12296 | tf_op jit(solution)/shard_map/ppermute | solution.py:51
  85.4 2.7 %collective-permute-start.27 = (bf16[256,2048]{1,0:T(8,128)(2,1)S(1)}, bf16[256,2048]{1,0:T(8,128)(2,1)S(1)}, u32[]{:S(2)}, u32[]{:S(2)}) collective-permute-start(bf16[256,2048]{1,0:T(8,128)(2,1)S(1)} %get-tuple-element.86.gap.own), channel_id=1, source_target_pairs={{0,64},{64,0},{1,65},{65,1},{2,66},{66,2},{3,67},{67,3},{4,68},{68... | collective-permute-start | bytes 3145736 | tf_op jit(solution)/shard_map/ppermute | solution.py:55
  85.5 2.6 %collective-permute-start.28 = (f32[2,128]{1,0:T(2,128)S(1)}, f32[2,128]{1,0:T(2,128)S(1)}, u32[]{:S(2)}, u32[]{:S(2)}) collective-permute-start(f32[2,128]{1,0:T(2,128)S(1)} %get-tuple-element.85), channel_id=1, source_target_pairs={{0,64},{64,0},{1,65},{65,1},{2,66},{66,2},{3,67},{67,3},{4,68},{68... | collective-permute-start | bytes 3080 | tf_op jit(solution)/shard_map/ppermute | solution.py:55
  91.3 9.0 %collective-permute-start.29 = (bf16[128,1792]{1,0:T(8,128)(2,1)S(1)}, bf16[128,1792]{1,0:T(8,128)(2,1)S(1)}, u32[]{:S(2)}, u32[]{:S(2)}) collective-permute-start(bf16[128,1792]{1,0:T(8,128)(2,1)S(1)} %get-tuple-element.93), channel_id=1, source_target_pairs={{0,48},{1,49},{2,50},{3,51},{4,52},{5,53},{6,54},{7,55},{8,56},{9,... | collective-permute-start | bytes 1376264 | tf_op jit(solution)/shard_map/ppermute | solution.py:51
  91.5 14.6 %collective-permute-start.30 = (bf16[128,1792]{1,0:T(8,128)(2,1)S(1)}, bf16[128,1792]{1,0:T(8,128)(2,1)S(1)}, u32[]{:S(2)}, u32[]{:S(2)}) collective-permute-start(bf16[128,1792]{1,0:T(8,128)(2,1)S(1)} %get-tuple-element.94), channel_id=1, source_target_pairs={{0,16},{1,17},{2,18},{3,19},{4,20},{5,21},{6,22},{7,23},{8,24},{9,... | collective-permute-start | bytes 1376264 | tf_op jit(solution)/shard_map/ppermute | solution.py:51
  93.4 12.7 %collective-permute-start.31 = (bf16[128,1792]{1,0:T(8,128)(2,1)S(1)}, bf16[128,1792]{1,0:T(8,128)(2,1)S(1)}, u32[]{:S(2)}, u32[]{:S(2)}) collective-permute-start(bf16[128,1792]{1,0:T(8,128)(2,1)S(1)} %get-tuple-element.95), channel_id=1, source_target_pairs={{0,32},{1,33},{2,34},{3,35},{4,36},{5,37},{6,38},{7,39},{8,40},{9,... | collective-permute-start | bytes 1376264 | tf_op jit(solution)/shard_map/ppermute | solution.py:51
  106.3 4.9 %collective-permute-start.32 = (bf16[32,1792]{1,0:T(8,128)(2,1)S(1)}, bf16[32,1792]{1,0:T(8,128)(2,1)S(1)}, u32[]{:S(2)}, u32[]{:S(2)}) collective-permute-start(bf16[32,1792]{1,0:T(8,128)(2,1)S(1)} %get-tuple-element.97), channel_id=1, source_target_pairs={{0,9},{1,8},{2,11},{3,10},{4,13},{5,12},{6,15},{7,14},{8,0},{9,1},... | collective-permute-start | bytes 344072 | tf_op jit(solution)/shard_map/ppermute | solution.py:51
  106.5 6.0 %collective-permute-start.33 = (bf16[32,1792]{1,0:T(8,128)(2,1)S(1)}, bf16[32,1792]{1,0:T(8,128)(2,1)S(1)}, u32[]{:S(2)}, u32[]{:S(2)}) collective-permute-start(bf16[32,1792]{1,0:T(8,128)(2,1)S(1)} %get-tuple-element.98), channel_id=1, source_target_pairs={{0,8},{1,9},{2,10},{3,11},{4,12},{5,13},{6,14},{7,15},{8,1},{9,0},... | collective-permute-start | bytes 344072 | tf_op jit(solution)/shard_map/ppermute | solution.py:51
  108.4 6.3 %collective-permute-start.34 = (bf16[32,1792]{1,0:T(8,128)(2,1)S(1)}, bf16[32,1792]{1,0:T(8,128)(2,1)S(1)}, u32[]{:S(2)}, u32[]{:S(2)}) collective-permute-start(bf16[32,1792]{1,0:T(8,128)(2,1)S(1)} %get-tuple-element.99), channel_id=1, source_target_pairs={{0,1},{1,0},{2,3},{3,2},{4,5},{5,4},{6,7},{7,6},{8,9},{9,8},{10,11... | collective-permute-start | bytes 344072 | tf_op jit(solution)/shard_map/ppermute | solution.py:51
  114.8 4.2 %collective-permute-start.35 = (f32[8,1792]{1,0:T(8,128)S(1)}, f32[8,1792]{1,0:T(8,128)S(1)}, u32[]{:S(2)}, u32[]{:S(2)}) collective-permute-start(f32[8,1792]{1,0:T(8,128)S(1)} %get-tuple-element.101), channel_id=1, source_target_pairs={{0,6},{1,7},{2,0},{3,1},{4,2},{5,3},{6,4},{7,5},{8,14},{9,15},{10,... | collective-permute-start | bytes 172040 | tf_op jit(solution)/shard_map/ppermute | solution.py:51
  114.9 5.5 %collective-permute-start.36 = (f32[8,1792]{1,0:T(8,128)S(1)}, f32[8,1792]{1,0:T(8,128)S(1)}, u32[]{:S(2)}, u32[]{:S(2)}) collective-permute-start(f32[8,1792]{1,0:T(8,128)S(1)} %get-tuple-element.102), channel_id=1, source_target_pairs={{0,2},{1,3},{2,4},{3,5},{4,6},{5,7},{6,0},{7,1},{8,10},{9,11},{10,... | collective-permute-start | bytes 172040 | tf_op jit(solution)/shard_map/ppermute | solution.py:51
  116.9 5.7 %collective-permute-start.37 = (f32[8,1792]{1,0:T(8,128)S(1)}, f32[8,1792]{1,0:T(8,128)S(1)}, u32[]{:S(2)}, u32[]{:S(2)}) collective-permute-start(f32[8,1792]{1,0:T(8,128)S(1)} %get-tuple-element.103), channel_id=1, source_target_pairs={{0,4},{1,5},{2,6},{3,7},{4,0},{5,1},{6,2},{7,3},{8,12},{9,13},{10,... | collective-permute-start | bytes 172040 | tf_op jit(solution)/shard_map/ppermute | solution.py:51

commit v5 on v4

--- a/solution.py
+++ b/solution.py
@@ -12,7 +12,7 @@
 tokens, teacher_width, student_width, vocab_local = 512, 2304, 1792, 2048
 width = teacher_width + student_width
 half = tokens // 2
-apart = 1536
+apart = 1664
 everyone = ("mp", "batch", "vocab")
 mega = 1024 * 1024
 
@@ -45,6 +45,14 @@
         at = place(source)
         pairs.append((source, index_of(moved(at, axes[at["core"]], by))))
     return pairs
+
+
+def planes():
+    groups = {}
+    for index in range(128):
+        at = place(index)
+        groups.setdefault((at["core"], at[reduce_axes[0][at["core"]]]), []).append(index)
+    return list(groups.values())
 
 
 def send(block, axes, by):
@@ -86,11 +94,11 @@
 
 
 def gathered(order, blocks, first, rows):
-    step = 256
+    step = 512
     for at in range(0, rows.shape[1], step):
-        cols = slice(first + at, first + at + step)
-        block = jnp.concatenate([x[:, cols] for x in blocks], axis=0)
-        rows[:, at : at + step] = jnp.dot(
+        end = min(at + step, rows.shape[1])
+        block = jnp.concatenate([x[:, first + at : first + end] for x in blocks], axis=0)
+        rows[:, at:end] = jnp.dot(
             order[...], block, preferred_element_type=jnp.float32
         ).astype(jnp.bfloat16)
 
@@ -144,6 +152,17 @@
     return ((owner - 32 * core) & 63) * 8 + row
 
 
+def reduce_place(row, at, core):
+    block = row // 8
+    digit, member = block >> 4, block & 15
+    offset = digit ^ (digit >> 1)
+    z = (1 - core) * ((at["z"] - offset) & 3) + core * (member >> 2)
+    y = (1 - core) * ((member >> 1) & 3) + core * ((at["y"] - offset) & 3)
+    x_lo = (1 - core) * (member >> 3) + core * ((member >> 1) & 1)
+    owner = z * 16 + x_lo * 8 + y * 2 + (member & 1)
+    return ((owner - 32 * core) & 63) * 8 + row % 8
+
+
 def setup_kernel(_, main_order, apart_order, places, first_core):
     core = lax.axis_index("mp")
     batch, vocab = lax.axis_index("batch"), lax.axis_index("vocab")
@@ -154,8 +173,8 @@
         goal = own_place(token, dict(at), axes_of, core)
         order[...] = jnp.where(rows == goal, 1.0, 0.0).astype(jnp.bfloat16)
     block = lax.broadcasted_iota(jnp.int32, (1, 128), 1) % 64 * 8
-    for i, axes_of in enumerate((main_axes, reduce_axes[::-1])):
-        places[i : i + 1] = own_place(block, dict(at), axes_of, core)
+    places[0:1] = own_place(block, dict(at), main_axes, core)
+    places[1:2] = reduce_place(block, at, core)
     first_core[...] = jnp.full(first_core.shape, 1.0, jnp.float32) * (core == 0).astype(jnp.float32)
 
 
@@ -387,48 +406,39 @@
     )(places, own, gap, weight)
 
 
-def total_of(keep, received, at, size):
-    rows = pl.ds(at, size)
-    return keep[rows] + sum(r[rows].astype(jnp.float32) for r in received)
-
-
 def first_sum_kernel(mine, *refs):
-    received, (keep, *sends) = refs[:3], refs[3:]
-    keep[...] = total_of(mine, received, 0, 32)
-    for j, send in enumerate(sends):
-        send[...] = total_of(mine, received, 32 * (j + 1), 32).astype(send.dtype)
+    received, out = refs[:3], refs[3]
+    total = mine[...] + sum(r[...].astype(jnp.float32) for r in received)
+    out[...] = total.astype(out.dtype)
 
 
 def first_sum(mine, received):
-    shape = (32, student_width)
     return pl.pallas_call(
         first_sum_kernel,
         in_specs=[whole()] * 4,
-        out_specs=[whole()] * 4,
-        out_shape=[jax.ShapeDtypeStruct(shape, jnp.float32)]
-        + [jax.ShapeDtypeStruct(shape, jnp.bfloat16)] * 3,
+        out_specs=whole(),
+        out_shape=jax.ShapeDtypeStruct(mine.shape, jnp.bfloat16),
         compiler_params=pltpu.CompilerParams(vmem_limit_bytes=6 * mega),
         cost_estimate=cost(128 * student_width * 4, 2 * mega),
     )(mine, *received)
 
 
-def second_sum_kernel(mine, *refs):
-    received, (keep, *sends) = refs[:3], refs[3:]
-    total = mine[...] + sum(r[...].astype(jnp.float32) for r in received)
-    keep[...] = total[:8]
-    for j, send in enumerate(sends):
-        send[...] = total[8 * (j + 1) : 8 * (j + 2)]
-
-
-def second_sum(mine, received):
-    return pl.pallas_call(
-        second_sum_kernel,
-        in_specs=[whole()] * 4,
-        out_specs=[whole()] * 4,
-        out_shape=[jax.ShapeDtypeStruct((8, student_width), jnp.float32)] * 4,
+def last_sum_kernel(received, out):
+    total = received[0].astype(jnp.float32)
+    for i in range(1, received.shape[0]):
+        total += received[i].astype(jnp.float32)
+    out[...] = total.astype(out.dtype)
+
+
+def last_sum(received):
+    return pl.pallas_call(
+        last_sum_kernel,
+        in_specs=[whole()],
+        out_specs=whole(),
+        out_shape=jax.ShapeDtypeStruct(received.shape[1:], received.dtype),
         compiler_params=pltpu.CompilerParams(vmem_limit_bytes=3 * mega),
-        cost_estimate=cost(32 * student_width * 4, mega),
-    )(mine, *received)
+        cost_estimate=cost(received.size, 2 * received.size),
+    )(received)
 
 
 def grad_weight_kernel(rows, own, other, out):
@@ -461,6 +471,7 @@
         return jnp.concatenate(blocks, axis=0)
 
     block = joined(shared_along(side_by_side(hidden_teacher, hidden_student), main_axes[0]))
+    block, places = lax.optimization_barrier((block, places))
     separate, main = block[:, :apart], block[:, apart:]
     main, separate = shared_along(main, main_axes[1]), shared_along(separate, apart_axes[1])
     main = joined(main)
@@ -490,7 +501,8 @@
     gap_other, divergence_other = lax.optimization_barrier((swap(gap), swap(divergence)))
 
     def sent_back(sends, axes):
-        return [send(b, axes, -by) for b, by in zip(sends, offsets[1:])]
+        far = send(sends[2], axes, -offsets[3])
+        return [send(b, axes, -by) for b, by in zip(sends[:2], offsets[1:3])] + [far]
 
     hidden = hidden_own(gap, student_weight)
     gap_other, hidden = lax.optimization_barrier((gap_other, hidden))
@@ -498,11 +510,9 @@
     received = sent_back(sends, reduce_axes[0])
     grad_weight = grad_weight_of(rows, gap, gap_other)
     keep, grad_weight = lax.optimization_barrier((keep, grad_weight))
-    keep, *sends = first_sum(keep, received)
-    received = sent_back(sends, reduce_axes[1])
-    keep, *sends = second_sum(keep, received)
-    received = sent_back(sends, reduce_axes[2])
-    grad_hidden = (keep + sum(received)).astype(jnp.bfloat16)
+    total = first_sum(keep, received).reshape(16, 8, student_width)
+    total = lax.all_to_all(total, everyone, 0, 0, axis_index_groups=planes())
+    grad_hidden = last_sum(total)
 
     first_core = first_core > 0.5
     divergence = jnp.concatenate(

time: 123 us -> 122 us (level)
  starting transfers between devices: 46.8 us -> 44.5 us
  Pallas kernels: 28.2 us -> 29.7 us
    ppermute x33 -> x27, waiting for transfers between devices: 40.2 us -> 31 us  [send(): return lax.ppermute(block, everyone, ring(axes, by))]
    all_to_all x0 -> x1, waiting for transfers between devices: none -> 8.73 us  [local(): total = lax.all_to_all(total, everyone, 0, 0, axis_index_groups=planes())]
    ppermute x33 -> x27, starting transfers between devices: 45.3 us -> 39.5 us  [send(): return lax.ppermute(block, everyone, ring(axes, by))]
    all_to_all x0 -> x1, starting transfers between devices: none -> 3.56 us  [local(): total = lax.all_to_all(total, everyone, 0, 0, axis_index_groups=planes())]
    pallas_call x2, Pallas kernels: 0.27 us -> 1.65 us  [the longest x1 0.98 us: first_sum(): pl.pallas_call(first_sum_kernel, in_specs=[whole()] * 4, out_specs=whole(...]
  transfers between devices with their start and end apart: 38 -> 33, of which waited for: 21 -> 17; matrix products, arithmetic and copies ran while one was open for 1% -> 1% of each run, Pallas kernels for 19% -> 19%
where the time goes in v5:
time: 122 us; the launch traced here: 121 us
  starting transfers between devices  44.5 us (36%)
  waiting for transfers between devices  40.2 us (33%)
  Pallas kernels  29.7 us (24%)
  local copies, waits for them, and re-layouts  5.29 us (4%)
    ppermute x27, starting transfers between devices, send(): return lax.ppermute(block, everyone, ring(axes, by))  39.5 us
    ppermute x27, waiting for transfers between devices, send(): return lax.ppermute(block, everyone, ring(axes, by))  31 us
    all_to_all x1, waiting for transfers between devices, local(): total = lax.all_to_all(total, everyone, 0, 0, axis_index_groups=planes())  8.73 us
    pallas_call x1, Pallas kernels, grad_weight_of(): pl.pallas_call(grad_weight_kernel, grid=(student_width // tile,), in_spec...  6.89 us
    pallas_call x1, Pallas kernels, teacher_logits(): pl.pallas_call(teacher_kernel, in_specs=[scalars()] + [whole()] * 5, out_...  5.83 us
    unnamed x17, local copies, waits for them, and re-layouts  5.25 us
    pallas_call x1, Pallas kernels, student_logits(): pl.pallas_call(student_kernel, in_specs=[whole()] * 11, out_specs=[whole(...  4.12 us
    all_to_all x1, starting transfers between devices, local(): total = lax.all_to_all(total, everyone, 0, 0, axis_index_groups=planes())  3.56 us
  transfers between devices with their start and end apart: 33, of which 17 were waited for; matrix products, arithmetic and copies ran while one was open for 1% of the time, Pallas kernels for 19%

profile of v5, /device:TPU:0, one launch (start us, length us, event | category | flops | bytes accessed | tf_op | source)
XLA Modules:
  0.0 121.3 jit_solution(16618302096508302443)
XLA Ops:
  0.6 0.8 copy-done.2
  1.4 0.7 copy-done.3
  2.2 3.4 %collective-permute-start.2 = (bf16[8,4096]{1,0:T(8,128)(2,1)S(1)}, bf16[8,4096]{1,0:T(8,128)(2,1)S(1)}, u32[]{:S(2)}, u32[]{:S(2)}) collective-permute-start(bf16[8,4096]{1,0:T(8,128)(2,1)S(1)} %shard_map.77), channel_id=1, source_target_pairs={{0,4},{1,5},{2,6},{3,7},{4,0},{5,1},{6,2},{7,3},{8,12},{9,13},{10,... | collective-permute-start | bytes 196616 | tf_op jit(solution)/shard_map/ppermute | solution.py:59
  5.6 1.1 collective-permute-start.1
  6.6 1.0 collective-permute-start
  7.6 3.7 %copy-done = bf16[2304,2048]{1,0:T(8,128)(2,1)S(1)} copy-done((bf16[2304,2048]{1,0:T(8,128)(2,1)S(1)}, bf16[2304,2048]{1,0:T(8,128)(2,1)}, u32[]{:S(2)}) %copy-start) | copy-done | bytes 9437208
  12.2 3.1 %collective-permute-start.5 = (bf16[32,2432]{1,0:T(8,128)(2,1)S(1)}, bf16[32,2432]{1,0:T(8,128)(2,1)S(1)}, u32[]{:S(2)}, u32[]{:S(2)}) collective-permute-start(bf16[32,2432]{1,0:T(8,128)(2,1)S(1)} %slice.6), channel_id=1, source_target_pairs={{0,1},{1,0},{2,3},{3,2},{4,5},{5,4},{6,7},{7,6},{8,9},{9,8},{10,11... | collective-permute-start | bytes 466952 | tf_op jit(solution)/shard_map/ppermute | solution.py:59
  15.3 1.1 collective-permute-start.4
  16.4 0.9 collective-permute-start.3
  17.3 4.0 %collective-permute-start.11 = (bf16[32,1664]{1,0:T(8,128)(2,1)S(1)}, bf16[32,1664]{1,0:T(8,128)(2,1)S(1)}, u32[]{:S(2)}, u32[]{:S(2)}) collective-permute-start(bf16[32,1664]{1,0:T(8,128)(2,1)S(1)} %slice.7), channel_id=1, source_target_pairs={{0,32},{1,33},{2,34},{3,35},{4,36},{5,37},{6,38},{7,39},{8,40},{9,... | collective-permute-start | bytes 319496 | tf_op jit(solution)/shard_map/ppermute | solution.py:59
  21.3 0.7 collective-permute-start.10
  22.0 1.3 %collective-permute-start.9 = (bf16[32,1664]{1,0:T(8,128)(2,1)S(1)}, bf16[32,1664]{1,0:T(8,128)(2,1)S(1)}, u32[]{:S(2)}, u32[]{:S(2)}) collective-permute-start(bf16[32,1664]{1,0:T(8,128)(2,1)S(1)} %slice.7), channel_id=1, source_target_pairs={{0,16},{1,17},{2,18},{3,19},{4,20},{5,21},{6,22},{7,23},{8,24},{9,... | collective-permute-start | bytes 319496 | tf_op jit(solution)/shard_map/ppermute | solution.py:59
  23.4 3.5 %collective-permute-start.8 = (bf16[128,2432]{1,0:T(8,128)(2,1)S(1)}, bf16[128,2432]{1,0:T(8,128)(2,1)S(1)}, u32[]{:S(2)}, u32[]{:S(2)}) collective-permute-start(bf16[128,2432]{1,0:T(8,128)(2,1)S(1)} %pad_maximum_fusion.x0.refs_0_), channel_id=1, source_target_pairs={{0,32},{1,33},{2,34},{3,35},{4,36},{5,37},{6,38},{7,39},{8,40},{9,... | collective-permute-start | bytes 1867784 | tf_op jit(solution)/shard_map/ppermute | solution.py:59
  26.9 0.7 collective-permute-start.7
  27.6 1.3 %collective-permute-start.6 = (bf16[128,2432]{1,0:T(8,128)(2,1)S(1)}, bf16[128,2432]{1,0:T(8,128)(2,1)S(1)}, u32[]{:S(2)}, u32[]{:S(2)}) collective-permute-start(bf16[128,2432]{1,0:T(8,128)(2,1)S(1)} %pad_maximum_fusion.x0.refs_0_), channel_id=1, source_target_pairs={{0,16},{1,17},{2,18},{3,19},{4,20},{5,21},{6,22},{7,23},{8,24},{9,... | collective-permute-start | bytes 1867784 | tf_op jit(solution)/shard_map/ppermute | solution.py:59
  29.0 0.9 collective-permute-start.14
  29.9 1.5 %collective-permute-start.13 = (bf16[128,1664]{1,0:T(8,128)(2,1)S(1)}, bf16[128,1664]{1,0:T(8,128)(2,1)S(1)}, u32[]{:S(2)}, u32[]{:S(2)}) collective-permute-start(bf16[128,1664]{1,0:T(8,128)(2,1)S(1)} %constant_dynamic-update-slice_fusion.refs_4_), channel_id=1, source_target_pairs={{0,9},{1,8},{2,11},{3,10},{4,13},{5,12},{6,15},{7,14},{8,0},{9,1},... | collective-permute-start | bytes 1277960 | tf_op jit(solution)/shard_map/ppermute | solution.py:59
  31.4 3.9 %collective-permute-done.8.x3.refs_3_ = bf16[128,2432]{1,0:T(8,128)(2,1)S(1)} collective-permute-done((bf16[128,2432]{1,0:T(8,128)(2,1)S(1)}, bf16[128,2432]{1,0:T(8,128)(2,1)S(1)}, u32[]{:S(2)}, u32[]{:S(2)}) %collective-permute-start.8) | collective-permute-done | bytes 622624 | tf_op jit(solution)/shard_map/ppermute | solution.py:59
  35.9 6.9 %collective-permute-done.7.x2.refs_2_ = bf16[128,2432]{1,0:T(8,128)(2,1)S(1)} collective-permute-done((bf16[128,2432]{1,0:T(8,128)(2,1)S(1)}, bf16[128,2432]{1,0:T(8,128)(2,1)S(1)}, u32[]{:S(2)}, u32[]{:S(2)}) %collective-permute-start.7) | collective-permute-done | bytes 622624 | tf_op jit(solution)/shard_map/ppermute | solution.py:59
  42.8 5.8 %shard_map.78 = (f32[256,2048]{1,0:T(8,128)S(1)}, f32[256,2048]{1,0:T(8,128)S(1)}) custom-call(s32[2,128]{1,0:T(2,128)S(1)} %get-tuple-element.50.places, bf16[128,2432]{1,0:T(8,128)(2,1)S(1)} %pad_maximum_fusion.x0.refs_0_, bf16[128,2432]{1,0:T(8,128)(2,1)S(1)} %collective-permute-done.6.x1.refs_1_, ...), custom_call_target="tpu_custom_call" | custom-call | flops 4831838208 | bytes 9437184 | tf_op jit(solution)/shard_map/pallas_call | solution.py:211
  49.0 4.1 %shard_map.79 = (f32[256,1536]{1,0:T(8,128)S(1)}, f32[256,1536]{1,0:T(8,128)S(1)}, bf16[512,1792]{1,0:T(8,128)(2,1)S(1)}) custom-call(bf16[512,512]{1,0:T(8,128)(2,1)S(1)} %get-tuple-element.53.main_order, bf16[512,512]{1,0:T(8,128)(2,1)S(1)} %get-tuple-element.54.apart_order, bf16[128,2432]{1,0:T(8,128)(2,1)S(1)} %pad_maximum_fusion.x0.refs_0_, ...), custom_call_target="tpu_custom_call" | custom-call | flops 2818572288 | bytes 7340032 | tf_op jit(solution)/shard_map/pallas_call | solution.py:226
  53.1 0.8 collective-permute-start.16
  53.9 1.1 shard_map.80
  55.1 1.4 %shard_map.81 = (f32[256,2048]{1,0:T(8,128)S(1)}, f32[256,2048]{1,0:T(8,128)S(1)}, f32[256,128]{1,0:T(8,128)S(1)}) custom-call(f32[256,2048]{1,0:T(8,128)S(1)} %get-tuple-element.66.own, f32[256,2048]{1,0:T(8,128)S(1)} %collective-permute-done.15.other), custom_call_target="tpu_custom_call" | custom-call | flops 4194304 | bytes 8388608 | tf_op jit(solution)/shard_map/pallas_call | solution.py:270
  56.9 1.8 %shard_map.82 = (f32[256,1536]{1,0:T(8,128)S(1)}, f32[256,1536]{1,0:T(8,128)S(1)}, f32[2,256,128]{2,1,0:T(8,128)S(1)}) custom-call(f32[256,2048]{1,0:T(8,128)S(1)} %get-tuple-element.68.refs_0_.refs_2_, f32[256,2048]{1,0:T(8,128)S(1)} %get-tuple-element.69.refs_1_.refs_3_, f32[256,1536]{1,0:T(8,128)S(1)} %get-tuple-element.70.refs_2_, ...), custom_call_target="tpu_custom_call" | custom-call | flops 6291456 | bytes 9437184 | tf_op jit(solution)/shard_map/pallas_call | solution.py:316
  58.8 0.8 shard_map.83
  59.6 2.3 %collective-permute-start.20 = (f32[8,128]{1,0:T(8,128)S(1)}, f32[8,128]{1,0:T(8,128)S(1)}, u32[]{:S(2)}, u32[]{:S(2)}) collective-permute-start(f32[8,128]{1,0:T(8,128)S(1)} %get-tuple-element.76), channel_id=1, source_target_pairs={{0,32},{1,33},{2,34},{3,35},{4,36},{5,37},{6,38},{7,39},{8,40},{9,... | collective-permute-start | bytes 12296 | tf_op jit(solution)/shard_map/ppermute | solution.py:59
  61.9 1.9 %collective-permute-start.19 = (f32[8,128]{1,0:T(8,128)S(1)}, f32[8,128]{1,0:T(8,128)S(1)}, u32[]{:S(2)}, u32[]{:S(2)}) collective-permute-start(f32[8,128]{1,0:T(8,128)S(1)} %get-tuple-element.76), channel_id=1, source_target_pairs={{0,48},{1,49},{2,50},{3,51},{4,52},{5,53},{6,54},{7,55},{8,56},{9,... | collective-permute-start | bytes 12296 | tf_op jit(solution)/shard_map/ppermute | solution.py:59
  64.0 0.8 collective-permute-done.20
  64.8 0.7 collective-permute-done.19
  65.5 3.2 %collective-permute-done.18 = f32[8,128]{1,0:T(8,128)S(1)} collective-permute-done((f32[8,128]{1,0:T(8,128)S(1)}, f32[8,128]{1,0:T(8,128)S(1)}, u32[]{:S(2)}, u32[]{:S(2)}) %collective-permute-start.18) | collective-permute-done | bytes 4128 | tf_op jit(solution)/shard_map/ppermute | solution.py:59
  68.7 2.8 %collective-permute-start.23 = (f32[8,128]{1,0:T(8,128)S(1)}, f32[8,128]{1,0:T(8,128)S(1)}, u32[]{:S(2)}, u32[]{:S(2)}) collective-permute-start(f32[8,128]{1,0:T(8,128)S(1)} %add_add_fusion.2), channel_id=1, source_target_pairs={{0,1},{1,0},{2,3},{3,2},{4,5},{5,4},{6,7},{7,6},{8,9},{9,8},{10,11... | collective-permute-start | bytes 12296 | tf_op jit(solution)/shard_map/ppermute | solution.py:59
  71.5 1.3 %collective-permute-start.22 = (f32[8,128]{1,0:T(8,128)S(1)}, f32[8,128]{1,0:T(8,128)S(1)}, u32[]{:S(2)}, u32[]{:S(2)}) collective-permute-start(f32[8,128]{1,0:T(8,128)S(1)} %add_add_fusion.2), channel_id=1, source_target_pairs={{0,9},{1,8},{2,11},{3,10},{4,13},{5,12},{6,15},{7,14},{8,0},{9,1},... | collective-permute-start | bytes 12296 | tf_op jit(solution)/shard_map/ppermute | solution.py:59
  72.8 0.8 collective-permute-start.21
  73.8 1.3 %collective-permute-done.22 = f32[8,128]{1,0:T(8,128)S(1)} collective-permute-done((f32[8,128]{1,0:T(8,128)S(1)}, f32[8,128]{1,0:T(8,128)S(1)}, u32[]{:S(2)}, u32[]{:S(2)}) %collective-permute-start.22) | collective-permute-done | bytes 4128 | tf_op jit(solution)/shard_map/ppermute | solution.py:59
  75.1 2.5 %collective-permute-done.21 = f32[8,128]{1,0:T(8,128)S(1)} collective-permute-done((f32[8,128]{1,0:T(8,128)S(1)}, f32[8,128]{1,0:T(8,128)S(1)}, u32[]{:S(2)}, u32[]{:S(2)}) %collective-permute-start.21) | collective-permute-done | bytes 4128 | tf_op jit(solution)/shard_map/ppermute | solution.py:59
  77.6 0.8 collective-permute-start.26
  78.5 2.3 %collective-permute-start.25 = (f32[8,128]{1,0:T(8,128)S(1)}, f32[8,128]{1,0:T(8,128)S(1)}, u32[]{:S(2)}, u32[]{:S(2)}) collective-permute-start(f32[8,128]{1,0:T(8,128)S(1)} %add_add_fusion.1), channel_id=1, source_target_pairs={{0,6},{1,7},{2,0},{3,1},{4,2},{5,3},{6,4},{7,5},{8,14},{9,15},{10,... | collective-permute-start | bytes 12296 | tf_op jit(solution)/shard_map/ppermute | solution.py:59
  80.8 1.9 %collective-permute-done.26 = f32[8,128]{1,0:T(8,128)S(1)} collective-permute-done((f32[8,128]{1,0:T(8,128)S(1)}, f32[8,128]{1,0:T(8,128)S(1)}, u32[]{:S(2)}, u32[]{:S(2)}) %collective-permute-start.26) | collective-permute-done | bytes 4128 | tf_op jit(solution)/shard_map/ppermute | solution.py:59
  82.7 2.9 %collective-permute-done.24 = f32[8,128]{1,0:T(8,128)S(1)} collective-permute-done((f32[8,128]{1,0:T(8,128)S(1)}, f32[8,128]{1,0:T(8,128)S(1)}, u32[]{:S(2)}, u32[]{:S(2)}) %collective-permute-start.24) | collective-permute-done | bytes 4128 | tf_op jit(solution)/shard_map/ppermute | solution.py:59
  86.7 2.1 %shard_map.85.own = f32[256,1792]{1,0:T(8,128)S(1)} custom-call(bf16[256,2048]{1,0:T(8,128)(2,1)S(1)} %get-tuple-element.82.gap.own, bf16[1792,2048]{1,0:T(8,128)(2,1)S(1)} %bitcast.5), custom_call_target="tpu_custom_call" | custom-call | flops 1879048192 | bytes 7340032 | tf_op jit(solution)/shard_map/pallas_call | solution.py:374
  88.8 3.2 %shard_map.86 = (f32[128,1792]{1,0:T(8,128)S(1)}, bf16[128,1792]{1,0:T(8,128)(2,1)S(1)}, bf16[128,1792]{1,0:T(8,128)(2,1)S(1)}, bf16[128,1792]{1,0:T(8,128)(2,1)S(1)}) custom-call(s32[2,128]{1,0:T(2,128)S(1)} %get-tuple-element.50.places, f32[256,1792]{1,0:T(8,128)S(1)} %shard_map.85.own, bf16[256,2048]{1,0:T(8,128)(2,1)S(1)} %collective-permute-done.27.gap.other, ...), custom_call_target="tpu_custom_call" | custom-call | flops 1879048192 | bytes 7340032 | tf_op jit(solution)/shard_map/pallas_call | solution.py:397
  92.1 1.9 %collective-permute-start.30 = (bf16[128,1792]{1,0:T(8,128)(2,1)S(1)}, bf16[128,1792]{1,0:T(8,128)(2,1)S(1)}, u32[]{:S(2)}, u32[]{:S(2)}) collective-permute-start(bf16[128,1792]{1,0:T(8,128)(2,1)S(1)} %get-tuple-element.90), channel_id=1, source_target_pairs={{0,16},{1,17},{2,18},{3,19},{4,20},{5,21},{6,22},{7,23},{8,24},{9,... | collective-permute-start | bytes 1376264 | tf_op jit(solution)/shard_map/ppermute | solution.py:59
  94.1 6.9 %shard_map.87 = bf16[1792,2048]{1,0:T(8,128)(2,1)} custom-call(bf16[512,1792]{1,0:T(8,128)(2,1)S(1)} %get-tuple-element.64.rows, bf16[256,2048]{1,0:T(8,128)(2,1)S(1)} %get-tuple-element.82.gap.own, bf16[256,2048]{1,0:T(8,128)(2,1)S(1)} %collective-permute-done.27.gap.other), custom_call_target="tpu_custom_call" | custom-call | flops 3758096384 | bytes 7340032 | tf_op jit(solution)/shard_map/pallas_call | solution.py:453
  101.0 5.8 %collective-permute-done.30.refs_1_ = bf16[128,1792]{1,0:T(8,128)(2,1)S(1)} collective-permute-done((bf16[128,1792]{1,0:T(8,128)(2,1)S(1)}, bf16[128,1792]{1,0:T(8,128)(2,1)S(1)}, u32[]{:S(2)}, u32[]{:S(2)}) %collective-permute-start.30) | collective-permute-done | bytes 458784 | tf_op jit(solution)/shard_map/ppermute | solution.py:59
  106.8 1.0 shard_map.88
  107.7 3.6 %all-to-all-start = ((bf16[16,8,1792]{2,1,0:T(8,128)(2,1)}), bf16[16,8,1792]{2,1,0:T(8,128)(2,1)S(1)}, u32[]{:S(2)}, u32[]{:S(2)}) async-start(bf16[16,8,1792]{2,1,0:T(8,128)(2,1)} %bitcast.2), calls=%async_computation | async-start | bytes 917504 | tf_op jit(solution)/shard_map/all_to_all | solution.py:514
  111.9 8.7 %all-to-all-done.received = bf16[16,8,1792]{2,1,0:T(8,128)(2,1)S(1)} async-done(((bf16[16,8,1792]{2,1,0:T(8,128)(2,1)}), bf16[16,8,1792]{2,1,0:T(8,128)(2,1)S(1)}, u32[]{:S(2)}, u32[]{:S(2)}) %all-to-all-start) | async-done | bytes 458784 | tf_op jit(solution)/shard_map/all_to_all | solution.py:514
  (60 shorter events, 5.4 us)
Async XLA Ops:
  0.6 0.8 copy-start.2
  1.4 0.7 copy-start.3
  2.2 9.4 %collective-permute-start.2 = (bf16[8,4096]{1,0:T(8,128)(2,1)S(1)}, bf16[8,4096]{1,0:T(8,128)(2,1)S(1)}, u32[]{:S(2)}, u32[]{:S(2)}) collective-permute-start(bf16[8,4096]{1,0:T(8,128)(2,1)S(1)} %shard_map.77), channel_id=1, source_target_pairs={{0,4},{1,5},{2,6},{3,7},{4,0},{5,1},{6,2},{7,3},{8,12},{9,13},{10,... | collective-permute-start | bytes 196616 | tf_op jit(solution)/shard_map/ppermute | solution.py:59
  5.6 6.0 %collective-permute-start.1 = (bf16[8,4096]{1,0:T(8,128)(2,1)S(1)}, bf16[8,4096]{1,0:T(8,128)(2,1)S(1)}, u32[]{:S(2)}, u32[]{:S(2)}) collective-permute-start(bf16[8,4096]{1,0:T(8,128)(2,1)S(1)} %shard_map.77), channel_id=1, source_target_pairs={{0,6},{1,7},{2,0},{3,1},{4,2},{5,3},{6,4},{7,5},{8,14},{9,15},{10,... | collective-permute-start | bytes 196616 | tf_op jit(solution)/shard_map/ppermute | solution.py:59
  6.6 5.5 %collective-permute-start = (bf16[8,4096]{1,0:T(8,128)(2,1)S(1)}, bf16[8,4096]{1,0:T(8,128)(2,1)S(1)}, u32[]{:S(2)}, u32[]{:S(2)}) collective-permute-start(bf16[8,4096]{1,0:T(8,128)(2,1)S(1)} %shard_map.77), channel_id=1, source_target_pairs={{0,2},{1,3},{2,4},{3,5},{4,6},{5,7},{6,0},{7,1},{8,10},{9,11},{10,... | collective-permute-start | bytes 196616 | tf_op jit(solution)/shard_map/ppermute | solution.py:59
  7.6 3.7 %copy-start = (bf16[2304,2048]{1,0:T(8,128)(2,1)S(1)}, bf16[2304,2048]{1,0:T(8,128)(2,1)}, u32[]{:S(2)}) copy-start(bf16[2304,2048]{1,0:T(8,128)(2,1)} %weight.4) | copy-start | bytes 28311556
  11.3 31.5 %copy-start.1 = (bf16[2304,2048]{1,0:T(8,128)(2,1)S(1)}, bf16[2304,2048]{1,0:T(8,128)(2,1)}, u32[]{:S(2)}) copy-start(bf16[2304,2048]{1,0:T(8,128)(2,1)} %weight.4) | copy-start | bytes 28311556
  12.2 9.8 %collective-permute-start.5 = (bf16[32,2432]{1,0:T(8,128)(2,1)S(1)}, bf16[32,2432]{1,0:T(8,128)(2,1)S(1)}, u32[]{:S(2)}, u32[]{:S(2)}) collective-permute-start(bf16[32,2432]{1,0:T(8,128)(2,1)S(1)} %slice.6), channel_id=1, source_target_pairs={{0,1},{1,0},{2,3},{3,2},{4,5},{5,4},{6,7},{7,6},{8,9},{9,8},{10,11... | collective-permute-start | bytes 466952 | tf_op jit(solution)/shard_map/ppermute | solution.py:59
  15.3 8.0 %collective-permute-start.4 = (bf16[32,2432]{1,0:T(8,128)(2,1)S(1)}, bf16[32,2432]{1,0:T(8,128)(2,1)S(1)}, u32[]{:S(2)}, u32[]{:S(2)}) collective-permute-start(bf16[32,2432]{1,0:T(8,128)(2,1)S(1)} %slice.6), channel_id=1, source_target_pairs={{0,9},{1,8},{2,11},{3,10},{4,13},{5,12},{6,15},{7,14},{8,0},{9,1},... | collective-permute-start | bytes 466952 | tf_op jit(solution)/shard_map/ppermute | solution.py:59
  16.4 6.9 %collective-permute-start.3 = (bf16[32,2432]{1,0:T(8,128)(2,1)S(1)}, bf16[32,2432]{1,0:T(8,128)(2,1)S(1)}, u32[]{:S(2)}, u32[]{:S(2)}) collective-permute-start(bf16[32,2432]{1,0:T(8,128)(2,1)S(1)} %slice.6), channel_id=1, source_target_pairs={{0,8},{1,9},{2,10},{3,11},{4,12},{5,13},{6,14},{7,15},{8,1},{9,0},... | collective-permute-start | bytes 466952 | tf_op jit(solution)/shard_map/ppermute | solution.py:59
  17.3 10.3 %collective-permute-start.11 = (bf16[32,1664]{1,0:T(8,128)(2,1)S(1)}, bf16[32,1664]{1,0:T(8,128)(2,1)S(1)}, u32[]{:S(2)}, u32[]{:S(2)}) collective-permute-start(bf16[32,1664]{1,0:T(8,128)(2,1)S(1)} %slice.7), channel_id=1, source_target_pairs={{0,32},{1,33},{2,34},{3,35},{4,36},{5,37},{6,38},{7,39},{8,40},{9,... | collective-permute-start | bytes 319496 | tf_op jit(solution)/shard_map/ppermute | solution.py:59
  21.3 7.6 %collective-permute-start.10 = (bf16[32,1664]{1,0:T(8,128)(2,1)S(1)}, bf16[32,1664]{1,0:T(8,128)(2,1)S(1)}, u32[]{:S(2)}, u32[]{:S(2)}) collective-permute-start(bf16[32,1664]{1,0:T(8,128)(2,1)S(1)} %slice.7), channel_id=1, source_target_pairs={{0,48},{1,49},{2,50},{3,51},{4,52},{5,53},{6,54},{7,55},{8,56},{9,... | collective-permute-start | bytes 319496 | tf_op jit(solution)/shard_map/ppermute | solution.py:59
  22.0 6.9 %collective-permute-start.9 = (bf16[32,1664]{1,0:T(8,128)(2,1)S(1)}, bf16[32,1664]{1,0:T(8,128)(2,1)S(1)}, u32[]{:S(2)}, u32[]{:S(2)}) collective-permute-start(bf16[32,1664]{1,0:T(8,128)(2,1)S(1)} %slice.7), channel_id=1, source_target_pairs={{0,16},{1,17},{2,18},{3,19},{4,20},{5,21},{6,22},{7,23},{8,24},{9,... | collective-permute-start | bytes 319496 | tf_op jit(solution)/shard_map/ppermute | solution.py:59
  23.4 11.9 %collective-permute-start.8 = (bf16[128,2432]{1,0:T(8,128)(2,1)S(1)}, bf16[128,2432]{1,0:T(8,128)(2,1)S(1)}, u32[]{:S(2)}, u32[]{:S(2)}) collective-permute-start(bf16[128,2432]{1,0:T(8,128)(2,1)S(1)} %pad_maximum_fusion.x0.refs_0_), channel_id=1, source_target_pairs={{0,32},{1,33},{2,34},{3,35},{4,36},{5,37},{6,38},{7,39},{8,40},{9,... | collective-permute-start | bytes 1867784 | tf_op jit(solution)/shard_map/ppermute | solution.py:59
  26.9 15.9 %collective-permute-start.7 = (bf16[128,2432]{1,0:T(8,128)(2,1)S(1)}, bf16[128,2432]{1,0:T(8,128)(2,1)S(1)}, u32[]{:S(2)}, u32[]{:S(2)}) collective-permute-start(bf16[128,2432]{1,0:T(8,128)(2,1)S(1)} %pad_maximum_fusion.x0.refs_0_), channel_id=1, source_target_pairs={{0,48},{1,49},{2,50},{3,51},{4,52},{5,53},{6,54},{7,55},{8,56},{9,... | collective-permute-start | bytes 1867784 | tf_op jit(solution)/shard_map/ppermute | solution.py:59
  27.6 15.2 %collective-permute-start.6 = (bf16[128,2432]{1,0:T(8,128)(2,1)S(1)}, bf16[128,2432]{1,0:T(8,128)(2,1)S(1)}, u32[]{:S(2)}, u32[]{:S(2)}) collective-permute-start(bf16[128,2432]{1,0:T(8,128)(2,1)S(1)} %pad_maximum_fusion.x0.refs_0_), channel_id=1, source_target_pairs={{0,16},{1,17},{2,18},{3,19},{4,20},{5,21},{6,22},{7,23},{8,24},{9,... | collective-permute-start | bytes 1867784 | tf_op jit(solution)/shard_map/ppermute | solution.py:59
  28.9 20.1 %slice-start = ((s8[7340032]{0:T(1024)(128)(4,1)}), s8[4194304]{0:T(1024)(128)(4,1)S(1)}, s32[]{:S(2)}) async-start(s8[7340032]{0:T(1024)(128)(4,1)} %bitcast.4), calls=%async_computation.1 | async-start | bytes 8388608
  29.0 20.0 %slice-start.1 = ((s8[7340032]{0:T(1024)(128)(4,1)}), s8[3145728]{0:T(1024)(128)(4,1)S(1)}, s32[]{:S(2)}) async-start(s8[7340032]{0:T(1024)(128)(4,1)} %bitcast.4), calls=%async_computation.2 | async-start | bytes 6291456
  29.0 19.6 %collective-permute-start.14 = (bf16[128,1664]{1,0:T(8,128)(2,1)S(1)}, bf16[128,1664]{1,0:T(8,128)(2,1)S(1)}, u32[]{:S(2)}, u32[]{:S(2)}) collective-permute-start(bf16[128,1664]{1,0:T(8,128)(2,1)S(1)} %constant_dynamic-update-slice_fusion.refs_4_), channel_id=1, source_target_pairs={{0,1},{1,0},{2,3},{3,2},{4,5},{5,4},{6,7},{7,6},{8,9},{9,8},{10,11... | collective-permute-start | bytes 1277960 | tf_op jit(solution)/shard_map/ppermute | solution.py:59
  29.9 18.8 %collective-permute-start.13 = (bf16[128,1664]{1,0:T(8,128)(2,1)S(1)}, bf16[128,1664]{1,0:T(8,128)(2,1)S(1)}, u32[]{:S(2)}, u32[]{:S(2)}) collective-permute-start(bf16[128,1664]{1,0:T(8,128)(2,1)S(1)} %constant_dynamic-update-slice_fusion.refs_4_), channel_id=1, source_target_pairs={{0,9},{1,8},{2,11},{3,10},{4,13},{5,12},{6,15},{7,14},{8,0},{9,1},... | collective-permute-start | bytes 1277960 | tf_op jit(solution)/shard_map/ppermute | solution.py:59
  35.3 13.7 %collective-permute-start.12 = (bf16[128,1664]{1,0:T(8,128)(2,1)S(1)}, bf16[128,1664]{1,0:T(8,128)(2,1)S(1)}, u32[]{:S(2)}, u32[]{:S(2)}) collective-permute-start(bf16[128,1664]{1,0:T(8,128)(2,1)S(1)} %constant_dynamic-update-slice_fusion.refs_4_), channel_id=1, source_target_pairs={{0,8},{1,9},{2,10},{3,11},{4,12},{5,13},{6,14},{7,15},{8,1},{9,0},... | collective-permute-start | bytes 1277960 | tf_op jit(solution)/shard_map/ppermute | solution.py:59
  49.0 6.1 %collective-permute-start.15 = (f32[256,2048]{1,0:T(8,128)S(1)}, f32[256,2048]{1,0:T(8,128)S(1)}, u32[]{:S(2)}, u32[]{:S(2)}) collective-permute-start(f32[256,2048]{1,0:T(8,128)S(1)} %get-tuple-element.67), channel_id=1, source_target_pairs={{0,64},{64,0},{1,65},{65,1},{2,66},{66,2},{3,67},{67,3},{4,68},{68... | collective-permute-start | bytes 6291464 | tf_op jit(solution)/shard_map/ppermute | solution.py:63
  53.1 3.8 %collective-permute-start.16 = (f32[256,1536]{1,0:T(8,128)S(1)}, f32[256,1536]{1,0:T(8,128)S(1)}, u32[]{:S(2)}, u32[]{:S(2)}) collective-permute-start(f32[256,1536]{1,0:T(8,128)S(1)} %get-tuple-element.71), channel_id=1, source_target_pairs={{0,64},{64,0},{1,65},{65,1},{2,66},{66,2},{3,67},{67,3},{4,68},{68... | collective-permute-start | bytes 4718600 | tf_op jit(solution)/shard_map/ppermute | solution.py:63
  55.0 3.8 %collective-permute-start.17 = (f32[256,512]{1,0:T(8,128)S(1)}, f32[256,512]{1,0:T(8,128)S(1)}, u32[]{:S(2)}, u32[]{:S(2)}) collective-permute-start(f32[256,512]{1,0:T(8,128)S(1)} %get-tuple-element.75), channel_id=1, source_target_pairs={{0,64},{64,0},{1,65},{65,1},{2,66},{66,2},{3,67},{67,3},{4,68},{68... | collective-permute-start | bytes 1572872 | tf_op jit(solution)/shard_map/ppermute | solution.py:63
  58.8 26.9 %copy-start.4 = (f32[512]{0:T(512)S(1)}, f32[512]{0:T(512)}, u32[]{:S(2)}) copy-start(f32[512]{0:T(512)} %param.9) | copy-start | bytes 6148
  59.6 5.2 %collective-permute-start.20 = (f32[8,128]{1,0:T(8,128)S(1)}, f32[8,128]{1,0:T(8,128)S(1)}, u32[]{:S(2)}, u32[]{:S(2)}) collective-permute-start(f32[8,128]{1,0:T(8,128)S(1)} %get-tuple-element.76), channel_id=1, source_target_pairs={{0,32},{1,33},{2,34},{3,35},{4,36},{5,37},{6,38},{7,39},{8,40},{9,... | collective-permute-start | bytes 12296 | tf_op jit(solution)/shard_map/ppermute | solution.py:59
  61.9 3.6 %collective-permute-start.19 = (f32[8,128]{1,0:T(8,128)S(1)}, f32[8,128]{1,0:T(8,128)S(1)}, u32[]{:S(2)}, u32[]{:S(2)}) collective-permute-start(f32[8,128]{1,0:T(8,128)S(1)} %get-tuple-element.76), channel_id=1, source_target_pairs={{0,48},{1,49},{2,50},{3,51},{4,52},{5,53},{6,54},{7,55},{8,56},{9,... | collective-permute-start | bytes 12296 | tf_op jit(solution)/shard_map/ppermute | solution.py:59
  63.9 4.8 %collective-permute-start.18 = (f32[8,128]{1,0:T(8,128)S(1)}, f32[8,128]{1,0:T(8,128)S(1)}, u32[]{:S(2)}, u32[]{:S(2)}) collective-permute-start(f32[8,128]{1,0:T(8,128)S(1)} %get-tuple-element.76), channel_id=1, source_target_pairs={{0,16},{1,17},{2,18},{3,19},{4,20},{5,21},{6,22},{7,23},{8,24},{9,... | collective-permute-start | bytes 12296 | tf_op jit(solution)/shard_map/ppermute | solution.py:59
  68.7 5.1 %collective-permute-start.23 = (f32[8,128]{1,0:T(8,128)S(1)}, f32[8,128]{1,0:T(8,128)S(1)}, u32[]{:S(2)}, u32[]{:S(2)}) collective-permute-start(f32[8,128]{1,0:T(8,128)S(1)} %add_add_fusion.2), channel_id=1, source_target_pairs={{0,1},{1,0},{2,3},{3,2},{4,5},{5,4},{6,7},{7,6},{8,9},{9,8},{10,11... | collective-permute-start | bytes 12296 | tf_op jit(solution)/shard_map/ppermute | solution.py:59
  71.5 3.6 %collective-permute-start.22 = (f32[8,128]{1,0:T(8,128)S(1)}, f32[8,128]{1,0:T(8,128)S(1)}, u32[]{:S(2)}, u32[]{:S(2)}) collective-permute-start(f32[8,128]{1,0:T(8,128)S(1)} %add_add_fusion.2), channel_id=1, source_target_pairs={{0,9},{1,8},{2,11},{3,10},{4,13},{5,12},{6,15},{7,14},{8,0},{9,1},... | collective-permute-start | bytes 12296 | tf_op jit(solution)/shard_map/ppermute | solution.py:59
  72.8 4.8 %collective-permute-start.21 = (f32[8,128]{1,0:T(8,128)S(1)}, f32[8,128]{1,0:T(8,128)S(1)}, u32[]{:S(2)}, u32[]{:S(2)}) collective-permute-start(f32[8,128]{1,0:T(8,128)S(1)} %add_add_fusion.2), channel_id=1, source_target_pairs={{0,8},{1,9},{2,10},{3,11},{4,12},{5,13},{6,14},{7,15},{8,1},{9,0},... | collective-permute-start | bytes 12296 | tf_op jit(solution)/shard_map/ppermute | solution.py:59
  77.6 5.1 %collective-permute-start.26 = (f32[8,128]{1,0:T(8,128)S(1)}, f32[8,128]{1,0:T(8,128)S(1)}, u32[]{:S(2)}, u32[]{:S(2)}) collective-permute-start(f32[8,128]{1,0:T(8,128)S(1)} %add_add_fusion.1), channel_id=1, source_target_pairs={{0,4},{1,5},{2,6},{3,7},{4,0},{5,1},{6,2},{7,3},{8,12},{9,13},{10,... | collective-permute-start | bytes 12296 | tf_op jit(solution)/shard_map/ppermute | solution.py:59
  78.5 4.3 %collective-permute-start.25 = (f32[8,128]{1,0:T(8,128)S(1)}, f32[8,128]{1,0:T(8,128)S(1)}, u32[]{:S(2)}, u32[]{:S(2)}) collective-permute-start(f32[8,128]{1,0:T(8,128)S(1)} %add_add_fusion.1), channel_id=1, source_target_pairs={{0,6},{1,7},{2,0},{3,1},{4,2},{5,3},{6,4},{7,5},{8,14},{9,15},{10,... | collective-permute-start | bytes 12296 | tf_op jit(solution)/shard_map/ppermute | solution.py:59
  80.8 4.8 %collective-permute-start.24 = (f32[8,128]{1,0:T(8,128)S(1)}, f32[8,128]{1,0:T(8,128)S(1)}, u32[]{:S(2)}, u32[]{:S(2)}) collective-permute-start(f32[8,128]{1,0:T(8,128)S(1)} %add_add_fusion.1), channel_id=1, source_target_pairs={{0,2},{1,3},{2,4},{3,5},{4,6},{5,7},{6,0},{7,1},{8,10},{9,11},{10,... | collective-permute-start | bytes 12296 | tf_op jit(solution)/shard_map/ppermute | solution.py:59
  86.1 2.7 %collective-permute-start.27 = (bf16[256,2048]{1,0:T(8,128)(2,1)S(1)}, bf16[256,2048]{1,0:T(8,128)(2,1)S(1)}, u32[]{:S(2)}, u32[]{:S(2)}) collective-permute-start(bf16[256,2048]{1,0:T(8,128)(2,1)S(1)} %get-tuple-element.82.gap.own), channel_id=1, source_target_pairs={{0,64},{64,0},{1,65},{65,1},{2,66},{66,2},{3,67},{67,3},{4,68},{68... | collective-permute-start | bytes 3145736 | tf_op jit(solution)/shard_map/ppermute | solution.py:63
  86.2 2.6 %collective-permute-start.28 = (f32[2,128]{1,0:T(2,128)S(1)}, f32[2,128]{1,0:T(2,128)S(1)}, u32[]{:S(2)}, u32[]{:S(2)}) collective-permute-start(f32[2,128]{1,0:T(2,128)S(1)} %get-tuple-element.81), channel_id=1, source_target_pairs={{0,64},{64,0},{1,65},{65,1},{2,66},{66,2},{3,67},{67,3},{4,68},{68... | collective-permute-start | bytes 3080 | tf_op jit(solution)/shard_map/ppermute | solution.py:63
  92.0 9.0 %collective-permute-start.29 = (bf16[128,1792]{1,0:T(8,128)(2,1)S(1)}, bf16[128,1792]{1,0:T(8,128)(2,1)S(1)}, u32[]{:S(2)}, u32[]{:S(2)}) collective-permute-start(bf16[128,1792]{1,0:T(8,128)(2,1)S(1)} %get-tuple-element.89), channel_id=1, source_target_pairs={{0,48},{1,49},{2,50},{3,51},{4,52},{5,53},{6,54},{7,55},{8,56},{9,... | collective-permute-start | bytes 1376264 | tf_op jit(solution)/shard_map/ppermute | solution.py:59
  92.1 14.6 %collective-permute-start.30 = (bf16[128,1792]{1,0:T(8,128)(2,1)S(1)}, bf16[128,1792]{1,0:T(8,128)(2,1)S(1)}, u32[]{:S(2)}, u32[]{:S(2)}) collective-permute-start(bf16[128,1792]{1,0:T(8,128)(2,1)S(1)} %get-tuple-element.90), channel_id=1, source_target_pairs={{0,16},{1,17},{2,18},{3,19},{4,20},{5,21},{6,22},{7,23},{8,24},{9,... | collective-permute-start | bytes 1376264 | tf_op jit(solution)/shard_map/ppermute | solution.py:59
  94.1 12.7 %collective-permute-start.31 = (bf16[128,1792]{1,0:T(8,128)(2,1)S(1)}, bf16[128,1792]{1,0:T(8,128)(2,1)S(1)}, u32[]{:S(2)}, u32[]{:S(2)}) collective-permute-start(bf16[128,1792]{1,0:T(8,128)(2,1)S(1)} %get-tuple-element.91), channel_id=1, source_target_pairs={{0,32},{1,33},{2,34},{3,35},{4,36},{5,37},{6,38},{7,39},{8,40},{9,... | collective-permute-start | bytes 1376264 | tf_op jit(solution)/shard_map/ppermute | solution.py:59
  107.7 12.9 %all-to-all-start = ((bf16[16,8,1792]{2,1,0:T(8,128)(2,1)}), bf16[16,8,1792]{2,1,0:T(8,128)(2,1)S(1)}, u32[]{:S(2)}, u32[]{:S(2)}) async-start(bf16[16,8,1792]{2,1,0:T(8,128)(2,1)} %bitcast.2), calls=%async_computation | async-start | bytes 917504 | tf_op jit(solution)/shard_map/all_to_all | solution.py:514

commit v6 on v5

--- a/solution.py
+++ b/solution.py
@@ -12,7 +12,7 @@
 tokens, teacher_width, student_width, vocab_local = 512, 2304, 1792, 2048
 width = teacher_width + student_width
 half = tokens // 2
-apart = 1664
+apart = 1536
 everyone = ("mp", "batch", "vocab")
 mega = 1024 * 1024
 
@@ -116,15 +116,26 @@
     return pl.ds(pl.multiple_of(places[which, block], 8), 8)
 
 
-def teacher_kernel(places, x0, x1, x2, x3, weight, own, other, rows, raw):
-    for i, x in enumerate((x0, x1, x2, x3)):
+def teacher_early_kernel(x0, weight, out):
+    step = 512
+    for at in range(0, vocab_local, step):
+        cols = slice(at, at + step)
+        out[:, cols] = jnp.dot(
+            x0[:, :teacher_width], weight[:, cols], preferred_element_type=jnp.float32
+        )
+
+
+def teacher_kernel(places, early, x1, x2, x3, weight, own, other, rows, raw):
+    for i, x in enumerate((x1, x2, x3)):
         rows[128 * i : 128 * (i + 1)] = x[:, :teacher_width]
     step = raw.shape[2]
     for i, at in enumerate(range(0, vocab_local, step)):
         cols, held = slice(at, at + step), raw.at[i % 2]
+        for block in range(16):
+            held[placed(places, 0, block)] = early[8 * block : 8 * (block + 1), cols]
         term = jnp.dot(rows[...], weight[:, cols], preferred_element_type=jnp.float32)
-        for block in range(64):
-            held[placed(places, 0, block)] = term[8 * block : 8 * (block + 1)]
+        for block in range(48):
+            held[placed(places, 0, 16 + block)] = term[8 * block : 8 * (block + 1)]
         own[:, cols], other[:, cols] = held[:half], held[half:]
 
 
@@ -207,19 +218,30 @@
     return pl.BlockSpec(memory_space=pltpu.SMEM)
 
 
-def teacher_logits(places, blocks, weight):
+def teacher_early(x0, weight):
+    return pl.pallas_call(
+        teacher_early_kernel,
+        in_specs=[whole()] * 2,
+        out_specs=whole(),
+        out_shape=jax.ShapeDtypeStruct((128, vocab_local), jnp.float32),
+        compiler_params=pltpu.CompilerParams(vmem_limit_bytes=16 * mega),
+        cost_estimate=cost(128 * weight.size, 2 * weight.size),
+    )(x0, weight)
+
+
+def teacher_logits(places, early, blocks, weight):
     return pl.pallas_call(
         teacher_kernel,
         in_specs=[scalars()] + [whole()] * 5,
         out_specs=[whole()] * 2,
         out_shape=raw_shapes(vocab_local),
         scratch_shapes=[
-            pltpu.VMEM((tokens, teacher_width), jnp.bfloat16),
+            pltpu.VMEM((384, teacher_width), jnp.bfloat16),
             pltpu.VMEM((2, tokens, 512), jnp.float32),
         ],
         compiler_params=pltpu.CompilerParams(vmem_limit_bytes=26 * mega),
-        cost_estimate=cost(tokens * weight.size, 2 * weight.size),
-    )(places, *blocks, weight)
+        cost_estimate=cost(384 * weight.size, 2 * weight.size),
+    )(places, early, *blocks, weight)
 
 
 def student_logits(main_order, apart_order, main, separate, weight, cols):
@@ -479,7 +501,8 @@
     separate = joined(separate)
     main = shared_along(main, main_axes[2])
     separate = shared_along(separate, apart_axes[2])
-    teacher_own, teacher_other = teacher_logits(places, main, teacher_weight)
+    early = teacher_early(main[0], teacher_weight)
+    teacher_own, teacher_other = teacher_logits(places, early, main[1:], teacher_weight)
     teacher_other, *separate = lax.optimization_barrier((teacher_other, *separate))
     teacher_other = swap(teacher_other)
     cols = 1536

time: 122 us -> 121 us (level)
  waiting for transfers between devices: 40.2 us -> 37.7 us
    ppermute x27, waiting for transfers between devices: 31 us -> 28.5 us  [send(): return lax.ppermute(block, everyone, ring(axes, by))]
    pallas_call x0 -> x1, Pallas kernels: none -> 1.51 us  [teacher_early(): pl.pallas_call(teacher_early_kernel, in_specs=[whole()] * 2, out_specs=wh...]
  transfers between devices with their start and end apart: 33 -> 33, of which waited for: 17 -> 16; matrix products, arithmetic and copies ran while one was open for 1% -> 1% of each run, Pallas kernels for 19% -> 20%
where the time goes in v6:
time: 121 us; the launch traced here: 120 us
  starting transfers between devices  45.4 us (38%)
  waiting for transfers between devices  37.7 us (31%)
  Pallas kernels  29.9 us (25%)
  local copies, waits for them, and re-layouts  5.26 us (4%)
    ppermute x27, starting transfers between devices, send(): return lax.ppermute(block, everyone, ring(axes, by))  40.4 us
    ppermute x27, waiting for transfers between devices, send(): return lax.ppermute(block, everyone, ring(axes, by))  28.5 us
    all_to_all x1, waiting for transfers between devices, local(): total = lax.all_to_all(total, everyone, 0, 0, axis_index_groups=planes())  8.73 us
    pallas_call x1, Pallas kernels, grad_weight_of(): pl.pallas_call(grad_weight_kernel, grid=(student_width // tile,), in_spec...  6.91 us
    unnamed x17, local copies, waits for them, and re-layouts  5.23 us
    pallas_call x1, Pallas kernels, teacher_logits(): pl.pallas_call(teacher_kernel, in_specs=[scalars()] + [whole()] * 5, out_...  4.67 us
    pallas_call x1, Pallas kernels, student_logits(): pl.pallas_call(student_kernel, in_specs=[whole()] * 11, out_specs=[whole(...  3.97 us
    all_to_all x1, starting transfers between devices, local(): total = lax.all_to_all(total, everyone, 0, 0, axis_index_groups=planes())  3.56 us
  transfers between devices with their start and end apart: 33, of which 16 were waited for; matrix products, arithmetic and copies ran while one was open for 1% of the time, Pallas kernels for 20%

profile of v6, /device:TPU:0, one launch (start us, length us, event | category | flops | bytes accessed | tf_op | source)
XLA Modules:
  0.0 119.9 jit_solution(7304155513133449447)
XLA Ops:
  0.6 0.8 copy-done.2
  1.4 0.7 copy-done.3
  2.2 3.4 %collective-permute-start.2 = (bf16[8,4096]{1,0:T(8,128)(2,1)S(1)}, bf16[8,4096]{1,0:T(8,128)(2,1)S(1)}, u32[]{:S(2)}, u32[]{:S(2)}) collective-permute-start(bf16[8,4096]{1,0:T(8,128)(2,1)S(1)} %shard_map.77), channel_id=1, source_target_pairs={{0,4},{1,5},{2,6},{3,7},{4,0},{5,1},{6,2},{7,3},{8,12},{9,13},{10,... | collective-permute-start | bytes 196616 | tf_op jit(solution)/shard_map/ppermute | solution.py:59
  5.6 1.1 collective-permute-start.1
  6.6 1.0 collective-permute-start
  7.6 3.7 %copy-done = bf16[2304,2048]{1,0:T(8,128)(2,1)S(1)} copy-done((bf16[2304,2048]{1,0:T(8,128)(2,1)S(1)}, bf16[2304,2048]{1,0:T(8,128)(2,1)}, u32[]{:S(2)}) %copy-start) | copy-done | bytes 9437208
  12.2 3.1 %collective-permute-start.5 = (bf16[32,2560]{1,0:T(8,128)(2,1)S(1)}, bf16[32,2560]{1,0:T(8,128)(2,1)S(1)}, u32[]{:S(2)}, u32[]{:S(2)}) collective-permute-start(bf16[32,2560]{1,0:T(8,128)(2,1)S(1)} %slice.6), channel_id=1, source_target_pairs={{0,1},{1,0},{2,3},{3,2},{4,5},{5,4},{6,7},{7,6},{8,9},{9,8},{10,11... | collective-permute-start | bytes 491528 | tf_op jit(solution)/shard_map/ppermute | solution.py:59
  15.3 1.1 collective-permute-start.4
  16.4 0.9 collective-permute-start.3
  17.3 4.0 %collective-permute-start.11 = (bf16[32,1536]{1,0:T(8,128)(2,1)S(1)}, bf16[32,1536]{1,0:T(8,128)(2,1)S(1)}, u32[]{:S(2)}, u32[]{:S(2)}) collective-permute-start(bf16[32,1536]{1,0:T(8,128)(2,1)S(1)} %slice.7), channel_id=1, source_target_pairs={{0,32},{1,33},{2,34},{3,35},{4,36},{5,37},{6,38},{7,39},{8,40},{9,... | collective-permute-start | bytes 294920 | tf_op jit(solution)/shard_map/ppermute | solution.py:59
  21.3 0.7 collective-permute-start.10
  22.0 1.3 %collective-permute-start.9 = (bf16[32,1536]{1,0:T(8,128)(2,1)S(1)}, bf16[32,1536]{1,0:T(8,128)(2,1)S(1)}, u32[]{:S(2)}, u32[]{:S(2)}) collective-permute-start(bf16[32,1536]{1,0:T(8,128)(2,1)S(1)} %slice.7), channel_id=1, source_target_pairs={{0,16},{1,17},{2,18},{3,19},{4,20},{5,21},{6,22},{7,23},{8,24},{9,... | collective-permute-start | bytes 294920 | tf_op jit(solution)/shard_map/ppermute | solution.py:59
  23.3 3.6 %collective-permute-start.8 = (bf16[128,2560]{1,0:T(8,128)(2,1)S(1)}, bf16[128,2560]{1,0:T(8,128)(2,1)S(1)}, u32[]{:S(2)}, u32[]{:S(2)}) collective-permute-start(bf16[128,2560]{1,0:T(8,128)(2,1)S(1)} %pad_maximum_fusion.x0.refs_0_), channel_id=1, source_target_pairs={{0,32},{1,33},{2,34},{3,35},{4,36},{5,37},{6,38},{7,39},{8,40},{9,... | collective-permute-start | bytes 1966088 | tf_op jit(solution)/shard_map/ppermute | solution.py:59
  27.7 1.3 %collective-permute-start.6 = (bf16[128,2560]{1,0:T(8,128)(2,1)S(1)}, bf16[128,2560]{1,0:T(8,128)(2,1)S(1)}, u32[]{:S(2)}, u32[]{:S(2)}) collective-permute-start(bf16[128,2560]{1,0:T(8,128)(2,1)S(1)} %pad_maximum_fusion.x0.refs_0_), channel_id=1, source_target_pairs={{0,16},{1,17},{2,18},{3,19},{4,20},{5,21},{6,22},{7,23},{8,24},{9,... | collective-permute-start | bytes 1966088 | tf_op jit(solution)/shard_map/ppermute | solution.py:59
  29.0 1.0 collective-permute-start.14
  30.0 1.4 %collective-permute-start.13 = (bf16[128,1536]{1,0:T(8,128)(2,1)S(1)}, bf16[128,1536]{1,0:T(8,128)(2,1)S(1)}, u32[]{:S(2)}, u32[]{:S(2)}) collective-permute-start(bf16[128,1536]{1,0:T(8,128)(2,1)S(1)} %constant_dynamic-update-slice_fusion.refs_4_), channel_id=1, source_target_pairs={{0,9},{1,8},{2,11},{3,10},{4,13},{5,12},{6,15},{7,14},{8,0},{9,1},... | collective-permute-start | bytes 1179656 | tf_op jit(solution)/shard_map/ppermute | solution.py:59
  31.5 4.1 %collective-permute-done.8.x3.refs_3_ = bf16[128,2560]{1,0:T(8,128)(2,1)S(1)} collective-permute-done((bf16[128,2560]{1,0:T(8,128)(2,1)S(1)}, bf16[128,2560]{1,0:T(8,128)(2,1)S(1)}, u32[]{:S(2)}, u32[]{:S(2)}) %collective-permute-start.8) | collective-permute-done | bytes 655392 | tf_op jit(solution)/shard_map/ppermute | solution.py:59
  35.6 0.8 collective-permute-start.12
  36.4 1.5 %shard_map.78.early = f32[128,2048]{1,0:T(8,128)S(1)} custom-call(bf16[128,2560]{1,0:T(8,128)(2,1)S(1)} %pad_maximum_fusion.x0.refs_0_, bf16[2304,2048]{1,0:T(8,128)(2,1)S(1)} %copy-done.1), custom_call_target="tpu_custom_call" | custom-call | flops 1207959552 | bytes 9437184 | tf_op jit(solution)/shard_map/pallas_call | solution.py:222
  37.9 5.7 %collective-permute-done.7.x2.refs_2_ = bf16[128,2560]{1,0:T(8,128)(2,1)S(1)} collective-permute-done((bf16[128,2560]{1,0:T(8,128)(2,1)S(1)}, bf16[128,2560]{1,0:T(8,128)(2,1)S(1)}, u32[]{:S(2)}, u32[]{:S(2)}) %collective-permute-start.7) | collective-permute-done | bytes 655392 | tf_op jit(solution)/shard_map/ppermute | solution.py:59
  43.6 4.7 %shard_map.79 = (f32[256,2048]{1,0:T(8,128)S(1)}, f32[256,2048]{1,0:T(8,128)S(1)}) custom-call(s32[2,128]{1,0:T(2,128)S(1)} %get-tuple-element.50.places, f32[128,2048]{1,0:T(8,128)S(1)} %shard_map.78.early, bf16[128,2560]{1,0:T(8,128)(2,1)S(1)} %collective-permute-done.6.x1.refs_1_, bf16[128,2560]{1,0:T(8,128)(2,1)S(1)} %collective-permute-done.7.x2.refs_2_, ...), custom_call_target="tpu_custom_call" | custom-call | flops 3623878656 | bytes 9437184 | tf_op jit(solution)/shard_map/pallas_call | solution.py:233
  48.6 4.0 %shard_map.80 = (f32[256,1536]{1,0:T(8,128)S(1)}, f32[256,1536]{1,0:T(8,128)S(1)}, bf16[512,1792]{1,0:T(8,128)(2,1)S(1)}) custom-call(bf16[512,512]{1,0:T(8,128)(2,1)S(1)} %get-tuple-element.53.main_order, bf16[512,512]{1,0:T(8,128)(2,1)S(1)} %get-tuple-element.54.apart_order, bf16[128,2560]{1,0:T(8,128)(2,1)S(1)} %pad_maximum_fusion.x0.refs_0_, ...), custom_call_target="tpu_custom_call" | custom-call | flops 2818572288 | bytes 7340032 | tf_op jit(solution)/shard_map/pallas_call | solution.py:248
  53.1 1.1 shard_map.81
  54.4 1.4 %shard_map.82 = (f32[256,2048]{1,0:T(8,128)S(1)}, f32[256,2048]{1,0:T(8,128)S(1)}, f32[256,128]{1,0:T(8,128)S(1)}) custom-call(f32[256,2048]{1,0:T(8,128)S(1)} %get-tuple-element.66.own, f32[256,2048]{1,0:T(8,128)S(1)} %collective-permute-done.15.other), custom_call_target="tpu_custom_call" | custom-call | flops 4194304 | bytes 8388608 | tf_op jit(solution)/shard_map/pallas_call | solution.py:292
  56.2 1.8 %shard_map.83 = (f32[256,1536]{1,0:T(8,128)S(1)}, f32[256,1536]{1,0:T(8,128)S(1)}, f32[2,256,128]{2,1,0:T(8,128)S(1)}) custom-call(f32[256,2048]{1,0:T(8,128)S(1)} %get-tuple-element.68.refs_0_.refs_2_, f32[256,2048]{1,0:T(8,128)S(1)} %get-tuple-element.69.refs_1_.refs_3_, f32[256,1536]{1,0:T(8,128)S(1)} %get-tuple-element.70.refs_2_, ...), custom_call_target="tpu_custom_call" | custom-call | flops 6291456 | bytes 9437184 | tf_op jit(solution)/shard_map/pallas_call | solution.py:338
  58.0 0.8 shard_map.84
  58.9 2.5 %collective-permute-start.20 = (f32[8,128]{1,0:T(8,128)S(1)}, f32[8,128]{1,0:T(8,128)S(1)}, u32[]{:S(2)}, u32[]{:S(2)}) collective-permute-start(f32[8,128]{1,0:T(8,128)S(1)} %get-tuple-element.76), channel_id=1, source_target_pairs={{0,32},{1,33},{2,34},{3,35},{4,36},{5,37},{6,38},{7,39},{8,40},{9,... | collective-permute-start | bytes 12296 | tf_op jit(solution)/shard_map/ppermute | solution.py:59
  61.4 1.2 %collective-permute-start.19 = (f32[8,128]{1,0:T(8,128)S(1)}, f32[8,128]{1,0:T(8,128)S(1)}, u32[]{:S(2)}, u32[]{:S(2)}) collective-permute-start(f32[8,128]{1,0:T(8,128)S(1)} %get-tuple-element.76), channel_id=1, source_target_pairs={{0,48},{1,49},{2,50},{3,51},{4,52},{5,53},{6,54},{7,55},{8,56},{9,... | collective-permute-start | bytes 12296 | tf_op jit(solution)/shard_map/ppermute | solution.py:59
  62.6 0.8 collective-permute-start.18
  64.0 1.0 collective-permute-done.19
  65.0 2.4 %collective-permute-done.18 = f32[8,128]{1,0:T(8,128)S(1)} collective-permute-done((f32[8,128]{1,0:T(8,128)S(1)}, f32[8,128]{1,0:T(8,128)S(1)}, u32[]{:S(2)}, u32[]{:S(2)}) %collective-permute-start.18) | collective-permute-done | bytes 4128 | tf_op jit(solution)/shard_map/ppermute | solution.py:59
  67.4 2.7 %collective-permute-start.23 = (f32[8,128]{1,0:T(8,128)S(1)}, f32[8,128]{1,0:T(8,128)S(1)}, u32[]{:S(2)}, u32[]{:S(2)}) collective-permute-start(f32[8,128]{1,0:T(8,128)S(1)} %add_add_fusion.2), channel_id=1, source_target_pairs={{0,1},{1,0},{2,3},{3,2},{4,5},{5,4},{6,7},{7,6},{8,9},{9,8},{10,11... | collective-permute-start | bytes 12296 | tf_op jit(solution)/shard_map/ppermute | solution.py:59
  70.1 1.2 %collective-permute-start.22 = (f32[8,128]{1,0:T(8,128)S(1)}, f32[8,128]{1,0:T(8,128)S(1)}, u32[]{:S(2)}, u32[]{:S(2)}) collective-permute-start(f32[8,128]{1,0:T(8,128)S(1)} %add_add_fusion.2), channel_id=1, source_target_pairs={{0,9},{1,8},{2,11},{3,10},{4,13},{5,12},{6,15},{7,14},{8,0},{9,1},... | collective-permute-start | bytes 12296 | tf_op jit(solution)/shard_map/ppermute | solution.py:59
  71.4 0.8 collective-permute-start.21
  72.6 1.2 collective-permute-done.22
  73.7 2.5 %collective-permute-done.21 = f32[8,128]{1,0:T(8,128)S(1)} collective-permute-done((f32[8,128]{1,0:T(8,128)S(1)}, f32[8,128]{1,0:T(8,128)S(1)}, u32[]{:S(2)}, u32[]{:S(2)}) %collective-permute-start.21) | collective-permute-done | bytes 4128 | tf_op jit(solution)/shard_map/ppermute | solution.py:59
  76.2 1.7 %collective-permute-start.26 = (f32[8,128]{1,0:T(8,128)S(1)}, f32[8,128]{1,0:T(8,128)S(1)}, u32[]{:S(2)}, u32[]{:S(2)}) collective-permute-start(f32[8,128]{1,0:T(8,128)S(1)} %add_add_fusion.1), channel_id=1, source_target_pairs={{0,4},{1,5},{2,6},{3,7},{4,0},{5,1},{6,2},{7,3},{8,12},{9,13},{10,... | collective-permute-start | bytes 12296 | tf_op jit(solution)/shard_map/ppermute | solution.py:59
  77.9 1.6 %collective-permute-start.25 = (f32[8,128]{1,0:T(8,128)S(1)}, f32[8,128]{1,0:T(8,128)S(1)}, u32[]{:S(2)}, u32[]{:S(2)}) collective-permute-start(f32[8,128]{1,0:T(8,128)S(1)} %add_add_fusion.1), channel_id=1, source_target_pairs={{0,6},{1,7},{2,0},{3,1},{4,2},{5,3},{6,4},{7,5},{8,14},{9,15},{10,... | collective-permute-start | bytes 12296 | tf_op jit(solution)/shard_map/ppermute | solution.py:59
  79.9 1.4 %collective-permute-done.26 = f32[8,128]{1,0:T(8,128)S(1)} collective-permute-done((f32[8,128]{1,0:T(8,128)S(1)}, f32[8,128]{1,0:T(8,128)S(1)}, u32[]{:S(2)}, u32[]{:S(2)}) %collective-permute-start.26) | collective-permute-done | bytes 4128 | tf_op jit(solution)/shard_map/ppermute | solution.py:59
  81.5 2.8 %collective-permute-done.24 = f32[8,128]{1,0:T(8,128)S(1)} collective-permute-done((f32[8,128]{1,0:T(8,128)S(1)}, f32[8,128]{1,0:T(8,128)S(1)}, u32[]{:S(2)}, u32[]{:S(2)}) %collective-permute-start.24) | collective-permute-done | bytes 4128 | tf_op jit(solution)/shard_map/ppermute | solution.py:59
  85.3 2.1 %shard_map.86.own = f32[256,1792]{1,0:T(8,128)S(1)} custom-call(bf16[256,2048]{1,0:T(8,128)(2,1)S(1)} %get-tuple-element.82.gap.own, bf16[1792,2048]{1,0:T(8,128)(2,1)S(1)} %bitcast.5), custom_call_target="tpu_custom_call" | custom-call | flops 1879048192 | bytes 7340032 | tf_op jit(solution)/shard_map/pallas_call | solution.py:396
  87.4 3.2 %shard_map.87 = (f32[128,1792]{1,0:T(8,128)S(1)}, bf16[128,1792]{1,0:T(8,128)(2,1)S(1)}, bf16[128,1792]{1,0:T(8,128)(2,1)S(1)}, bf16[128,1792]{1,0:T(8,128)(2,1)S(1)}) custom-call(s32[2,128]{1,0:T(2,128)S(1)} %get-tuple-element.50.places, f32[256,1792]{1,0:T(8,128)S(1)} %shard_map.86.own, bf16[256,2048]{1,0:T(8,128)(2,1)S(1)} %collective-permute-done.27.gap.other, ...), custom_call_target="tpu_custom_call" | custom-call | flops 1879048192 | bytes 7340032 | tf_op jit(solution)/shard_map/pallas_call | solution.py:419
  90.8 1.9 %collective-permute-start.30 = (bf16[128,1792]{1,0:T(8,128)(2,1)S(1)}, bf16[128,1792]{1,0:T(8,128)(2,1)S(1)}, u32[]{:S(2)}, u32[]{:S(2)}) collective-permute-start(bf16[128,1792]{1,0:T(8,128)(2,1)S(1)} %get-tuple-element.90), channel_id=1, source_target_pairs={{0,16},{1,17},{2,18},{3,19},{4,20},{5,21},{6,22},{7,23},{8,24},{9,... | collective-permute-start | bytes 1376264 | tf_op jit(solution)/shard_map/ppermute | solution.py:59
  92.7 6.9 %shard_map.88 = bf16[1792,2048]{1,0:T(8,128)(2,1)} custom-call(bf16[512,1792]{1,0:T(8,128)(2,1)S(1)} %get-tuple-element.64.rows, bf16[256,2048]{1,0:T(8,128)(2,1)S(1)} %get-tuple-element.82.gap.own, bf16[256,2048]{1,0:T(8,128)(2,1)S(1)} %collective-permute-done.27.gap.other), custom_call_target="tpu_custom_call" | custom-call | flops 3758096384 | bytes 7340032 | tf_op jit(solution)/shard_map/pallas_call | solution.py:475
  99.6 5.7 %collective-permute-done.30.refs_1_ = bf16[128,1792]{1,0:T(8,128)(2,1)S(1)} collective-permute-done((bf16[128,1792]{1,0:T(8,128)(2,1)S(1)}, bf16[128,1792]{1,0:T(8,128)(2,1)S(1)}, u32[]{:S(2)}, u32[]{:S(2)}) %collective-permute-start.30) | collective-permute-done | bytes 458784 | tf_op jit(solution)/shard_map/ppermute | solution.py:59
  105.4 1.0 shard_map.89
  106.4 3.6 %all-to-all-start = ((bf16[16,8,1792]{2,1,0:T(8,128)(2,1)}), bf16[16,8,1792]{2,1,0:T(8,128)(2,1)S(1)}, u32[]{:S(2)}, u32[]{:S(2)}) async-start(bf16[16,8,1792]{2,1,0:T(8,128)(2,1)} %bitcast.2), calls=%async_computation | async-start | bytes 917504 | tf_op jit(solution)/shard_map/all_to_all | solution.py:537
  110.5 8.7 %all-to-all-done.received = bf16[16,8,1792]{2,1,0:T(8,128)(2,1)S(1)} async-done(((bf16[16,8,1792]{2,1,0:T(8,128)(2,1)}), bf16[16,8,1792]{2,1,0:T(8,128)(2,1)S(1)}, u32[]{:S(2)}, u32[]{:S(2)}) %all-to-all-start) | async-done | bytes 458784 | tf_op jit(solution)/shard_map/all_to_all | solution.py:537
  (61 shorter events, 7.3 us)
Async XLA Ops:
  0.6 0.8 copy-start.2
  1.4 0.7 copy-start.3
  2.2 9.4 %collective-permute-start.2 = (bf16[8,4096]{1,0:T(8,128)(2,1)S(1)}, bf16[8,4096]{1,0:T(8,128)(2,1)S(1)}, u32[]{:S(2)}, u32[]{:S(2)}) collective-permute-start(bf16[8,4096]{1,0:T(8,128)(2,1)S(1)} %shard_map.77), channel_id=1, source_target_pairs={{0,4},{1,5},{2,6},{3,7},{4,0},{5,1},{6,2},{7,3},{8,12},{9,13},{10,... | collective-permute-start | bytes 196616 | tf_op jit(solution)/shard_map/ppermute | solution.py:59
  5.6 6.0 %collective-permute-start.1 = (bf16[8,4096]{1,0:T(8,128)(2,1)S(1)}, bf16[8,4096]{1,0:T(8,128)(2,1)S(1)}, u32[]{:S(2)}, u32[]{:S(2)}) collective-permute-start(bf16[8,4096]{1,0:T(8,128)(2,1)S(1)} %shard_map.77), channel_id=1, source_target_pairs={{0,6},{1,7},{2,0},{3,1},{4,2},{5,3},{6,4},{7,5},{8,14},{9,15},{10,... | collective-permute-start | bytes 196616 | tf_op jit(solution)/shard_map/ppermute | solution.py:59
  6.6 5.5 %collective-permute-start = (bf16[8,4096]{1,0:T(8,128)(2,1)S(1)}, bf16[8,4096]{1,0:T(8,128)(2,1)S(1)}, u32[]{:S(2)}, u32[]{:S(2)}) collective-permute-start(bf16[8,4096]{1,0:T(8,128)(2,1)S(1)} %shard_map.77), channel_id=1, source_target_pairs={{0,2},{1,3},{2,4},{3,5},{4,6},{5,7},{6,0},{7,1},{8,10},{9,11},{10,... | collective-permute-start | bytes 196616 | tf_op jit(solution)/shard_map/ppermute | solution.py:59
  7.6 3.7 %copy-start = (bf16[2304,2048]{1,0:T(8,128)(2,1)S(1)}, bf16[2304,2048]{1,0:T(8,128)(2,1)}, u32[]{:S(2)}) copy-start(bf16[2304,2048]{1,0:T(8,128)(2,1)} %weight.6) | copy-start | bytes 28311556
  11.3 25.1 %copy-start.1 = (bf16[2304,2048]{1,0:T(8,128)(2,1)S(1)}, bf16[2304,2048]{1,0:T(8,128)(2,1)}, u32[]{:S(2)}) copy-start(bf16[2304,2048]{1,0:T(8,128)(2,1)} %weight.6) | copy-start | bytes 28311556
  12.2 9.8 %collective-permute-start.5 = (bf16[32,2560]{1,0:T(8,128)(2,1)S(1)}, bf16[32,2560]{1,0:T(8,128)(2,1)S(1)}, u32[]{:S(2)}, u32[]{:S(2)}) collective-permute-start(bf16[32,2560]{1,0:T(8,128)(2,1)S(1)} %slice.6), channel_id=1, source_target_pairs={{0,1},{1,0},{2,3},{3,2},{4,5},{5,4},{6,7},{7,6},{8,9},{9,8},{10,11... | collective-permute-start | bytes 491528 | tf_op jit(solution)/shard_map/ppermute | solution.py:59
  15.3 8.0 %collective-permute-start.4 = (bf16[32,2560]{1,0:T(8,128)(2,1)S(1)}, bf16[32,2560]{1,0:T(8,128)(2,1)S(1)}, u32[]{:S(2)}, u32[]{:S(2)}) collective-permute-start(bf16[32,2560]{1,0:T(8,128)(2,1)S(1)} %slice.6), channel_id=1, source_target_pairs={{0,9},{1,8},{2,11},{3,10},{4,13},{5,12},{6,15},{7,14},{8,0},{9,1},... | collective-permute-start | bytes 491528 | tf_op jit(solution)/shard_map/ppermute | solution.py:59
  16.4 6.9 %collective-permute-start.3 = (bf16[32,2560]{1,0:T(8,128)(2,1)S(1)}, bf16[32,2560]{1,0:T(8,128)(2,1)S(1)}, u32[]{:S(2)}, u32[]{:S(2)}) collective-permute-start(bf16[32,2560]{1,0:T(8,128)(2,1)S(1)} %slice.6), channel_id=1, source_target_pairs={{0,8},{1,9},{2,10},{3,11},{4,12},{5,13},{6,14},{7,15},{8,1},{9,0},... | collective-permute-start | bytes 491528 | tf_op jit(solution)/shard_map/ppermute | solution.py:59
  17.3 10.4 %collective-permute-start.11 = (bf16[32,1536]{1,0:T(8,128)(2,1)S(1)}, bf16[32,1536]{1,0:T(8,128)(2,1)S(1)}, u32[]{:S(2)}, u32[]{:S(2)}) collective-permute-start(bf16[32,1536]{1,0:T(8,128)(2,1)S(1)} %slice.7), channel_id=1, source_target_pairs={{0,32},{1,33},{2,34},{3,35},{4,36},{5,37},{6,38},{7,39},{8,40},{9,... | collective-permute-start | bytes 294920 | tf_op jit(solution)/shard_map/ppermute | solution.py:59
  21.3 7.7 %collective-permute-start.10 = (bf16[32,1536]{1,0:T(8,128)(2,1)S(1)}, bf16[32,1536]{1,0:T(8,128)(2,1)S(1)}, u32[]{:S(2)}, u32[]{:S(2)}) collective-permute-start(bf16[32,1536]{1,0:T(8,128)(2,1)S(1)} %slice.7), channel_id=1, source_target_pairs={{0,48},{1,49},{2,50},{3,51},{4,52},{5,53},{6,54},{7,55},{8,56},{9,... | collective-permute-start | bytes 294920 | tf_op jit(solution)/shard_map/ppermute | solution.py:59
  22.0 7.0 %collective-permute-start.9 = (bf16[32,1536]{1,0:T(8,128)(2,1)S(1)}, bf16[32,1536]{1,0:T(8,128)(2,1)S(1)}, u32[]{:S(2)}, u32[]{:S(2)}) collective-permute-start(bf16[32,1536]{1,0:T(8,128)(2,1)S(1)} %slice.7), channel_id=1, source_target_pairs={{0,16},{1,17},{2,18},{3,19},{4,20},{5,21},{6,22},{7,23},{8,24},{9,... | collective-permute-start | bytes 294920 | tf_op jit(solution)/shard_map/ppermute | solution.py:59
  23.3 12.3 %collective-permute-start.8 = (bf16[128,2560]{1,0:T(8,128)(2,1)S(1)}, bf16[128,2560]{1,0:T(8,128)(2,1)S(1)}, u32[]{:S(2)}, u32[]{:S(2)}) collective-permute-start(bf16[128,2560]{1,0:T(8,128)(2,1)S(1)} %pad_maximum_fusion.x0.refs_0_), channel_id=1, source_target_pairs={{0,32},{1,33},{2,34},{3,35},{4,36},{5,37},{6,38},{7,39},{8,40},{9,... | collective-permute-start | bytes 1966088 | tf_op jit(solution)/shard_map/ppermute | solution.py:59
  26.9 16.6 %collective-permute-start.7 = (bf16[128,2560]{1,0:T(8,128)(2,1)S(1)}, bf16[128,2560]{1,0:T(8,128)(2,1)S(1)}, u32[]{:S(2)}, u32[]{:S(2)}) collective-permute-start(bf16[128,2560]{1,0:T(8,128)(2,1)S(1)} %pad_maximum_fusion.x0.refs_0_), channel_id=1, source_target_pairs={{0,48},{1,49},{2,50},{3,51},{4,52},{5,53},{6,54},{7,55},{8,56},{9,... | collective-permute-start | bytes 1966088 | tf_op jit(solution)/shard_map/ppermute | solution.py:59
  27.7 15.9 %collective-permute-start.6 = (bf16[128,2560]{1,0:T(8,128)(2,1)S(1)}, bf16[128,2560]{1,0:T(8,128)(2,1)S(1)}, u32[]{:S(2)}, u32[]{:S(2)}) collective-permute-start(bf16[128,2560]{1,0:T(8,128)(2,1)S(1)} %pad_maximum_fusion.x0.refs_0_), channel_id=1, source_target_pairs={{0,16},{1,17},{2,18},{3,19},{4,20},{5,21},{6,22},{7,23},{8,24},{9,... | collective-permute-start | bytes 1966088 | tf_op jit(solution)/shard_map/ppermute | solution.py:59
  29.0 19.2 %collective-permute-start.14 = (bf16[128,1536]{1,0:T(8,128)(2,1)S(1)}, bf16[128,1536]{1,0:T(8,128)(2,1)S(1)}, u32[]{:S(2)}, u32[]{:S(2)}) collective-permute-start(bf16[128,1536]{1,0:T(8,128)(2,1)S(1)} %constant_dynamic-update-slice_fusion.refs_4_), channel_id=1, source_target_pairs={{0,1},{1,0},{2,3},{3,2},{4,5},{5,4},{6,7},{7,6},{8,9},{9,8},{10,11... | collective-permute-start | bytes 1179656 | tf_op jit(solution)/shard_map/ppermute | solution.py:59
  30.0 18.2 %collective-permute-start.13 = (bf16[128,1536]{1,0:T(8,128)(2,1)S(1)}, bf16[128,1536]{1,0:T(8,128)(2,1)S(1)}, u32[]{:S(2)}, u32[]{:S(2)}) collective-permute-start(bf16[128,1536]{1,0:T(8,128)(2,1)S(1)} %constant_dynamic-update-slice_fusion.refs_4_), channel_id=1, source_target_pairs={{0,9},{1,8},{2,11},{3,10},{4,13},{5,12},{6,15},{7,14},{8,0},{9,1},... | collective-permute-start | bytes 1179656 | tf_op jit(solution)/shard_map/ppermute | solution.py:59
  35.6 12.7 %collective-permute-start.12 = (bf16[128,1536]{1,0:T(8,128)(2,1)S(1)}, bf16[128,1536]{1,0:T(8,128)(2,1)S(1)}, u32[]{:S(2)}, u32[]{:S(2)}) collective-permute-start(bf16[128,1536]{1,0:T(8,128)(2,1)S(1)} %constant_dynamic-update-slice_fusion.refs_4_), channel_id=1, source_target_pairs={{0,8},{1,9},{2,10},{3,11},{4,12},{5,13},{6,14},{7,15},{8,1},{9,0},... | collective-permute-start | bytes 1179656 | tf_op jit(solution)/shard_map/ppermute | solution.py:59
  36.4 12.2 %slice-start = ((s8[7340032]{0:T(1024)(128)(4,1)}), s8[4194304]{0:T(1024)(128)(4,1)S(1)}, s32[]{:S(2)}) async-start(s8[7340032]{0:T(1024)(128)(4,1)} %bitcast.4), calls=%async_computation.1 | async-start | bytes 8388608
  37.9 10.7 %slice-start.1 = ((s8[7340032]{0:T(1024)(128)(4,1)}), s8[3145728]{0:T(1024)(128)(4,1)S(1)}, s32[]{:S(2)}) async-start(s8[7340032]{0:T(1024)(128)(4,1)} %bitcast.4), calls=%async_computation.2 | async-start | bytes 6291456
  48.3 6.1 %collective-permute-start.15 = (f32[256,2048]{1,0:T(8,128)S(1)}, f32[256,2048]{1,0:T(8,128)S(1)}, u32[]{:S(2)}, u32[]{:S(2)}) collective-permute-start(f32[256,2048]{1,0:T(8,128)S(1)} %get-tuple-element.67), channel_id=1, source_target_pairs={{0,64},{64,0},{1,65},{65,1},{2,66},{66,2},{3,67},{67,3},{4,68},{68... | collective-permute-start | bytes 6291464 | tf_op jit(solution)/shard_map/ppermute | solution.py:63
  52.6 3.6 %collective-permute-start.16 = (f32[256,1536]{1,0:T(8,128)S(1)}, f32[256,1536]{1,0:T(8,128)S(1)}, u32[]{:S(2)}, u32[]{:S(2)}) collective-permute-start(f32[256,1536]{1,0:T(8,128)S(1)} %get-tuple-element.71), channel_id=1, source_target_pairs={{0,64},{64,0},{1,65},{65,1},{2,66},{66,2},{3,67},{67,3},{4,68},{68... | collective-permute-start | bytes 4718600 | tf_op jit(solution)/shard_map/ppermute | solution.py:63
  54.2 3.8 %collective-permute-start.17 = (f32[256,512]{1,0:T(8,128)S(1)}, f32[256,512]{1,0:T(8,128)S(1)}, u32[]{:S(2)}, u32[]{:S(2)}) collective-permute-start(f32[256,512]{1,0:T(8,128)S(1)} %get-tuple-element.75), channel_id=1, source_target_pairs={{0,64},{64,0},{1,65},{65,1},{2,66},{66,2},{3,67},{67,3},{4,68},{68... | collective-permute-start | bytes 1572872 | tf_op jit(solution)/shard_map/ppermute | solution.py:63
  58.0 26.2 %copy-start.4 = (f32[512]{0:T(512)S(1)}, f32[512]{0:T(512)}, u32[]{:S(2)}) copy-start(f32[512]{0:T(512)} %param.9) | copy-start | bytes 6148
  58.9 5.2 %collective-permute-start.20 = (f32[8,128]{1,0:T(8,128)S(1)}, f32[8,128]{1,0:T(8,128)S(1)}, u32[]{:S(2)}, u32[]{:S(2)}) collective-permute-start(f32[8,128]{1,0:T(8,128)S(1)} %get-tuple-element.76), channel_id=1, source_target_pairs={{0,32},{1,33},{2,34},{3,35},{4,36},{5,37},{6,38},{7,39},{8,40},{9,... | collective-permute-start | bytes 12296 | tf_op jit(solution)/shard_map/ppermute | solution.py:59
  61.4 3.6 %collective-permute-start.19 = (f32[8,128]{1,0:T(8,128)S(1)}, f32[8,128]{1,0:T(8,128)S(1)}, u32[]{:S(2)}, u32[]{:S(2)}) collective-permute-start(f32[8,128]{1,0:T(8,128)S(1)} %get-tuple-element.76), channel_id=1, source_target_pairs={{0,48},{1,49},{2,50},{3,51},{4,52},{5,53},{6,54},{7,55},{8,56},{9,... | collective-permute-start | bytes 12296 | tf_op jit(solution)/shard_map/ppermute | solution.py:59
  62.6 4.8 %collective-permute-start.18 = (f32[8,128]{1,0:T(8,128)S(1)}, f32[8,128]{1,0:T(8,128)S(1)}, u32[]{:S(2)}, u32[]{:S(2)}) collective-permute-start(f32[8,128]{1,0:T(8,128)S(1)} %get-tuple-element.76), channel_id=1, source_target_pairs={{0,16},{1,17},{2,18},{3,19},{4,20},{5,21},{6,22},{7,23},{8,24},{9,... | collective-permute-start | bytes 12296 | tf_op jit(solution)/shard_map/ppermute | solution.py:59
  67.4 5.1 %collective-permute-start.23 = (f32[8,128]{1,0:T(8,128)S(1)}, f32[8,128]{1,0:T(8,128)S(1)}, u32[]{:S(2)}, u32[]{:S(2)}) collective-permute-start(f32[8,128]{1,0:T(8,128)S(1)} %add_add_fusion.2), channel_id=1, source_target_pairs={{0,1},{1,0},{2,3},{3,2},{4,5},{5,4},{6,7},{7,6},{8,9},{9,8},{10,11... | collective-permute-start | bytes 12296 | tf_op jit(solution)/shard_map/ppermute | solution.py:59
  70.1 3.6 %collective-permute-start.22 = (f32[8,128]{1,0:T(8,128)S(1)}, f32[8,128]{1,0:T(8,128)S(1)}, u32[]{:S(2)}, u32[]{:S(2)}) collective-permute-start(f32[8,128]{1,0:T(8,128)S(1)} %add_add_fusion.2), channel_id=1, source_target_pairs={{0,9},{1,8},{2,11},{3,10},{4,13},{5,12},{6,15},{7,14},{8,0},{9,1},... | collective-permute-start | bytes 12296 | tf_op jit(solution)/shard_map/ppermute | solution.py:59
  71.4 4.8 %collective-permute-start.21 = (f32[8,128]{1,0:T(8,128)S(1)}, f32[8,128]{1,0:T(8,128)S(1)}, u32[]{:S(2)}, u32[]{:S(2)}) collective-permute-start(f32[8,128]{1,0:T(8,128)S(1)} %add_add_fusion.2), channel_id=1, source_target_pairs={{0,8},{1,9},{2,10},{3,11},{4,12},{5,13},{6,14},{7,15},{8,1},{9,0},... | collective-permute-start | bytes 12296 | tf_op jit(solution)/shard_map/ppermute | solution.py:59
  76.2 5.1 %collective-permute-start.26 = (f32[8,128]{1,0:T(8,128)S(1)}, f32[8,128]{1,0:T(8,128)S(1)}, u32[]{:S(2)}, u32[]{:S(2)}) collective-permute-start(f32[8,128]{1,0:T(8,128)S(1)} %add_add_fusion.1), channel_id=1, source_target_pairs={{0,4},{1,5},{2,6},{3,7},{4,0},{5,1},{6,2},{7,3},{8,12},{9,13},{10,... | collective-permute-start | bytes 12296 | tf_op jit(solution)/shard_map/ppermute | solution.py:59
  77.9 3.6 %collective-permute-start.25 = (f32[8,128]{1,0:T(8,128)S(1)}, f32[8,128]{1,0:T(8,128)S(1)}, u32[]{:S(2)}, u32[]{:S(2)}) collective-permute-start(f32[8,128]{1,0:T(8,128)S(1)} %add_add_fusion.1), channel_id=1, source_target_pairs={{0,6},{1,7},{2,0},{3,1},{4,2},{5,3},{6,4},{7,5},{8,14},{9,15},{10,... | collective-permute-start | bytes 12296 | tf_op jit(solution)/shard_map/ppermute | solution.py:59
  79.4 4.8 %collective-permute-start.24 = (f32[8,128]{1,0:T(8,128)S(1)}, f32[8,128]{1,0:T(8,128)S(1)}, u32[]{:S(2)}, u32[]{:S(2)}) collective-permute-start(f32[8,128]{1,0:T(8,128)S(1)} %add_add_fusion.1), channel_id=1, source_target_pairs={{0,2},{1,3},{2,4},{3,5},{4,6},{5,7},{6,0},{7,1},{8,10},{9,11},{10,... | collective-permute-start | bytes 12296 | tf_op jit(solution)/shard_map/ppermute | solution.py:59
  84.7 2.7 %collective-permute-start.27 = (bf16[256,2048]{1,0:T(8,128)(2,1)S(1)}, bf16[256,2048]{1,0:T(8,128)(2,1)S(1)}, u32[]{:S(2)}, u32[]{:S(2)}) collective-permute-start(bf16[256,2048]{1,0:T(8,128)(2,1)S(1)} %get-tuple-element.82.gap.own), channel_id=1, source_target_pairs={{0,64},{64,0},{1,65},{65,1},{2,66},{66,2},{3,67},{67,3},{4,68},{68... | collective-permute-start | bytes 3145736 | tf_op jit(solution)/shard_map/ppermute | solution.py:63
  84.8 2.6 %collective-permute-start.28 = (f32[2,128]{1,0:T(2,128)S(1)}, f32[2,128]{1,0:T(2,128)S(1)}, u32[]{:S(2)}, u32[]{:S(2)}) collective-permute-start(f32[2,128]{1,0:T(2,128)S(1)} %get-tuple-element.81), channel_id=1, source_target_pairs={{0,64},{64,0},{1,65},{65,1},{2,66},{66,2},{3,67},{67,3},{4,68},{68... | collective-permute-start | bytes 3080 | tf_op jit(solution)/shard_map/ppermute | solution.py:63
  90.6 9.0 %collective-permute-start.29 = (bf16[128,1792]{1,0:T(8,128)(2,1)S(1)}, bf16[128,1792]{1,0:T(8,128)(2,1)S(1)}, u32[]{:S(2)}, u32[]{:S(2)}) collective-permute-start(bf16[128,1792]{1,0:T(8,128)(2,1)S(1)} %get-tuple-element.89), channel_id=1, source_target_pairs={{0,48},{1,49},{2,50},{3,51},{4,52},{5,53},{6,54},{7,55},{8,56},{9,... | collective-permute-start | bytes 1376264 | tf_op jit(solution)/shard_map/ppermute | solution.py:59
  90.8 14.6 %collective-permute-start.30 = (bf16[128,1792]{1,0:T(8,128)(2,1)S(1)}, bf16[128,1792]{1,0:T(8,128)(2,1)S(1)}, u32[]{:S(2)}, u32[]{:S(2)}) collective-permute-start(bf16[128,1792]{1,0:T(8,128)(2,1)S(1)} %get-tuple-element.90), channel_id=1, source_target_pairs={{0,16},{1,17},{2,18},{3,19},{4,20},{5,21},{6,22},{7,23},{8,24},{9,... | collective-permute-start | bytes 1376264 | tf_op jit(solution)/shard_map/ppermute | solution.py:59
  92.7 12.7 %collective-permute-start.31 = (bf16[128,1792]{1,0:T(8,128)(2,1)S(1)}, bf16[128,1792]{1,0:T(8,128)(2,1)S(1)}, u32[]{:S(2)}, u32[]{:S(2)}) collective-permute-start(bf16[128,1792]{1,0:T(8,128)(2,1)S(1)} %get-tuple-element.91), channel_id=1, source_target_pairs={{0,32},{1,33},{2,34},{3,35},{4,36},{5,37},{6,38},{7,39},{8,40},{9,... | collective-permute-start | bytes 1376264 | tf_op jit(solution)/shard_map/ppermute | solution.py:59
  106.4 12.9 %all-to-all-start = ((bf16[16,8,1792]{2,1,0:T(8,128)(2,1)}), bf16[16,8,1792]{2,1,0:T(8,128)(2,1)S(1)}, u32[]{:S(2)}, u32[]{:S(2)}) async-start(bf16[16,8,1792]{2,1,0:T(8,128)(2,1)} %bitcast.2), calls=%async_computation | async-start | bytes 917504 | tf_op jit(solution)/shard_map/all_to_all | solution.py:537

commit v7 on v6

--- a/solution.py
+++ b/solution.py
@@ -17,9 +17,9 @@
 mega = 1024 * 1024
 
 offsets = (0, 1, 3, 2)
-main_axes = (("y", "z"), ("x", "x"), ("z", "y"))
-apart_axes = (("y", "z"), ("z", "y"), ("x", "x"))
-reduce_axes = (("z", "y"), ("x", "z"), ("y", "x"))
+main_axes = (("y", "x"), ("z", "z"), ("x", "y"))
+apart_axes = (("y", "x"), ("x", "y"), ("z", "z"))
+reduce_axes = (("x", "y"), ("z", "x"), ("y", "z"))
 
 
 def place(index):
@@ -167,10 +167,12 @@
     block = row // 8
     digit, member = block >> 4, block & 15
     offset = digit ^ (digit >> 1)
-    z = (1 - core) * ((at["z"] - offset) & 3) + core * (member >> 2)
-    y = (1 - core) * ((member >> 1) & 3) + core * ((at["y"] - offset) & 3)
-    x_lo = (1 - core) * (member >> 3) + core * ((member >> 1) & 1)
-    owner = z * 16 + x_lo * 8 + y * 2 + (member & 1)
+    x = (at["x"] - offset) & 3
+    z = member >> 2
+    y = (1 - core) * (member & 3) + core * ((at["y"] - offset) & 3)
+    x_lo = (1 - core) * (x & 1) + core * ((member >> 1) & 1)
+    x_hi = (1 - core) * (x >> 1) + core * (member & 1)
+    owner = z * 16 + x_lo * 8 + y * 2 + x_hi
     return ((owner - 32 * core) & 63) * 8 + row % 8
 
 

time: 121 us -> 120 us (level)
    ppermute x27, waiting for transfers between devices: 28.5 us -> 27.2 us  [send(): return lax.ppermute(block, everyone, ring(axes, by))]
  transfers between devices with their start and end apart: 33 -> 33, of which waited for: 16 -> 18; matrix products, arithmetic and copies ran while one was open for 1% -> 1% of each run, Pallas kernels for 20% -> 20%
where the time goes in v7:
time: 120 us
  starting transfers between devices  46 us (38%)
  waiting for transfers between devices  36.8 us (31%)
  Pallas kernels  30 us (25%)
  local copies, waits for them, and re-layouts  5.26 us (4%)
    ppermute x27, starting transfers between devices, send(): return lax.ppermute(block, everyone, ring(axes, by))  41.1 us
    ppermute x27, waiting for transfers between devices, send(): return lax.ppermute(block, everyone, ring(axes, by))  27.2 us
    all_to_all x1, waiting for transfers between devices, local(): total = lax.all_to_all(total, everyone, 0, 0, axis_index_groups=planes())  9.11 us
    pallas_call x1, Pallas kernels, grad_weight_of(): pl.pallas_call(grad_weight_kernel, grid=(student_width // tile,), in_spec...  6.91 us
    unnamed x17, local copies, waits for them, and re-layouts  5.23 us
    pallas_call x1, Pallas kernels, teacher_logits(): pl.pallas_call(teacher_kernel, in_specs=[scalars()] + [whole()] * 5, out_...  4.67 us
    pallas_call x1, Pallas kernels, student_logits(): pl.pallas_call(student_kernel, in_specs=[whole()] * 11, out_specs=[whole(...  3.97 us
    all_to_all x1, starting transfers between devices, local(): total = lax.all_to_all(total, everyone, 0, 0, axis_index_groups=planes())  3.56 us
  transfers between devices with their start and end apart: 33, of which 18 were waited for; matrix products, arithmetic and copies ran while one was open for 1% of the time, Pallas kernels for 20%

profile of v7, /device:TPU:0, one launch (start us, length us, event | category | flops | bytes accessed | tf_op | source)
XLA Modules:
  0.0 119.5 jit_solution(15135863448554299932)
XLA Ops:
  2.2 3.4 %collective-permute-start.2 = (bf16[8,4096]{1,0:T(8,128)(2,1)S(1)}, bf16[8,4096]{1,0:T(8,128)(2,1)S(1)}, u32[]{:S(2)}, u32[]{:S(2)}) collective-permute-start(bf16[8,4096]{1,0:T(8,128)(2,1)S(1)} %shard_map.77), channel_id=1, source_target_pairs={{0,4},{1,5},{2,6},{3,7},{4,0},{5,1},{6,2},{7,3},{8,12},{9,13},{10,... | collective-permute-start | bytes 196616 | tf_op jit(solution)/shard_map/ppermute | solution.py:59
  5.6 1.1 collective-permute-start.1
  6.6 1.0 collective-permute-start
  7.6 3.7 %copy-done = bf16[2304,2048]{1,0:T(8,128)(2,1)S(1)} copy-done((bf16[2304,2048]{1,0:T(8,128)(2,1)S(1)}, bf16[2304,2048]{1,0:T(8,128)(2,1)}, u32[]{:S(2)}) %copy-start) | copy-done | bytes 9437208
  12.2 4.0 %collective-permute-start.5 = (bf16[32,2560]{1,0:T(8,128)(2,1)S(1)}, bf16[32,2560]{1,0:T(8,128)(2,1)S(1)}, u32[]{:S(2)}, u32[]{:S(2)}) collective-permute-start(bf16[32,2560]{1,0:T(8,128)(2,1)S(1)} %slice.6), channel_id=1, source_target_pairs={{0,32},{1,33},{2,34},{3,35},{4,36},{5,37},{6,38},{7,39},{8,40},{9,... | collective-permute-start | bytes 491528 | tf_op jit(solution)/shard_map/ppermute | solution.py:59
  16.8 1.3 %collective-permute-start.3 = (bf16[32,2560]{1,0:T(8,128)(2,1)S(1)}, bf16[32,2560]{1,0:T(8,128)(2,1)S(1)}, u32[]{:S(2)}, u32[]{:S(2)}) collective-permute-start(bf16[32,2560]{1,0:T(8,128)(2,1)S(1)} %slice.6), channel_id=1, source_target_pairs={{0,16},{1,17},{2,18},{3,19},{4,20},{5,21},{6,22},{7,23},{8,24},{9,... | collective-permute-start | bytes 491528 | tf_op jit(solution)/shard_map/ppermute | solution.py:59
  18.2 3.1 %collective-permute-start.11 = (bf16[32,1536]{1,0:T(8,128)(2,1)S(1)}, bf16[32,1536]{1,0:T(8,128)(2,1)S(1)}, u32[]{:S(2)}, u32[]{:S(2)}) collective-permute-start(bf16[32,1536]{1,0:T(8,128)(2,1)S(1)} %slice.7), channel_id=1, source_target_pairs={{0,1},{1,0},{2,3},{3,2},{4,5},{5,4},{6,7},{7,6},{8,9},{9,8},{10,11... | collective-permute-start | bytes 294920 | tf_op jit(solution)/shard_map/ppermute | solution.py:59
  21.3 1.1 collective-permute-start.10
  22.4 0.9 collective-permute-start.9
  23.4 3.1 %collective-permute-start.8 = (bf16[128,2560]{1,0:T(8,128)(2,1)S(1)}, bf16[128,2560]{1,0:T(8,128)(2,1)S(1)}, u32[]{:S(2)}, u32[]{:S(2)}) collective-permute-start(bf16[128,2560]{1,0:T(8,128)(2,1)S(1)} %pad_maximum_fusion.x0.refs_0_), channel_id=1, source_target_pairs={{0,1},{1,0},{2,3},{3,2},{4,5},{5,4},{6,7},{7,6},{8,9},{9,8},{10,11... | collective-permute-start | bytes 1966088 | tf_op jit(solution)/shard_map/ppermute | solution.py:59
  26.5 1.1 collective-permute-start.7
  27.7 0.9 collective-permute-start.6
  28.6 1.4 %collective-permute-start.14 = (bf16[128,1536]{1,0:T(8,128)(2,1)S(1)}, bf16[128,1536]{1,0:T(8,128)(2,1)S(1)}, u32[]{:S(2)}, u32[]{:S(2)}) collective-permute-start(bf16[128,1536]{1,0:T(8,128)(2,1)S(1)} %constant_dynamic-update-slice_fusion.refs_4_), channel_id=1, source_target_pairs={{0,32},{1,33},{2,34},{3,35},{4,36},{5,37},{6,38},{7,39},{8,40},{9,... | collective-permute-start | bytes 1179656 | tf_op jit(solution)/shard_map/ppermute | solution.py:59
  30.0 2.0 %collective-permute-start.13 = (bf16[128,1536]{1,0:T(8,128)(2,1)S(1)}, bf16[128,1536]{1,0:T(8,128)(2,1)S(1)}, u32[]{:S(2)}, u32[]{:S(2)}) collective-permute-start(bf16[128,1536]{1,0:T(8,128)(2,1)S(1)} %constant_dynamic-update-slice_fusion.refs_4_), channel_id=1, source_target_pairs={{0,48},{1,49},{2,50},{3,51},{4,52},{5,53},{6,54},{7,55},{8,56},{9,... | collective-permute-start | bytes 1179656 | tf_op jit(solution)/shard_map/ppermute | solution.py:59
  32.1 3.6 %collective-permute-done.8.x3.refs_3_ = bf16[128,2560]{1,0:T(8,128)(2,1)S(1)} collective-permute-done((bf16[128,2560]{1,0:T(8,128)(2,1)S(1)}, bf16[128,2560]{1,0:T(8,128)(2,1)S(1)}, u32[]{:S(2)}, u32[]{:S(2)}) %collective-permute-start.8) | collective-permute-done | bytes 655392 | tf_op jit(solution)/shard_map/ppermute | solution.py:59
  35.7 0.9 collective-permute-start.12
  36.6 1.5 %shard_map.78.early = f32[128,2048]{1,0:T(8,128)S(1)} custom-call(bf16[128,2560]{1,0:T(8,128)(2,1)S(1)} %pad_maximum_fusion.x0.refs_0_, bf16[2304,2048]{1,0:T(8,128)(2,1)S(1)} %copy-done.1), custom_call_target="tpu_custom_call" | custom-call | flops 1207959552 | bytes 9437184 | tf_op jit(solution)/shard_map/pallas_call | solution.py:224
  38.2 4.6 %collective-permute-done.7.x2.refs_2_ = bf16[128,2560]{1,0:T(8,128)(2,1)S(1)} collective-permute-done((bf16[128,2560]{1,0:T(8,128)(2,1)S(1)}, bf16[128,2560]{1,0:T(8,128)(2,1)S(1)}, u32[]{:S(2)}, u32[]{:S(2)}) %collective-permute-start.7) | collective-permute-done | bytes 655392 | tf_op jit(solution)/shard_map/ppermute | solution.py:59
  42.7 4.7 %shard_map.79 = (f32[256,2048]{1,0:T(8,128)S(1)}, f32[256,2048]{1,0:T(8,128)S(1)}) custom-call(s32[2,128]{1,0:T(2,128)S(1)} %get-tuple-element.50.places, f32[128,2048]{1,0:T(8,128)S(1)} %shard_map.78.early, bf16[128,2560]{1,0:T(8,128)(2,1)S(1)} %collective-permute-done.6.x1.refs_1_, bf16[128,2560]{1,0:T(8,128)(2,1)S(1)} %collective-permute-done.7.x2.refs_2_, ...), custom_call_target="tpu_custom_call" | custom-call | flops 3623878656 | bytes 9437184 | tf_op jit(solution)/shard_map/pallas_call | solution.py:235
  47.4 1.3 %collective-permute-done.13.refs_6_ = bf16[128,1536]{1,0:T(8,128)(2,1)S(1)} collective-permute-done((bf16[128,1536]{1,0:T(8,128)(2,1)S(1)}, bf16[128,1536]{1,0:T(8,128)(2,1)S(1)}, u32[]{:S(2)}, u32[]{:S(2)}) %collective-permute-start.13) | collective-permute-done | bytes 393248 | tf_op jit(solution)/shard_map/ppermute | solution.py:59
  48.8 4.0 %shard_map.80 = (f32[256,1536]{1,0:T(8,128)S(1)}, f32[256,1536]{1,0:T(8,128)S(1)}, bf16[512,1792]{1,0:T(8,128)(2,1)S(1)}) custom-call(bf16[512,512]{1,0:T(8,128)(2,1)S(1)} %get-tuple-element.53.main_order, bf16[512,512]{1,0:T(8,128)(2,1)S(1)} %get-tuple-element.54.apart_order, bf16[128,2560]{1,0:T(8,128)(2,1)S(1)} %pad_maximum_fusion.x0.refs_0_, ...), custom_call_target="tpu_custom_call" | custom-call | flops 2818572288 | bytes 7340032 | tf_op jit(solution)/shard_map/pallas_call | solution.py:250
  53.3 1.1 shard_map.81
  54.5 1.4 %shard_map.82 = (f32[256,2048]{1,0:T(8,128)S(1)}, f32[256,2048]{1,0:T(8,128)S(1)}, f32[256,128]{1,0:T(8,128)S(1)}) custom-call(f32[256,2048]{1,0:T(8,128)S(1)} %get-tuple-element.66.own, f32[256,2048]{1,0:T(8,128)S(1)} %collective-permute-done.15.other), custom_call_target="tpu_custom_call" | custom-call | flops 4194304 | bytes 8388608 | tf_op jit(solution)/shard_map/pallas_call | solution.py:294
  56.4 1.8 %shard_map.83 = (f32[256,1536]{1,0:T(8,128)S(1)}, f32[256,1536]{1,0:T(8,128)S(1)}, f32[2,256,128]{2,1,0:T(8,128)S(1)}) custom-call(f32[256,2048]{1,0:T(8,128)S(1)} %get-tuple-element.68.refs_0_.refs_2_, f32[256,2048]{1,0:T(8,128)S(1)} %get-tuple-element.69.refs_1_.refs_3_, f32[256,1536]{1,0:T(8,128)S(1)} %get-tuple-element.70.refs_2_, ...), custom_call_target="tpu_custom_call" | custom-call | flops 6291456 | bytes 9437184 | tf_op jit(solution)/shard_map/pallas_call | solution.py:340
  58.2 0.8 shard_map.84
  59.1 1.9 %collective-permute-start.20 = (f32[8,128]{1,0:T(8,128)S(1)}, f32[8,128]{1,0:T(8,128)S(1)}, u32[]{:S(2)}, u32[]{:S(2)}) collective-permute-start(f32[8,128]{1,0:T(8,128)S(1)} %get-tuple-element.76), channel_id=1, source_target_pairs={{0,1},{1,0},{2,3},{3,2},{4,5},{5,4},{6,7},{7,6},{8,9},{9,8},{10,11... | collective-permute-start | bytes 12296 | tf_op jit(solution)/shard_map/ppermute | solution.py:59
  61.0 1.4 %collective-permute-start.19 = (f32[8,128]{1,0:T(8,128)S(1)}, f32[8,128]{1,0:T(8,128)S(1)}, u32[]{:S(2)}, u32[]{:S(2)}) collective-permute-start(f32[8,128]{1,0:T(8,128)S(1)} %get-tuple-element.76), channel_id=1, source_target_pairs={{0,9},{1,8},{2,11},{3,10},{4,13},{5,12},{6,15},{7,14},{8,0},{9,1},... | collective-permute-start | bytes 12296 | tf_op jit(solution)/shard_map/ppermute | solution.py:59
  63.0 1.3 %collective-permute-done.20 = f32[8,128]{1,0:T(8,128)S(1)} collective-permute-done((f32[8,128]{1,0:T(8,128)S(1)}, f32[8,128]{1,0:T(8,128)S(1)}, u32[]{:S(2)}, u32[]{:S(2)}) %collective-permute-start.20) | collective-permute-done | bytes 4128 | tf_op jit(solution)/shard_map/ppermute | solution.py:59
  64.6 2.6 %collective-permute-done.18 = f32[8,128]{1,0:T(8,128)S(1)} collective-permute-done((f32[8,128]{1,0:T(8,128)S(1)}, f32[8,128]{1,0:T(8,128)S(1)}, u32[]{:S(2)}, u32[]{:S(2)}) %collective-permute-start.18) | collective-permute-done | bytes 4128 | tf_op jit(solution)/shard_map/ppermute | solution.py:59
  67.2 2.5 %collective-permute-start.23 = (f32[8,128]{1,0:T(8,128)S(1)}, f32[8,128]{1,0:T(8,128)S(1)}, u32[]{:S(2)}, u32[]{:S(2)}) collective-permute-start(f32[8,128]{1,0:T(8,128)S(1)} %add_add_fusion.2), channel_id=1, source_target_pairs={{0,32},{1,33},{2,34},{3,35},{4,36},{5,37},{6,38},{7,39},{8,40},{9,... | collective-permute-start | bytes 12296 | tf_op jit(solution)/shard_map/ppermute | solution.py:59
  69.7 1.2 %collective-permute-start.22 = (f32[8,128]{1,0:T(8,128)S(1)}, f32[8,128]{1,0:T(8,128)S(1)}, u32[]{:S(2)}, u32[]{:S(2)}) collective-permute-start(f32[8,128]{1,0:T(8,128)S(1)} %add_add_fusion.2), channel_id=1, source_target_pairs={{0,48},{1,49},{2,50},{3,51},{4,52},{5,53},{6,54},{7,55},{8,56},{9,... | collective-permute-start | bytes 12296 | tf_op jit(solution)/shard_map/ppermute | solution.py:59
  70.9 0.8 collective-permute-start.21
  72.3 1.0 collective-permute-done.22
  73.3 2.4 %collective-permute-done.21 = f32[8,128]{1,0:T(8,128)S(1)} collective-permute-done((f32[8,128]{1,0:T(8,128)S(1)}, f32[8,128]{1,0:T(8,128)S(1)}, u32[]{:S(2)}, u32[]{:S(2)}) %collective-permute-start.21) | collective-permute-done | bytes 4128 | tf_op jit(solution)/shard_map/ppermute | solution.py:59
  75.7 1.7 %collective-permute-start.26 = (f32[8,128]{1,0:T(8,128)S(1)}, f32[8,128]{1,0:T(8,128)S(1)}, u32[]{:S(2)}, u32[]{:S(2)}) collective-permute-start(f32[8,128]{1,0:T(8,128)S(1)} %add_add_fusion.1), channel_id=1, source_target_pairs={{0,4},{1,5},{2,6},{3,7},{4,0},{5,1},{6,2},{7,3},{8,12},{9,13},{10,... | collective-permute-start | bytes 12296 | tf_op jit(solution)/shard_map/ppermute | solution.py:59
  77.4 1.2 collective-permute-start.25
  78.6 0.8 collective-permute-start.24
  79.5 1.3 %collective-permute-done.26 = f32[8,128]{1,0:T(8,128)S(1)} collective-permute-done((f32[8,128]{1,0:T(8,128)S(1)}, f32[8,128]{1,0:T(8,128)S(1)}, u32[]{:S(2)}, u32[]{:S(2)}) %collective-permute-start.26) | collective-permute-done | bytes 4128 | tf_op jit(solution)/shard_map/ppermute | solution.py:59
  81.1 2.4 %collective-permute-done.24 = f32[8,128]{1,0:T(8,128)S(1)} collective-permute-done((f32[8,128]{1,0:T(8,128)S(1)}, f32[8,128]{1,0:T(8,128)S(1)}, u32[]{:S(2)}, u32[]{:S(2)}) %collective-permute-start.24) | collective-permute-done | bytes 4128 | tf_op jit(solution)/shard_map/ppermute | solution.py:59
  84.5 2.1 %shard_map.86.own = f32[256,1792]{1,0:T(8,128)S(1)} custom-call(bf16[256,2048]{1,0:T(8,128)(2,1)S(1)} %get-tuple-element.82.gap.own, bf16[1792,2048]{1,0:T(8,128)(2,1)S(1)} %bitcast.5), custom_call_target="tpu_custom_call" | custom-call | flops 1879048192 | bytes 7340032 | tf_op jit(solution)/shard_map/pallas_call | solution.py:398
  86.6 3.2 %shard_map.87 = (f32[128,1792]{1,0:T(8,128)S(1)}, bf16[128,1792]{1,0:T(8,128)(2,1)S(1)}, bf16[128,1792]{1,0:T(8,128)(2,1)S(1)}, bf16[128,1792]{1,0:T(8,128)(2,1)S(1)}) custom-call(s32[2,128]{1,0:T(2,128)S(1)} %get-tuple-element.50.places, f32[256,1792]{1,0:T(8,128)S(1)} %shard_map.86.own, bf16[256,2048]{1,0:T(8,128)(2,1)S(1)} %collective-permute-done.27.gap.other, ...), custom_call_target="tpu_custom_call" | custom-call | flops 1879048192 | bytes 7340032 | tf_op jit(solution)/shard_map/pallas_call | solution.py:421
  90.0 2.0 %collective-permute-start.30 = (bf16[128,1792]{1,0:T(8,128)(2,1)S(1)}, bf16[128,1792]{1,0:T(8,128)(2,1)S(1)}, u32[]{:S(2)}, u32[]{:S(2)}) collective-permute-start(bf16[128,1792]{1,0:T(8,128)(2,1)S(1)} %get-tuple-element.90), channel_id=1, source_target_pairs={{0,8},{1,9},{2,10},{3,11},{4,12},{5,13},{6,14},{7,15},{8,1},{9,0},... | collective-permute-start | bytes 1376264 | tf_op jit(solution)/shard_map/ppermute | solution.py:59
  91.9 0.8 collective-permute-start.31
  92.7 6.9 %shard_map.88 = bf16[1792,2048]{1,0:T(8,128)(2,1)} custom-call(bf16[512,1792]{1,0:T(8,128)(2,1)S(1)} %get-tuple-element.64.rows, bf16[256,2048]{1,0:T(8,128)(2,1)S(1)} %get-tuple-element.82.gap.own, bf16[256,2048]{1,0:T(8,128)(2,1)S(1)} %collective-permute-done.27.gap.other), custom_call_target="tpu_custom_call" | custom-call | flops 3758096384 | bytes 7340032 | tf_op jit(solution)/shard_map/pallas_call | solution.py:477
  99.6 4.9 %collective-permute-done.30.refs_1_ = bf16[128,1792]{1,0:T(8,128)(2,1)S(1)} collective-permute-done((bf16[128,1792]{1,0:T(8,128)(2,1)S(1)}, bf16[128,1792]{1,0:T(8,128)(2,1)S(1)}, u32[]{:S(2)}, u32[]{:S(2)}) %collective-permute-start.30) | collective-permute-done | bytes 458784 | tf_op jit(solution)/shard_map/ppermute | solution.py:59
  104.6 1.0 shard_map.89
  105.6 3.6 %all-to-all-start = ((bf16[16,8,1792]{2,1,0:T(8,128)(2,1)}), bf16[16,8,1792]{2,1,0:T(8,128)(2,1)S(1)}, u32[]{:S(2)}, u32[]{:S(2)}) async-start(bf16[16,8,1792]{2,1,0:T(8,128)(2,1)} %bitcast.2), calls=%async_computation | async-start | bytes 917504 | tf_op jit(solution)/shard_map/all_to_all | solution.py:539
  109.8 9.1 %all-to-all-done.received = bf16[16,8,1792]{2,1,0:T(8,128)(2,1)S(1)} async-done(((bf16[16,8,1792]{2,1,0:T(8,128)(2,1)}), bf16[16,8,1792]{2,1,0:T(8,128)(2,1)S(1)}, u32[]{:S(2)}, u32[]{:S(2)}) %all-to-all-start) | async-done | bytes 458784 | tf_op jit(solution)/shard_map/all_to_all | solution.py:539
  (61 shorter events, 8.7 us)
Async XLA Ops:
  0.6 0.8 copy-start.2
  1.4 0.7 copy-start.3
  2.2 9.4 %collective-permute-start.2 = (bf16[8,4096]{1,0:T(8,128)(2,1)S(1)}, bf16[8,4096]{1,0:T(8,128)(2,1)S(1)}, u32[]{:S(2)}, u32[]{:S(2)}) collective-permute-start(bf16[8,4096]{1,0:T(8,128)(2,1)S(1)} %shard_map.77), channel_id=1, source_target_pairs={{0,4},{1,5},{2,6},{3,7},{4,0},{5,1},{6,2},{7,3},{8,12},{9,13},{10,... | collective-permute-start | bytes 196616 | tf_op jit(solution)/shard_map/ppermute | solution.py:59
  5.6 6.0 %collective-permute-start.1 = (bf16[8,4096]{1,0:T(8,128)(2,1)S(1)}, bf16[8,4096]{1,0:T(8,128)(2,1)S(1)}, u32[]{:S(2)}, u32[]{:S(2)}) collective-permute-start(bf16[8,4096]{1,0:T(8,128)(2,1)S(1)} %shard_map.77), channel_id=1, source_target_pairs={{0,6},{1,7},{2,0},{3,1},{4,2},{5,3},{6,4},{7,5},{8,14},{9,15},{10,... | collective-permute-start | bytes 196616 | tf_op jit(solution)/shard_map/ppermute | solution.py:59
  6.6 5.5 %collective-permute-start = (bf16[8,4096]{1,0:T(8,128)(2,1)S(1)}, bf16[8,4096]{1,0:T(8,128)(2,1)S(1)}, u32[]{:S(2)}, u32[]{:S(2)}) collective-permute-start(bf16[8,4096]{1,0:T(8,128)(2,1)S(1)} %shard_map.77), channel_id=1, source_target_pairs={{0,2},{1,3},{2,4},{3,5},{4,6},{5,7},{6,0},{7,1},{8,10},{9,11},{10,... | collective-permute-start | bytes 196616 | tf_op jit(solution)/shard_map/ppermute | solution.py:59
  7.6 3.7 %copy-start = (bf16[2304,2048]{1,0:T(8,128)(2,1)S(1)}, bf16[2304,2048]{1,0:T(8,128)(2,1)}, u32[]{:S(2)}) copy-start(bf16[2304,2048]{1,0:T(8,128)(2,1)} %weight.6) | copy-start | bytes 28311556
  11.3 25.3 %copy-start.1 = (bf16[2304,2048]{1,0:T(8,128)(2,1)S(1)}, bf16[2304,2048]{1,0:T(8,128)(2,1)}, u32[]{:S(2)}) copy-start(bf16[2304,2048]{1,0:T(8,128)(2,1)} %weight.6) | copy-start | bytes 28311556
  12.2 10.2 %collective-permute-start.5 = (bf16[32,2560]{1,0:T(8,128)(2,1)S(1)}, bf16[32,2560]{1,0:T(8,128)(2,1)S(1)}, u32[]{:S(2)}, u32[]{:S(2)}) collective-permute-start(bf16[32,2560]{1,0:T(8,128)(2,1)S(1)} %slice.6), channel_id=1, source_target_pairs={{0,32},{1,33},{2,34},{3,35},{4,36},{5,37},{6,38},{7,39},{8,40},{9,... | collective-permute-start | bytes 491528 | tf_op jit(solution)/shard_map/ppermute | solution.py:59
  16.1 7.2 %collective-permute-start.4 = (bf16[32,2560]{1,0:T(8,128)(2,1)S(1)}, bf16[32,2560]{1,0:T(8,128)(2,1)S(1)}, u32[]{:S(2)}, u32[]{:S(2)}) collective-permute-start(bf16[32,2560]{1,0:T(8,128)(2,1)S(1)} %slice.6), channel_id=1, source_target_pairs={{0,48},{1,49},{2,50},{3,51},{4,52},{5,53},{6,54},{7,55},{8,56},{9,... | collective-permute-start | bytes 491528 | tf_op jit(solution)/shard_map/ppermute | solution.py:59
  16.8 6.5 %collective-permute-start.3 = (bf16[32,2560]{1,0:T(8,128)(2,1)S(1)}, bf16[32,2560]{1,0:T(8,128)(2,1)S(1)}, u32[]{:S(2)}, u32[]{:S(2)}) collective-permute-start(bf16[32,2560]{1,0:T(8,128)(2,1)S(1)} %slice.6), channel_id=1, source_target_pairs={{0,16},{1,17},{2,18},{3,19},{4,20},{5,21},{6,22},{7,23},{8,24},{9,... | collective-permute-start | bytes 491528 | tf_op jit(solution)/shard_map/ppermute | solution.py:59
  18.2 9.5 %collective-permute-start.11 = (bf16[32,1536]{1,0:T(8,128)(2,1)S(1)}, bf16[32,1536]{1,0:T(8,128)(2,1)S(1)}, u32[]{:S(2)}, u32[]{:S(2)}) collective-permute-start(bf16[32,1536]{1,0:T(8,128)(2,1)S(1)} %slice.7), channel_id=1, source_target_pairs={{0,1},{1,0},{2,3},{3,2},{4,5},{5,4},{6,7},{7,6},{8,9},{9,8},{10,11... | collective-permute-start | bytes 294920 | tf_op jit(solution)/shard_map/ppermute | solution.py:59
  21.3 7.3 %collective-permute-start.10 = (bf16[32,1536]{1,0:T(8,128)(2,1)S(1)}, bf16[32,1536]{1,0:T(8,128)(2,1)S(1)}, u32[]{:S(2)}, u32[]{:S(2)}) collective-permute-start(bf16[32,1536]{1,0:T(8,128)(2,1)S(1)} %slice.7), channel_id=1, source_target_pairs={{0,9},{1,8},{2,11},{3,10},{4,13},{5,12},{6,15},{7,14},{8,0},{9,1},... | collective-permute-start | bytes 294920 | tf_op jit(solution)/shard_map/ppermute | solution.py:59
  22.4 6.2 %collective-permute-start.9 = (bf16[32,1536]{1,0:T(8,128)(2,1)S(1)}, bf16[32,1536]{1,0:T(8,128)(2,1)S(1)}, u32[]{:S(2)}, u32[]{:S(2)}) collective-permute-start(bf16[32,1536]{1,0:T(8,128)(2,1)S(1)} %slice.7), channel_id=1, source_target_pairs={{0,8},{1,9},{2,10},{3,11},{4,12},{5,13},{6,14},{7,15},{8,1},{9,0},... | collective-permute-start | bytes 294920 | tf_op jit(solution)/shard_map/ppermute | solution.py:59
  23.4 12.3 %collective-permute-start.8 = (bf16[128,2560]{1,0:T(8,128)(2,1)S(1)}, bf16[128,2560]{1,0:T(8,128)(2,1)S(1)}, u32[]{:S(2)}, u32[]{:S(2)}) collective-permute-start(bf16[128,2560]{1,0:T(8,128)(2,1)S(1)} %pad_maximum_fusion.x0.refs_0_), channel_id=1, source_target_pairs={{0,1},{1,0},{2,3},{3,2},{4,5},{5,4},{6,7},{7,6},{8,9},{9,8},{10,11... | collective-permute-start | bytes 1966088 | tf_op jit(solution)/shard_map/ppermute | solution.py:59
  26.5 16.2 %collective-permute-start.7 = (bf16[128,2560]{1,0:T(8,128)(2,1)S(1)}, bf16[128,2560]{1,0:T(8,128)(2,1)S(1)}, u32[]{:S(2)}, u32[]{:S(2)}) collective-permute-start(bf16[128,2560]{1,0:T(8,128)(2,1)S(1)} %pad_maximum_fusion.x0.refs_0_), channel_id=1, source_target_pairs={{0,9},{1,8},{2,11},{3,10},{4,13},{5,12},{6,15},{7,14},{8,0},{9,1},... | collective-permute-start | bytes 1966088 | tf_op jit(solution)/shard_map/ppermute | solution.py:59
  27.7 15.1 %collective-permute-start.6 = (bf16[128,2560]{1,0:T(8,128)(2,1)S(1)}, bf16[128,2560]{1,0:T(8,128)(2,1)S(1)}, u32[]{:S(2)}, u32[]{:S(2)}) collective-permute-start(bf16[128,2560]{1,0:T(8,128)(2,1)S(1)} %pad_maximum_fusion.x0.refs_0_), channel_id=1, source_target_pairs={{0,8},{1,9},{2,10},{3,11},{4,12},{5,13},{6,14},{7,15},{8,1},{9,0},... | collective-permute-start | bytes 1966088 | tf_op jit(solution)/shard_map/ppermute | solution.py:59
  28.6 18.8 %collective-permute-start.14 = (bf16[128,1536]{1,0:T(8,128)(2,1)S(1)}, bf16[128,1536]{1,0:T(8,128)(2,1)S(1)}, u32[]{:S(2)}, u32[]{:S(2)}) collective-permute-start(bf16[128,1536]{1,0:T(8,128)(2,1)S(1)} %constant_dynamic-update-slice_fusion.refs_4_), channel_id=1, source_target_pairs={{0,32},{1,33},{2,34},{3,35},{4,36},{5,37},{6,38},{7,39},{8,40},{9,... | collective-permute-start | bytes 1179656 | tf_op jit(solution)/shard_map/ppermute | solution.py:59
  30.0 18.7 %collective-permute-start.13 = (bf16[128,1536]{1,0:T(8,128)(2,1)S(1)}, bf16[128,1536]{1,0:T(8,128)(2,1)S(1)}, u32[]{:S(2)}, u32[]{:S(2)}) collective-permute-start(bf16[128,1536]{1,0:T(8,128)(2,1)S(1)} %constant_dynamic-update-slice_fusion.refs_4_), channel_id=1, source_target_pairs={{0,48},{1,49},{2,50},{3,51},{4,52},{5,53},{6,54},{7,55},{8,56},{9,... | collective-permute-start | bytes 1179656 | tf_op jit(solution)/shard_map/ppermute | solution.py:59
  35.7 13.1 %collective-permute-start.12 = (bf16[128,1536]{1,0:T(8,128)(2,1)S(1)}, bf16[128,1536]{1,0:T(8,128)(2,1)S(1)}, u32[]{:S(2)}, u32[]{:S(2)}) collective-permute-start(bf16[128,1536]{1,0:T(8,128)(2,1)S(1)} %constant_dynamic-update-slice_fusion.refs_4_), channel_id=1, source_target_pairs={{0,16},{1,17},{2,18},{3,19},{4,20},{5,21},{6,22},{7,23},{8,24},{9,... | collective-permute-start | bytes 1179656 | tf_op jit(solution)/shard_map/ppermute | solution.py:59
  36.6 12.1 %slice-start = ((s8[7340032]{0:T(1024)(128)(4,1)}), s8[4194304]{0:T(1024)(128)(4,1)S(1)}, s32[]{:S(2)}) async-start(s8[7340032]{0:T(1024)(128)(4,1)} %bitcast.4), calls=%async_computation.1 | async-start | bytes 8388608
  38.2 10.6 %slice-start.1 = ((s8[7340032]{0:T(1024)(128)(4,1)}), s8[3145728]{0:T(1024)(128)(4,1)S(1)}, s32[]{:S(2)}) async-start(s8[7340032]{0:T(1024)(128)(4,1)} %bitcast.4), calls=%async_computation.2 | async-start | bytes 6291456
  48.8 5.8 %collective-permute-start.15 = (f32[256,2048]{1,0:T(8,128)S(1)}, f32[256,2048]{1,0:T(8,128)S(1)}, u32[]{:S(2)}, u32[]{:S(2)}) collective-permute-start(f32[256,2048]{1,0:T(8,128)S(1)} %get-tuple-element.67), channel_id=1, source_target_pairs={{0,64},{64,0},{1,65},{65,1},{2,66},{66,2},{3,67},{67,3},{4,68},{68... | collective-permute-start | bytes 6291464 | tf_op jit(solution)/shard_map/ppermute | solution.py:63
  52.8 3.6 %collective-permute-start.16 = (f32[256,1536]{1,0:T(8,128)S(1)}, f32[256,1536]{1,0:T(8,128)S(1)}, u32[]{:S(2)}, u32[]{:S(2)}) collective-permute-start(f32[256,1536]{1,0:T(8,128)S(1)} %get-tuple-element.71), channel_id=1, source_target_pairs={{0,64},{64,0},{1,65},{65,1},{2,66},{66,2},{3,67},{67,3},{4,68},{68... | collective-permute-start | bytes 4718600 | tf_op jit(solution)/shard_map/ppermute | solution.py:63
  54.4 3.8 %collective-permute-start.17 = (f32[256,512]{1,0:T(8,128)S(1)}, f32[256,512]{1,0:T(8,128)S(1)}, u32[]{:S(2)}, u32[]{:S(2)}) collective-permute-start(f32[256,512]{1,0:T(8,128)S(1)} %get-tuple-element.75), channel_id=1, source_target_pairs={{0,64},{64,0},{1,65},{65,1},{2,66},{66,2},{3,67},{67,3},{4,68},{68... | collective-permute-start | bytes 1572872 | tf_op jit(solution)/shard_map/ppermute | solution.py:63
  58.2 25.3 %copy-start.4 = (f32[512]{0:T(512)S(1)}, f32[512]{0:T(512)}, u32[]{:S(2)}) copy-start(f32[512]{0:T(512)} %param.9) | copy-start | bytes 6148
  59.1 5.2 %collective-permute-start.20 = (f32[8,128]{1,0:T(8,128)S(1)}, f32[8,128]{1,0:T(8,128)S(1)}, u32[]{:S(2)}, u32[]{:S(2)}) collective-permute-start(f32[8,128]{1,0:T(8,128)S(1)} %get-tuple-element.76), channel_id=1, source_target_pairs={{0,1},{1,0},{2,3},{3,2},{4,5},{5,4},{6,7},{7,6},{8,9},{9,8},{10,11... | collective-permute-start | bytes 12296 | tf_op jit(solution)/shard_map/ppermute | solution.py:59
  61.0 3.6 %collective-permute-start.19 = (f32[8,128]{1,0:T(8,128)S(1)}, f32[8,128]{1,0:T(8,128)S(1)}, u32[]{:S(2)}, u32[]{:S(2)}) collective-permute-start(f32[8,128]{1,0:T(8,128)S(1)} %get-tuple-element.76), channel_id=1, source_target_pairs={{0,9},{1,8},{2,11},{3,10},{4,13},{5,12},{6,15},{7,14},{8,0},{9,1},... | collective-permute-start | bytes 12296 | tf_op jit(solution)/shard_map/ppermute | solution.py:59
  62.3 4.8 %collective-permute-start.18 = (f32[8,128]{1,0:T(8,128)S(1)}, f32[8,128]{1,0:T(8,128)S(1)}, u32[]{:S(2)}, u32[]{:S(2)}) collective-permute-start(f32[8,128]{1,0:T(8,128)S(1)} %get-tuple-element.76), channel_id=1, source_target_pairs={{0,8},{1,9},{2,10},{3,11},{4,12},{5,13},{6,14},{7,15},{8,1},{9,0},... | collective-permute-start | bytes 12296 | tf_op jit(solution)/shard_map/ppermute | solution.py:59
  67.2 5.1 %collective-permute-start.23 = (f32[8,128]{1,0:T(8,128)S(1)}, f32[8,128]{1,0:T(8,128)S(1)}, u32[]{:S(2)}, u32[]{:S(2)}) collective-permute-start(f32[8,128]{1,0:T(8,128)S(1)} %add_add_fusion.2), channel_id=1, source_target_pairs={{0,32},{1,33},{2,34},{3,35},{4,36},{5,37},{6,38},{7,39},{8,40},{9,... | collective-permute-start | bytes 12296 | tf_op jit(solution)/shard_map/ppermute | solution.py:59
  69.7 3.6 %collective-permute-start.22 = (f32[8,128]{1,0:T(8,128)S(1)}, f32[8,128]{1,0:T(8,128)S(1)}, u32[]{:S(2)}, u32[]{:S(2)}) collective-permute-start(f32[8,128]{1,0:T(8,128)S(1)} %add_add_fusion.2), channel_id=1, source_target_pairs={{0,48},{1,49},{2,50},{3,51},{4,52},{5,53},{6,54},{7,55},{8,56},{9,... | collective-permute-start | bytes 12296 | tf_op jit(solution)/shard_map/ppermute | solution.py:59
  70.9 4.8 %collective-permute-start.21 = (f32[8,128]{1,0:T(8,128)S(1)}, f32[8,128]{1,0:T(8,128)S(1)}, u32[]{:S(2)}, u32[]{:S(2)}) collective-permute-start(f32[8,128]{1,0:T(8,128)S(1)} %add_add_fusion.2), channel_id=1, source_target_pairs={{0,16},{1,17},{2,18},{3,19},{4,20},{5,21},{6,22},{7,23},{8,24},{9,... | collective-permute-start | bytes 12296 | tf_op jit(solution)/shard_map/ppermute | solution.py:59
  75.7 5.1 %collective-permute-start.26 = (f32[8,128]{1,0:T(8,128)S(1)}, f32[8,128]{1,0:T(8,128)S(1)}, u32[]{:S(2)}, u32[]{:S(2)}) collective-permute-start(f32[8,128]{1,0:T(8,128)S(1)} %add_add_fusion.1), channel_id=1, source_target_pairs={{0,4},{1,5},{2,6},{3,7},{4,0},{5,1},{6,2},{7,3},{8,12},{9,13},{10,... | collective-permute-start | bytes 12296 | tf_op jit(solution)/shard_map/ppermute | solution.py:59
  77.4 3.6 %collective-permute-start.25 = (f32[8,128]{1,0:T(8,128)S(1)}, f32[8,128]{1,0:T(8,128)S(1)}, u32[]{:S(2)}, u32[]{:S(2)}) collective-permute-start(f32[8,128]{1,0:T(8,128)S(1)} %add_add_fusion.1), channel_id=1, source_target_pairs={{0,6},{1,7},{2,0},{3,1},{4,2},{5,3},{6,4},{7,5},{8,14},{9,15},{10,... | collective-permute-start | bytes 12296 | tf_op jit(solution)/shard_map/ppermute | solution.py:59
  78.6 4.8 %collective-permute-start.24 = (f32[8,128]{1,0:T(8,128)S(1)}, f32[8,128]{1,0:T(8,128)S(1)}, u32[]{:S(2)}, u32[]{:S(2)}) collective-permute-start(f32[8,128]{1,0:T(8,128)S(1)} %add_add_fusion.1), channel_id=1, source_target_pairs={{0,2},{1,3},{2,4},{3,5},{4,6},{5,7},{6,0},{7,1},{8,10},{9,11},{10,... | collective-permute-start | bytes 12296 | tf_op jit(solution)/shard_map/ppermute | solution.py:59
  83.9 2.7 %collective-permute-start.27 = (bf16[256,2048]{1,0:T(8,128)(2,1)S(1)}, bf16[256,2048]{1,0:T(8,128)(2,1)S(1)}, u32[]{:S(2)}, u32[]{:S(2)}) collective-permute-start(bf16[256,2048]{1,0:T(8,128)(2,1)S(1)} %get-tuple-element.82.gap.own), channel_id=1, source_target_pairs={{0,64},{64,0},{1,65},{65,1},{2,66},{66,2},{3,67},{67,3},{4,68},{68... | collective-permute-start | bytes 3145736 | tf_op jit(solution)/shard_map/ppermute | solution.py:63
  84.0 2.6 %collective-permute-start.28 = (f32[2,128]{1,0:T(2,128)S(1)}, f32[2,128]{1,0:T(2,128)S(1)}, u32[]{:S(2)}, u32[]{:S(2)}) collective-permute-start(f32[2,128]{1,0:T(2,128)S(1)} %get-tuple-element.81), channel_id=1, source_target_pairs={{0,64},{64,0},{1,65},{65,1},{2,66},{66,2},{3,67},{67,3},{4,68},{68... | collective-permute-start | bytes 3080 | tf_op jit(solution)/shard_map/ppermute | solution.py:63
  89.8 9.8 %collective-permute-start.29 = (bf16[128,1792]{1,0:T(8,128)(2,1)S(1)}, bf16[128,1792]{1,0:T(8,128)(2,1)S(1)}, u32[]{:S(2)}, u32[]{:S(2)}) collective-permute-start(bf16[128,1792]{1,0:T(8,128)(2,1)S(1)} %get-tuple-element.89), channel_id=1, source_target_pairs={{0,9},{1,8},{2,11},{3,10},{4,13},{5,12},{6,15},{7,14},{8,0},{9,1},... | collective-permute-start | bytes 1376264 | tf_op jit(solution)/shard_map/ppermute | solution.py:59
  90.0 14.6 %collective-permute-start.30 = (bf16[128,1792]{1,0:T(8,128)(2,1)S(1)}, bf16[128,1792]{1,0:T(8,128)(2,1)S(1)}, u32[]{:S(2)}, u32[]{:S(2)}) collective-permute-start(bf16[128,1792]{1,0:T(8,128)(2,1)S(1)} %get-tuple-element.90), channel_id=1, source_target_pairs={{0,8},{1,9},{2,10},{3,11},{4,12},{5,13},{6,14},{7,15},{8,1},{9,0},... | collective-permute-start | bytes 1376264 | tf_op jit(solution)/shard_map/ppermute | solution.py:59
  91.9 12.7 %collective-permute-start.31 = (bf16[128,1792]{1,0:T(8,128)(2,1)S(1)}, bf16[128,1792]{1,0:T(8,128)(2,1)S(1)}, u32[]{:S(2)}, u32[]{:S(2)}) collective-permute-start(bf16[128,1792]{1,0:T(8,128)(2,1)S(1)} %get-tuple-element.91), channel_id=1, source_target_pairs={{0,1},{1,0},{2,3},{3,2},{4,5},{5,4},{6,7},{7,6},{8,9},{9,8},{10,11... | collective-permute-start | bytes 1376264 | tf_op jit(solution)/shard_map/ppermute | solution.py:59
  105.6 13.3 %all-to-all-start = ((bf16[16,8,1792]{2,1,0:T(8,128)(2,1)}), bf16[16,8,1792]{2,1,0:T(8,128)(2,1)S(1)}, u32[]{:S(2)}, u32[]{:S(2)}) async-start(bf16[16,8,1792]{2,1,0:T(8,128)(2,1)} %bitcast.2), calls=%async_computation | async-start | bytes 917504 | tf_op jit(solution)/shard_map/all_to_all | solution.py:539

commit v8 on v7

--- a/solution.py
+++ b/solution.py
@@ -507,7 +507,7 @@
     teacher_own, teacher_other = teacher_logits(places, early, main[1:], teacher_weight)
     teacher_other, *separate = lax.optimization_barrier((teacher_other, *separate))
     teacher_other = swap(teacher_other)
-    cols = 1536
+    cols = 1024
     own0, other0, rows = student_logits(
         main_order, apart_order, main, separate, student_weight, cols
     )

time: 120 us -> 120 us (level)
  transfers between devices with their start and end apart: 33 -> 33, of which waited for: 18 -> 17; matrix products, arithmetic and copies ran while one was open for 1% -> 1% of each run, Pallas kernels for 20% -> 19%
where the time goes in v8:
time: 120 us; the launch traced here: 119 us
  starting transfers between devices  45.8 us (38%)
  waiting for transfers between devices  36.7 us (31%)
  Pallas kernels  30 us (25%)
  local copies, waits for them, and re-layouts  5.26 us (4%)
    ppermute x27, starting transfers between devices, send(): return lax.ppermute(block, everyone, ring(axes, by))  40.8 us
    ppermute x27, waiting for transfers between devices, send(): return lax.ppermute(block, everyone, ring(axes, by))  27.6 us
    all_to_all x1, waiting for transfers between devices, local(): total = lax.all_to_all(total, everyone, 0, 0, axis_index_groups=planes())  9.11 us
    pallas_call x1, Pallas kernels, grad_weight_of(): pl.pallas_call(grad_weight_kernel, grid=(student_width // tile,), in_spec...  6.91 us
    unnamed x17, local copies, waits for them, and re-layouts  5.23 us
    pallas_call x1, Pallas kernels, teacher_logits(): pl.pallas_call(teacher_kernel, in_specs=[scalars()] + [whole()] * 5, out_...  4.67 us
    all_to_all x1, starting transfers between devices, local(): total = lax.all_to_all(total, everyone, 0, 0, axis_index_groups=planes())  3.56 us
    pallas_call x1, Pallas kernels, hidden_all(): pl.pallas_call(hidden_all_kernel, in_specs=[scalars()] + [whole()] * 3, o...  3.18 us
  transfers between devices with their start and end apart: 33, of which 17 were waited for; matrix products, arithmetic and copies ran while one was open for 1% of the time, Pallas kernels for 19%

profile of v8, /device:TPU:0, one launch (start us, length us, event | category | flops | bytes accessed | tf_op | source)
XLA Modules:
  0.0 119.4 jit_solution(2245563771318219175)
XLA Ops:
  0.6 0.8 copy-done.2
  2.2 3.4 %collective-permute-start.2 = (bf16[8,4096]{1,0:T(8,128)(2,1)S(1)}, bf16[8,4096]{1,0:T(8,128)(2,1)S(1)}, u32[]{:S(2)}, u32[]{:S(2)}) collective-permute-start(bf16[8,4096]{1,0:T(8,128)(2,1)S(1)} %shard_map.77), channel_id=1, source_target_pairs={{0,4},{1,5},{2,6},{3,7},{4,0},{5,1},{6,2},{7,3},{8,12},{9,13},{10,... | collective-permute-start | bytes 196616 | tf_op jit(solution)/shard_map/ppermute | solution.py:59
  5.6 1.1 collective-permute-start.1
  6.6 1.0 collective-permute-start
  7.6 3.7 %copy-done = bf16[2304,2048]{1,0:T(8,128)(2,1)S(1)} copy-done((bf16[2304,2048]{1,0:T(8,128)(2,1)S(1)}, bf16[2304,2048]{1,0:T(8,128)(2,1)}, u32[]{:S(2)}) %copy-start) | copy-done | bytes 9437208
  12.2 4.0 %collective-permute-start.5 = (bf16[32,2560]{1,0:T(8,128)(2,1)S(1)}, bf16[32,2560]{1,0:T(8,128)(2,1)S(1)}, u32[]{:S(2)}, u32[]{:S(2)}) collective-permute-start(bf16[32,2560]{1,0:T(8,128)(2,1)S(1)} %slice.6), channel_id=1, source_target_pairs={{0,32},{1,33},{2,34},{3,35},{4,36},{5,37},{6,38},{7,39},{8,40},{9,... | collective-permute-start | bytes 491528 | tf_op jit(solution)/shard_map/ppermute | solution.py:59
  16.8 1.3 %collective-permute-start.3 = (bf16[32,2560]{1,0:T(8,128)(2,1)S(1)}, bf16[32,2560]{1,0:T(8,128)(2,1)S(1)}, u32[]{:S(2)}, u32[]{:S(2)}) collective-permute-start(bf16[32,2560]{1,0:T(8,128)(2,1)S(1)} %slice.6), channel_id=1, source_target_pairs={{0,16},{1,17},{2,18},{3,19},{4,20},{5,21},{6,22},{7,23},{8,24},{9,... | collective-permute-start | bytes 491528 | tf_op jit(solution)/shard_map/ppermute | solution.py:59
  18.2 3.1 %collective-permute-start.11 = (bf16[32,1536]{1,0:T(8,128)(2,1)S(1)}, bf16[32,1536]{1,0:T(8,128)(2,1)S(1)}, u32[]{:S(2)}, u32[]{:S(2)}) collective-permute-start(bf16[32,1536]{1,0:T(8,128)(2,1)S(1)} %slice.7), channel_id=1, source_target_pairs={{0,1},{1,0},{2,3},{3,2},{4,5},{5,4},{6,7},{7,6},{8,9},{9,8},{10,11... | collective-permute-start | bytes 294920 | tf_op jit(solution)/shard_map/ppermute | solution.py:59
  21.3 1.1 collective-permute-start.10
  22.4 0.9 collective-permute-start.9
  23.4 3.1 %collective-permute-start.8 = (bf16[128,2560]{1,0:T(8,128)(2,1)S(1)}, bf16[128,2560]{1,0:T(8,128)(2,1)S(1)}, u32[]{:S(2)}, u32[]{:S(2)}) collective-permute-start(bf16[128,2560]{1,0:T(8,128)(2,1)S(1)} %pad_maximum_fusion.x0.refs_0_), channel_id=1, source_target_pairs={{0,1},{1,0},{2,3},{3,2},{4,5},{5,4},{6,7},{7,6},{8,9},{9,8},{10,11... | collective-permute-start | bytes 1966088 | tf_op jit(solution)/shard_map/ppermute | solution.py:59
  26.5 1.1 collective-permute-start.7
  27.7 0.9 collective-permute-start.6
  28.6 1.4 %collective-permute-start.14 = (bf16[128,1536]{1,0:T(8,128)(2,1)S(1)}, bf16[128,1536]{1,0:T(8,128)(2,1)S(1)}, u32[]{:S(2)}, u32[]{:S(2)}) collective-permute-start(bf16[128,1536]{1,0:T(8,128)(2,1)S(1)} %constant_dynamic-update-slice_fusion.refs_4_), channel_id=1, source_target_pairs={{0,32},{1,33},{2,34},{3,35},{4,36},{5,37},{6,38},{7,39},{8,40},{9,... | collective-permute-start | bytes 1179656 | tf_op jit(solution)/shard_map/ppermute | solution.py:59
  30.0 2.0 %collective-permute-start.13 = (bf16[128,1536]{1,0:T(8,128)(2,1)S(1)}, bf16[128,1536]{1,0:T(8,128)(2,1)S(1)}, u32[]{:S(2)}, u32[]{:S(2)}) collective-permute-start(bf16[128,1536]{1,0:T(8,128)(2,1)S(1)} %constant_dynamic-update-slice_fusion.refs_4_), channel_id=1, source_target_pairs={{0,48},{1,49},{2,50},{3,51},{4,52},{5,53},{6,54},{7,55},{8,56},{9,... | collective-permute-start | bytes 1179656 | tf_op jit(solution)/shard_map/ppermute | solution.py:59
  32.1 3.6 %collective-permute-done.8.x3.refs_3_ = bf16[128,2560]{1,0:T(8,128)(2,1)S(1)} collective-permute-done((bf16[128,2560]{1,0:T(8,128)(2,1)S(1)}, bf16[128,2560]{1,0:T(8,128)(2,1)S(1)}, u32[]{:S(2)}, u32[]{:S(2)}) %collective-permute-start.8) | collective-permute-done | bytes 655392 | tf_op jit(solution)/shard_map/ppermute | solution.py:59
  35.7 0.9 collective-permute-start.12
  36.6 1.5 %shard_map.78.early = f32[128,2048]{1,0:T(8,128)S(1)} custom-call(bf16[128,2560]{1,0:T(8,128)(2,1)S(1)} %pad_maximum_fusion.x0.refs_0_, bf16[2304,2048]{1,0:T(8,128)(2,1)S(1)} %copy-done.1), custom_call_target="tpu_custom_call" | custom-call | flops 1207959552 | bytes 9437184 | tf_op jit(solution)/shard_map/pallas_call | solution.py:224
  38.2 4.6 %collective-permute-done.7.x2.refs_2_ = bf16[128,2560]{1,0:T(8,128)(2,1)S(1)} collective-permute-done((bf16[128,2560]{1,0:T(8,128)(2,1)S(1)}, bf16[128,2560]{1,0:T(8,128)(2,1)S(1)}, u32[]{:S(2)}, u32[]{:S(2)}) %collective-permute-start.7) | collective-permute-done | bytes 655392 | tf_op jit(solution)/shard_map/ppermute | solution.py:59
  42.7 4.7 %shard_map.79 = (f32[256,2048]{1,0:T(8,128)S(1)}, f32[256,2048]{1,0:T(8,128)S(1)}) custom-call(s32[2,128]{1,0:T(2,128)S(1)} %get-tuple-element.50.places, f32[128,2048]{1,0:T(8,128)S(1)} %shard_map.78.early, bf16[128,2560]{1,0:T(8,128)(2,1)S(1)} %collective-permute-done.6.x1.refs_1_, bf16[128,2560]{1,0:T(8,128)(2,1)S(1)} %collective-permute-done.7.x2.refs_2_, ...), custom_call_target="tpu_custom_call" | custom-call | flops 3623878656 | bytes 9437184 | tf_op jit(solution)/shard_map/pallas_call | solution.py:235
  47.4 1.3 %collective-permute-done.13.refs_6_ = bf16[128,1536]{1,0:T(8,128)(2,1)S(1)} collective-permute-done((bf16[128,1536]{1,0:T(8,128)(2,1)S(1)}, bf16[128,1536]{1,0:T(8,128)(2,1)S(1)}, u32[]{:S(2)}, u32[]{:S(2)}) %collective-permute-start.13) | collective-permute-done | bytes 393248 | tf_op jit(solution)/shard_map/ppermute | solution.py:59
  48.8 3.0 %shard_map.80 = (f32[256,1024]{1,0:T(8,128)S(1)}, f32[256,1024]{1,0:T(8,128)S(1)}, bf16[512,1792]{1,0:T(8,128)(2,1)S(1)}) custom-call(bf16[512,512]{1,0:T(8,128)(2,1)S(1)} %get-tuple-element.53.main_order, bf16[512,512]{1,0:T(8,128)(2,1)S(1)} %get-tuple-element.54.apart_order, bf16[128,2560]{1,0:T(8,128)(2,1)S(1)} %pad_maximum_fusion.x0.refs_0_, ...), custom_call_target="tpu_custom_call" | custom-call | flops 1879048192 | bytes 7340032 | tf_op jit(solution)/shard_map/pallas_call | solution.py:250
  52.6 2.1 %shard_map.81 = (f32[256,1024]{1,0:T(8,128)S(1)}, f32[256,1024]{1,0:T(8,128)S(1)}) custom-call(bf16[512,1792]{1,0:T(8,128)(2,1)S(1)} %get-tuple-element.64.rows, bf16[1792,2048]{1,0:T(8,128)(2,1)S(1)} %bitcast.5), custom_call_target="tpu_custom_call" | custom-call | flops 1879048192 | bytes 7340032 | tf_op jit(solution)/shard_map/pallas_call | solution.py:261
  54.7 1.4 %shard_map.82 = (f32[256,2048]{1,0:T(8,128)S(1)}, f32[256,2048]{1,0:T(8,128)S(1)}, f32[256,128]{1,0:T(8,128)S(1)}) custom-call(f32[256,2048]{1,0:T(8,128)S(1)} %get-tuple-element.66.own, f32[256,2048]{1,0:T(8,128)S(1)} %collective-permute-done.15.other), custom_call_target="tpu_custom_call" | custom-call | flops 4194304 | bytes 8388608 | tf_op jit(solution)/shard_map/pallas_call | solution.py:294
  56.1 1.3 %shard_map.83 = (f32[256,1024]{1,0:T(8,128)S(1)}, f32[256,1024]{1,0:T(8,128)S(1)}, f32[2,256,128]{2,1,0:T(8,128)S(1)}) custom-call(f32[256,2048]{1,0:T(8,128)S(1)} %get-tuple-element.68.refs_0_.refs_2_, f32[256,2048]{1,0:T(8,128)S(1)} %get-tuple-element.69.refs_1_.refs_3_, f32[256,1024]{1,0:T(8,128)S(1)} %get-tuple-element.70.refs_2_, ...), custom_call_target="tpu_custom_call" | custom-call | flops 4194304 | bytes 6291456 | tf_op jit(solution)/shard_map/pallas_call | solution.py:340
  57.4 1.4 %shard_map.84 = (f32[256,1024]{1,0:T(8,128)S(1)}, f32[256,1024]{1,0:T(8,128)S(1)}, f32[8,128]{1,0:T(8,128)S(1)}) custom-call(f32[2,256,128]{2,1,0:T(8,128)S(1)} %get-tuple-element.72.refs_0_, f32[256,128]{1,0:T(8,128)S(1)} %get-tuple-element.73.refs_1_, f32[256,2048]{1,0:T(8,128)S(1)} %get-tuple-element.68.refs_0_.refs_2_, ...), custom_call_target="tpu_custom_call" | custom-call | flops 4194304 | bytes 6291456 | tf_op jit(solution)/shard_map/pallas_call | solution.py:340
  58.9 1.7 %collective-permute-start.20 = (f32[8,128]{1,0:T(8,128)S(1)}, f32[8,128]{1,0:T(8,128)S(1)}, u32[]{:S(2)}, u32[]{:S(2)}) collective-permute-start(f32[8,128]{1,0:T(8,128)S(1)} %get-tuple-element.76), channel_id=1, source_target_pairs={{0,1},{1,0},{2,3},{3,2},{4,5},{5,4},{6,7},{7,6},{8,9},{9,8},{10,11... | collective-permute-start | bytes 12296 | tf_op jit(solution)/shard_map/ppermute | solution.py:59
  60.6 1.5 %collective-permute-start.19 = (f32[8,128]{1,0:T(8,128)S(1)}, f32[8,128]{1,0:T(8,128)S(1)}, u32[]{:S(2)}, u32[]{:S(2)}) collective-permute-start(f32[8,128]{1,0:T(8,128)S(1)} %get-tuple-element.76), channel_id=1, source_target_pairs={{0,9},{1,8},{2,11},{3,10},{4,13},{5,12},{6,15},{7,14},{8,0},{9,1},... | collective-permute-start | bytes 12296 | tf_op jit(solution)/shard_map/ppermute | solution.py:59
  62.6 1.4 %collective-permute-done.20 = f32[8,128]{1,0:T(8,128)S(1)} collective-permute-done((f32[8,128]{1,0:T(8,128)S(1)}, f32[8,128]{1,0:T(8,128)S(1)}, u32[]{:S(2)}, u32[]{:S(2)}) %collective-permute-start.20) | collective-permute-done | bytes 4128 | tf_op jit(solution)/shard_map/ppermute | solution.py:59
  64.2 2.8 %collective-permute-done.18 = f32[8,128]{1,0:T(8,128)S(1)} collective-permute-done((f32[8,128]{1,0:T(8,128)S(1)}, f32[8,128]{1,0:T(8,128)S(1)}, u32[]{:S(2)}, u32[]{:S(2)}) %collective-permute-start.18) | collective-permute-done | bytes 4128 | tf_op jit(solution)/shard_map/ppermute | solution.py:59
  67.0 2.5 %collective-permute-start.23 = (f32[8,128]{1,0:T(8,128)S(1)}, f32[8,128]{1,0:T(8,128)S(1)}, u32[]{:S(2)}, u32[]{:S(2)}) collective-permute-start(f32[8,128]{1,0:T(8,128)S(1)} %add_add_fusion.2), channel_id=1, source_target_pairs={{0,32},{1,33},{2,34},{3,35},{4,36},{5,37},{6,38},{7,39},{8,40},{9,... | collective-permute-start | bytes 12296 | tf_op jit(solution)/shard_map/ppermute | solution.py:59
  69.5 1.2 %collective-permute-start.22 = (f32[8,128]{1,0:T(8,128)S(1)}, f32[8,128]{1,0:T(8,128)S(1)}, u32[]{:S(2)}, u32[]{:S(2)}) collective-permute-start(f32[8,128]{1,0:T(8,128)S(1)} %add_add_fusion.2), channel_id=1, source_target_pairs={{0,48},{1,49},{2,50},{3,51},{4,52},{5,53},{6,54},{7,55},{8,56},{9,... | collective-permute-start | bytes 12296 | tf_op jit(solution)/shard_map/ppermute | solution.py:59
  70.7 0.8 collective-permute-start.21
  72.1 1.0 collective-permute-done.22
  73.1 2.4 %collective-permute-done.21 = f32[8,128]{1,0:T(8,128)S(1)} collective-permute-done((f32[8,128]{1,0:T(8,128)S(1)}, f32[8,128]{1,0:T(8,128)S(1)}, u32[]{:S(2)}, u32[]{:S(2)}) %collective-permute-start.21) | collective-permute-done | bytes 4128 | tf_op jit(solution)/shard_map/ppermute | solution.py:59
  75.5 1.6 %collective-permute-start.26 = (f32[8,128]{1,0:T(8,128)S(1)}, f32[8,128]{1,0:T(8,128)S(1)}, u32[]{:S(2)}, u32[]{:S(2)}) collective-permute-start(f32[8,128]{1,0:T(8,128)S(1)} %add_add_fusion.1), channel_id=1, source_target_pairs={{0,4},{1,5},{2,6},{3,7},{4,0},{5,1},{6,2},{7,3},{8,12},{9,13},{10,... | collective-permute-start | bytes 12296 | tf_op jit(solution)/shard_map/ppermute | solution.py:59
  77.1 1.4 %collective-permute-start.25 = (f32[8,128]{1,0:T(8,128)S(1)}, f32[8,128]{1,0:T(8,128)S(1)}, u32[]{:S(2)}, u32[]{:S(2)}) collective-permute-start(f32[8,128]{1,0:T(8,128)S(1)} %add_add_fusion.1), channel_id=1, source_target_pairs={{0,6},{1,7},{2,0},{3,1},{4,2},{5,3},{6,4},{7,5},{8,14},{9,15},{10,... | collective-permute-start | bytes 12296 | tf_op jit(solution)/shard_map/ppermute | solution.py:59
  79.1 1.5 %collective-permute-done.26 = f32[8,128]{1,0:T(8,128)S(1)} collective-permute-done((f32[8,128]{1,0:T(8,128)S(1)}, f32[8,128]{1,0:T(8,128)S(1)}, u32[]{:S(2)}, u32[]{:S(2)}) %collective-permute-start.26) | collective-permute-done | bytes 4128 | tf_op jit(solution)/shard_map/ppermute | solution.py:59
  80.7 2.6 %collective-permute-done.24 = f32[8,128]{1,0:T(8,128)S(1)} collective-permute-done((f32[8,128]{1,0:T(8,128)S(1)}, f32[8,128]{1,0:T(8,128)S(1)}, u32[]{:S(2)}, u32[]{:S(2)}) %collective-permute-start.24) | collective-permute-done | bytes 4128 | tf_op jit(solution)/shard_map/ppermute | solution.py:59
  84.3 2.1 %shard_map.86.own = f32[256,1792]{1,0:T(8,128)S(1)} custom-call(bf16[256,2048]{1,0:T(8,128)(2,1)S(1)} %get-tuple-element.82.gap.own, bf16[1792,2048]{1,0:T(8,128)(2,1)S(1)} %bitcast.5), custom_call_target="tpu_custom_call" | custom-call | flops 1879048192 | bytes 7340032 | tf_op jit(solution)/shard_map/pallas_call | solution.py:398
  86.5 3.2 %shard_map.87 = (f32[128,1792]{1,0:T(8,128)S(1)}, bf16[128,1792]{1,0:T(8,128)(2,1)S(1)}, bf16[128,1792]{1,0:T(8,128)(2,1)S(1)}, bf16[128,1792]{1,0:T(8,128)(2,1)S(1)}) custom-call(s32[2,128]{1,0:T(2,128)S(1)} %get-tuple-element.50.places, f32[256,1792]{1,0:T(8,128)S(1)} %shard_map.86.own, bf16[256,2048]{1,0:T(8,128)(2,1)S(1)} %collective-permute-done.27.gap.other, ...), custom_call_target="tpu_custom_call" | custom-call | flops 1879048192 | bytes 7340032 | tf_op jit(solution)/shard_map/pallas_call | solution.py:421
  89.8 1.9 %collective-permute-start.30 = (bf16[128,1792]{1,0:T(8,128)(2,1)S(1)}, bf16[128,1792]{1,0:T(8,128)(2,1)S(1)}, u32[]{:S(2)}, u32[]{:S(2)}) collective-permute-start(bf16[128,1792]{1,0:T(8,128)(2,1)S(1)} %get-tuple-element.90), channel_id=1, source_target_pairs={{0,8},{1,9},{2,10},{3,11},{4,12},{5,13},{6,14},{7,15},{8,1},{9,0},... | collective-permute-start | bytes 1376264 | tf_op jit(solution)/shard_map/ppermute | solution.py:59
  91.8 0.8 collective-permute-start.31
  92.6 6.9 %shard_map.88 = bf16[1792,2048]{1,0:T(8,128)(2,1)} custom-call(bf16[512,1792]{1,0:T(8,128)(2,1)S(1)} %get-tuple-element.64.rows, bf16[256,2048]{1,0:T(8,128)(2,1)S(1)} %get-tuple-element.82.gap.own, bf16[256,2048]{1,0:T(8,128)(2,1)S(1)} %collective-permute-done.27.gap.other), custom_call_target="tpu_custom_call" | custom-call | flops 3758096384 | bytes 7340032 | tf_op jit(solution)/shard_map/pallas_call | solution.py:477
  99.5 4.9 %collective-permute-done.30.refs_1_ = bf16[128,1792]{1,0:T(8,128)(2,1)S(1)} collective-permute-done((bf16[128,1792]{1,0:T(8,128)(2,1)S(1)}, bf16[128,1792]{1,0:T(8,128)(2,1)S(1)}, u32[]{:S(2)}, u32[]{:S(2)}) %collective-permute-start.30) | collective-permute-done | bytes 458784 | tf_op jit(solution)/shard_map/ppermute | solution.py:59
  104.4 1.0 shard_map.89
  105.4 3.6 %all-to-all-start = ((bf16[16,8,1792]{2,1,0:T(8,128)(2,1)}), bf16[16,8,1792]{2,1,0:T(8,128)(2,1)S(1)}, u32[]{:S(2)}, u32[]{:S(2)}) async-start(bf16[16,8,1792]{2,1,0:T(8,128)(2,1)} %bitcast.2), calls=%async_computation | async-start | bytes 917504 | tf_op jit(solution)/shard_map/all_to_all | solution.py:539
  109.6 9.1 %all-to-all-done.received = bf16[16,8,1792]{2,1,0:T(8,128)(2,1)S(1)} async-done(((bf16[16,8,1792]{2,1,0:T(8,128)(2,1)}), bf16[16,8,1792]{2,1,0:T(8,128)(2,1)S(1)}, u32[]{:S(2)}, u32[]{:S(2)}) %all-to-all-start) | async-done | bytes 458784 | tf_op jit(solution)/shard_map/all_to_all | solution.py:539
  (61 shorter events, 7.9 us)
Async XLA Ops:
  0.6 0.8 copy-start.2
  1.4 0.7 copy-start.3
  2.2 9.4 %collective-permute-start.2 = (bf16[8,4096]{1,0:T(8,128)(2,1)S(1)}, bf16[8,4096]{1,0:T(8,128)(2,1)S(1)}, u32[]{:S(2)}, u32[]{:S(2)}) collective-permute-start(bf16[8,4096]{1,0:T(8,128)(2,1)S(1)} %shard_map.77), channel_id=1, source_target_pairs={{0,4},{1,5},{2,6},{3,7},{4,0},{5,1},{6,2},{7,3},{8,12},{9,13},{10,... | collective-permute-start | bytes 196616 | tf_op jit(solution)/shard_map/ppermute | solution.py:59
  5.6 6.0 %collective-permute-start.1 = (bf16[8,4096]{1,0:T(8,128)(2,1)S(1)}, bf16[8,4096]{1,0:T(8,128)(2,1)S(1)}, u32[]{:S(2)}, u32[]{:S(2)}) collective-permute-start(bf16[8,4096]{1,0:T(8,128)(2,1)S(1)} %shard_map.77), channel_id=1, source_target_pairs={{0,6},{1,7},{2,0},{3,1},{4,2},{5,3},{6,4},{7,5},{8,14},{9,15},{10,... | collective-permute-start | bytes 196616 | tf_op jit(solution)/shard_map/ppermute | solution.py:59
  6.6 5.5 %collective-permute-start = (bf16[8,4096]{1,0:T(8,128)(2,1)S(1)}, bf16[8,4096]{1,0:T(8,128)(2,1)S(1)}, u32[]{:S(2)}, u32[]{:S(2)}) collective-permute-start(bf16[8,4096]{1,0:T(8,128)(2,1)S(1)} %shard_map.77), channel_id=1, source_target_pairs={{0,2},{1,3},{2,4},{3,5},{4,6},{5,7},{6,0},{7,1},{8,10},{9,11},{10,... | collective-permute-start | bytes 196616 | tf_op jit(solution)/shard_map/ppermute | solution.py:59
  7.6 3.7 %copy-start = (bf16[2304,2048]{1,0:T(8,128)(2,1)S(1)}, bf16[2304,2048]{1,0:T(8,128)(2,1)}, u32[]{:S(2)}) copy-start(bf16[2304,2048]{1,0:T(8,128)(2,1)} %weight.6) | copy-start | bytes 28311556
  11.3 25.3 %copy-start.1 = (bf16[2304,2048]{1,0:T(8,128)(2,1)S(1)}, bf16[2304,2048]{1,0:T(8,128)(2,1)}, u32[]{:S(2)}) copy-start(bf16[2304,2048]{1,0:T(8,128)(2,1)} %weight.6) | copy-start | bytes 28311556
  12.2 10.2 %collective-permute-start.5 = (bf16[32,2560]{1,0:T(8,128)(2,1)S(1)}, bf16[32,2560]{1,0:T(8,128)(2,1)S(1)}, u32[]{:S(2)}, u32[]{:S(2)}) collective-permute-start(bf16[32,2560]{1,0:T(8,128)(2,1)S(1)} %slice.6), channel_id=1, source_target_pairs={{0,32},{1,33},{2,34},{3,35},{4,36},{5,37},{6,38},{7,39},{8,40},{9,... | collective-permute-start | bytes 491528 | tf_op jit(solution)/shard_map/ppermute | solution.py:59
  16.1 7.2 %collective-permute-start.4 = (bf16[32,2560]{1,0:T(8,128)(2,1)S(1)}, bf16[32,2560]{1,0:T(8,128)(2,1)S(1)}, u32[]{:S(2)}, u32[]{:S(2)}) collective-permute-start(bf16[32,2560]{1,0:T(8,128)(2,1)S(1)} %slice.6), channel_id=1, source_target_pairs={{0,48},{1,49},{2,50},{3,51},{4,52},{5,53},{6,54},{7,55},{8,56},{9,... | collective-permute-start | bytes 491528 | tf_op jit(solution)/shard_map/ppermute | solution.py:59
  16.8 6.5 %collective-permute-start.3 = (bf16[32,2560]{1,0:T(8,128)(2,1)S(1)}, bf16[32,2560]{1,0:T(8,128)(2,1)S(1)}, u32[]{:S(2)}, u32[]{:S(2)}) collective-permute-start(bf16[32,2560]{1,0:T(8,128)(2,1)S(1)} %slice.6), channel_id=1, source_target_pairs={{0,16},{1,17},{2,18},{3,19},{4,20},{5,21},{6,22},{7,23},{8,24},{9,... | collective-permute-start | bytes 491528 | tf_op jit(solution)/shard_map/ppermute | solution.py:59
  18.2 9.5 %collective-permute-start.11 = (bf16[32,1536]{1,0:T(8,128)(2,1)S(1)}, bf16[32,1536]{1,0:T(8,128)(2,1)S(1)}, u32[]{:S(2)}, u32[]{:S(2)}) collective-permute-start(bf16[32,1536]{1,0:T(8,128)(2,1)S(1)} %slice.7), channel_id=1, source_target_pairs={{0,1},{1,0},{2,3},{3,2},{4,5},{5,4},{6,7},{7,6},{8,9},{9,8},{10,11... | collective-permute-start | bytes 294920 | tf_op jit(solution)/shard_map/ppermute | solution.py:59
  21.3 7.3 %collective-permute-start.10 = (bf16[32,1536]{1,0:T(8,128)(2,1)S(1)}, bf16[32,1536]{1,0:T(8,128)(2,1)S(1)}, u32[]{:S(2)}, u32[]{:S(2)}) collective-permute-start(bf16[32,1536]{1,0:T(8,128)(2,1)S(1)} %slice.7), channel_id=1, source_target_pairs={{0,9},{1,8},{2,11},{3,10},{4,13},{5,12},{6,15},{7,14},{8,0},{9,1},... | collective-permute-start | bytes 294920 | tf_op jit(solution)/shard_map/ppermute | solution.py:59
  22.4 6.2 %collective-permute-start.9 = (bf16[32,1536]{1,0:T(8,128)(2,1)S(1)}, bf16[32,1536]{1,0:T(8,128)(2,1)S(1)}, u32[]{:S(2)}, u32[]{:S(2)}) collective-permute-start(bf16[32,1536]{1,0:T(8,128)(2,1)S(1)} %slice.7), channel_id=1, source_target_pairs={{0,8},{1,9},{2,10},{3,11},{4,12},{5,13},{6,14},{7,15},{8,1},{9,0},... | collective-permute-start | bytes 294920 | tf_op jit(solution)/shard_map/ppermute | solution.py:59
  23.4 12.3 %collective-permute-start.8 = (bf16[128,2560]{1,0:T(8,128)(2,1)S(1)}, bf16[128,2560]{1,0:T(8,128)(2,1)S(1)}, u32[]{:S(2)}, u32[]{:S(2)}) collective-permute-start(bf16[128,2560]{1,0:T(8,128)(2,1)S(1)} %pad_maximum_fusion.x0.refs_0_), channel_id=1, source_target_pairs={{0,1},{1,0},{2,3},{3,2},{4,5},{5,4},{6,7},{7,6},{8,9},{9,8},{10,11... | collective-permute-start | bytes 1966088 | tf_op jit(solution)/shard_map/ppermute | solution.py:59
  26.5 16.2 %collective-permute-start.7 = (bf16[128,2560]{1,0:T(8,128)(2,1)S(1)}, bf16[128,2560]{1,0:T(8,128)(2,1)S(1)}, u32[]{:S(2)}, u32[]{:S(2)}) collective-permute-start(bf16[128,2560]{1,0:T(8,128)(2,1)S(1)} %pad_maximum_fusion.x0.refs_0_), channel_id=1, source_target_pairs={{0,9},{1,8},{2,11},{3,10},{4,13},{5,12},{6,15},{7,14},{8,0},{9,1},... | collective-permute-start | bytes 1966088 | tf_op jit(solution)/shard_map/ppermute | solution.py:59
  27.7 15.1 %collective-permute-start.6 = (bf16[128,2560]{1,0:T(8,128)(2,1)S(1)}, bf16[128,2560]{1,0:T(8,128)(2,1)S(1)}, u32[]{:S(2)}, u32[]{:S(2)}) collective-permute-start(bf16[128,2560]{1,0:T(8,128)(2,1)S(1)} %pad_maximum_fusion.x0.refs_0_), channel_id=1, source_target_pairs={{0,8},{1,9},{2,10},{3,11},{4,12},{5,13},{6,14},{7,15},{8,1},{9,0},... | collective-permute-start | bytes 1966088 | tf_op jit(solution)/shard_map/ppermute | solution.py:59
  28.6 18.8 %collective-permute-start.14 = (bf16[128,1536]{1,0:T(8,128)(2,1)S(1)}, bf16[128,1536]{1,0:T(8,128)(2,1)S(1)}, u32[]{:S(2)}, u32[]{:S(2)}) collective-permute-start(bf16[128,1536]{1,0:T(8,128)(2,1)S(1)} %constant_dynamic-update-slice_fusion.refs_4_), channel_id=1, source_target_pairs={{0,32},{1,33},{2,34},{3,35},{4,36},{5,37},{6,38},{7,39},{8,40},{9,... | collective-permute-start | bytes 1179656 | tf_op jit(solution)/shard_map/ppermute | solution.py:59
  30.0 18.7 %collective-permute-start.13 = (bf16[128,1536]{1,0:T(8,128)(2,1)S(1)}, bf16[128,1536]{1,0:T(8,128)(2,1)S(1)}, u32[]{:S(2)}, u32[]{:S(2)}) collective-permute-start(bf16[128,1536]{1,0:T(8,128)(2,1)S(1)} %constant_dynamic-update-slice_fusion.refs_4_), channel_id=1, source_target_pairs={{0,48},{1,49},{2,50},{3,51},{4,52},{5,53},{6,54},{7,55},{8,56},{9,... | collective-permute-start | bytes 1179656 | tf_op jit(solution)/shard_map/ppermute | solution.py:59
  35.7 13.1 %collective-permute-start.12 = (bf16[128,1536]{1,0:T(8,128)(2,1)S(1)}, bf16[128,1536]{1,0:T(8,128)(2,1)S(1)}, u32[]{:S(2)}, u32[]{:S(2)}) collective-permute-start(bf16[128,1536]{1,0:T(8,128)(2,1)S(1)} %constant_dynamic-update-slice_fusion.refs_4_), channel_id=1, source_target_pairs={{0,16},{1,17},{2,18},{3,19},{4,20},{5,21},{6,22},{7,23},{8,24},{9,... | collective-permute-start | bytes 1179656 | tf_op jit(solution)/shard_map/ppermute | solution.py:59
  36.6 12.1 %slice-start = ((s8[7340032]{0:T(1024)(128)(4,1)}), s8[4194304]{0:T(1024)(128)(4,1)S(1)}, s32[]{:S(2)}) async-start(s8[7340032]{0:T(1024)(128)(4,1)} %bitcast.4), calls=%async_computation.1 | async-start | bytes 8388608
  38.2 10.6 %slice-start.1 = ((s8[7340032]{0:T(1024)(128)(4,1)}), s8[3145728]{0:T(1024)(128)(4,1)S(1)}, s32[]{:S(2)}) async-start(s8[7340032]{0:T(1024)(128)(4,1)} %bitcast.4), calls=%async_computation.2 | async-start | bytes 6291456
  48.8 6.0 %collective-permute-start.15 = (f32[256,2048]{1,0:T(8,128)S(1)}, f32[256,2048]{1,0:T(8,128)S(1)}, u32[]{:S(2)}, u32[]{:S(2)}) collective-permute-start(f32[256,2048]{1,0:T(8,128)S(1)} %get-tuple-element.67), channel_id=1, source_target_pairs={{0,64},{64,0},{1,65},{65,1},{2,66},{66,2},{3,67},{67,3},{4,68},{68... | collective-permute-start | bytes 6291464 | tf_op jit(solution)/shard_map/ppermute | solution.py:63
  51.8 4.3 %collective-permute-start.16 = (f32[256,1024]{1,0:T(8,128)S(1)}, f32[256,1024]{1,0:T(8,128)S(1)}, u32[]{:S(2)}, u32[]{:S(2)}) collective-permute-start(f32[256,1024]{1,0:T(8,128)S(1)} %get-tuple-element.71), channel_id=1, source_target_pairs={{0,64},{64,0},{1,65},{65,1},{2,66},{66,2},{3,67},{67,3},{4,68},{68... | collective-permute-start | bytes 3145736 | tf_op jit(solution)/shard_map/ppermute | solution.py:63
  54.6 2.8 %collective-permute-start.17 = (f32[256,1024]{1,0:T(8,128)S(1)}, f32[256,1024]{1,0:T(8,128)S(1)}, u32[]{:S(2)}, u32[]{:S(2)}) collective-permute-start(f32[256,1024]{1,0:T(8,128)S(1)} %get-tuple-element.75), channel_id=1, source_target_pairs={{0,64},{64,0},{1,65},{65,1},{2,66},{66,2},{3,67},{67,3},{4,68},{68... | collective-permute-start | bytes 3145736 | tf_op jit(solution)/shard_map/ppermute | solution.py:63
  57.4 25.9 %copy-start.4 = (f32[512]{0:T(512)S(1)}, f32[512]{0:T(512)}, u32[]{:S(2)}) copy-start(f32[512]{0:T(512)} %param.9) | copy-start | bytes 6148
  58.9 5.2 %collective-permute-start.20 = (f32[8,128]{1,0:T(8,128)S(1)}, f32[8,128]{1,0:T(8,128)S(1)}, u32[]{:S(2)}, u32[]{:S(2)}) collective-permute-start(f32[8,128]{1,0:T(8,128)S(1)} %get-tuple-element.76), channel_id=1, source_target_pairs={{0,1},{1,0},{2,3},{3,2},{4,5},{5,4},{6,7},{7,6},{8,9},{9,8},{10,11... | collective-permute-start | bytes 12296 | tf_op jit(solution)/shard_map/ppermute | solution.py:59
  60.6 3.6 %collective-permute-start.19 = (f32[8,128]{1,0:T(8,128)S(1)}, f32[8,128]{1,0:T(8,128)S(1)}, u32[]{:S(2)}, u32[]{:S(2)}) collective-permute-start(f32[8,128]{1,0:T(8,128)S(1)} %get-tuple-element.76), channel_id=1, source_target_pairs={{0,9},{1,8},{2,11},{3,10},{4,13},{5,12},{6,15},{7,14},{8,0},{9,1},... | collective-permute-start | bytes 12296 | tf_op jit(solution)/shard_map/ppermute | solution.py:59
  62.1 4.8 %collective-permute-start.18 = (f32[8,128]{1,0:T(8,128)S(1)}, f32[8,128]{1,0:T(8,128)S(1)}, u32[]{:S(2)}, u32[]{:S(2)}) collective-permute-start(f32[8,128]{1,0:T(8,128)S(1)} %get-tuple-element.76), channel_id=1, source_target_pairs={{0,8},{1,9},{2,10},{3,11},{4,12},{5,13},{6,14},{7,15},{8,1},{9,0},... | collective-permute-start | bytes 12296 | tf_op jit(solution)/shard_map/ppermute | solution.py:59
  67.0 5.1 %collective-permute-start.23 = (f32[8,128]{1,0:T(8,128)S(1)}, f32[8,128]{1,0:T(8,128)S(1)}, u32[]{:S(2)}, u32[]{:S(2)}) collective-permute-start(f32[8,128]{1,0:T(8,128)S(1)} %add_add_fusion.2), channel_id=1, source_target_pairs={{0,32},{1,33},{2,34},{3,35},{4,36},{5,37},{6,38},{7,39},{8,40},{9,... | collective-permute-start | bytes 12296 | tf_op jit(solution)/shard_map/ppermute | solution.py:59
  69.5 3.6 %collective-permute-start.22 = (f32[8,128]{1,0:T(8,128)S(1)}, f32[8,128]{1,0:T(8,128)S(1)}, u32[]{:S(2)}, u32[]{:S(2)}) collective-permute-start(f32[8,128]{1,0:T(8,128)S(1)} %add_add_fusion.2), channel_id=1, source_target_pairs={{0,48},{1,49},{2,50},{3,51},{4,52},{5,53},{6,54},{7,55},{8,56},{9,... | collective-permute-start | bytes 12296 | tf_op jit(solution)/shard_map/ppermute | solution.py:59
  70.7 4.8 %collective-permute-start.21 = (f32[8,128]{1,0:T(8,128)S(1)}, f32[8,128]{1,0:T(8,128)S(1)}, u32[]{:S(2)}, u32[]{:S(2)}) collective-permute-start(f32[8,128]{1,0:T(8,128)S(1)} %add_add_fusion.2), channel_id=1, source_target_pairs={{0,16},{1,17},{2,18},{3,19},{4,20},{5,21},{6,22},{7,23},{8,24},{9,... | collective-permute-start | bytes 12296 | tf_op jit(solution)/shard_map/ppermute | solution.py:59
  75.5 5.1 %collective-permute-start.26 = (f32[8,128]{1,0:T(8,128)S(1)}, f32[8,128]{1,0:T(8,128)S(1)}, u32[]{:S(2)}, u32[]{:S(2)}) collective-permute-start(f32[8,128]{1,0:T(8,128)S(1)} %add_add_fusion.1), channel_id=1, source_target_pairs={{0,4},{1,5},{2,6},{3,7},{4,0},{5,1},{6,2},{7,3},{8,12},{9,13},{10,... | collective-permute-start | bytes 12296 | tf_op jit(solution)/shard_map/ppermute | solution.py:59
  77.1 3.6 %collective-permute-start.25 = (f32[8,128]{1,0:T(8,128)S(1)}, f32[8,128]{1,0:T(8,128)S(1)}, u32[]{:S(2)}, u32[]{:S(2)}) collective-permute-start(f32[8,128]{1,0:T(8,128)S(1)} %add_add_fusion.1), channel_id=1, source_target_pairs={{0,6},{1,7},{2,0},{3,1},{4,2},{5,3},{6,4},{7,5},{8,14},{9,15},{10,... | collective-permute-start | bytes 12296 | tf_op jit(solution)/shard_map/ppermute | solution.py:59
  78.4 4.8 %collective-permute-start.24 = (f32[8,128]{1,0:T(8,128)S(1)}, f32[8,128]{1,0:T(8,128)S(1)}, u32[]{:S(2)}, u32[]{:S(2)}) collective-permute-start(f32[8,128]{1,0:T(8,128)S(1)} %add_add_fusion.1), channel_id=1, source_target_pairs={{0,2},{1,3},{2,4},{3,5},{4,6},{5,7},{6,0},{7,1},{8,10},{9,11},{10,... | collective-permute-start | bytes 12296 | tf_op jit(solution)/shard_map/ppermute | solution.py:59
  83.7 2.7 %collective-permute-start.27 = (bf16[256,2048]{1,0:T(8,128)(2,1)S(1)}, bf16[256,2048]{1,0:T(8,128)(2,1)S(1)}, u32[]{:S(2)}, u32[]{:S(2)}) collective-permute-start(bf16[256,2048]{1,0:T(8,128)(2,1)S(1)} %get-tuple-element.82.gap.own), channel_id=1, source_target_pairs={{0,64},{64,0},{1,65},{65,1},{2,66},{66,2},{3,67},{67,3},{4,68},{68... | collective-permute-start | bytes 3145736 | tf_op jit(solution)/shard_map/ppermute | solution.py:63
  83.8 2.6 %collective-permute-start.28 = (f32[2,128]{1,0:T(2,128)S(1)}, f32[2,128]{1,0:T(2,128)S(1)}, u32[]{:S(2)}, u32[]{:S(2)}) collective-permute-start(f32[2,128]{1,0:T(2,128)S(1)} %get-tuple-element.81), channel_id=1, source_target_pairs={{0,64},{64,0},{1,65},{65,1},{2,66},{66,2},{3,67},{67,3},{4,68},{68... | collective-permute-start | bytes 3080 | tf_op jit(solution)/shard_map/ppermute | solution.py:63
  89.7 9.8 %collective-permute-start.29 = (bf16[128,1792]{1,0:T(8,128)(2,1)S(1)}, bf16[128,1792]{1,0:T(8,128)(2,1)S(1)}, u32[]{:S(2)}, u32[]{:S(2)}) collective-permute-start(bf16[128,1792]{1,0:T(8,128)(2,1)S(1)} %get-tuple-element.89), channel_id=1, source_target_pairs={{0,9},{1,8},{2,11},{3,10},{4,13},{5,12},{6,15},{7,14},{8,0},{9,1},... | collective-permute-start | bytes 1376264 | tf_op jit(solution)/shard_map/ppermute | solution.py:59
  89.8 14.6 %collective-permute-start.30 = (bf16[128,1792]{1,0:T(8,128)(2,1)S(1)}, bf16[128,1792]{1,0:T(8,128)(2,1)S(1)}, u32[]{:S(2)}, u32[]{:S(2)}) collective-permute-start(bf16[128,1792]{1,0:T(8,128)(2,1)S(1)} %get-tuple-element.90), channel_id=1, source_target_pairs={{0,8},{1,9},{2,10},{3,11},{4,12},{5,13},{6,14},{7,15},{8,1},{9,0},... | collective-permute-start | bytes 1376264 | tf_op jit(solution)/shard_map/ppermute | solution.py:59
  91.8 12.7 %collective-permute-start.31 = (bf16[128,1792]{1,0:T(8,128)(2,1)S(1)}, bf16[128,1792]{1,0:T(8,128)(2,1)S(1)}, u32[]{:S(2)}, u32[]{:S(2)}) collective-permute-start(bf16[128,1792]{1,0:T(8,128)(2,1)S(1)} %get-tuple-element.91), channel_id=1, source_target_pairs={{0,1},{1,0},{2,3},{3,2},{4,5},{5,4},{6,7},{7,6},{8,9},{9,8},{10,11... | collective-permute-start | bytes 1376264 | tf_op jit(solution)/shard_map/ppermute | solution.py:59
  105.4 13.3 %all-to-all-start = ((bf16[16,8,1792]{2,1,0:T(8,128)(2,1)}), bf16[16,8,1792]{2,1,0:T(8,128)(2,1)S(1)}, u32[]{:S(2)}, u32[]{:S(2)}) async-start(bf16[16,8,1792]{2,1,0:T(8,128)(2,1)} %bitcast.2), calls=%async_computation | async-start | bytes 917504 | tf_op jit(solution)/shard_map/all_to_all | solution.py:539

commit v9 on v8

--- a/solution.py
+++ b/solution.py
@@ -432,8 +432,10 @@
 
 def first_sum_kernel(mine, *refs):
     received, out = refs[:3], refs[3]
-    total = mine[...] + sum(r[...].astype(jnp.float32) for r in received)
-    out[...] = total.astype(out.dtype)
+    for at in range(0, mine.shape[0], 16):
+        rows = slice(at, at + 16)
+        total = mine[rows] + sum(r[rows].astype(jnp.float32) for r in received)
+        out[rows] = total.astype(out.dtype)
 
 
 def first_sum(mine, received):

time: 120 us -> 120 us (level)
  no operation moved by 1% of the time
where the time goes in v9:
time: 120 us; the launch traced here: 119 us
  starting transfers between devices  45.8 us (38%)
  waiting for transfers between devices  36.7 us (31%)
  Pallas kernels  30 us (25%)
  local copies, waits for them, and re-layouts  5.26 us (4%)
    ppermute x27, starting transfers between devices, send(): return lax.ppermute(block, everyone, ring(axes, by))  40.8 us
    ppermute x27, waiting for transfers between devices, send(): return lax.ppermute(block, everyone, ring(axes, by))  27.6 us
    all_to_all x1, waiting for transfers between devices, local(): total = lax.all_to_all(total, everyone, 0, 0, axis_index_groups=planes())  9.11 us
    pallas_call x1, Pallas kernels, grad_weight_of(): pl.pallas_call(grad_weight_kernel, grid=(student_width // tile,), in_spec...  6.91 us
    unnamed x17, local copies, waits for them, and re-layouts  5.23 us
    pallas_call x1, Pallas kernels, teacher_logits(): pl.pallas_call(teacher_kernel, in_specs=[scalars()] + [whole()] * 5, out_...  4.67 us
    all_to_all x1, starting transfers between devices, local(): total = lax.all_to_all(total, everyone, 0, 0, axis_index_groups=planes())  3.56 us
    pallas_call x1, Pallas kernels, hidden_all(): pl.pallas_call(hidden_all_kernel, in_specs=[scalars()] + [whole()] * 3, o...  3.18 us
  transfers between devices with their start and end apart: 33, of which 17 were waited for; matrix products, arithmetic and copies ran while one was open for 1% of the time, Pallas kernels for 19%

profile of v9, /device:TPU:0, one launch (start us, length us, event | category | flops | bytes accessed | tf_op | source)
XLA Modules:
  0.0 119.4 jit_solution(2245563771318219175)
XLA Ops:
  0.6 0.8 copy-done.2
  2.2 3.4 %collective-permute-start.2 = (bf16[8,4096]{1,0:T(8,128)(2,1)S(1)}, bf16[8,4096]{1,0:T(8,128)(2,1)S(1)}, u32[]{:S(2)}, u32[]{:S(2)}) collective-permute-start(bf16[8,4096]{1,0:T(8,128)(2,1)S(1)} %shard_map.77), channel_id=1, source_target_pairs={{0,4},{1,5},{2,6},{3,7},{4,0},{5,1},{6,2},{7,3},{8,12},{9,13},{10,... | collective-permute-start | bytes 196616 | tf_op jit(solution)/shard_map/ppermute | solution.py:59
  5.6 1.1 collective-permute-start.1
  6.6 1.0 collective-permute-start
  7.6 3.7 %copy-done = bf16[2304,2048]{1,0:T(8,128)(2,1)S(1)} copy-done((bf16[2304,2048]{1,0:T(8,128)(2,1)S(1)}, bf16[2304,2048]{1,0:T(8,128)(2,1)}, u32[]{:S(2)}) %copy-start) | copy-done | bytes 9437208
  12.2 4.0 %collective-permute-start.5 = (bf16[32,2560]{1,0:T(8,128)(2,1)S(1)}, bf16[32,2560]{1,0:T(8,128)(2,1)S(1)}, u32[]{:S(2)}, u32[]{:S(2)}) collective-permute-start(bf16[32,2560]{1,0:T(8,128)(2,1)S(1)} %slice.6), channel_id=1, source_target_pairs={{0,32},{1,33},{2,34},{3,35},{4,36},{5,37},{6,38},{7,39},{8,40},{9,... | collective-permute-start | bytes 491528 | tf_op jit(solution)/shard_map/ppermute | solution.py:59
  16.8 1.3 %collective-permute-start.3 = (bf16[32,2560]{1,0:T(8,128)(2,1)S(1)}, bf16[32,2560]{1,0:T(8,128)(2,1)S(1)}, u32[]{:S(2)}, u32[]{:S(2)}) collective-permute-start(bf16[32,2560]{1,0:T(8,128)(2,1)S(1)} %slice.6), channel_id=1, source_target_pairs={{0,16},{1,17},{2,18},{3,19},{4,20},{5,21},{6,22},{7,23},{8,24},{9,... | collective-permute-start | bytes 491528 | tf_op jit(solution)/shard_map/ppermute | solution.py:59
  18.2 3.1 %collective-permute-start.11 = (bf16[32,1536]{1,0:T(8,128)(2,1)S(1)}, bf16[32,1536]{1,0:T(8,128)(2,1)S(1)}, u32[]{:S(2)}, u32[]{:S(2)}) collective-permute-start(bf16[32,1536]{1,0:T(8,128)(2,1)S(1)} %slice.7), channel_id=1, source_target_pairs={{0,1},{1,0},{2,3},{3,2},{4,5},{5,4},{6,7},{7,6},{8,9},{9,8},{10,11... | collective-permute-start | bytes 294920 | tf_op jit(solution)/shard_map/ppermute | solution.py:59
  21.3 1.1 collective-permute-start.10
  22.4 0.9 collective-permute-start.9
  23.4 3.1 %collective-permute-start.8 = (bf16[128,2560]{1,0:T(8,128)(2,1)S(1)}, bf16[128,2560]{1,0:T(8,128)(2,1)S(1)}, u32[]{:S(2)}, u32[]{:S(2)}) collective-permute-start(bf16[128,2560]{1,0:T(8,128)(2,1)S(1)} %pad_maximum_fusion.x0.refs_0_), channel_id=1, source_target_pairs={{0,1},{1,0},{2,3},{3,2},{4,5},{5,4},{6,7},{7,6},{8,9},{9,8},{10,11... | collective-permute-start | bytes 1966088 | tf_op jit(solution)/shard_map/ppermute | solution.py:59
  26.5 1.1 collective-permute-start.7
  27.7 0.9 collective-permute-start.6
  28.6 1.4 %collective-permute-start.14 = (bf16[128,1536]{1,0:T(8,128)(2,1)S(1)}, bf16[128,1536]{1,0:T(8,128)(2,1)S(1)}, u32[]{:S(2)}, u32[]{:S(2)}) collective-permute-start(bf16[128,1536]{1,0:T(8,128)(2,1)S(1)} %constant_dynamic-update-slice_fusion.refs_4_), channel_id=1, source_target_pairs={{0,32},{1,33},{2,34},{3,35},{4,36},{5,37},{6,38},{7,39},{8,40},{9,... | collective-permute-start | bytes 1179656 | tf_op jit(solution)/shard_map/ppermute | solution.py:59
  30.0 2.0 %collective-permute-start.13 = (bf16[128,1536]{1,0:T(8,128)(2,1)S(1)}, bf16[128,1536]{1,0:T(8,128)(2,1)S(1)}, u32[]{:S(2)}, u32[]{:S(2)}) collective-permute-start(bf16[128,1536]{1,0:T(8,128)(2,1)S(1)} %constant_dynamic-update-slice_fusion.refs_4_), channel_id=1, source_target_pairs={{0,48},{1,49},{2,50},{3,51},{4,52},{5,53},{6,54},{7,55},{8,56},{9,... | collective-permute-start | bytes 1179656 | tf_op jit(solution)/shard_map/ppermute | solution.py:59
  32.1 3.6 %collective-permute-done.8.x3.refs_3_ = bf16[128,2560]{1,0:T(8,128)(2,1)S(1)} collective-permute-done((bf16[128,2560]{1,0:T(8,128)(2,1)S(1)}, bf16[128,2560]{1,0:T(8,128)(2,1)S(1)}, u32[]{:S(2)}, u32[]{:S(2)}) %collective-permute-start.8) | collective-permute-done | bytes 655392 | tf_op jit(solution)/shard_map/ppermute | solution.py:59
  35.7 0.9 collective-permute-start.12
  36.6 1.5 %shard_map.78.early = f32[128,2048]{1,0:T(8,128)S(1)} custom-call(bf16[128,2560]{1,0:T(8,128)(2,1)S(1)} %pad_maximum_fusion.x0.refs_0_, bf16[2304,2048]{1,0:T(8,128)(2,1)S(1)} %copy-done.1), custom_call_target="tpu_custom_call" | custom-call | flops 1207959552 | bytes 9437184 | tf_op jit(solution)/shard_map/pallas_call | solution.py:224
  38.2 4.6 %collective-permute-done.7.x2.refs_2_ = bf16[128,2560]{1,0:T(8,128)(2,1)S(1)} collective-permute-done((bf16[128,2560]{1,0:T(8,128)(2,1)S(1)}, bf16[128,2560]{1,0:T(8,128)(2,1)S(1)}, u32[]{:S(2)}, u32[]{:S(2)}) %collective-permute-start.7) | collective-permute-done | bytes 655392 | tf_op jit(solution)/shard_map/ppermute | solution.py:59
  42.7 4.7 %shard_map.79 = (f32[256,2048]{1,0:T(8,128)S(1)}, f32[256,2048]{1,0:T(8,128)S(1)}) custom-call(s32[2,128]{1,0:T(2,128)S(1)} %get-tuple-element.50.places, f32[128,2048]{1,0:T(8,128)S(1)} %shard_map.78.early, bf16[128,2560]{1,0:T(8,128)(2,1)S(1)} %collective-permute-done.6.x1.refs_1_, bf16[128,2560]{1,0:T(8,128)(2,1)S(1)} %collective-permute-done.7.x2.refs_2_, ...), custom_call_target="tpu_custom_call" | custom-call | flops 3623878656 | bytes 9437184 | tf_op jit(solution)/shard_map/pallas_call | solution.py:235
  47.4 1.3 %collective-permute-done.13.refs_6_ = bf16[128,1536]{1,0:T(8,128)(2,1)S(1)} collective-permute-done((bf16[128,1536]{1,0:T(8,128)(2,1)S(1)}, bf16[128,1536]{1,0:T(8,128)(2,1)S(1)}, u32[]{:S(2)}, u32[]{:S(2)}) %collective-permute-start.13) | collective-permute-done | bytes 393248 | tf_op jit(solution)/shard_map/ppermute | solution.py:59
  48.8 3.0 %shard_map.80 = (f32[256,1024]{1,0:T(8,128)S(1)}, f32[256,1024]{1,0:T(8,128)S(1)}, bf16[512,1792]{1,0:T(8,128)(2,1)S(1)}) custom-call(bf16[512,512]{1,0:T(8,128)(2,1)S(1)} %get-tuple-element.53.main_order, bf16[512,512]{1,0:T(8,128)(2,1)S(1)} %get-tuple-element.54.apart_order, bf16[128,2560]{1,0:T(8,128)(2,1)S(1)} %pad_maximum_fusion.x0.refs_0_, ...), custom_call_target="tpu_custom_call" | custom-call | flops 1879048192 | bytes 7340032 | tf_op jit(solution)/shard_map/pallas_call | solution.py:250
  52.6 2.1 %shard_map.81 = (f32[256,1024]{1,0:T(8,128)S(1)}, f32[256,1024]{1,0:T(8,128)S(1)}) custom-call(bf16[512,1792]{1,0:T(8,128)(2,1)S(1)} %get-tuple-element.64.rows, bf16[1792,2048]{1,0:T(8,128)(2,1)S(1)} %bitcast.5), custom_call_target="tpu_custom_call" | custom-call | flops 1879048192 | bytes 7340032 | tf_op jit(solution)/shard_map/pallas_call | solution.py:261
  54.7 1.4 %shard_map.82 = (f32[256,2048]{1,0:T(8,128)S(1)}, f32[256,2048]{1,0:T(8,128)S(1)}, f32[256,128]{1,0:T(8,128)S(1)}) custom-call(f32[256,2048]{1,0:T(8,128)S(1)} %get-tuple-element.66.own, f32[256,2048]{1,0:T(8,128)S(1)} %collective-permute-done.15.other), custom_call_target="tpu_custom_call" | custom-call | flops 4194304 | bytes 8388608 | tf_op jit(solution)/shard_map/pallas_call | solution.py:294
  56.1 1.3 %shard_map.83 = (f32[256,1024]{1,0:T(8,128)S(1)}, f32[256,1024]{1,0:T(8,128)S(1)}, f32[2,256,128]{2,1,0:T(8,128)S(1)}) custom-call(f32[256,2048]{1,0:T(8,128)S(1)} %get-tuple-element.68.refs_0_.refs_2_, f32[256,2048]{1,0:T(8,128)S(1)} %get-tuple-element.69.refs_1_.refs_3_, f32[256,1024]{1,0:T(8,128)S(1)} %get-tuple-element.70.refs_2_, ...), custom_call_target="tpu_custom_call" | custom-call | flops 4194304 | bytes 6291456 | tf_op jit(solution)/shard_map/pallas_call | solution.py:340
  57.4 1.4 %shard_map.84 = (f32[256,1024]{1,0:T(8,128)S(1)}, f32[256,1024]{1,0:T(8,128)S(1)}, f32[8,128]{1,0:T(8,128)S(1)}) custom-call(f32[2,256,128]{2,1,0:T(8,128)S(1)} %get-tuple-element.72.refs_0_, f32[256,128]{1,0:T(8,128)S(1)} %get-tuple-element.73.refs_1_, f32[256,2048]{1,0:T(8,128)S(1)} %get-tuple-element.68.refs_0_.refs_2_, ...), custom_call_target="tpu_custom_call" | custom-call | flops 4194304 | bytes 6291456 | tf_op jit(solution)/shard_map/pallas_call | solution.py:340
  58.9 1.7 %collective-permute-start.20 = (f32[8,128]{1,0:T(8,128)S(1)}, f32[8,128]{1,0:T(8,128)S(1)}, u32[]{:S(2)}, u32[]{:S(2)}) collective-permute-start(f32[8,128]{1,0:T(8,128)S(1)} %get-tuple-element.76), channel_id=1, source_target_pairs={{0,1},{1,0},{2,3},{3,2},{4,5},{5,4},{6,7},{7,6},{8,9},{9,8},{10,11... | collective-permute-start | bytes 12296 | tf_op jit(solution)/shard_map/ppermute | solution.py:59
  60.6 1.5 %collective-permute-start.19 = (f32[8,128]{1,0:T(8,128)S(1)}, f32[8,128]{1,0:T(8,128)S(1)}, u32[]{:S(2)}, u32[]{:S(2)}) collective-permute-start(f32[8,128]{1,0:T(8,128)S(1)} %get-tuple-element.76), channel_id=1, source_target_pairs={{0,9},{1,8},{2,11},{3,10},{4,13},{5,12},{6,15},{7,14},{8,0},{9,1},... | collective-permute-start | bytes 12296 | tf_op jit(solution)/shard_map/ppermute | solution.py:59
  62.6 1.4 %collective-permute-done.20 = f32[8,128]{1,0:T(8,128)S(1)} collective-permute-done((f32[8,128]{1,0:T(8,128)S(1)}, f32[8,128]{1,0:T(8,128)S(1)}, u32[]{:S(2)}, u32[]{:S(2)}) %collective-permute-start.20) | collective-permute-done | bytes 4128 | tf_op jit(solution)/shard_map/ppermute | solution.py:59
  64.2 2.8 %collective-permute-done.18 = f32[8,128]{1,0:T(8,128)S(1)} collective-permute-done((f32[8,128]{1,0:T(8,128)S(1)}, f32[8,128]{1,0:T(8,128)S(1)}, u32[]{:S(2)}, u32[]{:S(2)}) %collective-permute-start.18) | collective-permute-done | bytes 4128 | tf_op jit(solution)/shard_map/ppermute | solution.py:59
  67.0 2.5 %collective-permute-start.23 = (f32[8,128]{1,0:T(8,128)S(1)}, f32[8,128]{1,0:T(8,128)S(1)}, u32[]{:S(2)}, u32[]{:S(2)}) collective-permute-start(f32[8,128]{1,0:T(8,128)S(1)} %add_add_fusion.2), channel_id=1, source_target_pairs={{0,32},{1,33},{2,34},{3,35},{4,36},{5,37},{6,38},{7,39},{8,40},{9,... | collective-permute-start | bytes 12296 | tf_op jit(solution)/shard_map/ppermute | solution.py:59
  69.5 1.2 %collective-permute-start.22 = (f32[8,128]{1,0:T(8,128)S(1)}, f32[8,128]{1,0:T(8,128)S(1)}, u32[]{:S(2)}, u32[]{:S(2)}) collective-permute-start(f32[8,128]{1,0:T(8,128)S(1)} %add_add_fusion.2), channel_id=1, source_target_pairs={{0,48},{1,49},{2,50},{3,51},{4,52},{5,53},{6,54},{7,55},{8,56},{9,... | collective-permute-start | bytes 12296 | tf_op jit(solution)/shard_map/ppermute | solution.py:59
  70.7 0.8 collective-permute-start.21
  72.1 1.0 collective-permute-done.22
  73.1 2.4 %collective-permute-done.21 = f32[8,128]{1,0:T(8,128)S(1)} collective-permute-done((f32[8,128]{1,0:T(8,128)S(1)}, f32[8,128]{1,0:T(8,128)S(1)}, u32[]{:S(2)}, u32[]{:S(2)}) %collective-permute-start.21) | collective-permute-done | bytes 4128 | tf_op jit(solution)/shard_map/ppermute | solution.py:59
  75.5 1.6 %collective-permute-start.26 = (f32[8,128]{1,0:T(8,128)S(1)}, f32[8,128]{1,0:T(8,128)S(1)}, u32[]{:S(2)}, u32[]{:S(2)}) collective-permute-start(f32[8,128]{1,0:T(8,128)S(1)} %add_add_fusion.1), channel_id=1, source_target_pairs={{0,4},{1,5},{2,6},{3,7},{4,0},{5,1},{6,2},{7,3},{8,12},{9,13},{10,... | collective-permute-start | bytes 12296 | tf_op jit(solution)/shard_map/ppermute | solution.py:59
  77.1 1.4 %collective-permute-start.25 = (f32[8,128]{1,0:T(8,128)S(1)}, f32[8,128]{1,0:T(8,128)S(1)}, u32[]{:S(2)}, u32[]{:S(2)}) collective-permute-start(f32[8,128]{1,0:T(8,128)S(1)} %add_add_fusion.1), channel_id=1, source_target_pairs={{0,6},{1,7},{2,0},{3,1},{4,2},{5,3},{6,4},{7,5},{8,14},{9,15},{10,... | collective-permute-start | bytes 12296 | tf_op jit(solution)/shard_map/ppermute | solution.py:59
  79.1 1.5 %collective-permute-done.26 = f32[8,128]{1,0:T(8,128)S(1)} collective-permute-done((f32[8,128]{1,0:T(8,128)S(1)}, f32[8,128]{1,0:T(8,128)S(1)}, u32[]{:S(2)}, u32[]{:S(2)}) %collective-permute-start.26) | collective-permute-done | bytes 4128 | tf_op jit(solution)/shard_map/ppermute | solution.py:59
  80.7 2.6 %collective-permute-done.24 = f32[8,128]{1,0:T(8,128)S(1)} collective-permute-done((f32[8,128]{1,0:T(8,128)S(1)}, f32[8,128]{1,0:T(8,128)S(1)}, u32[]{:S(2)}, u32[]{:S(2)}) %collective-permute-start.24) | collective-permute-done | bytes 4128 | tf_op jit(solution)/shard_map/ppermute | solution.py:59
  84.3 2.1 %shard_map.86.own = f32[256,1792]{1,0:T(8,128)S(1)} custom-call(bf16[256,2048]{1,0:T(8,128)(2,1)S(1)} %get-tuple-element.82.gap.own, bf16[1792,2048]{1,0:T(8,128)(2,1)S(1)} %bitcast.5), custom_call_target="tpu_custom_call" | custom-call | flops 1879048192 | bytes 7340032 | tf_op jit(solution)/shard_map/pallas_call | solution.py:398
  86.5 3.2 %shard_map.87 = (f32[128,1792]{1,0:T(8,128)S(1)}, bf16[128,1792]{1,0:T(8,128)(2,1)S(1)}, bf16[128,1792]{1,0:T(8,128)(2,1)S(1)}, bf16[128,1792]{1,0:T(8,128)(2,1)S(1)}) custom-call(s32[2,128]{1,0:T(2,128)S(1)} %get-tuple-element.50.places, f32[256,1792]{1,0:T(8,128)S(1)} %shard_map.86.own, bf16[256,2048]{1,0:T(8,128)(2,1)S(1)} %collective-permute-done.27.gap.other, ...), custom_call_target="tpu_custom_call" | custom-call | flops 1879048192 | bytes 7340032 | tf_op jit(solution)/shard_map/pallas_call | solution.py:421
  89.8 1.9 %collective-permute-start.30 = (bf16[128,1792]{1,0:T(8,128)(2,1)S(1)}, bf16[128,1792]{1,0:T(8,128)(2,1)S(1)}, u32[]{:S(2)}, u32[]{:S(2)}) collective-permute-start(bf16[128,1792]{1,0:T(8,128)(2,1)S(1)} %get-tuple-element.90), channel_id=1, source_target_pairs={{0,8},{1,9},{2,10},{3,11},{4,12},{5,13},{6,14},{7,15},{8,1},{9,0},... | collective-permute-start | bytes 1376264 | tf_op jit(solution)/shard_map/ppermute | solution.py:59
  91.8 0.8 collective-permute-start.31
  92.6 6.9 %shard_map.88 = bf16[1792,2048]{1,0:T(8,128)(2,1)} custom-call(bf16[512,1792]{1,0:T(8,128)(2,1)S(1)} %get-tuple-element.64.rows, bf16[256,2048]{1,0:T(8,128)(2,1)S(1)} %get-tuple-element.82.gap.own, bf16[256,2048]{1,0:T(8,128)(2,1)S(1)} %collective-permute-done.27.gap.other), custom_call_target="tpu_custom_call" | custom-call | flops 3758096384 | bytes 7340032 | tf_op jit(solution)/shard_map/pallas_call | solution.py:479
  99.5 4.9 %collective-permute-done.30.refs_1_ = bf16[128,1792]{1,0:T(8,128)(2,1)S(1)} collective-permute-done((bf16[128,1792]{1,0:T(8,128)(2,1)S(1)}, bf16[128,1792]{1,0:T(8,128)(2,1)S(1)}, u32[]{:S(2)}, u32[]{:S(2)}) %collective-permute-start.30) | collective-permute-done | bytes 458784 | tf_op jit(solution)/shard_map/ppermute | solution.py:59
  104.4 1.0 shard_map.89
  105.4 3.6 %all-to-all-start = ((bf16[16,8,1792]{2,1,0:T(8,128)(2,1)}), bf16[16,8,1792]{2,1,0:T(8,128)(2,1)S(1)}, u32[]{:S(2)}, u32[]{:S(2)}) async-start(bf16[16,8,1792]{2,1,0:T(8,128)(2,1)} %bitcast.2), calls=%async_computation | async-start | bytes 917504 | tf_op jit(solution)/shard_map/all_to_all | solution.py:541
  109.6 9.1 %all-to-all-done.received = bf16[16,8,1792]{2,1,0:T(8,128)(2,1)S(1)} async-done(((bf16[16,8,1792]{2,1,0:T(8,128)(2,1)}), bf16[16,8,1792]{2,1,0:T(8,128)(2,1)S(1)}, u32[]{:S(2)}, u32[]{:S(2)}) %all-to-all-start) | async-done | bytes 458784 | tf_op jit(solution)/shard_map/all_to_all | solution.py:541
  (61 shorter events, 7.9 us)
Async XLA Ops:
  0.6 0.8 copy-start.2
  1.4 0.7 copy-start.3
  2.2 9.4 %collective-permute-start.2 = (bf16[8,4096]{1,0:T(8,128)(2,1)S(1)}, bf16[8,4096]{1,0:T(8,128)(2,1)S(1)}, u32[]{:S(2)}, u32[]{:S(2)}) collective-permute-start(bf16[8,4096]{1,0:T(8,128)(2,1)S(1)} %shard_map.77), channel_id=1, source_target_pairs={{0,4},{1,5},{2,6},{3,7},{4,0},{5,1},{6,2},{7,3},{8,12},{9,13},{10,... | collective-permute-start | bytes 196616 | tf_op jit(solution)/shard_map/ppermute | solution.py:59
  5.6 6.0 %collective-permute-start.1 = (bf16[8,4096]{1,0:T(8,128)(2,1)S(1)}, bf16[8,4096]{1,0:T(8,128)(2,1)S(1)}, u32[]{:S(2)}, u32[]{:S(2)}) collective-permute-start(bf16[8,4096]{1,0:T(8,128)(2,1)S(1)} %shard_map.77), channel_id=1, source_target_pairs={{0,6},{1,7},{2,0},{3,1},{4,2},{5,3},{6,4},{7,5},{8,14},{9,15},{10,... | collective-permute-start | bytes 196616 | tf_op jit(solution)/shard_map/ppermute | solution.py:59
  6.6 5.5 %collective-permute-start = (bf16[8,4096]{1,0:T(8,128)(2,1)S(1)}, bf16[8,4096]{1,0:T(8,128)(2,1)S(1)}, u32[]{:S(2)}, u32[]{:S(2)}) collective-permute-start(bf16[8,4096]{1,0:T(8,128)(2,1)S(1)} %shard_map.77), channel_id=1, source_target_pairs={{0,2},{1,3},{2,4},{3,5},{4,6},{5,7},{6,0},{7,1},{8,10},{9,11},{10,... | collective-permute-start | bytes 196616 | tf_op jit(solution)/shard_map/ppermute | solution.py:59
  7.6 3.7 %copy-start = (bf16[2304,2048]{1,0:T(8,128)(2,1)S(1)}, bf16[2304,2048]{1,0:T(8,128)(2,1)}, u32[]{:S(2)}) copy-start(bf16[2304,2048]{1,0:T(8,128)(2,1)} %weight.6) | copy-start | bytes 28311556
  11.3 25.3 %copy-start.1 = (bf16[2304,2048]{1,0:T(8,128)(2,1)S(1)}, bf16[2304,2048]{1,0:T(8,128)(2,1)}, u32[]{:S(2)}) copy-start(bf16[2304,2048]{1,0:T(8,128)(2,1)} %weight.6) | copy-start | bytes 28311556
  12.2 10.2 %collective-permute-start.5 = (bf16[32,2560]{1,0:T(8,128)(2,1)S(1)}, bf16[32,2560]{1,0:T(8,128)(2,1)S(1)}, u32[]{:S(2)}, u32[]{:S(2)}) collective-permute-start(bf16[32,2560]{1,0:T(8,128)(2,1)S(1)} %slice.6), channel_id=1, source_target_pairs={{0,32},{1,33},{2,34},{3,35},{4,36},{5,37},{6,38},{7,39},{8,40},{9,... | collective-permute-start | bytes 491528 | tf_op jit(solution)/shard_map/ppermute | solution.py:59
  16.1 7.2 %collective-permute-start.4 = (bf16[32,2560]{1,0:T(8,128)(2,1)S(1)}, bf16[32,2560]{1,0:T(8,128)(2,1)S(1)}, u32[]{:S(2)}, u32[]{:S(2)}) collective-permute-start(bf16[32,2560]{1,0:T(8,128)(2,1)S(1)} %slice.6), channel_id=1, source_target_pairs={{0,48},{1,49},{2,50},{3,51},{4,52},{5,53},{6,54},{7,55},{8,56},{9,... | collective-permute-start | bytes 491528 | tf_op jit(solution)/shard_map/ppermute | solution.py:59
  16.8 6.5 %collective-permute-start.3 = (bf16[32,2560]{1,0:T(8,128)(2,1)S(1)}, bf16[32,2560]{1,0:T(8,128)(2,1)S(1)}, u32[]{:S(2)}, u32[]{:S(2)}) collective-permute-start(bf16[32,2560]{1,0:T(8,128)(2,1)S(1)} %slice.6), channel_id=1, source_target_pairs={{0,16},{1,17},{2,18},{3,19},{4,20},{5,21},{6,22},{7,23},{8,24},{9,... | collective-permute-start | bytes 491528 | tf_op jit(solution)/shard_map/ppermute | solution.py:59
  18.2 9.5 %collective-permute-start.11 = (bf16[32,1536]{1,0:T(8,128)(2,1)S(1)}, bf16[32,1536]{1,0:T(8,128)(2,1)S(1)}, u32[]{:S(2)}, u32[]{:S(2)}) collective-permute-start(bf16[32,1536]{1,0:T(8,128)(2,1)S(1)} %slice.7), channel_id=1, source_target_pairs={{0,1},{1,0},{2,3},{3,2},{4,5},{5,4},{6,7},{7,6},{8,9},{9,8},{10,11... | collective-permute-start | bytes 294920 | tf_op jit(solution)/shard_map/ppermute | solution.py:59
  21.3 7.3 %collective-permute-start.10 = (bf16[32,1536]{1,0:T(8,128)(2,1)S(1)}, bf16[32,1536]{1,0:T(8,128)(2,1)S(1)}, u32[]{:S(2)}, u32[]{:S(2)}) collective-permute-start(bf16[32,1536]{1,0:T(8,128)(2,1)S(1)} %slice.7), channel_id=1, source_target_pairs={{0,9},{1,8},{2,11},{3,10},{4,13},{5,12},{6,15},{7,14},{8,0},{9,1},... | collective-permute-start | bytes 294920 | tf_op jit(solution)/shard_map/ppermute | solution.py:59
  22.4 6.2 %collective-permute-start.9 = (bf16[32,1536]{1,0:T(8,128)(2,1)S(1)}, bf16[32,1536]{1,0:T(8,128)(2,1)S(1)}, u32[]{:S(2)}, u32[]{:S(2)}) collective-permute-start(bf16[32,1536]{1,0:T(8,128)(2,1)S(1)} %slice.7), channel_id=1, source_target_pairs={{0,8},{1,9},{2,10},{3,11},{4,12},{5,13},{6,14},{7,15},{8,1},{9,0},... | collective-permute-start | bytes 294920 | tf_op jit(solution)/shard_map/ppermute | solution.py:59
  23.4 12.3 %collective-permute-start.8 = (bf16[128,2560]{1,0:T(8,128)(2,1)S(1)}, bf16[128,2560]{1,0:T(8,128)(2,1)S(1)}, u32[]{:S(2)}, u32[]{:S(2)}) collective-permute-start(bf16[128,2560]{1,0:T(8,128)(2,1)S(1)} %pad_maximum_fusion.x0.refs_0_), channel_id=1, source_target_pairs={{0,1},{1,0},{2,3},{3,2},{4,5},{5,4},{6,7},{7,6},{8,9},{9,8},{10,11... | collective-permute-start | bytes 1966088 | tf_op jit(solution)/shard_map/ppermute | solution.py:59
  26.5 16.2 %collective-permute-start.7 = (bf16[128,2560]{1,0:T(8,128)(2,1)S(1)}, bf16[128,2560]{1,0:T(8,128)(2,1)S(1)}, u32[]{:S(2)}, u32[]{:S(2)}) collective-permute-start(bf16[128,2560]{1,0:T(8,128)(2,1)S(1)} %pad_maximum_fusion.x0.refs_0_), channel_id=1, source_target_pairs={{0,9},{1,8},{2,11},{3,10},{4,13},{5,12},{6,15},{7,14},{8,0},{9,1},... | collective-permute-start | bytes 1966088 | tf_op jit(solution)/shard_map/ppermute | solution.py:59
  27.7 15.1 %collective-permute-start.6 = (bf16[128,2560]{1,0:T(8,128)(2,1)S(1)}, bf16[128,2560]{1,0:T(8,128)(2,1)S(1)}, u32[]{:S(2)}, u32[]{:S(2)}) collective-permute-start(bf16[128,2560]{1,0:T(8,128)(2,1)S(1)} %pad_maximum_fusion.x0.refs_0_), channel_id=1, source_target_pairs={{0,8},{1,9},{2,10},{3,11},{4,12},{5,13},{6,14},{7,15},{8,1},{9,0},... | collective-permute-start | bytes 1966088 | tf_op jit(solution)/shard_map/ppermute | solution.py:59
  28.6 18.8 %collective-permute-start.14 = (bf16[128,1536]{1,0:T(8,128)(2,1)S(1)}, bf16[128,1536]{1,0:T(8,128)(2,1)S(1)}, u32[]{:S(2)}, u32[]{:S(2)}) collective-permute-start(bf16[128,1536]{1,0:T(8,128)(2,1)S(1)} %constant_dynamic-update-slice_fusion.refs_4_), channel_id=1, source_target_pairs={{0,32},{1,33},{2,34},{3,35},{4,36},{5,37},{6,38},{7,39},{8,40},{9,... | collective-permute-start | bytes 1179656 | tf_op jit(solution)/shard_map/ppermute | solution.py:59
  30.0 18.7 %collective-permute-start.13 = (bf16[128,1536]{1,0:T(8,128)(2,1)S(1)}, bf16[128,1536]{1,0:T(8,128)(2,1)S(1)}, u32[]{:S(2)}, u32[]{:S(2)}) collective-permute-start(bf16[128,1536]{1,0:T(8,128)(2,1)S(1)} %constant_dynamic-update-slice_fusion.refs_4_), channel_id=1, source_target_pairs={{0,48},{1,49},{2,50},{3,51},{4,52},{5,53},{6,54},{7,55},{8,56},{9,... | collective-permute-start | bytes 1179656 | tf_op jit(solution)/shard_map/ppermute | solution.py:59
  35.7 13.1 %collective-permute-start.12 = (bf16[128,1536]{1,0:T(8,128)(2,1)S(1)}, bf16[128,1536]{1,0:T(8,128)(2,1)S(1)}, u32[]{:S(2)}, u32[]{:S(2)}) collective-permute-start(bf16[128,1536]{1,0:T(8,128)(2,1)S(1)} %constant_dynamic-update-slice_fusion.refs_4_), channel_id=1, source_target_pairs={{0,16},{1,17},{2,18},{3,19},{4,20},{5,21},{6,22},{7,23},{8,24},{9,... | collective-permute-start | bytes 1179656 | tf_op jit(solution)/shard_map/ppermute | solution.py:59
  36.6 12.1 %slice-start = ((s8[7340032]{0:T(1024)(128)(4,1)}), s8[4194304]{0:T(1024)(128)(4,1)S(1)}, s32[]{:S(2)}) async-start(s8[7340032]{0:T(1024)(128)(4,1)} %bitcast.4), calls=%async_computation.1 | async-start | bytes 8388608
  38.2 10.6 %slice-start.1 = ((s8[7340032]{0:T(1024)(128)(4,1)}), s8[3145728]{0:T(1024)(128)(4,1)S(1)}, s32[]{:S(2)}) async-start(s8[7340032]{0:T(1024)(128)(4,1)} %bitcast.4), calls=%async_computation.2 | async-start | bytes 6291456
  48.8 6.0 %collective-permute-start.15 = (f32[256,2048]{1,0:T(8,128)S(1)}, f32[256,2048]{1,0:T(8,128)S(1)}, u32[]{:S(2)}, u32[]{:S(2)}) collective-permute-start(f32[256,2048]{1,0:T(8,128)S(1)} %get-tuple-element.67), channel_id=1, source_target_pairs={{0,64},{64,0},{1,65},{65,1},{2,66},{66,2},{3,67},{67,3},{4,68},{68... | collective-permute-start | bytes 6291464 | tf_op jit(solution)/shard_map/ppermute | solution.py:63
  51.8 4.3 %collective-permute-start.16 = (f32[256,1024]{1,0:T(8,128)S(1)}, f32[256,1024]{1,0:T(8,128)S(1)}, u32[]{:S(2)}, u32[]{:S(2)}) collective-permute-start(f32[256,1024]{1,0:T(8,128)S(1)} %get-tuple-element.71), channel_id=1, source_target_pairs={{0,64},{64,0},{1,65},{65,1},{2,66},{66,2},{3,67},{67,3},{4,68},{68... | collective-permute-start | bytes 3145736 | tf_op jit(solution)/shard_map/ppermute | solution.py:63
  54.6 2.8 %collective-permute-start.17 = (f32[256,1024]{1,0:T(8,128)S(1)}, f32[256,1024]{1,0:T(8,128)S(1)}, u32[]{:S(2)}, u32[]{:S(2)}) collective-permute-start(f32[256,1024]{1,0:T(8,128)S(1)} %get-tuple-element.75), channel_id=1, source_target_pairs={{0,64},{64,0},{1,65},{65,1},{2,66},{66,2},{3,67},{67,3},{4,68},{68... | collective-permute-start | bytes 3145736 | tf_op jit(solution)/shard_map/ppermute | solution.py:63
  57.4 25.9 %copy-start.4 = (f32[512]{0:T(512)S(1)}, f32[512]{0:T(512)}, u32[]{:S(2)}) copy-start(f32[512]{0:T(512)} %param.9) | copy-start | bytes 6148
  58.9 5.2 %collective-permute-start.20 = (f32[8,128]{1,0:T(8,128)S(1)}, f32[8,128]{1,0:T(8,128)S(1)}, u32[]{:S(2)}, u32[]{:S(2)}) collective-permute-start(f32[8,128]{1,0:T(8,128)S(1)} %get-tuple-element.76), channel_id=1, source_target_pairs={{0,1},{1,0},{2,3},{3,2},{4,5},{5,4},{6,7},{7,6},{8,9},{9,8},{10,11... | collective-permute-start | bytes 12296 | tf_op jit(solution)/shard_map/ppermute | solution.py:59
  60.6 3.6 %collective-permute-start.19 = (f32[8,128]{1,0:T(8,128)S(1)}, f32[8,128]{1,0:T(8,128)S(1)}, u32[]{:S(2)}, u32[]{:S(2)}) collective-permute-start(f32[8,128]{1,0:T(8,128)S(1)} %get-tuple-element.76), channel_id=1, source_target_pairs={{0,9},{1,8},{2,11},{3,10},{4,13},{5,12},{6,15},{7,14},{8,0},{9,1},... | collective-permute-start | bytes 12296 | tf_op jit(solution)/shard_map/ppermute | solution.py:59
  62.1 4.8 %collective-permute-start.18 = (f32[8,128]{1,0:T(8,128)S(1)}, f32[8,128]{1,0:T(8,128)S(1)}, u32[]{:S(2)}, u32[]{:S(2)}) collective-permute-start(f32[8,128]{1,0:T(8,128)S(1)} %get-tuple-element.76), channel_id=1, source_target_pairs={{0,8},{1,9},{2,10},{3,11},{4,12},{5,13},{6,14},{7,15},{8,1},{9,0},... | collective-permute-start | bytes 12296 | tf_op jit(solution)/shard_map/ppermute | solution.py:59
  67.0 5.1 %collective-permute-start.23 = (f32[8,128]{1,0:T(8,128)S(1)}, f32[8,128]{1,0:T(8,128)S(1)}, u32[]{:S(2)}, u32[]{:S(2)}) collective-permute-start(f32[8,128]{1,0:T(8,128)S(1)} %add_add_fusion.2), channel_id=1, source_target_pairs={{0,32},{1,33},{2,34},{3,35},{4,36},{5,37},{6,38},{7,39},{8,40},{9,... | collective-permute-start | bytes 12296 | tf_op jit(solution)/shard_map/ppermute | solution.py:59
  69.5 3.6 %collective-permute-start.22 = (f32[8,128]{1,0:T(8,128)S(1)}, f32[8,128]{1,0:T(8,128)S(1)}, u32[]{:S(2)}, u32[]{:S(2)}) collective-permute-start(f32[8,128]{1,0:T(8,128)S(1)} %add_add_fusion.2), channel_id=1, source_target_pairs={{0,48},{1,49},{2,50},{3,51},{4,52},{5,53},{6,54},{7,55},{8,56},{9,... | collective-permute-start | bytes 12296 | tf_op jit(solution)/shard_map/ppermute | solution.py:59
  70.7 4.8 %collective-permute-start.21 = (f32[8,128]{1,0:T(8,128)S(1)}, f32[8,128]{1,0:T(8,128)S(1)}, u32[]{:S(2)}, u32[]{:S(2)}) collective-permute-start(f32[8,128]{1,0:T(8,128)S(1)} %add_add_fusion.2), channel_id=1, source_target_pairs={{0,16},{1,17},{2,18},{3,19},{4,20},{5,21},{6,22},{7,23},{8,24},{9,... | collective-permute-start | bytes 12296 | tf_op jit(solution)/shard_map/ppermute | solution.py:59
  75.5 5.1 %collective-permute-start.26 = (f32[8,128]{1,0:T(8,128)S(1)}, f32[8,128]{1,0:T(8,128)S(1)}, u32[]{:S(2)}, u32[]{:S(2)}) collective-permute-start(f32[8,128]{1,0:T(8,128)S(1)} %add_add_fusion.1), channel_id=1, source_target_pairs={{0,4},{1,5},{2,6},{3,7},{4,0},{5,1},{6,2},{7,3},{8,12},{9,13},{10,... | collective-permute-start | bytes 12296 | tf_op jit(solution)/shard_map/ppermute | solution.py:59
  77.1 3.6 %collective-permute-start.25 = (f32[8,128]{1,0:T(8,128)S(1)}, f32[8,128]{1,0:T(8,128)S(1)}, u32[]{:S(2)}, u32[]{:S(2)}) collective-permute-start(f32[8,128]{1,0:T(8,128)S(1)} %add_add_fusion.1), channel_id=1, source_target_pairs={{0,6},{1,7},{2,0},{3,1},{4,2},{5,3},{6,4},{7,5},{8,14},{9,15},{10,... | collective-permute-start | bytes 12296 | tf_op jit(solution)/shard_map/ppermute | solution.py:59
  78.4 4.8 %collective-permute-start.24 = (f32[8,128]{1,0:T(8,128)S(1)}, f32[8,128]{1,0:T(8,128)S(1)}, u32[]{:S(2)}, u32[]{:S(2)}) collective-permute-start(f32[8,128]{1,0:T(8,128)S(1)} %add_add_fusion.1), channel_id=1, source_target_pairs={{0,2},{1,3},{2,4},{3,5},{4,6},{5,7},{6,0},{7,1},{8,10},{9,11},{10,... | collective-permute-start | bytes 12296 | tf_op jit(solution)/shard_map/ppermute | solution.py:59
  83.7 2.7 %collective-permute-start.27 = (bf16[256,2048]{1,0:T(8,128)(2,1)S(1)}, bf16[256,2048]{1,0:T(8,128)(2,1)S(1)}, u32[]{:S(2)}, u32[]{:S(2)}) collective-permute-start(bf16[256,2048]{1,0:T(8,128)(2,1)S(1)} %get-tuple-element.82.gap.own), channel_id=1, source_target_pairs={{0,64},{64,0},{1,65},{65,1},{2,66},{66,2},{3,67},{67,3},{4,68},{68... | collective-permute-start | bytes 3145736 | tf_op jit(solution)/shard_map/ppermute | solution.py:63
  83.8 2.6 %collective-permute-start.28 = (f32[2,128]{1,0:T(2,128)S(1)}, f32[2,128]{1,0:T(2,128)S(1)}, u32[]{:S(2)}, u32[]{:S(2)}) collective-permute-start(f32[2,128]{1,0:T(2,128)S(1)} %get-tuple-element.81), channel_id=1, source_target_pairs={{0,64},{64,0},{1,65},{65,1},{2,66},{66,2},{3,67},{67,3},{4,68},{68... | collective-permute-start | bytes 3080 | tf_op jit(solution)/shard_map/ppermute | solution.py:63
  89.7 9.8 %collective-permute-start.29 = (bf16[128,1792]{1,0:T(8,128)(2,1)S(1)}, bf16[128,1792]{1,0:T(8,128)(2,1)S(1)}, u32[]{:S(2)}, u32[]{:S(2)}) collective-permute-start(bf16[128,1792]{1,0:T(8,128)(2,1)S(1)} %get-tuple-element.89), channel_id=1, source_target_pairs={{0,9},{1,8},{2,11},{3,10},{4,13},{5,12},{6,15},{7,14},{8,0},{9,1},... | collective-permute-start | bytes 1376264 | tf_op jit(solution)/shard_map/ppermute | solution.py:59
  89.8 14.6 %collective-permute-start.30 = (bf16[128,1792]{1,0:T(8,128)(2,1)S(1)}, bf16[128,1792]{1,0:T(8,128)(2,1)S(1)}, u32[]{:S(2)}, u32[]{:S(2)}) collective-permute-start(bf16[128,1792]{1,0:T(8,128)(2,1)S(1)} %get-tuple-element.90), channel_id=1, source_target_pairs={{0,8},{1,9},{2,10},{3,11},{4,12},{5,13},{6,14},{7,15},{8,1},{9,0},... | collective-permute-start | bytes 1376264 | tf_op jit(solution)/shard_map/ppermute | solution.py:59
  91.8 12.7 %collective-permute-start.31 = (bf16[128,1792]{1,0:T(8,128)(2,1)S(1)}, bf16[128,1792]{1,0:T(8,128)(2,1)S(1)}, u32[]{:S(2)}, u32[]{:S(2)}) collective-permute-start(bf16[128,1792]{1,0:T(8,128)(2,1)S(1)} %get-tuple-element.91), channel_id=1, source_target_pairs={{0,1},{1,0},{2,3},{3,2},{4,5},{5,4},{6,7},{7,6},{8,9},{9,8},{10,11... | collective-permute-start | bytes 1376264 | tf_op jit(solution)/shard_map/ppermute | solution.py:59
  105.4 13.3 %all-to-all-start = ((bf16[16,8,1792]{2,1,0:T(8,128)(2,1)}), bf16[16,8,1792]{2,1,0:T(8,128)(2,1)S(1)}, u32[]{:S(2)}, u32[]{:S(2)}) async-start(bf16[16,8,1792]{2,1,0:T(8,128)(2,1)} %bitcast.2), calls=%async_computation | async-start | bytes 917504 | tf_op jit(solution)/shard_map/all_to_all | solution.py:541
